TPU v7x, 32 devices: a whole 2x2x4 slice. The times are simulated.
32 devices in a mesh: row: 4 (over z), col: 8 (over y, x, core).
Axes of the slice: x: 2, y: 2, z: 4, core: 2. Of those that a mesh axis runs over, the one named last changes fastest.
Arguments:
- field: bfloat16 [64, 256, 512], P('row', 'col'), may hold values from -6 to 6
- cotangent: bfloat16 [64, 256, 512], P('row', 'col'), may hold values from -6 to 6
- gains: float32 [2, 512], replicated, may hold values from 0.1 to 1.9
- weights: bfloat16 [2, 4, 512, 512], replicated, as said below
Outputs:
- output: bfloat16 [64, 256, 512], P('row', 'col')
- field_grad: bfloat16 [64, 256, 512], P('row', 'col')
- weight_grad: float32 [8, 512, 512], P(None, ('row', 'col'))
Inputs may be any that keep to these rules, and one draw needn't show every extreme that they name: `weights`: finite projection matrices, one per block and role.
All inputs are finite; a program needn't handle non-finite values.
Results may differ from a plain program's by a relative error of at most 0.014.
Values may be sent and summed in bfloat16 or wider, within the bound.
No kernel may reach another device: no remote copies, remote signals or barrier semaphores. Data moves between devices by JAX's collectives and lax.ppermute only.
A program may use at most 128 MiB of HBM per device.

v0:
```python
import functools

import jax
import jax.numpy as jnp
from jax import lax
from jax.experimental import pallas as pl
from jax.experimental.pallas import tpu as pltpu
from jax.sharding import PartitionSpec as P

HEADS = 8
eps = 1e-05
F32 = jnp.float32
BF16 = jnp.bfloat16


def log2(n):
    assert n & (n - 1) == 0
    return n.bit_length() - 1


def dot(left, right):
    return jnp.dot(left, right, preferred_element_type=F32)


def dot_nt(left, right):
    return lax.dot_general(left, right, (((1,), (1,)), ((), ())), preferred_element_type=F32)


def dot_tn(left, right):
    return lax.dot_general(left, right, (((0,), (0,)), ((), ())), preferred_element_type=F32)


def digits(index, sizes):
    out = []
    for size in reversed(sizes):
        out.append(index & (size - 1))
        index = index >> log2(size)
    return out[::-1]


def reorder(sizes, order, transposed=False):
    total = 1
    for size in sizes:
        total *= size
    out_axis, in_axis = (1, 0) if transposed else (0, 1)
    index = lax.broadcasted_iota(jnp.int32, (total, total), out_axis)
    found = digits(index, [sizes[axis] for axis in order])
    source = jnp.zeros_like(index)
    for axis, size in enumerate(sizes):
        source = source * size + found[order.index(axis)]
    hit = source == lax.broadcasted_iota(jnp.int32, (total, total), in_axis)
    return jnp.where(hit, 1.0, 0.0).astype(BF16)


def statistics(values):
    average = jnp.mean(values, axis=-1, keepdims=True)
    centred = values - average
    spread = jnp.mean(centred * centred, axis=-1, keepdims=True)
    return centred, lax.rsqrt(spread + eps)


def norm_back(values, gain, d_normed):
    centred, inverse = statistics(values)
    unit = centred * inverse
    scaled = d_normed * gain
    return inverse * (
        scaled
        - jnp.mean(scaled, axis=-1, keepdims=True)
        - unit * jnp.mean(scaled * unit, axis=-1, keepdims=True)
    )


def head_lanes(count, width):
    return lax.broadcasted_iota(jnp.int32, (count, 2 * width), 1) < width


def attention_forward(q_ref, k_ref, v_ref, att_ref, p_ref, groups, count, width, span):
    first = head_lanes(count, width)
    pairs = HEADS // 2

    def step(index, carry):
        group, pair = index // pairs, index % pairs
        rows = pl.ds(pl.multiple_of(group * count, count), count)
        lanes = pl.ds(pl.multiple_of(pair * 2 * width, 2 * width), 2 * width)
        query, key, value = q_ref[rows, lanes], k_ref[rows, lanes], v_ref[rows, lanes]
        total = jnp.zeros((count, 2 * width), F32)
        for half in range(2):
            mine = first if half == 0 else jnp.logical_not(first)
            scores = dot_nt(jnp.where(mine, query, jnp.zeros_like(query)), key)
            scores = scores * (width ** (-0.5))
            if span < count:
                shift = log2(span)
                same = (lax.broadcasted_iota(jnp.int32, (count, count), 0) >> shift) == (
                    lax.broadcasted_iota(jnp.int32, (count, count), 1) >> shift
                )
                scores = jnp.where(same, scores, -jnp.inf)
            expo = jnp.exp(scores - jnp.max(scores, axis=-1, keepdims=True))
            probs = (expo * (1.0 / jnp.sum(expo, axis=-1, keepdims=True))).astype(BF16)
            p_ref[index * 2 + half] = probs
            total += dot(probs, jnp.where(mine, value, jnp.zeros_like(value)))
        att_ref[rows, lanes] = total.astype(BF16)
        return carry

    lax.fori_loop(0, groups * pairs, step, 0)


def attention_back(q_ref, k_ref, v_ref, p_ref, da_ref, dqkv_ref, groups, count, width):
    first = head_lanes(count, width)
    pairs = HEADS // 2
    channels = HEADS * width

    def step(index, carry):
        group, pair = index // pairs, index % pairs
        rows = pl.ds(pl.multiple_of(group * count, count), count)
        lanes = pl.ds(pl.multiple_of(pair * 2 * width, 2 * width), 2 * width)
        query, key, value = q_ref[rows, lanes], k_ref[rows, lanes], v_ref[rows, lanes]
        d_out = da_ref[rows, lanes]
        zero = jnp.zeros_like(query)
        d_query = jnp.zeros((count, 2 * width), F32)
        d_key, d_value = d_query, d_query
        for half in range(2):
            mine = first if half == 0 else jnp.logical_not(first)
            probs = p_ref[index * 2 + half]
            d_mine = jnp.where(mine, d_out, zero)
            d_probs = dot_nt(d_mine, value)
            probs32 = probs.astype(F32)
            weighted = probs32 * d_probs
            total = jnp.sum(weighted, axis=-1, keepdims=True)
            d_scores = ((weighted - probs32 * total) * (width ** (-0.5))).astype(BF16)
            d_query += dot(d_scores, jnp.where(mine, key, zero))
            d_key += dot_tn(d_scores, jnp.where(mine, query, zero))
            d_value += dot_tn(probs, d_mine)
        for part, item in enumerate((d_query, d_key, d_value)):
            at = pl.ds(pl.multiple_of(part * channels + pair * 2 * width, 2 * width), 2 * width)
            dqkv_ref[rows, at] = item.astype(BF16)
        return carry

    lax.fori_loop(0, groups * pairs, step, 0)


def weight_grads(normed, attended, dqkv_ref, d_top, grads_ref, shards):
    channels = normed.shape[-1]
    row_parts, plane, core, piece = shards
    turn = reorder((row_parts, plane, core, piece), (2, 1, 0, 3), transposed=True)
    normed = dot(normed, turn).astype(BF16)
    attended = dot(attended, turn).astype(BF16)
    size = row_parts * piece
    for part in range(4):
        if part < 3:
            whole = dot_tn(normed, dqkv_ref[:, part * channels : (part + 1) * channels])
        else:
            whole = dot_tn(attended, d_top)
        whole = whole.astype(BF16)
        for group in range(plane * core):
            grads_ref[group, part] = whole[group * size : (group + 1) * size]


def input_back(dqkv_ref, w_ref):
    channels = w_ref.shape[-1]
    total = dot_nt(dqkv_ref[:, :channels], w_ref[0, 0])
    total += dot_nt(dqkv_ref[:, channels : 2 * channels], w_ref[0, 1])
    total += dot_nt(dqkv_ref[:, 2 * channels :], w_ref[0, 2])
    return total.astype(BF16).astype(F32)


def project_in(values, gain, w_ref, n_ref, q_ref, k_ref, v_ref):
    centred, inverse = statistics(values)
    normed = (centred * inverse * gain).astype(BF16)
    n_ref[...] = normed
    q_ref[...] = dot(normed, w_ref[0, 0]).astype(BF16)
    k_ref[...] = dot(normed, w_ref[0, 1]).astype(BF16)
    v_ref[...] = dot(normed, w_ref[0, 2]).astype(BF16)


def row_forward(sizes, x_ref, g_ref, w_ref, mid_ref, n_ref, q_ref, k_ref, v_ref, att_ref, p_ref):
    rows, col_parts, row_parts, cols, width = sizes
    channels = x_ref.shape[-1]
    length = col_parts * row_parts * cols
    field = jnp.concatenate([x_ref[:, i].reshape(length, channels) for i in range(rows)], axis=0)
    field = field.astype(F32)
    project_in(field, g_ref[0:1], w_ref, n_ref, q_ref, k_ref, v_ref)
    attention_forward(q_ref, k_ref, v_ref, att_ref, p_ref, rows, length, width, length)
    middle = (field + dot(att_ref[...], w_ref[0, 3])).astype(BF16)
    turn = reorder((rows, col_parts, row_parts, cols), (2, 1, 0, 3))
    mid_ref[...] = dot(turn, middle).astype(BF16)


def row_back(sizes, shards, d_ref, x_ref, g_ref, w_ref, n_ref, q_ref, k_ref, v_ref, att_ref, p_ref,
             fg_ref, grads_ref, da_ref, dqkv_ref):
    rows, col_parts, row_parts, cols, width = sizes
    channels = x_ref.shape[-1]
    length = col_parts * row_parts * cols
    turn = reorder((row_parts, col_parts, rows, cols), (2, 1, 0, 3))
    d_middle = dot(turn, d_ref[...]).astype(BF16)
    da_ref[...] = dot_nt(d_middle, w_ref[0, 3]).astype(BF16)
    attention_back(q_ref, k_ref, v_ref, p_ref, da_ref, dqkv_ref, rows, length, width)
    weight_grads(n_ref[...], att_ref[...], dqkv_ref, d_middle, grads_ref, shards)
    d_normed = input_back(dqkv_ref, w_ref)
    field = jnp.concatenate([x_ref[:, i].reshape(length, channels) for i in range(rows)], axis=0)
    result = d_middle.astype(F32) + norm_back(field.astype(F32), g_ref[0:1], d_normed)
    result = result.astype(BF16)
    for i in range(rows):
        piece = result[i * length : (i + 1) * length]
        fg_ref[:, i] = piece.reshape(col_parts, row_parts * cols, channels)


def column_both(sizes, shards, m_ref, c_ref, g_ref, w_ref, out_ref, dm_ref, grads_ref,
                n_ref, q_ref, k_ref, v_ref, att_ref, p_ref, da_ref, dqkv_ref):
    height, cols, width, together = sizes
    turn = reorder((height, cols), (1, 0))
    turn_back = reorder((height, cols), (1, 0), transposed=True)
    middle = dot(turn, m_ref[...])
    cotangent = dot(turn, c_ref[...]).astype(BF16)
    project_in(middle, g_ref[1:2], w_ref, n_ref, q_ref, k_ref, v_ref)
    count = together * height
    groups = cols // together
    attention_forward(q_ref, k_ref, v_ref, att_ref, p_ref, groups, count, width, height)
    output = (middle + dot(att_ref[...], w_ref[0, 3])).astype(BF16)
    out_ref[...] = dot(turn_back, output).astype(BF16)
    da_ref[...] = dot_nt(cotangent, w_ref[0, 3]).astype(BF16)
    attention_back(q_ref, k_ref, v_ref, p_ref, da_ref, dqkv_ref, groups, count, width)
    weight_grads(n_ref[...], att_ref[...], dqkv_ref, cotangent, grads_ref, shards)
    d_normed = input_back(dqkv_ref, w_ref)
    d_middle = cotangent.astype(F32) + norm_back(middle, g_ref[1:2], d_normed)
    dm_ref[...] = dot(turn_back, d_middle.astype(BF16)).astype(BF16)


def call(kernel, outs, scratch, args, block, flops):
    def whole(shape):
        return pl.BlockSpec(shape, lambda i: (0,) * len(shape))

    specs = []
    for arg in args:
        if arg.ndim == 4 and arg.shape[0] == 2 and arg.shape[1] == 4 and arg.shape[2] == arg.shape[3]:
            specs.append(pl.BlockSpec((1,) + arg.shape[1:], lambda i: (block, 0, 0, 0)))
        else:
            specs.append(whole(arg.shape))
    moved = sum(item.size * item.dtype.itemsize for item in list(args) + list(outs))
    return pl.pallas_call(
        kernel,
        grid=(1,),
        in_specs=specs,
        out_specs=[whole(item.shape) for item in outs],
        out_shape=outs,
        scratch_shapes=scratch,
        compiler_params=pltpu.CompilerParams(
            dimension_semantics=("arbitrary",), vmem_limit_bytes=40 * 1024 * 1024
        ),
        cost_estimate=pl.CostEstimate(flops=flops, bytes_accessed=moved, transcendentals=0),
    )(*args)


def reduce_grads(grads, row_parts, plane, core):
    groups, parts, size, channels = grads.shape
    total = plane * core
    pairs = [[p * core + c for c in range(core)] for p in range(plane)]
    planes = [[p * core + c for p in range(plane)] for c in range(core)]
    got = lax.all_to_all(
        grads.reshape(core, plane, parts, size, channels), "col", 0, 0, axis_index_groups=pairs, tiled=True
    )
    held = jnp.sum(got.astype(F32), axis=0).astype(BF16)
    got = lax.all_to_all(held, "col", 0, 0, axis_index_groups=planes, tiled=True)
    held = jnp.sum(got.astype(F32), axis=0).astype(BF16)
    held = held.reshape(parts, row_parts, size // row_parts, channels).transpose(1, 0, 2, 3)
    got = lax.all_to_all(held, "row", 0, 0, tiled=True)
    return jnp.sum(got.astype(F32), axis=0)


def body(row_parts, col_parts, field, cotangent, gains, weights):
    high, wide, channels = field.shape
    core = 2
    plane = col_parts // core
    rows = high // col_parts
    cols = wide // row_parts
    tokens = high * wide
    height = high * row_parts
    length = wide * col_parts
    width = channels // HEADS
    together = min(cols, max(1, 256 // height))
    devices = row_parts * col_parts
    shards = (row_parts, plane, core, channels // devices)

    def like(*shape, dtype=BF16):
        return jax.ShapeDtypeStruct(shape, dtype)

    flat = like(tokens, channels)
    x = lax.all_to_all(field.reshape(col_parts, rows, wide, channels), "col", 0, 0, tiled=True)
    cot = cotangent.reshape(high, row_parts, cols, channels).transpose(1, 0, 2, 3)
    cot = lax.all_to_all(cot, "row", 0, 0, tiled=True).reshape(tokens, channels)

    sizes = (rows, col_parts, row_parts, cols, width)
    probs = like(rows * HEADS, length, length)
    unit = 2 * tokens * channels * channels
    mid, *saved = call(
        functools.partial(row_forward, sizes),
        [flat, flat, flat, flat, flat, flat, probs], [], (x, gains, weights), 0, 5 * unit,
    )
    mid = lax.all_to_all(
        mid.reshape(devices, rows * cols, channels), ("row", "col"), 0, 0, tiled=True
    ).reshape(tokens, channels)

    count = together * height
    scratch = [pltpu.VMEM((tokens, channels), BF16) for _ in range(5)]
    scratch += [
        pltpu.VMEM((cols // together * HEADS, count, count), BF16),
        pltpu.VMEM((tokens, channels), BF16),
        pltpu.VMEM((tokens, 3 * channels), BF16),
    ]
    packed = like(col_parts, 4, channels // col_parts, channels)
    out, d_mid, grads_b = call(
        functools.partial(column_both, (height, cols, width, together), shards),
        [flat, flat, packed], scratch, (mid, cot, gains, weights), 1, 18 * unit,
    )
    d_mid = lax.all_to_all(
        d_mid.reshape(devices, rows * cols, channels), ("row", "col"), 0, 0, tiled=True
    ).reshape(tokens, channels)
    out = lax.all_to_all(out.reshape(row_parts, high, cols, channels), "row", 0, 0, tiled=True)
    output = out.transpose(1, 0, 2, 3).reshape(high, wide, channels)

    scratch = [pltpu.VMEM((tokens, channels), BF16), pltpu.VMEM((tokens, 3 * channels), BF16)]
    field_grad, grads_a = call(
        functools.partial(row_back, sizes, shards),
        [like(col_parts, rows, wide, channels), packed], scratch,
        (d_mid, x, gains, weights, *saved), 0, 12 * unit,
    )
    field_grad = lax.all_to_all(field_grad, "col", 0, 0, tiled=True).reshape(high, wide, channels)
    weight_grad = jnp.concatenate(
        [reduce_grads(grads_a, row_parts, plane, core), reduce_grads(grads_b, row_parts, plane, core)], axis=0
    )
    return output, field_grad, weight_grad


def solution(mesh):
    return jax.shard_map(
        functools.partial(body, mesh.shape["row"], mesh.shape["col"]),
        mesh=mesh,
        in_specs=(P("row", "col", None), P("row", "col", None), P(), P()),
        out_specs=(P("row", "col", None), P("row", "col", None), P(None, ("row", "col"), None)),
        check_vma=False,
    )
```

profile of v0, /device:TPU:0, one launch (start us, length us, event | category | flops | bytes accessed | tf_op | source)
XLA Modules:
  0.0 202.5 jit_solution(2897732033842278916)
XLA Ops:
  0.7 5.3 %all-to-all-start = ((bf16[8,2,32,512]{3,2,1,0:T(8,128)(2,1)}), bf16[8,2,32,512]{3,2,1,0:T(8,128)(2,1)S(1)}, u32[]{:S(2)}, u32[]{:S(2)}) async-start(bf16[8,2,32,512]{3,2,1,0:T(8,128)(2,1)} %bitcast.36), calls=%async_computation | async-start | bytes 1048576 | tf_op jit(solution)/shard_map/all_to_all | solution.py:287
  6.8 8.9 %all-to-all-done.x_ref = bf16[8,2,32,512]{3,2,1,0:T(8,128)(2,1)S(1)} async-done(((bf16[8,2,32,512]{3,2,1,0:T(8,128)(2,1)}), bf16[8,2,32,512]{3,2,1,0:T(8,128)(2,1)S(1)}, u32[]{:S(2)}, u32[]{:S(2)}) %all-to-all-start) | async-done | bytes 524320 | tf_op jit(solution)/shard_map/all_to_all | solution.py:287
  15.7 4.9 %all-to-all-start.2 = ((bf16[4,16,8,512]{3,2,1,0:T(8,128)(2,1)}), bf16[4,16,8,512]{3,2,1,0:T(8,128)(2,1)S(1)}, u32[]{:S(2)}, u32[]{:S(2)}) async-start(bf16[4,16,8,512]{3,2,1,0:T(8,128)(2,1)} %copy_bitcast_fusion.1), calls=%async_computation.2 | async-start | bytes 1048576 | tf_op jit(solution)/shard_map/all_to_all | solution.py:289
  20.6 2.2 %copy-done.2 = bf16[2,4,512,512]{3,2,1,0:T(8,128)(2,1)S(1)} copy-done((bf16[2,4,512,512]{3,2,1,0:T(8,128)(2,1)S(1)}, bf16[2,4,512,512]{3,2,1,0:T(8,128)(2,1)}, u32[]{:S(2)}) %copy-start.2) | copy-done | bytes 4194328
  22.8 6.4 %shard_map.67 = (bf16[512,512]{1,0:T(8,128)(2,1)S(1)}, bf16[512,512]{1,0:T(8,128)(2,1)S(1)}, bf16[512,512]{1,0:T(8,128)(2,1)S(1)}, bf16[512,512]{1,0:T(8,128)(2,...) custom-call(bf16[8,2,32,512]{3,2,1,0:T(8,128)(2,1)S(1)} %all-to-all-done.x_ref, ...), custom_call_target="tpu_custom_call" | custom-call | flops 1342177280 | bytes 9965568 | tf_op jit(solution)/shard_map/pallas_call | solution.py:239
  33.0 19.5 %all_to_all.60 = bf16[32,16,512]{2,1,0:T(8,128)(2,1)S(1)} all-to-all(bf16[32,16,512]{2,1,0:T(8,128)(2,1)S(1)} %bitcast.30), channel_id=1, replica_groups=mesh['row'=4,'col'=8] {'row','col'}, dimensions={0} | all-to-all | bytes 1048576 | tf_op jit(solution)/shard_map/all_to_all | solution.py:298
  52.5 2.2 %copy-done.3 = bf16[2,4,512,512]{3,2,1,0:T(8,128)(2,1)S(1)} copy-done((bf16[2,4,512,512]{3,2,1,0:T(8,128)(2,1)S(1)}, bf16[2,4,512,512]{3,2,1,0:T(8,128)(2,1)}, u32[]{:S(2)}) %copy-start.3) | copy-done | bytes 4194328
  54.7 15.9 %shard_map.68 = (bf16[512,512]{1,0:T(8,128)(2,1)}, bf16[512,512]{1,0:T(8,128)(2,1)S(1)}, bf16[8,4,64,512]{3,2,1,0:T(8,128)(2,1)S(1)}) custom-call(bf16[512,512]{1,0:T(8,128)(2,1)S(1)} %bitcast.32, bf16[512,512]{1,0:T(8,128)(2,1)S(1)} %bitcast.28, f32[2,512]{1,0:T(2,128)S(1)} %copy-done.5, bf16[2,4,512,512]{3,2,1,0:T(8,128)(2,1)S(1)} %copy-done.3), custom_call_target="tpu_custom_call" | custom-call | flops 4831838208 | bytes 8392704 | tf_op jit(solution)/shard_map/pallas_call | solution.py:239
  70.6 6.3 %all_to_all.61 = bf16[2,4,4,64,512]{4,3,2,1,0:T(8,128)(2,1)} all-to-all(bf16[2,4,4,64,512]{4,3,2,1,0:T(8,128)(2,1)S(1)} %bitcast.27), channel_id=1, replica_groups={{0,1},{2,3},{4,5},{6,7},{8,9},{10,11},{12,13},{14,15},{16,17},{18,19},{..., dimensions={0} | all-to-all | bytes 4194304 | tf_op jit(solution)/shard_map/all_to_all | solution.py:258
  76.9 3.3 %reduce_sum.69 = bf16[4,4,64,512]{3,2,1,0:T(8,128)(2,1)} reduce(bf16[2,4,4,64,512]{4,3,2,1,0:T(8,128)(2,1)} %all_to_all.61, bf16[]{:T(256)} %constant.5.clone.1), dimensions={0}, to_apply=%region_3.0 | reduce | flops 524288 | bytes 3145730 | tf_op jit(solution)/shard_map/reduce_sum | solution.py:261
  80.2 18.2 %all_to_all.62 = bf16[4,4,64,512]{3,2,1,0:T(8,128)(2,1)S(1)} all-to-all(bf16[4,4,64,512]{3,2,1,0:T(8,128)(2,1)} %reduce_sum.69), channel_id=1, replica_groups={{0,2,4,6},{1,3,5,7},{8,10,12,14},{9,11,13,15},{16,18,20,22},{17,19,21,2..., dimensions={0} | all-to-all | bytes 2097152 | tf_op jit(solution)/shard_map/all_to_all | solution.py:262
  98.4 17.9 %all_to_all.63 = bf16[32,16,512]{2,1,0:T(8,128)(2,1)} all-to-all(bf16[32,16,512]{2,1,0:T(8,128)(2,1)S(1)} %bitcast.31), channel_id=1, replica_groups=mesh['row'=4,'col'=8] {'row','col'}, dimensions={0} | all-to-all | bytes 1048576 | tf_op jit(solution)/shard_map/all_to_all | solution.py:314
  116.3 4.3 %all-to-all-start.3 = ((bf16[4,16,8,512]{3,2,1,0:T(8,128)(2,1)}), bf16[4,16,8,512]{3,2,1,0:T(8,128)(2,1)}, u32[]{:S(2)}, u32[]{:S(2)}) async-start(bf16[4,16,8,512]{3,2,1,0:T(8,128)(2,1)} %bitcast.6), calls=%async_computation.3 | async-start | bytes 1048576 | tf_op jit(solution)/shard_map/all_to_all | solution.py:317
  122.6 2.2 %copy-done.4 = bf16[2,4,512,512]{3,2,1,0:T(8,128)(2,1)S(1)} copy-done((bf16[2,4,512,512]{3,2,1,0:T(8,128)(2,1)S(1)}, bf16[2,4,512,512]{3,2,1,0:T(8,128)(2,1)}, u32[]{:S(2)}) %copy-start.4) | copy-done | bytes 4194328
  131.6 10.1 %shard_map.69 = (bf16[8,2,32,512]{3,2,1,0:T(8,128)(2,1)}, bf16[8,4,64,512]{3,2,1,0:T(8,128)(2,1)S(1)}) custom-call(bf16[512,512]{1,0:T(8,128)(2,1)S(1)} %bitcast.29, bf16[8,2,32,512]{3,2,1,0:T(8,128)(2,1)S(1)} %all-to-all-done.x_ref, f32[2,512]{1,0:T(2,128)S(1)} %copy-done.5, bf16[2,4,512,512]{3,2,1,0:T(8,128)(2,1)S(1)} %copy-done.4, ...), custom_call_target="tpu_custom_call" | custom-call | flops 3221225472 | bytes 12587008 | tf_op jit(solution)/shard_map/pallas_call | solution.py:239
  141.7 6.3 %all_to_all.64 = bf16[2,4,4,64,512]{4,3,2,1,0:T(8,128)(2,1)} all-to-all(bf16[2,4,4,64,512]{4,3,2,1,0:T(8,128)(2,1)S(1)} %bitcast.26), channel_id=1, replica_groups={{0,1},{2,3},{4,5},{6,7},{8,9},{10,11},{12,13},{14,15},{16,17},{18,19},{..., dimensions={0} | all-to-all | bytes 4194304 | tf_op jit(solution)/shard_map/all_to_all | solution.py:258
  147.9 4.9 %all-to-all-start.11 = ((bf16[4,4,16,512]{3,2,1,0:T(8,128)(2,1)}), bf16[4,4,16,512]{3,2,1,0:T(8,128)(2,1)S(1)}, u32[]{:S(2)}, u32[]{:S(2)}) async-start(bf16[4,4,16,512]{3,2,1,0:T(8,128)(2,1)} %copy.18), calls=%async_computation.11 | async-start | bytes 524288 | tf_op jit(solution)/shard_map/all_to_all | solution.py:265
  152.8 2.1 %reduce_sum.66 = bf16[4,4,64,512]{3,2,1,0:T(8,128)(2,1)S(1)} reduce(bf16[2,4,4,64,512]{4,3,2,1,0:T(8,128)(2,1)} %all_to_all.64, bf16[]{:T(256)} %constant.5.clone.1), dimensions={0}, to_apply=%region_0.0 | reduce | flops 524288 | bytes 3145730 | tf_op jit(solution)/shard_map/reduce_sum | solution.py:261
  154.9 7.1 %all-to-all-done.11 = bf16[4,4,16,512]{3,2,1,0:T(8,128)(2,1)S(1)} async-done(((bf16[4,4,16,512]{3,2,1,0:T(8,128)(2,1)}), bf16[4,4,16,512]{3,2,1,0:T(8,128)(2,1)S(1)}, u32[]{:S(2)}, u32[]{:S(2)}) %all-to-all-start.11) | async-done | bytes 262176 | tf_op jit(solution)/shard_map/all_to_all | solution.py:265
  162.0 15.3 %all_to_all.65 = bf16[4,4,64,512]{3,2,1,0:T(8,128)(2,1)S(1)} all-to-all(bf16[4,4,64,512]{3,2,1,0:T(8,128)(2,1)S(1)} %reduce_sum.66), channel_id=1, replica_groups={{0,2,4,6},{1,3,5,7},{8,10,12,14},{9,11,13,15},{16,18,20,22},{17,19,21,2..., dimensions={0} | all-to-all | bytes 2097152 | tf_op jit(solution)/shard_map/all_to_all | solution.py:262
  177.3 3.5 %all-to-all-start.5 = ((bf16[8,2,32,512]{3,2,1,0:T(8,128)(2,1)}), bf16[8,2,32,512]{3,2,1,0:T(8,128)(2,1)S(1)}, u32[]{:S(2)}, u32[]{:S(2)}) async-start(bf16[8,2,32,512]{3,2,1,0:T(8,128)(2,1)} %get-tuple-element.24), calls=%async_computation.5 | async-start | bytes 1048576 | tf_op jit(solution)/shard_map/all_to_all | solution.py:326
  181.7 8.7 %all-to-all-done.5 = bf16[8,2,32,512]{3,2,1,0:T(8,128)(2,1)S(1)} async-done(((bf16[8,2,32,512]{3,2,1,0:T(8,128)(2,1)}), bf16[8,2,32,512]{3,2,1,0:T(8,128)(2,1)S(1)}, u32[]{:S(2)}, u32[]{:S(2)}) %all-to-all-start.5) | async-done | bytes 524320 | tf_op jit(solution)/shard_map/all_to_all | solution.py:326
  190.5 3.7 %all-to-all-start.8 = ((bf16[4,4,16,512]{3,2,1,0:T(8,128)(2,1)}), bf16[4,4,16,512]{3,2,1,0:T(8,128)(2,1)S(1)}, u32[]{:S(2)}, u32[]{:S(2)}) async-start(bf16[4,4,16,512]{3,2,1,0:T(8,128)(2,1)} %copy.17), calls=%async_computation.8 | async-start | bytes 524288 | tf_op jit(solution)/shard_map/all_to_all | solution.py:265
  196.1 4.8 %all-to-all-done.8 = bf16[4,4,16,512]{3,2,1,0:T(8,128)(2,1)S(1)} async-done(((bf16[4,4,16,512]{3,2,1,0:T(8,128)(2,1)}), bf16[4,4,16,512]{3,2,1,0:T(8,128)(2,1)S(1)}, u32[]{:S(2)}, u32[]{:S(2)}) %all-to-all-start.8) | async-done | bytes 262176 | tf_op jit(solution)/shard_map/all_to_all | solution.py:265
  (45 shorter events, 17.8 us)
Async XLA Ops:
  0.6 5.3 %copy-start = (bf16[16,32,512]{2,1,0:T(8,128)(2,1)S(1)}, bf16[16,32,512]{2,1,0:T(8,128)(2,1)}, u32[]{:S(2)}) copy-start(bf16[16,32,512]{2,1,0:T(8,128)(2,1)} %param.5) | copy-start | bytes 1572868
  0.6 19.9 %copy-start.5 = (f32[2,512]{1,0:T(2,128)S(1)}, f32[2,512]{1,0:T(2,128)}, u32[]{:S(2)}) copy-start(f32[2,512]{1,0:T(2,128)} %g_ref.5) | copy-start | bytes 12292
  0.7 15.1 %all-to-all-start = ((bf16[8,2,32,512]{3,2,1,0:T(8,128)(2,1)}), bf16[8,2,32,512]{3,2,1,0:T(8,128)(2,1)S(1)}, u32[]{:S(2)}, u32[]{:S(2)}) async-start(bf16[8,2,32,512]{3,2,1,0:T(8,128)(2,1)} %bitcast.36), calls=%async_computation | async-start | bytes 1048576 | tf_op jit(solution)/shard_map/all_to_all | solution.py:287
  15.7 17.3 %all-to-all-start.2 = ((bf16[4,16,8,512]{3,2,1,0:T(8,128)(2,1)}), bf16[4,16,8,512]{3,2,1,0:T(8,128)(2,1)S(1)}, u32[]{:S(2)}, u32[]{:S(2)}) async-start(bf16[4,16,8,512]{3,2,1,0:T(8,128)(2,1)} %copy_bitcast_fusion.1), calls=%async_computation.2 | async-start | bytes 1048576 | tf_op jit(solution)/shard_map/all_to_all | solution.py:289
  20.6 2.2 %copy-start.2 = (bf16[2,4,512,512]{3,2,1,0:T(8,128)(2,1)S(1)}, bf16[2,4,512,512]{3,2,1,0:T(8,128)(2,1)}, u32[]{:S(2)}) copy-start(bf16[2,4,512,512]{3,2,1,0:T(8,128)(2,1)} %w_ref.5) | copy-start | bytes 12582916
  29.2 1.3 copy-start.6
  30.5 0.8 copy-start.8
  31.3 0.8 copy-start.14
  32.2 0.8 copy-start.16
  33.0 37.6 %copy-start.10 = (bf16[512,512]{1,0:T(8,128)(2,1)}, bf16[512,512]{1,0:T(8,128)(2,1)S(1)}, u32[]{:S(2)}) copy-start(bf16[512,512]{1,0:T(8,128)(2,1)S(1)} %get-tuple-element.19.q_ref) | copy-start | bytes 1572868
  33.0 37.6 %copy-start.12 = (bf16[512,512]{1,0:T(8,128)(2,1)}, bf16[512,512]{1,0:T(8,128)(2,1)S(1)}, u32[]{:S(2)}) copy-start(bf16[512,512]{1,0:T(8,128)(2,1)S(1)} %get-tuple-element.20.k_ref) | copy-start | bytes 1572868
  52.5 2.2 %copy-start.3 = (bf16[2,4,512,512]{3,2,1,0:T(8,128)(2,1)S(1)}, bf16[2,4,512,512]{3,2,1,0:T(8,128)(2,1)}, u32[]{:S(2)}) copy-start(bf16[2,4,512,512]{3,2,1,0:T(8,128)(2,1)} %w_ref.5) | copy-start | bytes 12582916
  116.3 25.4 %all-to-all-start.3 = ((bf16[4,16,8,512]{3,2,1,0:T(8,128)(2,1)}), bf16[4,16,8,512]{3,2,1,0:T(8,128)(2,1)}, u32[]{:S(2)}, u32[]{:S(2)}) async-start(bf16[4,16,8,512]{3,2,1,0:T(8,128)(2,1)} %bitcast.6), calls=%async_computation.3 | async-start | bytes 1048576 | tf_op jit(solution)/shard_map/all_to_all | solution.py:317
  121.6 1.0 copy-start.1
  122.6 2.2 %copy-start.4 = (bf16[2,4,512,512]{3,2,1,0:T(8,128)(2,1)S(1)}, bf16[2,4,512,512]{3,2,1,0:T(8,128)(2,1)}, u32[]{:S(2)}) copy-start(bf16[2,4,512,512]{3,2,1,0:T(8,128)(2,1)} %w_ref.5) | copy-start | bytes 12582916
  124.8 1.6 copy-start.7
  126.4 1.0 copy-start.9
  127.4 1.0 copy-start.11
  128.5 1.0 copy-start.13
  129.5 1.0 copy-start.15
  130.5 1.0 copy-start.17
  147.9 14.1 %all-to-all-start.11 = ((bf16[4,4,16,512]{3,2,1,0:T(8,128)(2,1)}), bf16[4,4,16,512]{3,2,1,0:T(8,128)(2,1)S(1)}, u32[]{:S(2)}, u32[]{:S(2)}) async-start(bf16[4,4,16,512]{3,2,1,0:T(8,128)(2,1)} %copy.18), calls=%async_computation.11 | async-start | bytes 524288 | tf_op jit(solution)/shard_map/all_to_all | solution.py:265
  177.3 13.2 %all-to-all-start.5 = ((bf16[8,2,32,512]{3,2,1,0:T(8,128)(2,1)}), bf16[8,2,32,512]{3,2,1,0:T(8,128)(2,1)S(1)}, u32[]{:S(2)}, u32[]{:S(2)}) async-start(bf16[8,2,32,512]{3,2,1,0:T(8,128)(2,1)} %get-tuple-element.24), calls=%async_computation.5 | async-start | bytes 1048576 | tf_op jit(solution)/shard_map/all_to_all | solution.py:326
  190.5 10.5 %all-to-all-start.8 = ((bf16[4,4,16,512]{3,2,1,0:T(8,128)(2,1)}), bf16[4,4,16,512]{3,2,1,0:T(8,128)(2,1)S(1)}, u32[]{:S(2)}, u32[]{:S(2)}) async-start(bf16[4,4,16,512]{3,2,1,0:T(8,128)(2,1)} %copy.17), calls=%async_computation.8 | async-start | bytes 524288 | tf_op jit(solution)/shard_map/all_to_all | solution.py:265
where the time goes:
time: 204 us; the launch traced here: 203 us
  blocking collectives  83.5 us (41%)
  Pallas kernels  32.3 us (16%)
  waiting for transfers between devices  29.6 us (15%)
  starting transfers between devices  26.6 us (13%)
  local copies, waits for them, and re-layouts  23.1 us (11%)
  other arithmetic  6.63 us (3%)
    all_to_all x2, blocking collectives, reduce_grads(): lax.all_to_all(held, 'col', 0, 0, axis_index_groups=planes, tiled=True)  33.5 us
    pallas_call x3, Pallas kernels, call(): pl.pallas_call(kernel, grid=(1,), in_specs=specs, out_specs=[whole(item.s...  32.3 us
    all_to_all x1, blocking collectives, body(): lax.all_to_all(mid.reshape(devices, rows * cols, channels), ('row', 'col'...  19.5 us
    unnamed x37, local copies, waits for them, and re-layouts  19 us
    all_to_all x1, blocking collectives, body(): lax.all_to_all(d_mid.reshape(devices, rows * cols, channels), ('row', 'co...  17.9 us
    all_to_all x2, blocking collectives, reduce_grads(): lax.all_to_all(grads.reshape(core, plane, parts, size, channels), 'col',...  12.6 us
    all_to_all x2, waiting for transfers between devices, reduce_grads(): got = lax.all_to_all(held, 'row', 0, 0, tiled=True)  11.9 us
    all_to_all x1, waiting for transfers between devices, body(): lax.all_to_all(field.reshape(col_parts, rows, wide, channels), 'col', 0,...  8.9 us
  transfers between devices with their start and end apart: 6, of which 4 were waited for; matrix products, arithmetic and copies ran while one was open for 3% of the time, Pallas kernels for 8%

commit v1 on v0

v1 whole, which is shorter than its diff:
```python
import functools
import math

import jax
import jax.numpy as jnp
import numpy as np
from jax import lax
from jax.experimental import pallas as pl
from jax.experimental.pallas import tpu as pltpu
from jax.sharding import PartitionSpec as P

HEADS = 8
eps = 1e-05
F32 = jnp.float32
BF16 = jnp.bfloat16


def log2(n):
    assert n & (n - 1) == 0
    return n.bit_length() - 1


def dot(left, right):
    return jnp.dot(left, right, preferred_element_type=F32)


def dot_nt(left, right):
    return lax.dot_general(left, right, (((1,), (1,)), ((), ())), preferred_element_type=F32)


def dot_tn(left, right):
    return lax.dot_general(left, right, (((0,), (0,)), ((), ())), preferred_element_type=F32)


def one_hot(sizes, order, me=None, lead=0):
    total = math.prod(sizes)
    index = np.arange(total)
    found = {}
    for axis in reversed(order):
        found[axis] = index % sizes[axis]
        index = index // sizes[axis]
    source = 0
    for axis, size in enumerate(sizes):
        digit = found[axis].astype(np.int32)
        if me and axis in me:
            digit = digit ^ me[axis]
        source = source * size + digit
    source = jnp.expand_dims(source, 1 - lead)
    return (source == lax.broadcasted_iota(jnp.int32, (total, total), 1 - lead)).astype(BF16)


def statistics(values):
    average = jnp.mean(values, axis=-1, keepdims=True)
    centred = values - average
    spread = jnp.mean(centred * centred, axis=-1, keepdims=True)
    return centred, lax.rsqrt(spread + eps)


def norm_back(values, gain, d_normed):
    centred, inverse = statistics(values)
    unit = centred * inverse
    scaled = d_normed * gain
    return inverse * (
        scaled
        - jnp.mean(scaled, axis=-1, keepdims=True)
        - unit * jnp.mean(scaled * unit, axis=-1, keepdims=True)
    )


def head_lanes(count, width):
    return lax.broadcasted_iota(jnp.int32, (count, 2 * width), 1) < width


def attention_forward(q_ref, k_ref, v_ref, att_ref, p_ref, groups, count, width, span):
    first = head_lanes(count, width)
    pairs = HEADS // 2

    def step(index, carry):
        group, pair = index // pairs, index % pairs
        rows = pl.ds(pl.multiple_of(group * count, count), count)
        lanes = pl.ds(pl.multiple_of(pair * 2 * width, 2 * width), 2 * width)
        query, key, value = q_ref[rows, lanes], k_ref[rows, lanes], v_ref[rows, lanes]
        total = jnp.zeros((count, 2 * width), F32)
        for half in range(2):
            mine = first if half == 0 else jnp.logical_not(first)
            scores = dot_nt(jnp.where(mine, query, jnp.zeros_like(query)), key)
            scores = scores * (width ** (-0.5))
            if span < count:
                shift = log2(span)
                same = (lax.broadcasted_iota(jnp.int32, (count, count), 0) >> shift) == (
                    lax.broadcasted_iota(jnp.int32, (count, count), 1) >> shift
                )
                scores = jnp.where(same, scores, -jnp.inf)
            expo = jnp.exp(scores - jnp.max(scores, axis=-1, keepdims=True))
            probs = (expo * (1.0 / jnp.sum(expo, axis=-1, keepdims=True))).astype(BF16)
            p_ref[index * 2 + half] = probs
            total += dot(probs, jnp.where(mine, value, jnp.zeros_like(value)))
        att_ref[rows, lanes] = total.astype(BF16)
        return carry

    lax.fori_loop(0, groups * pairs, step, 0)


def attention_back(q_ref, k_ref, v_ref, p_ref, da_ref, dqkv_ref, groups, count, width):
    first = head_lanes(count, width)
    pairs = HEADS // 2
    channels = HEADS * width

    def step(index, carry):
        group, pair = index // pairs, index % pairs
        rows = pl.ds(pl.multiple_of(group * count, count), count)
        lanes = pl.ds(pl.multiple_of(pair * 2 * width, 2 * width), 2 * width)
        query, key, value = q_ref[rows, lanes], k_ref[rows, lanes], v_ref[rows, lanes]
        d_out = da_ref[rows, lanes]
        zero = jnp.zeros_like(query)
        d_query = jnp.zeros((count, 2 * width), F32)
        d_key, d_value = d_query, d_query
        for half in range(2):
            mine = first if half == 0 else jnp.logical_not(first)
            probs = p_ref[index * 2 + half]
            d_mine = jnp.where(mine, d_out, zero)
            d_probs = dot_nt(d_mine, value)
            probs32 = probs.astype(F32)
            weighted = probs32 * d_probs
            total = jnp.sum(weighted, axis=-1, keepdims=True)
            d_scores = ((weighted - probs32 * total) * (width ** (-0.5))).astype(BF16)
            d_query += dot(d_scores, jnp.where(mine, key, zero))
            d_key += dot_tn(d_scores, jnp.where(mine, query, zero))
            d_value += dot_tn(probs, d_mine)
        for part, item in enumerate((d_query, d_key, d_value)):
            at = pl.ds(pl.multiple_of(part * channels + pair * 2 * width, 2 * width), 2 * width)
            dqkv_ref[rows, at] = item.astype(BF16)
        return carry

    lax.fori_loop(0, groups * pairs, step, 0)


def start(source, target, sem):
    copy = pltpu.make_async_copy(source, target, sem)
    copy.start()
    return copy


def start_all(pairs, sems, first=0):
    return [start(source, target, sems.at[first + at]) for at, (source, target) in enumerate(pairs)]


def weight_grads(normed, attended, dqkv_ref, d_top, turn, keep_ref, send_ref):
    channels = normed.shape[-1]
    plane, _, size, _ = keep_ref.shape
    normed = dot(normed, turn).astype(BF16)
    attended = dot(attended, turn).astype(BF16)
    for part in range(4):
        if part < 3:
            whole = dot_tn(normed, dqkv_ref[:, part * channels : (part + 1) * channels])
        else:
            whole = dot_tn(attended, d_top)
        whole = whole.astype(BF16)
        for group in range(plane):
            keep_ref[group, part] = whole[group * size : (group + 1) * size]
            at = plane + group
            send_ref[group, part] = whole[at * size : (at + 1) * size]


def input_back(dqkv_ref, w_ref):
    channels = w_ref.shape[-1]
    total = dot_nt(dqkv_ref[:, :channels], w_ref[0])
    total += dot_nt(dqkv_ref[:, channels : 2 * channels], w_ref[1])
    total += dot_nt(dqkv_ref[:, 2 * channels :], w_ref[2])
    return total.astype(BF16).astype(F32)


def row_forward(sizes, x_ref, g_ref, w_hbm, turn_hbm, mid_ref, n_hbm, q_hbm, k_hbm, v_hbm, att_hbm, p_hbm,
                w_ref, turn_ref, n_ref, q_ref, k_ref, v_ref, att_ref, p_ref, in_sem, out_sem):
    rows, length, width = sizes
    channels = x_ref.shape[-1]
    coming = start_all([(w_hbm.at[0, part], w_ref.at[part]) for part in range(4)], in_sem)
    coming.append(start(turn_hbm, turn_ref, in_sem.at[4]))
    field = jnp.concatenate([x_ref[:, i].reshape(length, channels) for i in range(rows)], axis=0)
    field = field.astype(F32)
    centred, inverse = statistics(field)
    normed = (centred * inverse * g_ref[0:1]).astype(BF16)
    n_ref[...] = normed
    going = [start(n_ref, n_hbm, out_sem.at[0])]
    for part, (ref, hbm) in enumerate(((q_ref, q_hbm), (k_ref, k_hbm), (v_ref, v_hbm))):
        coming[part].wait()
        ref[...] = dot(normed, w_ref[part]).astype(BF16)
        going.append(start(ref, hbm, out_sem.at[1 + part]))
    attention_forward(q_ref, k_ref, v_ref, att_ref, p_ref, rows, length, width, length)
    going.append(start(att_ref, att_hbm, out_sem.at[4]))
    going.append(start(p_ref, p_hbm, out_sem.at[5]))
    coming[3].wait()
    middle = (field + dot(att_ref[...], w_ref[3])).astype(BF16)
    coming[4].wait()
    mid_ref[...] = dot(turn_ref[...], middle).astype(BF16)
    for copy in going:
        copy.wait()


def row_back(sizes, d_ref, x_ref, g_ref, w_hbm, turn_hbm, tg_hbm, n_hbm, q_hbm, k_hbm, v_hbm, att_hbm, p_hbm,
             fg_ref, keep_ref, send_ref,
             w_ref, turn_ref, tg_ref, n_ref, q_ref, k_ref, v_ref, att_ref, p_ref, da_ref, dqkv_ref, in_sem):
    rows, length, width = sizes
    channels = x_ref.shape[-1]
    coming = start_all(
        [(turn_hbm, turn_ref), (w_hbm.at[0, 3], w_ref.at[3]), (p_hbm, p_ref), (v_hbm, v_ref), (k_hbm, k_ref),
         (q_hbm, q_ref), (tg_hbm, tg_ref), (n_hbm, n_ref), (att_hbm, att_ref),
         (w_hbm.at[0, 0:3], w_ref.at[0:3])],
        in_sem,
    )
    coming[0].wait()
    d_middle = dot(turn_ref[...], d_ref[...]).astype(BF16)
    coming[1].wait()
    da_ref[...] = dot_nt(d_middle, w_ref[3]).astype(BF16)
    for copy in coming[2:6]:
        copy.wait()
    attention_back(q_ref, k_ref, v_ref, p_ref, da_ref, dqkv_ref, rows, length, width)
    for copy in coming[6:10]:
        copy.wait()
    weight_grads(n_ref[...], att_ref[...], dqkv_ref, d_middle, tg_ref[...], keep_ref, send_ref)
    d_normed = input_back(dqkv_ref, w_ref)
    field = jnp.concatenate([x_ref[:, i].reshape(length, channels) for i in range(rows)], axis=0)
    result = d_middle.astype(F32) + norm_back(field.astype(F32), g_ref[0:1], d_normed)
    result = result.astype(BF16)
    for i in range(rows):
        piece = result[i * length : (i + 1) * length]
        fg_ref[:, i] = piece.reshape(fg_ref.shape[0], fg_ref.shape[2], channels)


def column_both(sizes, parts, m_ref, *refs):
    height, cols, width, together = sizes
    c_refs, refs = refs[:parts], refs[parts:]
    g_ref, w_hbm, tm_hbm, tc_hbm, to_hbm, td_hbm, tg_hbm = refs[:7]
    out_refs, refs = refs[7 : 7 + parts], refs[7 + parts :]
    dm_ref, keep_ref, send_ref = refs[:3]
    w_ref, t_ref, n_ref, q_ref, k_ref, v_ref, att_ref, p_ref, da_ref, dqkv_ref, in_sem = refs[3:]
    coming = start_all([(tm_hbm, t_ref.at[0])], in_sem)
    coming += start_all([(w_hbm.at[1, part], w_ref.at[part]) for part in range(4)], in_sem, 1)
    coming += start_all(
        [(hbm, t_ref.at[1 + at]) for at, hbm in enumerate((tc_hbm, to_hbm, td_hbm, tg_hbm))], in_sem, 5
    )
    coming[0].wait()
    middle = dot(t_ref[0], m_ref[...])
    centred, inverse = statistics(middle)
    normed = (centred * inverse * g_ref[1:2]).astype(BF16)
    n_ref[...] = normed
    for part, ref in enumerate((q_ref, k_ref, v_ref)):
        coming[1 + part].wait()
        ref[...] = dot(normed, w_ref[part]).astype(BF16)
    count = together * height
    groups = cols // together
    attention_forward(q_ref, k_ref, v_ref, att_ref, p_ref, groups, count, width, height)
    for copy in coming[4:]:
        copy.wait()
    output = (middle + dot(att_ref[...], w_ref[3])).astype(BF16)
    output = dot(t_ref[2], output).astype(BF16)
    size = output.shape[0] // parts
    for part in range(parts):
        out_refs[part][...] = output[part * size : (part + 1) * size]
    cotangent = jnp.concatenate([ref[...] for ref in c_refs], axis=0)
    cotangent = dot(t_ref[1], cotangent).astype(BF16)
    da_ref[...] = dot_nt(cotangent, w_ref[3]).astype(BF16)
    attention_back(q_ref, k_ref, v_ref, p_ref, da_ref, dqkv_ref, groups, count, width)
    weight_grads(n_ref[...], att_ref[...], dqkv_ref, cotangent, t_ref[4], keep_ref, send_ref)
    d_normed = input_back(dqkv_ref, w_ref)
    d_middle = cotangent.astype(F32) + norm_back(middle, g_ref[1:2], d_normed)
    dm_ref[...] = dot(t_ref[3], d_middle.astype(BF16)).astype(BF16)


VMEM = pl.BlockSpec(memory_space=pltpu.VMEM)
HBM = pl.BlockSpec(memory_space=pltpu.HBM)


def call(kernel, ins, outs, scratch, flops):
    moved = sum(item.size * item.dtype.itemsize for item, _ in list(ins) + list(outs))
    return pl.pallas_call(
        kernel,
        in_specs=[spec for _, spec in ins],
        out_specs=[spec for _, spec in outs],
        out_shape=[shape for shape, _ in outs],
        scratch_shapes=scratch,
        compiler_params=pltpu.CompilerParams(vmem_limit_bytes=40 * 1024 * 1024),
        cost_estimate=pl.CostEstimate(flops=flops, bytes_accessed=moved, transcendentals=0),
    )(*[item for item, _ in ins])


def swap(item, axis, count, step):
    return lax.ppermute(item, axis, [(at, at ^ step) for at in range(count)])


def reduce_grads(keep, send, row_parts, plane, core):
    _, parts, size, channels = keep.shape
    got = swap(send, "col", plane * core, 1)
    total = (keep.astype(F32) + got.astype(F32)).astype(BF16)
    held = total[0].astype(F32)
    for step in range(1, plane):
        held = held + swap(total[step], "col", plane * core, step * core).astype(F32)
    held = held.astype(BF16).reshape(parts, row_parts, size // row_parts, channels)
    result = held[:, 0].astype(F32)
    for step in range(1, row_parts):
        result = result + swap(held[:, step], "row", row_parts, step).astype(F32)
    return result


def body(row_parts, col_parts, field, cotangent, gains, weights):
    high, wide, channels = field.shape
    core = 2
    plane = col_parts // core
    rows = high // col_parts
    cols = wide // row_parts
    tokens = high * wide
    height = high * row_parts
    length = wide * col_parts
    width = channels // HEADS
    together = min(cols, max(1, 256 // height))
    devices = row_parts * col_parts
    my_row, my_col = lax.axis_index("row"), lax.axis_index("col")

    def like(*shape):
        return jax.ShapeDtypeStruct(shape, BF16)

    flat = like(tokens, channels)
    square = pltpu.VMEM((channels, channels), BF16)
    plain = pltpu.VMEM((tokens, channels), BF16)
    copies = pltpu.SemaphoreType.DMA
    packed = (like(plane, 4, channels // col_parts, channels), VMEM)
    turn_rows = one_hot((rows, col_parts, row_parts, cols), (2, 1, 0, 3))
    turn_rows_back = one_hot((row_parts, col_parts, rows, cols), (2, 1, 0, 3))
    turn_in = one_hot((height, cols), (1, 0))
    turn_out = one_hot((cols, height), (1, 0))
    turn_cot = one_hot((row_parts, high, cols), (2, 0, 1), {0: my_row})
    turn_output = one_hot((cols, row_parts, high), (1, 2, 0), {1: my_row})
    turn_grads = one_hot(
        (row_parts, plane, core, channels // devices), (2, 1, 0, 3),
        {0: my_row, 1: my_col // core, 2: my_col % core}, lead=1,
    )

    x = lax.all_to_all(field.reshape(col_parts, rows, wide, channels), "col", 0, 0, tiled=True)
    cots = []
    for step in range(row_parts):
        piece = lax.dynamic_slice_in_dim(cotangent, (my_row ^ step) * cols, cols, axis=1)
        piece = piece if step == 0 else swap(piece, "row", row_parts, step)
        cots.append(piece.reshape(high * cols, channels))

    sizes = (rows, length, width)
    probs = like(rows * HEADS, length, length)
    probs_ref = pltpu.VMEM(probs.shape, BF16)
    unit = 2 * tokens * channels * channels
    mid, *saved = call(
        functools.partial(row_forward, sizes),
        [(x, VMEM), (gains, VMEM), (weights, HBM), (turn_rows, HBM)],
        [(flat, VMEM)] + [(flat, HBM)] * 5 + [(probs, HBM)],
        [pltpu.VMEM((4, channels, channels), BF16), plain, plain, plain, plain, plain, plain, probs_ref,
         copies((5,)), copies((6,))],
        5 * unit,
    )
    mid = lax.all_to_all(
        mid.reshape(devices, rows * cols, channels), ("row", "col"), 0, 0, tiled=True
    ).reshape(tokens, channels)

    count = together * height
    results = call(
        functools.partial(column_both, (height, cols, width, together), row_parts),
        [(mid, VMEM)] + [(item, VMEM) for item in cots] + [(gains, VMEM), (weights, HBM)]
        + [(turn, HBM) for turn in (turn_in, turn_cot, turn_output, turn_out, turn_grads)],
        [(like(high * cols, channels), VMEM)] * row_parts + [(flat, VMEM), packed, packed],
        [pltpu.VMEM((4, channels, channels), BF16), pltpu.VMEM((5, tokens, channels), BF16),
         plain, plain, plain, plain, plain, pltpu.VMEM((cols // together * HEADS, count, count), BF16),
         plain, pltpu.VMEM((tokens, 3 * channels), BF16), copies((9,))],
        18 * unit,
    )
    outs, (d_mid, keep_b, send_b) = results[:row_parts], results[row_parts:]
    d_mid = lax.all_to_all(
        d_mid.reshape(devices, rows * cols, channels), ("row", "col"), 0, 0, tiled=True
    ).reshape(tokens, channels)
    output = jnp.zeros((high, wide, channels), BF16)
    for step in range(row_parts):
        piece = outs[step].reshape(high, cols, channels)
        piece = piece if step == 0 else swap(piece, "row", row_parts, step)
        output = lax.dynamic_update_slice_in_dim(output, piece, (my_row ^ step) * cols, axis=1)
    grads_b = reduce_grads(keep_b, send_b, row_parts, plane, core)

    field_grad, keep_a, send_a = call(
        functools.partial(row_back, sizes),
        [(d_mid, VMEM), (x, VMEM), (gains, VMEM), (weights, HBM), (turn_rows_back, HBM), (turn_grads, HBM)]
        + [(item, HBM) for item in saved],
        [(like(col_parts, rows, wide, channels), VMEM), packed, packed],
        [pltpu.VMEM((4, channels, channels), BF16), plain, square, plain, plain, plain, plain, plain, probs_ref,
         plain, pltpu.VMEM((tokens, 3 * channels), BF16), copies((10,))],
        12 * unit,
    )
    field_grad = lax.all_to_all(field_grad, "col", 0, 0, tiled=True).reshape(high, wide, channels)
    grads_a = reduce_grads(keep_a, send_a, row_parts, plane, core)
    return output, field_grad, jnp.concatenate([grads_a, grads_b], axis=0)


def solution(mesh):
    return jax.shard_map(
        functools.partial(body, mesh.shape["row"], mesh.shape["col"]),
        mesh=mesh,
        in_specs=(P("row", "col", None), P("row", "col", None), P(), P()),
        out_specs=(P("row", "col", None), P("row", "col", None), P(None, ("row", "col"), None)),
        check_vma=False,
    )
```

time: 204 us -> 174 us (0.85)
  blocking collectives: 83.5 us -> 0 us
  starting transfers between devices: 26.6 us -> 51.8 us
  local copies, waits for them, and re-layouts: 23.1 us -> 33.8 us
  waiting for transfers between devices: 29.6 us -> 39.9 us
  Pallas kernels: 32.3 us -> 36.7 us
  other arithmetic: 6.63 us -> 9.07 us
    all_to_all x6 -> x0, blocking collectives: 83.5 us -> none  [the longest x2 33.5 us: reduce_grads(): lax.all_to_all(held, 'col', 0, 0, axis_index_groups=planes, tiled=True)]
    ppermute x0 -> x20, starting transfers between devices: none -> 35.5 us  [swap(): return lax.ppermute(item, axis, [(at, at ^ step) for at in range(count)])]
    ppermute x0 -> x20, waiting for transfers between devices: none -> 15.7 us  [swap(): return lax.ppermute(item, axis, [(at, at ^ step) for at in range(count)])]
    unnamed x37 -> x73, local copies, waits for them, and re-layouts: 19 us -> 30.8 us
    all_to_all x4 -> x2, starting transfers between devices: 17.8 us -> 7.27 us  [the longest x1 3.96 us: body(): lax.all_to_all(mid.reshape(devices, rows * cols, channels), ('row', 'col'...]
    all_to_all x4 -> x2, waiting for transfers between devices: 12 us -> 20.9 us  [the longest x1 11 us: body(): lax.all_to_all(mid.reshape(devices, rows * cols, channels), ('row', 'col'...]
    all_to_all x1, waiting for transfers between devices: 8.73 us -> 0.01 us  [body(): lax.all_to_all(field_grad, 'col', 0, 0, tiled=True)]
    convert_element_type x0 -> x9, other arithmetic: none -> 6.83 us  [the longest x5 3.48 us: one_hot(): (source == lax.broadcasted_iota(jnp.int32, (total, total), 1 - lead)).ast...]
  transfers between devices with their start and end apart: 6 -> 24, of which waited for: 4 -> 7; matrix products, arithmetic and copies ran while one was open for 3% -> 7% of each run, Pallas kernels for 8% -> 11%
where the time goes in v1:
time: 174 us; the launch traced here: 172 us
  starting transfers between devices  51.8 us (30%)
  waiting for transfers between devices  39.9 us (23%)
  Pallas kernels  36.7 us (21%)
  local copies, waits for them, and re-layouts  33.8 us (19%)
  other arithmetic  9.07 us (5%)
    pallas_call x3, Pallas kernels, call(): pl.pallas_call(kernel, in_specs=[spec for _, spec in ins], out_specs=[spe...  36.7 us
    ppermute x20, starting transfers between devices, swap(): return lax.ppermute(item, axis, [(at, at ^ step) for at in range(count)])  35.5 us
    unnamed x73, local copies, waits for them, and re-layouts  30.8 us
    ppermute x20, waiting for transfers between devices, swap(): return lax.ppermute(item, axis, [(at, at ^ step) for at in range(count)])  15.7 us
    all_to_all x1, waiting for transfers between devices, body(): lax.all_to_all(mid.reshape(devices, rows * cols, channels), ('row', 'col'...  11 us
    all_to_all x1, waiting for transfers between devices, body(): lax.all_to_all(d_mid.reshape(devices, rows * cols, channels), ('row', 'co...  9.88 us
    all_to_all x1, starting transfers between devices, body(): lax.all_to_all(field.reshape(col_parts, rows, wide, channels), 'col', 0,...  5.31 us
    all_to_all x1, starting transfers between devices, body(): lax.all_to_all(mid.reshape(devices, rows * cols, channels), ('row', 'col'...  3.96 us
  transfers between devices with their start and end apart: 24, of which 7 were waited for; matrix products, arithmetic and copies ran while one was open for 7% of the time, Pallas kernels for 11%

profile of v1, /device:TPU:0, one launch (start us, length us, event | category | flops | bytes accessed | tf_op | source)
XLA Modules:
  0.0 172.4 jit_solution(2294988370244608664)
XLA Ops:
  0.7 5.3 %all-to-all-start = ((bf16[8,2,32,512]{3,2,1,0:T(8,128)(2,1)}), bf16[8,2,32,512]{3,2,1,0:T(8,128)(2,1)S(1)}, u32[]{:S(2)}, u32[]{:S(2)}) async-start(bf16[8,2,32,512]{3,2,1,0:T(8,128)(2,1)} %bitcast.91), calls=%async_computation | async-start | bytes 1048576 | tf_op jit(solution)/shard_map/all_to_all | solution.py:338
  6.0 1.9 %constant_dynamic-slice_fusion = (bf16[16,8,512]{2,1,0:T(8,128)(2,1)}, bf16[16,8,512]{2,1,0:T(8,128)(2,1)}, bf16[128,512]{1,0:T(8,128)(2,1)S(1)}, bf16[16,8,512]{2,1,0:T(8,128)(2,1)}) fusion(bf16[16,32,512]{2,1,0:T(8,128)(2,1)} %param.19, s32[]{:T(128)S(6)} %select_n.30, s32[]{:T(128)S(6)} %select_n.28, s32[]{:T(128)S(6)} %select_n.27, s32[]{:T(128)S(6)} %select_n.29), kind=kLoop, calls=%fused_computation.64 | loop fusion | bytes 1048592 | tf_op jit(solution)/shard_map/dynamic_slice | solution.py:341
  9.4 2.6 %collective-permute-start.1 = (bf16[16,8,512]{2,1,0:T(8,128)(2,1)}, bf16[16,8,512]{2,1,0:T(8,128)(2,1)S(1)}, u32[]{:S(2)}, u32[]{:S(2)}) collective-permute-start(bf16[16,8,512]{2,1,0:T(8,128)(2,1)} %get-tuple-element.46), channel_id=1, source_target_pairs={{0,16},{8,24},{16,0},{24,8},{1,17},{9,25},{17,1},{25,9},{2,18},{10... | collective-permute-start | bytes 393224 | tf_op jit(solution)/shard_map/ppermute | solution.py:288
  12.4 3.3 %all-to-all-done.x_ref = bf16[8,2,32,512]{3,2,1,0:T(8,128)(2,1)S(1)} async-done(((bf16[8,2,32,512]{3,2,1,0:T(8,128)(2,1)}), bf16[8,2,32,512]{3,2,1,0:T(8,128)(2,1)S(1)}, u32[]{:S(2)}, u32[]{:S(2)}) %all-to-all-start) | async-done | bytes 524320 | tf_op jit(solution)/shard_map/all_to_all | solution.py:338
  15.7 2.2 %copy-done = bf16[2,4,512,512]{3,2,1,0:T(8,128)(2,1)S(1)} copy-done((bf16[2,4,512,512]{3,2,1,0:T(8,128)(2,1)S(1)}, bf16[2,4,512,512]{3,2,1,0:T(8,128)(2,1)}, u32[]{:S(2)}) %copy-start) | copy-done | bytes 4194328
  17.9 8.3 %shard_map.193 = (bf16[512,512]{1,0:T(8,128)(2,1)}, bf16[512,512]{1,0:T(8,128)(2,1)S(1)}, bf16[512,512]{1,0:T(8,128)(2,1)S(1)}, bf16[512,512]{1,0:T(8,128)(2,1)S...) custom-call(bf16[8,2,32,512]{3,2,1,0:T(8,128)(2,1)S(1)} %all-to-all-done.x_ref, ...), custom_call_target="tpu_custom_call" | custom-call | flops 1342177280 | bytes 10489856 | tf_op jit(solution)/shard_map/pallas_call | solution.py:276
  31.6 4.0 %all-to-all-start.1 = ((bf16[32,16,512]{2,1,0:T(8,128)(2,1)}), bf16[32,16,512]{2,1,0:T(8,128)(2,1)S(1)}, u32[]{:S(2)}, u32[]{:S(2)}) async-start(bf16[32,16,512]{2,1,0:T(8,128)(2,1)} %bitcast.1), calls=%async_computation.1 | async-start | bytes 1048576 | tf_op jit(solution)/shard_map/all_to_all | solution.py:357
  40.1 11.0 %all-to-all-done.1 = bf16[32,16,512]{2,1,0:T(8,128)(2,1)S(1)} async-done(((bf16[32,16,512]{2,1,0:T(8,128)(2,1)}), bf16[32,16,512]{2,1,0:T(8,128)(2,1)S(1)}, u32[]{:S(2)}, u32[]{:S(2)}) %all-to-all-start.1) | async-done | bytes 524320 | tf_op jit(solution)/shard_map/all_to_all | solution.py:357
  51.1 2.2 %copy-done.1 = bf16[2,4,512,512]{3,2,1,0:T(8,128)(2,1)S(1)} copy-done((bf16[2,4,512,512]{3,2,1,0:T(8,128)(2,1)S(1)}, bf16[2,4,512,512]{3,2,1,0:T(8,128)(2,1)}, u32[]{:S(2)}) %copy-start.1) | copy-done | bytes 4194328
  57.3 17.6 %shard_map.194 = (bf16[128,512]{1,0:T(8,128)(2,1)S(1)}, bf16[128,512]{1,0:T(8,128)(2,1)S(1)}, bf16[128,512]{1,0:T(8,128)(2,1)S(1)}, bf16[128,512]{1,0:T(8,128)(2...) custom-call(bf16[512,512]{1,0:T(8,128)(2,1)S(1)} %bitcast.78, ...), custom_call_target="tpu_custom_call" | custom-call | flops 4831838208 | bytes 11014144 | tf_op jit(solution)/shard_map/pallas_call | solution.py:276
  78.7 3.3 %all-to-all-start.2 = ((bf16[32,16,512]{2,1,0:T(8,128)(2,1)}), bf16[32,16,512]{2,1,0:T(8,128)(2,1)S(1)}, u32[]{:S(2)}, u32[]{:S(2)}) async-start(bf16[32,16,512]{2,1,0:T(8,128)(2,1)} %bitcast.80), calls=%async_computation.2 | async-start | bytes 1048576 | tf_op jit(solution)/shard_map/all_to_all | solution.py:373
  84.8 2.4 %collective-permute-start.4 = (bf16[16,8,512]{2,1,0:T(8,128)(2,1)}, bf16[16,8,512]{2,1,0:T(8,128)(2,1)S(1)}, u32[]{:S(2)}, u32[]{:S(2)}) collective-permute-start(bf16[16,8,512]{2,1,0:T(8,128)(2,1)} %bitcast.84), channel_id=1, source_target_pairs={{0,16},{8,24},{16,0},{24,8},{1,17},{9,25},{17,1},{25,9},{2,18},{10... | collective-permute-start | bytes 393224 | tf_op jit(solution)/shard_map/ppermute | solution.py:288
  87.5 9.9 %all-to-all-done.2 = bf16[32,16,512]{2,1,0:T(8,128)(2,1)S(1)} async-done(((bf16[32,16,512]{2,1,0:T(8,128)(2,1)}), bf16[32,16,512]{2,1,0:T(8,128)(2,1)S(1)}, u32[]{:S(2)}, u32[]{:S(2)}) %all-to-all-start.2) | async-done | bytes 524320 | tf_op jit(solution)/shard_map/all_to_all | solution.py:373
  98.1 2.2 %copy-done.2 = bf16[2,4,512,512]{3,2,1,0:T(8,128)(2,1)S(1)} copy-done((bf16[2,4,512,512]{3,2,1,0:T(8,128)(2,1)S(1)}, bf16[2,4,512,512]{3,2,1,0:T(8,128)(2,1)}, u32[]{:S(2)}) %copy-start.2) | copy-done | bytes 4194328
  109.2 10.9 %shard_map.195 = (bf16[8,2,32,512]{3,2,1,0:T(8,128)(2,1)}, bf16[4,4,64,512]{3,2,1,0:T(8,128)(2,1)S(1)}, bf16[4,4,64,512]{3,2,1,0:T(8,128)(2,1)}) custom-call(bf16[512,512]{1,0:T(8,128)(2,1)S(1)} %bitcast.79, bf16[8,2,32,512]{3,2,1,0:T(8,128)(2,1)S(1)} %all-to-all-done.x_ref, f32[2,512]{1,0:T(2,128)S(1)} %copy-done.10, ...), custom_call_target="tpu_custom_call" | custom-call | flops 3221225472 | bytes 13635584 | tf_op jit(solution)/shard_map/pallas_call | solution.py:276
  121.3 3.7 %all-to-all-start.3 = ((bf16[8,2,32,512]{3,2,1,0:T(8,128)(2,1)}), bf16[8,2,32,512]{3,2,1,0:T(8,128)(2,1)S(1)}, u32[]{:S(2)}, u32[]{:S(2)}) async-start(bf16[8,2,32,512]{3,2,1,0:T(8,128)(2,1)} %get-tuple-element.32), calls=%async_computation.3 | async-start | bytes 1048576 | tf_op jit(solution)/shard_map/all_to_all | solution.py:392
  126.6 2.1 %collective-permute-start.14 = (bf16[4,64,512]{2,1,0:T(8,128)(2,1)S(1)}, bf16[4,64,512]{2,1,0:T(8,128)(2,1)S(1)}, u32[]{:S(2)}, u32[]{:S(2)}) collective-permute-start(bf16[4,64,512]{2,1,0:T(8,128)(2,1)S(1)} %get-tuple-element.40), channel_id=1, source_target_pairs={{0,2},{1,3},{2,0},{3,1},{4,6},{5,7},{6,4},{7,5},{8,10},{9,11},{10,... | collective-permute-start | bytes 786440 | tf_op jit(solution)/shard_map/ppermute | solution.py:288
  131.8 2.0 %collective-permute-start.7 = (bf16[4,64,512]{2,1,0:T(8,128)(2,1)S(1)}, bf16[4,64,512]{2,1,0:T(8,128)(2,1)S(1)}, u32[]{:S(2)}, u32[]{:S(2)}) collective-permute-start(bf16[4,64,512]{2,1,0:T(8,128)(2,1)S(1)} %get-tuple-element.37), channel_id=1, source_target_pairs={{0,2},{1,3},{2,0},{3,1},{4,6},{5,7},{6,4},{7,5},{8,10},{9,11},{10,... | collective-permute-start | bytes 786440 | tf_op jit(solution)/shard_map/ppermute | solution.py:288
  135.3 4.6 %collective-permute-done.14 = bf16[4,64,512]{2,1,0:T(8,128)(2,1)S(1)} collective-permute-done((bf16[4,64,512]{2,1,0:T(8,128)(2,1)S(1)}, bf16[4,64,512]{2,1,0:T(8,128)(2,1)S(1)}, u32[]{:S(2)}, u32[]{:S(2)}) %collective-permute-start.14) | collective-permute-done | bytes 262176 | tf_op jit(solution)/shard_map/ppermute | solution.py:288
  141.4 5.1 %collective-permute-done.16 = bf16[4,64,512]{2,1,0:T(8,128)(2,1)S(1)} collective-permute-done((bf16[4,64,512]{2,1,0:T(8,128)(2,1)S(1)}, bf16[4,64,512]{2,1,0:T(8,128)(2,1)S(1)}, u32[]{:S(2)}, u32[]{:S(2)}) %collective-permute-start.16) | collective-permute-done | bytes 262176 | tf_op jit(solution)/shard_map/ppermute | solution.py:288
  147.7 6.3 %collective-permute-start.18 = (bf16[4,16,512]{2,1,0:T(8,128)(2,1)S(1)}, bf16[4,16,512]{2,1,0:T(8,128)(2,1)S(1)}, u32[]{:S(2)}, u32[]{:S(2)}) collective-permute-start(bf16[4,16,512]{2,1,0:T(8,128)(2,1)S(1)} %get-tuple-element.51), channel_id=1, source_target_pairs={{0,16},{8,24},{16,0},{24,8},{1,17},{9,25},{17,1},{25,9},{2,18},{10... | collective-permute-start | bytes 196616 | tf_op jit(solution)/shard_map/ppermute | solution.py:288
  154.0 3.9 %collective-permute-start.19 = (bf16[4,16,512]{2,1,0:T(8,128)(2,1)S(1)}, bf16[4,16,512]{2,1,0:T(8,128)(2,1)S(1)}, u32[]{:S(2)}, u32[]{:S(2)}) collective-permute-start(bf16[4,16,512]{2,1,0:T(8,128)(2,1)S(1)} %get-tuple-element.52), channel_id=1, source_target_pairs={{0,24},{8,16},{16,8},{24,0},{1,25},{9,17},{17,9},{25,1},{2,26},{10... | collective-permute-start | bytes 196616 | tf_op jit(solution)/shard_map/ppermute | solution.py:288
  158.5 6.3 %collective-permute-start.11 = (bf16[4,16,512]{2,1,0:T(8,128)(2,1)S(1)}, bf16[4,16,512]{2,1,0:T(8,128)(2,1)S(1)}, u32[]{:S(2)}, u32[]{:S(2)}) collective-permute-start(bf16[4,16,512]{2,1,0:T(8,128)(2,1)S(1)} %get-tuple-element.48), channel_id=1, source_target_pairs={{0,16},{8,24},{16,0},{24,8},{1,17},{9,25},{17,1},{25,9},{2,18},{10... | collective-permute-start | bytes 196616 | tf_op jit(solution)/shard_map/ppermute | solution.py:288
  164.9 4.3 %collective-permute-done.11 = bf16[4,16,512]{2,1,0:T(8,128)(2,1)S(1)} collective-permute-done((bf16[4,16,512]{2,1,0:T(8,128)(2,1)S(1)}, bf16[4,16,512]{2,1,0:T(8,128)(2,1)S(1)}, u32[]{:S(2)}, u32[]{:S(2)}) %collective-permute-start.11) | collective-permute-done | bytes 65568 | tf_op jit(solution)/shard_map/ppermute | solution.py:288
  (124 shorter events, 46.1 us)
Async XLA Ops:
  0.7 15.1 %all-to-all-start = ((bf16[8,2,32,512]{3,2,1,0:T(8,128)(2,1)}), bf16[8,2,32,512]{3,2,1,0:T(8,128)(2,1)S(1)}, u32[]{:S(2)}, u32[]{:S(2)}) async-start(bf16[8,2,32,512]{3,2,1,0:T(8,128)(2,1)} %bitcast.91), calls=%async_computation | async-start | bytes 1048576 | tf_op jit(solution)/shard_map/all_to_all | solution.py:338
  7.8 31.6 %collective-permute-start = (bf16[16,8,512]{2,1,0:T(8,128)(2,1)}, bf16[16,8,512]{2,1,0:T(8,128)(2,1)S(1)}, u32[]{:S(2)}, u32[]{:S(2)}) collective-permute-start(bf16[16,8,512]{2,1,0:T(8,128)(2,1)} %get-tuple-element.44), channel_id=1, source_target_pairs={{0,8},{8,0},{16,24},{24,16},{1,9},{9,1},{17,25},{25,17},{2,10},{10... | collective-permute-start | bytes 393224 | tf_op jit(solution)/shard_map/ppermute | solution.py:288
  9.4 30.1 %collective-permute-start.1 = (bf16[16,8,512]{2,1,0:T(8,128)(2,1)}, bf16[16,8,512]{2,1,0:T(8,128)(2,1)S(1)}, u32[]{:S(2)}, u32[]{:S(2)}) collective-permute-start(bf16[16,8,512]{2,1,0:T(8,128)(2,1)} %get-tuple-element.46), channel_id=1, source_target_pairs={{0,16},{8,24},{16,0},{24,8},{1,17},{9,25},{17,1},{25,9},{2,18},{10... | collective-permute-start | bytes 393224 | tf_op jit(solution)/shard_map/ppermute | solution.py:288
  12.0 28.1 %collective-permute-start.2 = (bf16[16,8,512]{2,1,0:T(8,128)(2,1)}, bf16[16,8,512]{2,1,0:T(8,128)(2,1)}, u32[]{:S(2)}, u32[]{:S(2)}) collective-permute-start(bf16[16,8,512]{2,1,0:T(8,128)(2,1)} %get-tuple-element.43), channel_id=1, source_target_pairs={{0,24},{8,16},{16,8},{24,0},{1,25},{9,17},{17,9},{25,1},{2,26},{10... | collective-permute-start | bytes 393224 | tf_op jit(solution)/shard_map/ppermute | solution.py:288
  31.6 19.5 %all-to-all-start.1 = ((bf16[32,16,512]{2,1,0:T(8,128)(2,1)}), bf16[32,16,512]{2,1,0:T(8,128)(2,1)S(1)}, u32[]{:S(2)}, u32[]{:S(2)}) async-start(bf16[32,16,512]{2,1,0:T(8,128)(2,1)} %bitcast.1), calls=%async_computation.1 | async-start | bytes 1048576 | tf_op jit(solution)/shard_map/all_to_all | solution.py:357
  78.7 18.7 %all-to-all-start.2 = ((bf16[32,16,512]{2,1,0:T(8,128)(2,1)}), bf16[32,16,512]{2,1,0:T(8,128)(2,1)S(1)}, u32[]{:S(2)}, u32[]{:S(2)}) async-start(bf16[32,16,512]{2,1,0:T(8,128)(2,1)} %bitcast.80), calls=%async_computation.2 | async-start | bytes 1048576 | tf_op jit(solution)/shard_map/all_to_all | solution.py:373
  82.0 43.0 %collective-permute-start.13 = (bf16[4,4,64,512]{3,2,1,0:T(8,128)(2,1)}, bf16[4,4,64,512]{3,2,1,0:T(8,128)(2,1)}, u32[]{:S(2)}, u32[]{:S(2)}) collective-permute-start(bf16[4,4,64,512]{3,2,1,0:T(8,128)(2,1)} %copy-done.13), channel_id=1, source_target_pairs={{0,1},{1,0},{2,3},{3,2},{4,5},{5,4},{6,7},{7,6},{8,9},{9,8},{10,11... | collective-permute-start | bytes 3145736 | tf_op jit(solution)/shard_map/ppermute | solution.py:288
  83.1 37.2 %collective-permute-start.3 = (bf16[16,8,512]{2,1,0:T(8,128)(2,1)}, bf16[16,8,512]{2,1,0:T(8,128)(2,1)}, u32[]{:S(2)}, u32[]{:S(2)}) collective-permute-start(bf16[16,8,512]{2,1,0:T(8,128)(2,1)} %bitcast.85), channel_id=1, source_target_pairs={{0,8},{8,0},{16,24},{24,16},{1,9},{9,1},{17,25},{25,17},{2,10},{10... | collective-permute-start | bytes 393224 | tf_op jit(solution)/shard_map/ppermute | solution.py:288
  84.8 36.4 %collective-permute-start.4 = (bf16[16,8,512]{2,1,0:T(8,128)(2,1)}, bf16[16,8,512]{2,1,0:T(8,128)(2,1)S(1)}, u32[]{:S(2)}, u32[]{:S(2)}) collective-permute-start(bf16[16,8,512]{2,1,0:T(8,128)(2,1)} %bitcast.84), channel_id=1, source_target_pairs={{0,16},{8,24},{16,0},{24,8},{1,17},{9,25},{17,1},{25,9},{2,18},{10... | collective-permute-start | bytes 393224 | tf_op jit(solution)/shard_map/ppermute | solution.py:288
  87.2 34.1 %collective-permute-start.5 = (bf16[16,8,512]{2,1,0:T(8,128)(2,1)}, bf16[16,8,512]{2,1,0:T(8,128)(2,1)S(1)}, u32[]{:S(2)}, u32[]{:S(2)}) collective-permute-start(bf16[16,8,512]{2,1,0:T(8,128)(2,1)} %bitcast.83), channel_id=1, source_target_pairs={{0,24},{8,16},{16,8},{24,0},{1,25},{9,17},{17,9},{25,1},{2,26},{10... | collective-permute-start | bytes 393224 | tf_op jit(solution)/shard_map/ppermute | solution.py:288
  120.1 10.1 %collective-permute-start.6 = (bf16[4,4,64,512]{3,2,1,0:T(8,128)(2,1)}, bf16[4,4,64,512]{3,2,1,0:T(8,128)(2,1)}, u32[]{:S(2)}, u32[]{:S(2)}) collective-permute-start(bf16[4,4,64,512]{3,2,1,0:T(8,128)(2,1)} %get-tuple-element.34), channel_id=1, source_target_pairs={{0,1},{1,0},{2,3},{3,2},{4,5},{5,4},{6,7},{7,6},{8,9},{9,8},{10,11... | collective-permute-start | bytes 3145736 | tf_op jit(solution)/shard_map/ppermute | solution.py:288
  121.3 43.6 %all-to-all-start.3 = ((bf16[8,2,32,512]{3,2,1,0:T(8,128)(2,1)}), bf16[8,2,32,512]{3,2,1,0:T(8,128)(2,1)S(1)}, u32[]{:S(2)}, u32[]{:S(2)}) async-start(bf16[8,2,32,512]{3,2,1,0:T(8,128)(2,1)} %get-tuple-element.32), calls=%async_computation.3 | async-start | bytes 1048576 | tf_op jit(solution)/shard_map/all_to_all | solution.py:392
  126.6 13.3 %collective-permute-start.14 = (bf16[4,64,512]{2,1,0:T(8,128)(2,1)S(1)}, bf16[4,64,512]{2,1,0:T(8,128)(2,1)S(1)}, u32[]{:S(2)}, u32[]{:S(2)}) collective-permute-start(bf16[4,64,512]{2,1,0:T(8,128)(2,1)S(1)} %get-tuple-element.40), channel_id=1, source_target_pairs={{0,2},{1,3},{2,0},{3,1},{4,6},{5,7},{6,4},{7,5},{8,10},{9,11},{10,... | collective-permute-start | bytes 786440 | tf_op jit(solution)/shard_map/ppermute | solution.py:288
  128.7 12.7 %collective-permute-start.15 = (bf16[4,64,512]{2,1,0:T(8,128)(2,1)S(1)}, bf16[4,64,512]{2,1,0:T(8,128)(2,1)S(1)}, u32[]{:S(2)}, u32[]{:S(2)}) collective-permute-start(bf16[4,64,512]{2,1,0:T(8,128)(2,1)S(1)} %get-tuple-element.42), channel_id=1, source_target_pairs={{0,4},{1,5},{2,6},{3,7},{4,0},{5,1},{6,2},{7,3},{8,12},{9,13},{10,... | collective-permute-start | bytes 786440 | tf_op jit(solution)/shard_map/ppermute | solution.py:288
  130.1 16.3 %collective-permute-start.16 = (bf16[4,64,512]{2,1,0:T(8,128)(2,1)S(1)}, bf16[4,64,512]{2,1,0:T(8,128)(2,1)S(1)}, u32[]{:S(2)}, u32[]{:S(2)}) collective-permute-start(bf16[4,64,512]{2,1,0:T(8,128)(2,1)S(1)} %get-tuple-element.41), channel_id=1, source_target_pairs={{0,6},{1,7},{2,4},{3,5},{4,2},{5,3},{6,0},{7,1},{8,14},{9,15},{10,... | collective-permute-start | bytes 786440 | tf_op jit(solution)/shard_map/ppermute | solution.py:288
  131.8 22.2 %collective-permute-start.7 = (bf16[4,64,512]{2,1,0:T(8,128)(2,1)S(1)}, bf16[4,64,512]{2,1,0:T(8,128)(2,1)S(1)}, u32[]{:S(2)}, u32[]{:S(2)}) collective-permute-start(bf16[4,64,512]{2,1,0:T(8,128)(2,1)S(1)} %get-tuple-element.37), channel_id=1, source_target_pairs={{0,2},{1,3},{2,0},{3,1},{4,6},{5,7},{6,4},{7,5},{8,10},{9,11},{10,... | collective-permute-start | bytes 786440 | tf_op jit(solution)/shard_map/ppermute | solution.py:288
  133.8 24.1 %collective-permute-start.8 = (bf16[4,64,512]{2,1,0:T(8,128)(2,1)S(1)}, bf16[4,64,512]{2,1,0:T(8,128)(2,1)S(1)}, u32[]{:S(2)}, u32[]{:S(2)}) collective-permute-start(bf16[4,64,512]{2,1,0:T(8,128)(2,1)S(1)} %get-tuple-element.39), channel_id=1, source_target_pairs={{0,4},{1,5},{2,6},{3,7},{4,0},{5,1},{6,2},{7,3},{8,12},{9,13},{10,... | collective-permute-start | bytes 786440 | tf_op jit(solution)/shard_map/ppermute | solution.py:288
  139.9 18.0 %collective-permute-start.9 = (bf16[4,64,512]{2,1,0:T(8,128)(2,1)S(1)}, bf16[4,64,512]{2,1,0:T(8,128)(2,1)S(1)}, u32[]{:S(2)}, u32[]{:S(2)}) collective-permute-start(bf16[4,64,512]{2,1,0:T(8,128)(2,1)S(1)} %get-tuple-element.38), channel_id=1, source_target_pairs={{0,6},{1,7},{2,4},{3,5},{4,2},{5,3},{6,0},{7,1},{8,14},{9,15},{10,... | collective-permute-start | bytes 786440 | tf_op jit(solution)/shard_map/ppermute | solution.py:288
  146.6 18.1 %collective-permute-start.17 = (bf16[4,16,512]{2,1,0:T(8,128)(2,1)S(1)}, bf16[4,16,512]{2,1,0:T(8,128)(2,1)S(1)}, u32[]{:S(2)}, u32[]{:S(2)}) collective-permute-start(bf16[4,16,512]{2,1,0:T(8,128)(2,1)S(1)} %get-tuple-element.50), channel_id=1, source_target_pairs={{0,8},{8,0},{16,24},{24,16},{1,9},{9,1},{17,25},{25,17},{2,10},{10... | collective-permute-start | bytes 196616 | tf_op jit(solution)/shard_map/ppermute | solution.py:288
  147.7 17.1 %collective-permute-start.18 = (bf16[4,16,512]{2,1,0:T(8,128)(2,1)S(1)}, bf16[4,16,512]{2,1,0:T(8,128)(2,1)S(1)}, u32[]{:S(2)}, u32[]{:S(2)}) collective-permute-start(bf16[4,16,512]{2,1,0:T(8,128)(2,1)S(1)} %get-tuple-element.51), channel_id=1, source_target_pairs={{0,16},{8,24},{16,0},{24,8},{1,17},{9,25},{17,1},{25,9},{2,18},{10... | collective-permute-start | bytes 196616 | tf_op jit(solution)/shard_map/ppermute | solution.py:288
  154.0 10.8 %collective-permute-start.19 = (bf16[4,16,512]{2,1,0:T(8,128)(2,1)S(1)}, bf16[4,16,512]{2,1,0:T(8,128)(2,1)S(1)}, u32[]{:S(2)}, u32[]{:S(2)}) collective-permute-start(bf16[4,16,512]{2,1,0:T(8,128)(2,1)S(1)} %get-tuple-element.52), channel_id=1, source_target_pairs={{0,24},{8,16},{16,8},{24,0},{1,25},{9,17},{17,9},{25,1},{2,26},{10... | collective-permute-start | bytes 196616 | tf_op jit(solution)/shard_map/ppermute | solution.py:288
  158.1 6.7 %collective-permute-start.10 = (bf16[4,16,512]{2,1,0:T(8,128)(2,1)S(1)}, bf16[4,16,512]{2,1,0:T(8,128)(2,1)S(1)}, u32[]{:S(2)}, u32[]{:S(2)}) collective-permute-start(bf16[4,16,512]{2,1,0:T(8,128)(2,1)S(1)} %get-tuple-element.47), channel_id=1, source_target_pairs={{0,8},{8,0},{16,24},{24,16},{1,9},{9,1},{17,25},{25,17},{2,10},{10... | collective-permute-start | bytes 196616 | tf_op jit(solution)/shard_map/ppermute | solution.py:288
  158.5 10.7 %collective-permute-start.11 = (bf16[4,16,512]{2,1,0:T(8,128)(2,1)S(1)}, bf16[4,16,512]{2,1,0:T(8,128)(2,1)S(1)}, u32[]{:S(2)}, u32[]{:S(2)}) collective-permute-start(bf16[4,16,512]{2,1,0:T(8,128)(2,1)S(1)} %get-tuple-element.48), channel_id=1, source_target_pairs={{0,16},{8,24},{16,0},{24,8},{1,17},{9,25},{17,1},{25,9},{2,18},{10... | collective-permute-start | bytes 196616 | tf_op jit(solution)/shard_map/ppermute | solution.py:288
  164.8 6.1 %collective-permute-start.12 = (bf16[4,16,512]{2,1,0:T(8,128)(2,1)S(1)}, bf16[4,16,512]{2,1,0:T(8,128)(2,1)S(1)}, u32[]{:S(2)}, u32[]{:S(2)}) collective-permute-start(bf16[4,16,512]{2,1,0:T(8,128)(2,1)S(1)} %get-tuple-element.49), channel_id=1, source_target_pairs={{0,24},{8,16},{16,8},{24,0},{1,25},{9,17},{17,9},{25,1},{2,26},{10... | collective-permute-start | bytes 196616 | tf_op jit(solution)/shard_map/ppermute | solution.py:288
  (36 other events, 147.7 us)

commit v2 on v1

--- a/solution.py
+++ b/solution.py
@@ -74,43 +74,45 @@
 def attention_forward(q_ref, k_ref, v_ref, att_ref, p_ref, groups, count, width, span):
     first = head_lanes(count, width)
     pairs = HEADS // 2
+    scale = width ** (-0.5)
 
     def step(index, carry):
         group, pair = index // pairs, index % pairs
         rows = pl.ds(pl.multiple_of(group * count, count), count)
         lanes = pl.ds(pl.multiple_of(pair * 2 * width, 2 * width), 2 * width)
-        query, key, value = q_ref[rows, lanes], k_ref[rows, lanes], v_ref[rows, lanes]
+        query, key, value = q_ref[rows, lanes] * scale, k_ref[rows, lanes], v_ref[rows, lanes]
+        zero = jnp.zeros_like(query)
         total = jnp.zeros((count, 2 * width), F32)
         for half in range(2):
             mine = first if half == 0 else jnp.logical_not(first)
-            scores = dot_nt(jnp.where(mine, query, jnp.zeros_like(query)), key)
-            scores = scores * (width ** (-0.5))
+            scores = dot_nt(key, jnp.where(mine, query, zero))
             if span < count:
                 shift = log2(span)
                 same = (lax.broadcasted_iota(jnp.int32, (count, count), 0) >> shift) == (
                     lax.broadcasted_iota(jnp.int32, (count, count), 1) >> shift
                 )
                 scores = jnp.where(same, scores, -jnp.inf)
-            expo = jnp.exp(scores - jnp.max(scores, axis=-1, keepdims=True))
-            probs = (expo * (1.0 / jnp.sum(expo, axis=-1, keepdims=True))).astype(BF16)
+            expo = jnp.exp(scores - jnp.max(scores, axis=0, keepdims=True))
+            probs = (expo * (1.0 / jnp.sum(expo, axis=0, keepdims=True))).astype(BF16)
             p_ref[index * 2 + half] = probs
-            total += dot(probs, jnp.where(mine, value, jnp.zeros_like(value)))
+            total += dot_tn(probs, jnp.where(mine, value, zero))
         att_ref[rows, lanes] = total.astype(BF16)
         return carry
 
-    lax.fori_loop(0, groups * pairs, step, 0)
+    lax.fori_loop(0, groups * pairs, step, 0, unroll=2)
 
 
 def attention_back(q_ref, k_ref, v_ref, p_ref, da_ref, dqkv_ref, groups, count, width):
     first = head_lanes(count, width)
     pairs = HEADS // 2
     channels = HEADS * width
+    scale = width ** (-0.5)
 
     def step(index, carry):
         group, pair = index // pairs, index % pairs
         rows = pl.ds(pl.multiple_of(group * count, count), count)
         lanes = pl.ds(pl.multiple_of(pair * 2 * width, 2 * width), 2 * width)
-        query, key, value = q_ref[rows, lanes], k_ref[rows, lanes], v_ref[rows, lanes]
+        query, key, value = q_ref[rows, lanes] * scale, k_ref[rows, lanes], v_ref[rows, lanes]
         d_out = da_ref[rows, lanes]
         zero = jnp.zeros_like(query)
         d_query = jnp.zeros((count, 2 * width), F32)
@@ -119,20 +121,20 @@
             mine = first if half == 0 else jnp.logical_not(first)
             probs = p_ref[index * 2 + half]
             d_mine = jnp.where(mine, d_out, zero)
-            d_probs = dot_nt(d_mine, value)
+            d_probs = dot_nt(value, d_mine)
             probs32 = probs.astype(F32)
             weighted = probs32 * d_probs
-            total = jnp.sum(weighted, axis=-1, keepdims=True)
-            d_scores = ((weighted - probs32 * total) * (width ** (-0.5))).astype(BF16)
-            d_query += dot(d_scores, jnp.where(mine, key, zero))
-            d_key += dot_tn(d_scores, jnp.where(mine, query, zero))
-            d_value += dot_tn(probs, d_mine)
-        for part, item in enumerate((d_query, d_key, d_value)):
+            total = jnp.sum(weighted, axis=0, keepdims=True)
+            d_scores = (weighted - probs32 * total).astype(BF16)
+            d_query += dot_tn(d_scores, jnp.where(mine, key, zero))
+            d_key += dot(d_scores, jnp.where(mine, query, zero))
+            d_value += dot(probs, d_mine)
+        for part, item in enumerate((d_query * scale, d_key, d_value)):
             at = pl.ds(pl.multiple_of(part * channels + pair * 2 * width, 2 * width), 2 * width)
             dqkv_ref[rows, at] = item.astype(BF16)
         return carry
 
-    lax.fori_loop(0, groups * pairs, step, 0)
+    lax.fori_loop(0, groups * pairs, step, 0, unroll=2)
 
 
 def start(source, target, sem):
@@ -197,50 +199,63 @@
         copy.wait()
 
 
-def row_back(sizes, d_ref, x_ref, g_ref, w_hbm, turn_hbm, tg_hbm, n_hbm, q_hbm, k_hbm, v_hbm, att_hbm, p_hbm,
-             fg_ref, keep_ref, send_ref,
-             w_ref, turn_ref, tg_ref, n_ref, q_ref, k_ref, v_ref, att_ref, p_ref, da_ref, dqkv_ref, in_sem):
+def row_back(sizes, d_ref, w_hbm, turn_hbm, tg_hbm, n_hbm, q_hbm, k_hbm, v_hbm, att_hbm, p_hbm,
+             dm_ref, dqkv_ref, keep_ref, send_ref,
+             w_ref, turn_ref, tg_ref, n_ref, q_ref, k_ref, v_ref, att_ref, p_ref, da_ref, in_sem):
     rows, length, width = sizes
-    channels = x_ref.shape[-1]
     coming = start_all(
-        [(turn_hbm, turn_ref), (w_hbm.at[0, 3], w_ref.at[3]), (p_hbm, p_ref), (v_hbm, v_ref), (k_hbm, k_ref),
-         (q_hbm, q_ref), (tg_hbm, tg_ref), (n_hbm, n_ref), (att_hbm, att_ref),
-         (w_hbm.at[0, 0:3], w_ref.at[0:3])],
+        [(turn_hbm, turn_ref), (w_hbm.at[0, 3], w_ref), (p_hbm, p_ref), (v_hbm, v_ref), (k_hbm, k_ref),
+         (q_hbm, q_ref), (tg_hbm, tg_ref), (n_hbm, n_ref), (att_hbm, att_ref)],
         in_sem,
     )
     coming[0].wait()
     d_middle = dot(turn_ref[...], d_ref[...]).astype(BF16)
+    dm_ref[...] = d_middle
     coming[1].wait()
-    da_ref[...] = dot_nt(d_middle, w_ref[3]).astype(BF16)
+    da_ref[...] = dot_nt(d_middle, w_ref[...]).astype(BF16)
     for copy in coming[2:6]:
         copy.wait()
     attention_back(q_ref, k_ref, v_ref, p_ref, da_ref, dqkv_ref, rows, length, width)
-    for copy in coming[6:10]:
+    for copy in coming[6:9]:
         copy.wait()
     weight_grads(n_ref[...], att_ref[...], dqkv_ref, d_middle, tg_ref[...], keep_ref, send_ref)
+
+
+def field_back(rows, x_ref, dm_ref, dqkv_ref, g_ref, w_hbm, fg_ref, w_ref, in_sem):
+    channels = x_ref.shape[-1]
+    copy = start(w_hbm.at[0, 0:3], w_ref, in_sem)
+    length = dm_ref.shape[0] // rows
+    field = jnp.concatenate([x_ref[:, i].reshape(length, channels) for i in range(rows)], axis=0)
+    copy.wait()
     d_normed = input_back(dqkv_ref, w_ref)
-    field = jnp.concatenate([x_ref[:, i].reshape(length, channels) for i in range(rows)], axis=0)
-    result = d_middle.astype(F32) + norm_back(field.astype(F32), g_ref[0:1], d_normed)
+    result = dm_ref[...].astype(F32) + norm_back(field.astype(F32), g_ref[0:1], d_normed)
     result = result.astype(BF16)
     for i in range(rows):
         piece = result[i * length : (i + 1) * length]
         fg_ref[:, i] = piece.reshape(fg_ref.shape[0], fg_ref.shape[2], channels)
 
 
-def column_both(sizes, parts, m_ref, *refs):
+def column_first(parts, *refs):
+    c_refs, (w_hbm, tc_hbm, cot_ref, da_ref, w_ref, t_ref, in_sem) = refs[:parts], refs[parts:]
+    coming = start_all([(tc_hbm, t_ref), (w_hbm.at[1, 3], w_ref)], in_sem)
+    cotangent = jnp.concatenate([ref[...] for ref in c_refs], axis=0)
+    coming[0].wait()
+    cotangent = dot(t_ref[...], cotangent).astype(BF16)
+    cot_ref[...] = cotangent
+    coming[1].wait()
+    da_ref[...] = dot_nt(cotangent, w_ref[...]).astype(BF16)
+
+
+def column_main(sizes, m_ref, cot_ref, da_ref, g_ref, w_hbm, tm_hbm, td_hbm,
+                dm_ref, mid_ref, n_ref, att_ref, dqkv_ref,
+                w_ref, t_ref, q_ref, k_ref, v_ref, p_ref, in_sem):
     height, cols, width, together = sizes
-    c_refs, refs = refs[:parts], refs[parts:]
-    g_ref, w_hbm, tm_hbm, tc_hbm, to_hbm, td_hbm, tg_hbm = refs[:7]
-    out_refs, refs = refs[7 : 7 + parts], refs[7 + parts :]
-    dm_ref, keep_ref, send_ref = refs[:3]
-    w_ref, t_ref, n_ref, q_ref, k_ref, v_ref, att_ref, p_ref, da_ref, dqkv_ref, in_sem = refs[3:]
     coming = start_all([(tm_hbm, t_ref.at[0])], in_sem)
-    coming += start_all([(w_hbm.at[1, part], w_ref.at[part]) for part in range(4)], in_sem, 1)
-    coming += start_all(
-        [(hbm, t_ref.at[1 + at]) for at, hbm in enumerate((tc_hbm, to_hbm, td_hbm, tg_hbm))], in_sem, 5
-    )
+    coming += start_all([(w_hbm.at[1, part], w_ref.at[part]) for part in range(3)], in_sem, 1)
+    coming += start_all([(td_hbm, t_ref.at[1])], in_sem, 4)
     coming[0].wait()
     middle = dot(t_ref[0], m_ref[...])
+    mid_ref[...] = middle.astype(BF16)
     centred, inverse = statistics(middle)
     normed = (centred * inverse * g_ref[1:2]).astype(BF16)
     n_ref[...] = normed
@@ -250,21 +265,26 @@
     count = together * height
     groups = cols // together
     attention_forward(q_ref, k_ref, v_ref, att_ref, p_ref, groups, count, width, height)
-    for copy in coming[4:]:
-        copy.wait()
-    output = (middle + dot(att_ref[...], w_ref[3])).astype(BF16)
-    output = dot(t_ref[2], output).astype(BF16)
+    attention_back(q_ref, k_ref, v_ref, p_ref, da_ref, dqkv_ref, groups, count, width)
+    d_normed = input_back(dqkv_ref, w_ref)
+    middle = mid_ref[...].astype(F32)
+    d_middle = cot_ref[...].astype(F32) + norm_back(middle, g_ref[1:2], d_normed)
+    coming[4].wait()
+    dm_ref[...] = dot(t_ref[1], d_middle.astype(BF16)).astype(BF16)
+
+
+def column_last(parts, cot_ref, mid_ref, n_ref, att_ref, dqkv_ref, w_hbm, to_hbm, tg_hbm, *refs):
+    out_refs, (keep_ref, send_ref, w_ref, to_ref, tg_ref, in_sem) = refs[:parts], refs[parts:]
+    coming = start_all([(tg_hbm, tg_ref), (w_hbm.at[1, 3], w_ref), (to_hbm, to_ref)], in_sem)
+    coming[0].wait()
+    weight_grads(n_ref[...], att_ref[...], dqkv_ref, cot_ref[...], tg_ref[...], keep_ref, send_ref)
+    coming[1].wait()
+    output = (mid_ref[...].astype(F32) + dot(att_ref[...], w_ref[...])).astype(BF16)
+    coming[2].wait()
+    output = dot(to_ref[...], output).astype(BF16)
     size = output.shape[0] // parts
     for part in range(parts):
         out_refs[part][...] = output[part * size : (part + 1) * size]
-    cotangent = jnp.concatenate([ref[...] for ref in c_refs], axis=0)
-    cotangent = dot(t_ref[1], cotangent).astype(BF16)
-    da_ref[...] = dot_nt(cotangent, w_ref[3]).astype(BF16)
-    attention_back(q_ref, k_ref, v_ref, p_ref, da_ref, dqkv_ref, groups, count, width)
-    weight_grads(n_ref[...], att_ref[...], dqkv_ref, cotangent, t_ref[4], keep_ref, send_ref)
-    d_normed = input_back(dqkv_ref, w_ref)
-    d_middle = cotangent.astype(F32) + norm_back(middle, g_ref[1:2], d_normed)
-    dm_ref[...] = dot(t_ref[3], d_middle.astype(BF16)).astype(BF16)
 
 
 VMEM = pl.BlockSpec(memory_space=pltpu.VMEM)
@@ -279,7 +299,7 @@
         out_specs=[spec for _, spec in outs],
         out_shape=[shape for shape, _ in outs],
         scratch_shapes=scratch,
-        compiler_params=pltpu.CompilerParams(vmem_limit_bytes=40 * 1024 * 1024),
+        compiler_params=pltpu.CompilerParams(vmem_limit_bytes=61 * 1024 * 1024),
         cost_estimate=pl.CostEstimate(flops=flops, bytes_accessed=moved, transcendentals=0),
     )(*[item for item, _ in ins])
 
@@ -288,10 +308,13 @@
     return lax.ppermute(item, axis, [(at, at ^ step) for at in range(count)])
 
 
-def reduce_grads(keep, send, row_parts, plane, core):
-    _, parts, size, channels = keep.shape
+def add_pair(keep, send, plane, core):
     got = swap(send, "col", plane * core, 1)
-    total = (keep.astype(F32) + got.astype(F32)).astype(BF16)
+    return (keep.astype(F32) + got.astype(F32)).astype(BF16)
+
+
+def reduce_grads(total, row_parts, plane, core):
+    _, parts, size, channels = total.shape
     held = total[0].astype(F32)
     for step in range(1, plane):
         held = held + swap(total[step], "col", plane * core, step * core).astype(F32)
@@ -354,43 +377,61 @@
          copies((5,)), copies((6,))],
         5 * unit,
     )
+    sent = mid
     mid = lax.all_to_all(
         mid.reshape(devices, rows * cols, channels), ("row", "col"), 0, 0, tiled=True
     ).reshape(tokens, channels)
 
+    cots[0], _ = lax.optimization_barrier((cots[0], sent))
+    cot, d_att = call(
+        functools.partial(column_first, row_parts),
+        [(item, VMEM) for item in cots] + [(weights, HBM), (turn_cot, HBM)],
+        [(flat, VMEM), (flat, VMEM)], [square, plain, copies((2,))], 2 * unit,
+    )
     count = together * height
-    results = call(
-        functools.partial(column_both, (height, cols, width, together), row_parts),
-        [(mid, VMEM)] + [(item, VMEM) for item in cots] + [(gains, VMEM), (weights, HBM)]
-        + [(turn, HBM) for turn in (turn_in, turn_cot, turn_output, turn_out, turn_grads)],
-        [(like(high * cols, channels), VMEM)] * row_parts + [(flat, VMEM), packed, packed],
-        [pltpu.VMEM((4, channels, channels), BF16), pltpu.VMEM((5, tokens, channels), BF16),
-         plain, plain, plain, plain, plain, pltpu.VMEM((cols // together * HEADS, count, count), BF16),
-         plain, pltpu.VMEM((tokens, 3 * channels), BF16), copies((9,))],
-        18 * unit,
-    )
-    outs, (d_mid, keep_b, send_b) = results[:row_parts], results[row_parts:]
+    wide_flat = like(tokens, 3 * channels)
+    d_mid, mid_kept, normed_b, att_b, dqkv_b = call(
+        functools.partial(column_main, (height, cols, width, together)),
+        [(mid, VMEM), (cot, VMEM), (d_att, VMEM), (gains, VMEM), (weights, HBM), (turn_in, HBM), (turn_out, HBM)],
+        [(flat, VMEM)] * 4 + [(wide_flat, VMEM)],
+        [pltpu.VMEM((3, channels, channels), BF16), pltpu.VMEM((2, tokens, channels), BF16),
+         plain, plain, plain, pltpu.VMEM((cols // together * HEADS, count, count), BF16), copies((5,))],
+        13 * unit,
+    )
     d_mid = lax.all_to_all(
         d_mid.reshape(devices, rows * cols, channels), ("row", "col"), 0, 0, tiled=True
     ).reshape(tokens, channels)
+    *outs, keep_b, send_b = call(
+        functools.partial(column_last, row_parts),
+        [(item, VMEM) for item in (cot, mid_kept, normed_b, att_b, dqkv_b)]
+        + [(item, HBM) for item in (weights, turn_output, turn_grads)],
+        [(like(high * cols, channels), VMEM)] * row_parts + [packed, packed],
+        [square, plain, square, copies((3,))], 8 * unit,
+    )
+    sum_b = add_pair(keep_b, send_b, plane, core)
+    d_mid, sum_b = lax.optimization_barrier((d_mid, sum_b))
     output = jnp.zeros((high, wide, channels), BF16)
     for step in range(row_parts):
         piece = outs[step].reshape(high, cols, channels)
         piece = piece if step == 0 else swap(piece, "row", row_parts, step)
         output = lax.dynamic_update_slice_in_dim(output, piece, (my_row ^ step) * cols, axis=1)
-    grads_b = reduce_grads(keep_b, send_b, row_parts, plane, core)
-
-    field_grad, keep_a, send_a = call(
+
+    d_mid, dqkv_a, keep_a, send_a = call(
         functools.partial(row_back, sizes),
-        [(d_mid, VMEM), (x, VMEM), (gains, VMEM), (weights, HBM), (turn_rows_back, HBM), (turn_grads, HBM)]
-        + [(item, HBM) for item in saved],
-        [(like(col_parts, rows, wide, channels), VMEM), packed, packed],
-        [pltpu.VMEM((4, channels, channels), BF16), plain, square, plain, plain, plain, plain, plain, probs_ref,
-         plain, pltpu.VMEM((tokens, 3 * channels), BF16), copies((10,))],
-        12 * unit,
+        [(d_mid, VMEM), (weights, HBM), (turn_rows_back, HBM), (turn_grads, HBM)] + [(item, HBM) for item in saved],
+        [(flat, VMEM), (wide_flat, VMEM), packed, packed],
+        [square, plain, square, plain, plain, plain, plain, plain, probs_ref, plain, copies((9,))],
+        10 * unit,
+    )
+    field_grad, = call(
+        functools.partial(field_back, rows),
+        [(x, VMEM), (d_mid, VMEM), (dqkv_a, VMEM), (gains, VMEM), (weights, HBM)],
+        [(like(col_parts, rows, wide, channels), VMEM)],
+        [pltpu.VMEM((3, channels, channels), BF16), copies], 3 * unit,
     )
     field_grad = lax.all_to_all(field_grad, "col", 0, 0, tiled=True).reshape(high, wide, channels)
-    grads_a = reduce_grads(keep_a, send_a, row_parts, plane, core)
+    grads_b = reduce_grads(sum_b, row_parts, plane, core)
+    grads_a = reduce_grads(add_pair(keep_a, send_a, plane, core), row_parts, plane, core)
     return output, field_grad, jnp.concatenate([grads_a, grads_b], axis=0)
 
 

time: 174 us -> 162 us (0.931)
  local copies, waits for them, and re-layouts: 33.8 us -> 6.96 us
  Pallas kernels: 36.7 us -> 54.1 us
  starting transfers between devices: 51.8 us -> 42 us
  waiting for transfers between devices: 39.9 us -> 46.5 us
    unnamed x73 -> x49, local copies, waits for them, and re-layouts: 30.8 us -> 4.02 us
    pallas_call x3 -> x6, Pallas kernels: 36.7 us -> 54.1 us  [call(): pl.pallas_call(kernel, in_specs=[spec for _, spec in ins], out_specs=[spe...]
    ppermute x20, starting transfers between devices: 35.5 us -> 25.8 us  [swap(): return lax.ppermute(item, axis, [(at, at ^ step) for at in range(count)])]
    ppermute x20, waiting for transfers between devices: 15.7 us -> 23.7 us  [swap(): return lax.ppermute(item, axis, [(at, at ^ step) for at in range(count)])]
    all_to_all x1, waiting for transfers between devices: 11 us -> 6.51 us  [body(): lax.all_to_all(mid.reshape(devices, rows * cols, channels), ('row', 'col'...]
    all_to_all x1, waiting for transfers between devices: 9.88 us -> 13.8 us  [body(): lax.all_to_all(d_mid.reshape(devices, rows * cols, channels), ('row', 'co...]
    convert_element_type x5, other arithmetic: 3.48 us -> 5.3 us  [one_hot(): (source == lax.broadcasted_iota(jnp.int32, (total, total), 1 - lead)).ast...]
  transfers between devices with their start and end apart: 24 -> 24, of which waited for: 7 -> 8; matrix products, arithmetic and copies ran while one was open for 7% -> 8% of each run, Pallas kernels for 11% -> 12%
where the time goes in v2:
time: 162 us; the launch traced here: 161 us
  Pallas kernels  54.1 us (33%)
  waiting for transfers between devices  46.5 us (29%)
  starting transfers between devices  42 us (26%)
  other arithmetic  10.5 us (6%)
  local copies, waits for them, and re-layouts  6.96 us (4%)
    pallas_call x6, Pallas kernels, call(): pl.pallas_call(kernel, in_specs=[spec for _, spec in ins], out_specs=[spe...  54.1 us
    ppermute x20, starting transfers between devices, swap(): return lax.ppermute(item, axis, [(at, at ^ step) for at in range(count)])  25.8 us
    ppermute x20, waiting for transfers between devices, swap(): return lax.ppermute(item, axis, [(at, at ^ step) for at in range(count)])  23.7 us
    all_to_all x1, waiting for transfers between devices, body(): lax.all_to_all(d_mid.reshape(devices, rows * cols, channels), ('row', 'co...  13.8 us
    all_to_all x1, waiting for transfers between devices, body(): lax.all_to_all(mid.reshape(devices, rows * cols, channels), ('row', 'col'...  6.51 us
    all_to_all x1, starting transfers between devices, body(): lax.all_to_all(field.reshape(col_parts, rows, wide, channels), 'col', 0,...  5.31 us
    convert_element_type x5, other arithmetic, one_hot(): (source == lax.broadcasted_iota(jnp.int32, (total, total), 1 - lead)).ast...  5.3 us
    unnamed x49, local copies, waits for them, and re-layouts  4.02 us
  transfers between devices with their start and end apart: 24, of which 8 were waited for; matrix products, arithmetic and copies ran while one was open for 8% of the time, Pallas kernels for 12%

profile of v2, /device:TPU:0, one launch (start us, length us, event | category | flops | bytes accessed | tf_op | source)
XLA Modules:
  0.0 161.1 jit_solution(6918602146507571659)
XLA Ops:
  0.7 5.3 %all-to-all-start = ((bf16[8,2,32,512]{3,2,1,0:T(8,128)(2,1)}), bf16[8,2,32,512]{3,2,1,0:T(8,128)(2,1)S(1)}, u32[]{:S(2)}, u32[]{:S(2)}) async-start(bf16[8,2,32,512]{3,2,1,0:T(8,128)(2,1)} %bitcast.82), calls=%async_computation | async-start | bytes 1048576 | tf_op jit(solution)/shard_map/all_to_all | solution.py:361
  9.4 2.6 %collective-permute-start.1 = (bf16[16,8,512]{2,1,0:T(8,128)(2,1)S(1)}, bf16[16,8,512]{2,1,0:T(8,128)(2,1)S(1)}, u32[]{:S(2)}, u32[]{:S(2)}) collective-permute-start(bf16[16,8,512]{2,1,0:T(8,128)(2,1)S(1)} %get-tuple-element.66), channel_id=1, source_target_pairs={{0,16},{8,24},{16,0},{24,8},{1,17},{9,25},{17,1},{25,9},{2,18},{10... | collective-permute-start | bytes 393224 | tf_op jit(solution)/shard_map/ppermute | solution.py:308
  13.2 2.5 %all-to-all-done.x_ref = bf16[8,2,32,512]{3,2,1,0:T(8,128)(2,1)S(1)} async-done(((bf16[8,2,32,512]{3,2,1,0:T(8,128)(2,1)}), bf16[8,2,32,512]{3,2,1,0:T(8,128)(2,1)S(1)}, u32[]{:S(2)}, u32[]{:S(2)}) %all-to-all-start) | async-done | bytes 524320 | tf_op jit(solution)/shard_map/all_to_all | solution.py:361
  16.6 9.9 %shard_map.193 = (bf16[512,512]{1,0:T(8,128)(2,1)}, bf16[512,512]{1,0:T(8,128)(2,1)}, bf16[512,512]{1,0:T(8,128)(2,1)}, bf16[512,512]{1,0:T(8,128)(2,1)}, bf16[5...) custom-call(bf16[8,2,32,512]{3,2,1,0:T(8,128)(2,1)} %copy-done, f32[2,512]{1,0:T(2,128)} %g_ref.5, ...), custom_call_target="tpu_custom_call" | custom-call | flops 1342177280 | bytes 10489856 | tf_op jit(solution)/shard_map/pallas_call | solution.py:296
  26.5 4.0 %all-to-all-start.1 = ((bf16[32,16,512]{2,1,0:T(8,128)(2,1)}), bf16[32,16,512]{2,1,0:T(8,128)(2,1)S(1)}, u32[]{:S(2)}, u32[]{:S(2)}) async-start(bf16[32,16,512]{2,1,0:T(8,128)(2,1)} %bitcast.84), calls=%async_computation.1 | async-start | bytes 1048576 | tf_op jit(solution)/shard_map/all_to_all | solution.py:381
  35.6 3.9 %shard_map.194 = (bf16[512,512]{1,0:T(8,128)(2,1)}, bf16[512,512]{1,0:T(8,128)(2,1)}) custom-call(bf16[128,512]{1,0:T(8,128)(2,1)} %get-tuple-element.31.refs_0_, bf16[128,512]{1,0:T(8,128)(2,1)} %bitcast.85, bf16[128,512]{1,0:T(8,128)(2,1)} %bitcast.86, bf16[128,512]{1,0:T(8,128)(2,1)} %bitcast.87, bf16[2,4,512,512]{3,2,1,0:T(8,128)(2,1)} %w_hbm.9, ...), custom_call_target="tpu_custom_call" | custom-call | flops 536870912 | bytes 6291456 | tf_op jit(solution)/shard_map/pallas_call | solution.py:296
  39.5 6.5 %all-to-all-done.1 = bf16[32,16,512]{2,1,0:T(8,128)(2,1)S(1)} async-done(((bf16[32,16,512]{2,1,0:T(8,128)(2,1)}), bf16[32,16,512]{2,1,0:T(8,128)(2,1)S(1)}, u32[]{:S(2)}, u32[]{:S(2)}) %all-to-all-start.1) | async-done | bytes 524320 | tf_op jit(solution)/shard_map/all_to_all | solution.py:381
  46.8 16.4 %shard_map.195 = (bf16[512,512]{1,0:T(8,128)(2,1)}, bf16[512,512]{1,0:T(8,128)(2,1)}, bf16[512,512]{1,0:T(8,128)(2,1)}, bf16[512,512]{1,0:T(8,128)(2,1)}, bf16[512,1536]{1,0:T(8,128)(2,1)}) custom-call(bf16[512,512]{1,0:T(8,128)(2,1)} %bitcast.83, bf16[512,512]{1,0:T(8,128)(2,1)} %get-tuple-element.32.cot_ref, bf16[512,512]{1,0:T(8,128)(2,1)} %get-tuple-element.33.da_ref, ...), custom_call_target="tpu_custom_call" | custom-call | flops 3489660928 | bytes 10489856 | tf_op jit(solution)/shard_map/pallas_call | solution.py:296
  63.2 7.2 %shard_map.196 = (bf16[128,512]{1,0:T(8,128)(2,1)}, bf16[128,512]{1,0:T(8,128)(2,1)}, bf16[128,512]{1,0:T(8,128)(2,1)}, bf16[128,512]{1,0:T(8,128)(2,1)}, bf16[4...) custom-call(bf16[512,512]{1,0:T(8,128)(2,1)} %get-tuple-element.32.cot_ref, ...), custom_call_target="tpu_custom_call" | custom-call | flops 2147483648 | bytes 11534336 | tf_op jit(solution)/shard_map/pallas_call | solution.py:296
  70.5 3.4 %all-to-all-start.2 = ((bf16[32,16,512]{2,1,0:T(8,128)(2,1)}), bf16[32,16,512]{2,1,0:T(8,128)(2,1)S(1)}, u32[]{:S(2)}, u32[]{:S(2)}) async-start(bf16[32,16,512]{2,1,0:T(8,128)(2,1)} %bitcast.11), calls=%async_computation.2 | async-start | bytes 1048576 | tf_op jit(solution)/shard_map/all_to_all | solution.py:401
  75.5 13.8 %all-to-all-done.2 = bf16[32,16,512]{2,1,0:T(8,128)(2,1)S(1)} async-done(((bf16[32,16,512]{2,1,0:T(8,128)(2,1)}), bf16[32,16,512]{2,1,0:T(8,128)(2,1)S(1)}, u32[]{:S(2)}, u32[]{:S(2)}) %all-to-all-start.2) | async-done | bytes 524320 | tf_op jit(solution)/shard_map/all_to_all | solution.py:401
  90.1 11.3 %shard_map.197 = (bf16[512,512]{1,0:T(8,128)(2,1)}, bf16[512,1536]{1,0:T(8,128)(2,1)}, bf16[4,4,64,512]{3,2,1,0:T(8,128)(2,1)}, bf16[4,4,64,512]{3,2,1,0:T(8,128)(2,1)}) custom-call(bf16[512,512]{1,0:T(8,128)(2,1)} %bitcast.76, bf16[2,4,512,512]{3,2,1,0:T(8,128)(2,1)} %w_hbm.9, bf16[512,512]{1,0:T(8,128)(2,1)} %get-tuple-element.78.turn_hbm, ...), custom_call_target="tpu_custom_call" | custom-call | flops 2684354560 | bytes 14680064 | tf_op jit(solution)/shard_map/pallas_call | solution.py:296
  103.3 2.7 %collective-permute-start.5 = (bf16[16,8,512]{2,1,0:T(8,128)(2,1)S(1)}, bf16[16,8,512]{2,1,0:T(8,128)(2,1)S(1)}, u32[]{:S(2)}, u32[]{:S(2)}) collective-permute-start(bf16[16,8,512]{2,1,0:T(8,128)(2,1)S(1)} %bitcast.88), channel_id=1, source_target_pairs={{0,24},{8,16},{16,8},{24,0},{1,25},{9,17},{17,9},{25,1},{2,26},{10... | collective-permute-start | bytes 393224 | tf_op jit(solution)/shard_map/ppermute | solution.py:308
  106.0 2.8 %collective-permute-done.3 = bf16[16,8,512]{2,1,0:T(8,128)(2,1)S(1)} collective-permute-done((bf16[16,8,512]{2,1,0:T(8,128)(2,1)S(1)}, bf16[16,8,512]{2,1,0:T(8,128)(2,1)S(1)}, u32[]{:S(2)}, u32[]{:S(2)}) %collective-permute-start.3) | collective-permute-done | bytes 131104 | tf_op jit(solution)/shard_map/ppermute | solution.py:308
  108.9 6.7 %collective-permute-done.4 = bf16[16,8,512]{2,1,0:T(8,128)(2,1)S(1)} collective-permute-done((bf16[16,8,512]{2,1,0:T(8,128)(2,1)S(1)}, bf16[16,8,512]{2,1,0:T(8,128)(2,1)S(1)}, u32[]{:S(2)}, u32[]{:S(2)}) %collective-permute-start.4) | collective-permute-done | bytes 131104 | tf_op jit(solution)/shard_map/ppermute | solution.py:308
  120.0 5.4 %shard_map.198 = bf16[8,2,32,512]{3,2,1,0:T(8,128)(2,1)} custom-call(bf16[8,2,32,512]{3,2,1,0:T(8,128)(2,1)} %copy-done, bf16[512,512]{1,0:T(8,128)(2,1)} %get-tuple-element.52.dm_ref, bf16[512,1536]{1,0:T(8,128)(2,1)} %get-tuple-element.53.dqkv_ref, f32[2,512]{1,0:T(2,128)} %g_ref.5, bf16[2,4,512,512]{3,2,1,0:T(8,128)(2,1)} %w_hbm.9), custom_call_target="tpu_custom_call" | custom-call | flops 805306368 | bytes 7344128 | tf_op jit(solution)/shard_map/pallas_call | solution.py:296
  125.4 3.5 %all-to-all-start.3 = ((bf16[8,2,32,512]{3,2,1,0:T(8,128)(2,1)}), bf16[8,2,32,512]{3,2,1,0:T(8,128)(2,1)S(1)}, u32[]{:S(2)}, u32[]{:S(2)}) async-start(bf16[8,2,32,512]{3,2,1,0:T(8,128)(2,1)} %shard_map.198), calls=%async_computation.3 | async-start | bytes 1048576 | tf_op jit(solution)/shard_map/all_to_all | solution.py:432
  130.6 2.9 %collective-permute-start.10 = (bf16[4,64,512]{2,1,0:T(8,128)(2,1)S(1)}, bf16[4,64,512]{2,1,0:T(8,128)(2,1)S(1)}, u32[]{:S(2)}, u32[]{:S(2)}) collective-permute-start(bf16[4,64,512]{2,1,0:T(8,128)(2,1)S(1)} %get-tuple-element.58), channel_id=1, source_target_pairs={{0,6},{1,7},{2,4},{3,5},{4,2},{5,3},{6,0},{7,1},{8,14},{9,15},{10,... | collective-permute-start | bytes 786440 | tf_op jit(solution)/shard_map/ppermute | solution.py:308
  135.4 2.8 %collective-permute-start.17 = (bf16[4,16,512]{2,1,0:T(8,128)(2,1)S(1)}, bf16[4,16,512]{2,1,0:T(8,128)(2,1)S(1)}, u32[]{:S(2)}, u32[]{:S(2)}) collective-permute-start(bf16[4,16,512]{2,1,0:T(8,128)(2,1)S(1)} %get-tuple-element.70), channel_id=1, source_target_pairs={{0,8},{8,0},{16,24},{24,16},{1,9},{9,1},{17,25},{25,17},{2,10},{10... | collective-permute-start | bytes 196616 | tf_op jit(solution)/shard_map/ppermute | solution.py:308
  138.2 6.6 %collective-permute-done.10 = bf16[4,64,512]{2,1,0:T(8,128)(2,1)S(1)} collective-permute-done((bf16[4,64,512]{2,1,0:T(8,128)(2,1)S(1)}, bf16[4,64,512]{2,1,0:T(8,128)(2,1)S(1)}, u32[]{:S(2)}, u32[]{:S(2)}) %collective-permute-start.10) | collective-permute-done | bytes 262176 | tf_op jit(solution)/shard_map/ppermute | solution.py:308
  146.5 2.5 %collective-permute-done.8 = bf16[4,64,512]{2,1,0:T(8,128)(2,1)S(1)} collective-permute-done((bf16[4,64,512]{2,1,0:T(8,128)(2,1)S(1)}, bf16[4,64,512]{2,1,0:T(8,128)(2,1)S(1)}, u32[]{:S(2)}, u32[]{:S(2)}) %collective-permute-start.8) | collective-permute-done | bytes 262176 | tf_op jit(solution)/shard_map/ppermute | solution.py:308
  149.1 2.8 %collective-permute-start.11 = (bf16[4,16,512]{2,1,0:T(8,128)(2,1)S(1)}, bf16[4,16,512]{2,1,0:T(8,128)(2,1)S(1)}, u32[]{:S(2)}, u32[]{:S(2)}) collective-permute-start(bf16[4,16,512]{2,1,0:T(8,128)(2,1)S(1)} %get-tuple-element.67), channel_id=1, source_target_pairs={{0,8},{8,0},{16,24},{24,16},{1,9},{9,1},{17,25},{25,17},{2,10},{10... | collective-permute-start | bytes 196616 | tf_op jit(solution)/shard_map/ppermute | solution.py:308
  151.9 2.4 %collective-permute-start.13 = (bf16[4,16,512]{2,1,0:T(8,128)(2,1)S(1)}, bf16[4,16,512]{2,1,0:T(8,128)(2,1)S(1)}, u32[]{:S(2)}, u32[]{:S(2)}) collective-permute-start(bf16[4,16,512]{2,1,0:T(8,128)(2,1)S(1)} %get-tuple-element.69), channel_id=1, source_target_pairs={{0,24},{8,16},{16,8},{24,0},{1,25},{9,17},{17,9},{25,1},{2,26},{10... | collective-permute-start | bytes 196616 | tf_op jit(solution)/shard_map/ppermute | solution.py:308
  154.4 5.1 %collective-permute-done.12 = bf16[4,16,512]{2,1,0:T(8,128)(2,1)S(1)} collective-permute-done((bf16[4,16,512]{2,1,0:T(8,128)(2,1)S(1)}, bf16[4,16,512]{2,1,0:T(8,128)(2,1)S(1)}, u32[]{:S(2)}, u32[]{:S(2)}) %collective-permute-start.12) | collective-permute-done | bytes 65568 | tf_op jit(solution)/shard_map/ppermute | solution.py:308
  (103 shorter events, 27.2 us)
Async XLA Ops:
  0.7 15.1 %all-to-all-start = ((bf16[8,2,32,512]{3,2,1,0:T(8,128)(2,1)}), bf16[8,2,32,512]{3,2,1,0:T(8,128)(2,1)S(1)}, u32[]{:S(2)}, u32[]{:S(2)}) async-start(bf16[8,2,32,512]{3,2,1,0:T(8,128)(2,1)} %bitcast.82), calls=%async_computation | async-start | bytes 1048576 | tf_op jit(solution)/shard_map/all_to_all | solution.py:361
  7.8 27.1 %collective-permute-start = (bf16[16,8,512]{2,1,0:T(8,128)(2,1)S(1)}, bf16[16,8,512]{2,1,0:T(8,128)(2,1)S(1)}, u32[]{:S(2)}, u32[]{:S(2)}) collective-permute-start(bf16[16,8,512]{2,1,0:T(8,128)(2,1)S(1)} %get-tuple-element.64), channel_id=1, source_target_pairs={{0,8},{8,0},{16,24},{24,16},{1,9},{9,1},{17,25},{25,17},{2,10},{10... | collective-permute-start | bytes 393224 | tf_op jit(solution)/shard_map/ppermute | solution.py:308
  9.4 25.5 %collective-permute-start.1 = (bf16[16,8,512]{2,1,0:T(8,128)(2,1)S(1)}, bf16[16,8,512]{2,1,0:T(8,128)(2,1)S(1)}, u32[]{:S(2)}, u32[]{:S(2)}) collective-permute-start(bf16[16,8,512]{2,1,0:T(8,128)(2,1)S(1)} %get-tuple-element.66), channel_id=1, source_target_pairs={{0,16},{8,24},{16,0},{24,8},{1,17},{9,25},{17,1},{25,9},{2,18},{10... | collective-permute-start | bytes 393224 | tf_op jit(solution)/shard_map/ppermute | solution.py:308
  12.0 22.9 %collective-permute-start.2 = (bf16[16,8,512]{2,1,0:T(8,128)(2,1)S(1)}, bf16[16,8,512]{2,1,0:T(8,128)(2,1)S(1)}, u32[]{:S(2)}, u32[]{:S(2)}) collective-permute-start(bf16[16,8,512]{2,1,0:T(8,128)(2,1)S(1)} %get-tuple-element.63), channel_id=1, source_target_pairs={{0,24},{8,16},{16,8},{24,0},{1,25},{9,17},{17,9},{25,1},{2,26},{10... | collective-permute-start | bytes 393224 | tf_op jit(solution)/shard_map/ppermute | solution.py:308
  26.5 19.5 %all-to-all-start.1 = ((bf16[32,16,512]{2,1,0:T(8,128)(2,1)}), bf16[32,16,512]{2,1,0:T(8,128)(2,1)S(1)}, u32[]{:S(2)}, u32[]{:S(2)}) async-start(bf16[32,16,512]{2,1,0:T(8,128)(2,1)} %bitcast.84), calls=%async_computation.1 | async-start | bytes 1048576 | tf_op jit(solution)/shard_map/all_to_all | solution.py:381
  70.5 3.5 %collective-permute-start.6 = (bf16[4,4,64,512]{3,2,1,0:T(8,128)(2,1)}, bf16[4,4,64,512]{3,2,1,0:T(8,128)(2,1)S(1)}, u32[]{:S(2)}, u32[]{:S(2)}) collective-permute-start(bf16[4,4,64,512]{3,2,1,0:T(8,128)(2,1)} %get-tuple-element.44), channel_id=1, source_target_pairs={{0,1},{1,0},{2,3},{3,2},{4,5},{5,4},{6,7},{7,6},{8,9},{9,8},{10,11... | collective-permute-start | bytes 3145736 | tf_op jit(solution)/shard_map/ppermute | solution.py:308
  70.5 18.7 %all-to-all-start.2 = ((bf16[32,16,512]{2,1,0:T(8,128)(2,1)}), bf16[32,16,512]{2,1,0:T(8,128)(2,1)S(1)}, u32[]{:S(2)}, u32[]{:S(2)}) async-start(bf16[32,16,512]{2,1,0:T(8,128)(2,1)} %bitcast.11), calls=%async_computation.2 | async-start | bytes 1048576 | tf_op jit(solution)/shard_map/all_to_all | solution.py:401
  101.4 27.6 %collective-permute-start.7 = (bf16[4,4,64,512]{3,2,1,0:T(8,128)(2,1)}, bf16[4,4,64,512]{3,2,1,0:T(8,128)(2,1)}, u32[]{:S(2)}, u32[]{:S(2)}) collective-permute-start(bf16[4,4,64,512]{3,2,1,0:T(8,128)(2,1)} %get-tuple-element.55), channel_id=1, source_target_pairs={{0,1},{1,0},{2,3},{3,2},{4,5},{5,4},{6,7},{7,6},{8,9},{9,8},{10,11... | collective-permute-start | bytes 3145736 | tf_op jit(solution)/shard_map/ppermute | solution.py:308
  101.5 7.4 %collective-permute-start.3 = (bf16[16,8,512]{2,1,0:T(8,128)(2,1)S(1)}, bf16[16,8,512]{2,1,0:T(8,128)(2,1)S(1)}, u32[]{:S(2)}, u32[]{:S(2)}) collective-permute-start(bf16[16,8,512]{2,1,0:T(8,128)(2,1)S(1)} %bitcast.90), channel_id=1, source_target_pairs={{0,8},{8,0},{16,24},{24,16},{1,9},{9,1},{17,25},{25,17},{2,10},{10... | collective-permute-start | bytes 393224 | tf_op jit(solution)/shard_map/ppermute | solution.py:308
  102.8 12.7 %collective-permute-start.4 = (bf16[16,8,512]{2,1,0:T(8,128)(2,1)S(1)}, bf16[16,8,512]{2,1,0:T(8,128)(2,1)S(1)}, u32[]{:S(2)}, u32[]{:S(2)}) collective-permute-start(bf16[16,8,512]{2,1,0:T(8,128)(2,1)S(1)} %bitcast.89), channel_id=1, source_target_pairs={{0,16},{8,24},{16,0},{24,8},{1,17},{9,25},{17,1},{25,9},{2,18},{10... | collective-permute-start | bytes 393224 | tf_op jit(solution)/shard_map/ppermute | solution.py:308
  103.3 12.2 %collective-permute-start.5 = (bf16[16,8,512]{2,1,0:T(8,128)(2,1)S(1)}, bf16[16,8,512]{2,1,0:T(8,128)(2,1)S(1)}, u32[]{:S(2)}, u32[]{:S(2)}) collective-permute-start(bf16[16,8,512]{2,1,0:T(8,128)(2,1)S(1)} %bitcast.88), channel_id=1, source_target_pairs={{0,24},{8,16},{16,8},{24,0},{1,25},{9,17},{17,9},{25,1},{2,26},{10... | collective-permute-start | bytes 393224 | tf_op jit(solution)/shard_map/ppermute | solution.py:308
  116.5 17.5 %collective-permute-start.14 = (bf16[4,64,512]{2,1,0:T(8,128)(2,1)}, bf16[4,64,512]{2,1,0:T(8,128)(2,1)S(1)}, u32[]{:S(2)}, u32[]{:S(2)}) collective-permute-start(bf16[4,64,512]{2,1,0:T(8,128)(2,1)} %get-tuple-element.60), channel_id=1, source_target_pairs={{0,2},{1,3},{2,0},{3,1},{4,6},{5,7},{6,4},{7,5},{8,10},{9,11},{10,... | collective-permute-start | bytes 786440 | tf_op jit(solution)/shard_map/ppermute | solution.py:308
  117.5 16.7 %collective-permute-start.15 = (bf16[4,64,512]{2,1,0:T(8,128)(2,1)}, bf16[4,64,512]{2,1,0:T(8,128)(2,1)}, u32[]{:S(2)}, u32[]{:S(2)}) collective-permute-start(bf16[4,64,512]{2,1,0:T(8,128)(2,1)} %get-tuple-element.62), channel_id=1, source_target_pairs={{0,4},{1,5},{2,6},{3,7},{4,0},{5,1},{6,2},{7,3},{8,12},{9,13},{10,... | collective-permute-start | bytes 786440 | tf_op jit(solution)/shard_map/ppermute | solution.py:308
  118.0 16.1 %collective-permute-start.16 = (bf16[4,64,512]{2,1,0:T(8,128)(2,1)}, bf16[4,64,512]{2,1,0:T(8,128)(2,1)}, u32[]{:S(2)}, u32[]{:S(2)}) collective-permute-start(bf16[4,64,512]{2,1,0:T(8,128)(2,1)} %get-tuple-element.61), channel_id=1, source_target_pairs={{0,6},{1,7},{2,4},{3,5},{4,2},{5,3},{6,0},{7,1},{8,14},{9,15},{10,... | collective-permute-start | bytes 786440 | tf_op jit(solution)/shard_map/ppermute | solution.py:308
  125.4 29.0 %all-to-all-start.3 = ((bf16[8,2,32,512]{3,2,1,0:T(8,128)(2,1)}), bf16[8,2,32,512]{3,2,1,0:T(8,128)(2,1)S(1)}, u32[]{:S(2)}, u32[]{:S(2)}) async-start(bf16[8,2,32,512]{3,2,1,0:T(8,128)(2,1)} %shard_map.198), calls=%async_computation.3 | async-start | bytes 1048576 | tf_op jit(solution)/shard_map/all_to_all | solution.py:432
  130.6 14.2 %collective-permute-start.10 = (bf16[4,64,512]{2,1,0:T(8,128)(2,1)S(1)}, bf16[4,64,512]{2,1,0:T(8,128)(2,1)S(1)}, u32[]{:S(2)}, u32[]{:S(2)}) collective-permute-start(bf16[4,64,512]{2,1,0:T(8,128)(2,1)S(1)} %get-tuple-element.58), channel_id=1, source_target_pairs={{0,6},{1,7},{2,4},{3,5},{4,2},{5,3},{6,0},{7,1},{8,14},{9,15},{10,... | collective-permute-start | bytes 786440 | tf_op jit(solution)/shard_map/ppermute | solution.py:308
  133.5 15.5 %collective-permute-start.8 = (bf16[4,64,512]{2,1,0:T(8,128)(2,1)S(1)}, bf16[4,64,512]{2,1,0:T(8,128)(2,1)S(1)}, u32[]{:S(2)}, u32[]{:S(2)}) collective-permute-start(bf16[4,64,512]{2,1,0:T(8,128)(2,1)S(1)} %get-tuple-element.57), channel_id=1, source_target_pairs={{0,2},{1,3},{2,0},{3,1},{4,6},{5,7},{6,4},{7,5},{8,10},{9,11},{10,... | collective-permute-start | bytes 786440 | tf_op jit(solution)/shard_map/ppermute | solution.py:308
  134.0 14.9 %collective-permute-start.9 = (bf16[4,64,512]{2,1,0:T(8,128)(2,1)S(1)}, bf16[4,64,512]{2,1,0:T(8,128)(2,1)S(1)}, u32[]{:S(2)}, u32[]{:S(2)}) collective-permute-start(bf16[4,64,512]{2,1,0:T(8,128)(2,1)S(1)} %get-tuple-element.59), channel_id=1, source_target_pairs={{0,4},{1,5},{2,6},{3,7},{4,0},{5,1},{6,2},{7,3},{8,12},{9,13},{10,... | collective-permute-start | bytes 786440 | tf_op jit(solution)/shard_map/ppermute | solution.py:308
  135.4 16.6 %collective-permute-start.17 = (bf16[4,16,512]{2,1,0:T(8,128)(2,1)S(1)}, bf16[4,16,512]{2,1,0:T(8,128)(2,1)S(1)}, u32[]{:S(2)}, u32[]{:S(2)}) collective-permute-start(bf16[4,16,512]{2,1,0:T(8,128)(2,1)S(1)} %get-tuple-element.70), channel_id=1, source_target_pairs={{0,8},{8,0},{16,24},{24,16},{1,9},{9,1},{17,25},{25,17},{2,10},{10... | collective-permute-start | bytes 196616 | tf_op jit(solution)/shard_map/ppermute | solution.py:308
  138.2 16.2 %collective-permute-start.18 = (bf16[4,16,512]{2,1,0:T(8,128)(2,1)S(1)}, bf16[4,16,512]{2,1,0:T(8,128)(2,1)S(1)}, u32[]{:S(2)}, u32[]{:S(2)}) collective-permute-start(bf16[4,16,512]{2,1,0:T(8,128)(2,1)S(1)} %get-tuple-element.71), channel_id=1, source_target_pairs={{0,16},{8,24},{16,0},{24,8},{1,17},{9,25},{17,1},{25,9},{2,18},{10... | collective-permute-start | bytes 196616 | tf_op jit(solution)/shard_map/ppermute | solution.py:308
  144.8 9.6 %collective-permute-start.19 = (bf16[4,16,512]{2,1,0:T(8,128)(2,1)S(1)}, bf16[4,16,512]{2,1,0:T(8,128)(2,1)S(1)}, u32[]{:S(2)}, u32[]{:S(2)}) collective-permute-start(bf16[4,16,512]{2,1,0:T(8,128)(2,1)S(1)} %get-tuple-element.72), channel_id=1, source_target_pairs={{0,24},{8,16},{16,8},{24,0},{1,25},{9,17},{17,9},{25,1},{2,26},{10... | collective-permute-start | bytes 196616 | tf_op jit(solution)/shard_map/ppermute | solution.py:308
  149.1 5.3 %collective-permute-start.11 = (bf16[4,16,512]{2,1,0:T(8,128)(2,1)S(1)}, bf16[4,16,512]{2,1,0:T(8,128)(2,1)S(1)}, u32[]{:S(2)}, u32[]{:S(2)}) collective-permute-start(bf16[4,16,512]{2,1,0:T(8,128)(2,1)S(1)} %get-tuple-element.67), channel_id=1, source_target_pairs={{0,8},{8,0},{16,24},{24,16},{1,9},{9,1},{17,25},{25,17},{2,10},{10... | collective-permute-start | bytes 196616 | tf_op jit(solution)/shard_map/ppermute | solution.py:308
  151.9 7.6 %collective-permute-start.12 = (bf16[4,16,512]{2,1,0:T(8,128)(2,1)S(1)}, bf16[4,16,512]{2,1,0:T(8,128)(2,1)S(1)}, u32[]{:S(2)}, u32[]{:S(2)}) collective-permute-start(bf16[4,16,512]{2,1,0:T(8,128)(2,1)S(1)} %get-tuple-element.68), channel_id=1, source_target_pairs={{0,16},{8,24},{16,0},{24,8},{1,17},{9,25},{17,1},{25,9},{2,18},{10... | collective-permute-start | bytes 196616 | tf_op jit(solution)/shard_map/ppermute | solution.py:308
  151.9 7.6 %collective-permute-start.13 = (bf16[4,16,512]{2,1,0:T(8,128)(2,1)S(1)}, bf16[4,16,512]{2,1,0:T(8,128)(2,1)S(1)}, u32[]{:S(2)}, u32[]{:S(2)}) collective-permute-start(bf16[4,16,512]{2,1,0:T(8,128)(2,1)S(1)} %get-tuple-element.69), channel_id=1, source_target_pairs={{0,24},{8,16},{16,8},{24,0},{1,25},{9,17},{17,9},{25,1},{2,26},{10... | collective-permute-start | bytes 196616 | tf_op jit(solution)/shard_map/ppermute | solution.py:308
  (24 other events, 243.3 us)

commit v3 on v2

v3 whole, which is shorter than its diff:
```python
import functools
import math

import jax
import jax.numpy as jnp
from jax import lax
from jax.experimental import pallas as pl
from jax.experimental.pallas import tpu as pltpu
from jax.sharding import PartitionSpec as P

HEADS = 8
eps = 1e-05
F32 = jnp.float32
BF16 = jnp.bfloat16


def log2(n):
    assert n & (n - 1) == 0
    return n.bit_length() - 1


def dot(left, right):
    return jnp.dot(left, right, preferred_element_type=F32)


def dot_nt(left, right):
    return lax.dot_general(left, right, (((1,), (1,)), ((), ())), preferred_element_type=F32)


def dot_tn(left, right):
    return lax.dot_general(left, right, (((0,), (0,)), ((), ())), preferred_element_type=F32)


def one_hot(sizes, order, me=None, lead=0):
    total = math.prod(sizes)
    index = lax.broadcasted_iota(jnp.int32, (total, total), lead)
    found = {}
    for axis in reversed(order):
        found[axis] = index & (sizes[axis] - 1)
        index = index >> log2(sizes[axis])
    source, shift = None, 0
    for axis in reversed(range(len(sizes))):
        digit = found[axis] << shift
        source = digit if source is None else source | digit
        shift += log2(sizes[axis])
    if me:
        place, shift = 0, 0
        for axis in reversed(range(len(sizes))):
            if axis in me:
                place = place | (me[axis] << shift)
            shift += log2(sizes[axis])
        source = source ^ place
    hit = source == lax.broadcasted_iota(jnp.int32, (total, total), 1 - lead)
    return jnp.where(hit, 1.0, 0.0).astype(BF16)


def statistics(values):
    average = jnp.mean(values, axis=-1, keepdims=True)
    centred = values - average
    spread = jnp.mean(centred * centred, axis=-1, keepdims=True)
    return centred, lax.rsqrt(spread + eps)


def norm_back(values, gain, d_normed):
    centred, inverse = statistics(values)
    unit = centred * inverse
    scaled = d_normed * gain
    return inverse * (
        scaled
        - jnp.mean(scaled, axis=-1, keepdims=True)
        - unit * jnp.mean(scaled * unit, axis=-1, keepdims=True)
    )


def head_lanes(count, width):
    return lax.broadcasted_iota(jnp.int32, (count, 2 * width), 1) < width


def attention_forward(q_ref, k_ref, v_ref, att_ref, p_ref, groups, count, width, span):
    first = head_lanes(count, width)
    pairs = HEADS // 2
    scale = width ** (-0.5)

    def step(index, carry):
        group, pair = index // pairs, index % pairs
        rows = pl.ds(pl.multiple_of(group * count, count), count)
        lanes = pl.ds(pl.multiple_of(pair * 2 * width, 2 * width), 2 * width)
        query, key, value = q_ref[rows, lanes] * scale, k_ref[rows, lanes], v_ref[rows, lanes]
        zero = jnp.zeros_like(query)
        total = jnp.zeros((count, 2 * width), F32)
        for half in range(2):
            mine = first if half == 0 else jnp.logical_not(first)
            scores = dot_nt(key, jnp.where(mine, query, zero))
            if span < count:
                shift = log2(span)
                same = (lax.broadcasted_iota(jnp.int32, (count, count), 0) >> shift) == (
                    lax.broadcasted_iota(jnp.int32, (count, count), 1) >> shift
                )
                scores = jnp.where(same, scores, -jnp.inf)
            expo = jnp.exp(scores - jnp.max(scores, axis=0, keepdims=True))
            probs = (expo * (1.0 / jnp.sum(expo, axis=0, keepdims=True))).astype(BF16)
            p_ref[index * 2 + half] = probs
            total += dot_tn(probs, jnp.where(mine, value, zero))
        att_ref[rows, lanes] = total.astype(BF16)
        return carry

    lax.fori_loop(0, groups * pairs, step, 0, unroll=2)


def attention_back(q_ref, k_ref, v_ref, p_ref, da_ref, dqkv_ref, groups, count, width):
    first = head_lanes(count, width)
    pairs = HEADS // 2
    channels = HEADS * width
    scale = width ** (-0.5)

    def step(index, carry):
        group, pair = index // pairs, index % pairs
        rows = pl.ds(pl.multiple_of(group * count, count), count)
        lanes = pl.ds(pl.multiple_of(pair * 2 * width, 2 * width), 2 * width)
        query, key, value = q_ref[rows, lanes] * scale, k_ref[rows, lanes], v_ref[rows, lanes]
        d_out = da_ref[rows, lanes]
        zero = jnp.zeros_like(query)
        d_query = jnp.zeros((count, 2 * width), F32)
        d_key, d_value = d_query, d_query
        for half in range(2):
            mine = first if half == 0 else jnp.logical_not(first)
            probs = p_ref[index * 2 + half]
            d_mine = jnp.where(mine, d_out, zero)
            d_probs = dot_nt(value, d_mine)
            probs32 = probs.astype(F32)
            weighted = probs32 * d_probs
            total = jnp.sum(weighted, axis=0, keepdims=True)
            d_scores = (weighted - probs32 * total).astype(BF16)
            d_query += dot_tn(d_scores, jnp.where(mine, key, zero))
            d_key += dot(d_scores, jnp.where(mine, query, zero))
            d_value += dot(probs, d_mine)
        for part, item in enumerate((d_query * scale, d_key, d_value)):
            at = pl.ds(pl.multiple_of(part * channels + pair * 2 * width, 2 * width), 2 * width)
            dqkv_ref[rows, at] = item.astype(BF16)
        return carry

    lax.fori_loop(0, groups * pairs, step, 0, unroll=2)


def start(source, target, sem):
    copy = pltpu.make_async_copy(source, target, sem)
    copy.start()
    return copy


def finish(copies):
    for copy in copies:
        copy.wait()


def set_up(turns, w_hbm, w_ref, turn_ref, sem):
    copy = start(w_hbm, w_ref, sem)
    my_row, my_col = lax.axis_index("row"), lax.axis_index("col")
    for at, (sizes, order, me, lead) in enumerate(turns):
        places = {"row": my_row, "plane": my_col >> 1, "core": my_col & 1}
        turn_ref[at] = one_hot(sizes, order, {axis: places[name] for axis, name in me.items()}, lead)
    copy.wait()


def weight_grads(normed, attended, dqkv_ref, d_top, turn, keep_ref, send_ref, send_hbm, sems):
    channels = normed.shape[-1]
    plane, _, size, _ = keep_ref.shape
    normed = dot(normed, turn).astype(BF16)
    attended = dot(attended, turn).astype(BF16)
    going = []
    for part in (3, 0, 1, 2):
        if part < 3:
            whole = dot_tn(normed, dqkv_ref[:, part * channels : (part + 1) * channels])
        else:
            whole = dot_tn(attended, d_top)
        whole = whole.astype(BF16)
        for group in range(plane):
            at = plane + group
            send_ref[group, part] = whole[at * size : (at + 1) * size]
            keep_ref[group, part] = whole[group * size : (group + 1) * size]
        going.append(start(send_ref.at[:, part], send_hbm.at[:, part], sems.at[part]))
    return going


def send_turned(turn_ref, values, stage_ref, targets, sems):
    size = values.shape[0] // len(targets)
    going = []
    for at, target in enumerate(targets):
        piece = pl.ds(at * size, size)
        stage_ref[piece] = dot(turn_ref[piece], values).astype(BF16)
        going.append(start(stage_ref.at[piece], target, sems.at[at]))
    return going


def quarters(ref):
    size = ref.shape[0] // 4
    return [ref.at[pl.ds(at * size, size)] for at in range(4)]


def input_back(dqkv_ref, w_ref):
    channels = w_ref.shape[-1]
    total = dot_nt(dqkv_ref[:, :channels], w_ref[0])
    total += dot_nt(dqkv_ref[:, channels : 2 * channels], w_ref[1])
    total += dot_nt(dqkv_ref[:, 2 * channels :], w_ref[2])
    return total.astype(BF16).astype(F32)


def row_forward(sizes, x_ref, g_ref, w_ref, turn_ref, mid_hbm, n_ref, q_ref, k_ref, v_ref, att_ref, p_ref,
                mid_ref, sems):
    rows, length, width = sizes
    channels = x_ref.shape[-1]
    field = jnp.concatenate([x_ref[:, i].reshape(length, channels) for i in range(rows)], axis=0)
    field = field.astype(F32)
    centred, inverse = statistics(field)
    normed = (centred * inverse * g_ref[0:1]).astype(BF16)
    n_ref[...] = normed
    for part, ref in enumerate((q_ref, k_ref, v_ref)):
        ref[...] = dot(normed, w_ref[0, part]).astype(BF16)
    attention_forward(q_ref, k_ref, v_ref, att_ref, p_ref, rows, length, width, length)
    field = jnp.concatenate([x_ref[:, i].reshape(length, channels) for i in range(rows)], axis=0)
    middle = (field.astype(F32) + dot(att_ref[...], w_ref[0, 3])).astype(BF16)
    finish(send_turned(turn_ref.at[0], middle, mid_ref, quarters(mid_hbm), sems))


def row_back(sizes, d_ref, w_ref, turn_ref, n_ref, q_ref, k_ref, v_ref, att_ref, p_ref,
             dm_ref, dqkv_ref, keep_ref, send_hbm, da_ref, send_ref, sems):
    rows, length, width = sizes
    d_middle = dot(turn_ref[1], d_ref[...]).astype(BF16)
    dm_ref[...] = d_middle
    da_ref[...] = dot_nt(d_middle, w_ref[0, 3]).astype(BF16)
    attention_back(q_ref, k_ref, v_ref, p_ref, da_ref, dqkv_ref, rows, length, width)
    finish(weight_grads(
        n_ref[...], att_ref[...], dqkv_ref, d_middle, turn_ref[6], keep_ref, send_ref, send_hbm, sems
    ))


def field_back(rows, x_ref, dm_ref, dqkv_ref, g_ref, w_ref, fg_hbm, fg_ref, sem):
    channels = x_ref.shape[-1]
    length = dm_ref.shape[0] // rows
    field = jnp.concatenate([x_ref[:, i].reshape(length, channels) for i in range(rows)], axis=0)
    d_normed = input_back(dqkv_ref, w_ref.at[0])
    result = dm_ref[...].astype(F32) + norm_back(field.astype(F32), g_ref[0:1], d_normed)
    result = result.astype(BF16)
    for i in range(rows):
        piece = result[i * length : (i + 1) * length]
        fg_ref[:, i] = piece.reshape(fg_ref.shape[0], fg_ref.shape[2], channels)
    start(fg_ref, fg_hbm, sem).wait()


def column_first(parts, *refs):
    c_refs, (w_ref, turn_ref, cot_ref, da_ref) = refs[:parts], refs[parts:]
    cotangent = jnp.concatenate([ref[...] for ref in c_refs], axis=0)
    cotangent = dot(turn_ref[4], cotangent).astype(BF16)
    cot_ref[...] = cotangent
    da_ref[...] = dot_nt(cotangent, w_ref[1, 3]).astype(BF16)


def column_main(sizes, m_ref, cot_ref, da_ref, g_ref, w_ref, turn_ref,
                dm_hbm, mid_ref, n_ref, att_ref, dqkv_ref, dm_ref, q_ref, k_ref, v_ref, p_ref, sems):
    height, cols, width, together = sizes
    middle = dot(turn_ref[2], m_ref[...])
    mid_ref[...] = middle.astype(BF16)
    centred, inverse = statistics(middle)
    normed = (centred * inverse * g_ref[1:2]).astype(BF16)
    n_ref[...] = normed
    for part, ref in enumerate((q_ref, k_ref, v_ref)):
        ref[...] = dot(normed, w_ref[1, part]).astype(BF16)
    count = together * height
    groups = cols // together
    attention_forward(q_ref, k_ref, v_ref, att_ref, p_ref, groups, count, width, height)
    attention_back(q_ref, k_ref, v_ref, p_ref, da_ref, dqkv_ref, groups, count, width)
    d_normed = input_back(dqkv_ref, w_ref.at[1])
    middle = mid_ref[...].astype(F32)
    d_middle = cot_ref[...].astype(F32) + norm_back(middle, g_ref[1:2], d_normed)
    finish(send_turned(turn_ref.at[3], d_middle.astype(BF16), dm_ref, quarters(dm_hbm), sems))


def column_last(parts, cot_ref, mid_ref, n_ref, att_ref, dqkv_ref, w_ref, turn_ref, *refs):
    out_hbms, (keep_ref, send_hbm, out_ref, send_ref, sems, out_sems) = refs[:parts], refs[parts:]
    going = weight_grads(
        n_ref[...], att_ref[...], dqkv_ref, cot_ref[...], turn_ref[6], keep_ref, send_ref, send_hbm, sems
    )
    output = (mid_ref[...].astype(F32) + dot(att_ref[...], w_ref[1, 3])).astype(BF16)
    going += send_turned(turn_ref.at[5], output, out_ref, out_hbms, out_sems)
    finish(going)


def call(kernel, ins, outs, scratch, micros):
    def spec(far):
        return pl.BlockSpec(memory_space=pltpu.HBM if far else pltpu.VMEM)

    def place(item, far):
        return pltpu.with_memory_space_constraint(item, pltpu.HBM if far else pltpu.VMEM)

    return pl.pallas_call(
        kernel,
        in_specs=[spec(far) for _, far in ins],
        out_specs=[spec(far) for _, far in outs],
        out_shape=[(pltpu.HBM if far else pltpu.VMEM)(shape, BF16) for shape, far in outs],
        scratch_shapes=scratch,
        compiler_params=pltpu.CompilerParams(vmem_limit_bytes=20 * 1024 * 1024),
        cost_estimate=pl.CostEstimate(flops=int(micros * 1.1e9), bytes_accessed=1 << 20, transcendentals=0),
    )(*[place(item, far) for item, far in ins])


def swap(item, axis, count, step):
    return lax.ppermute(item, axis, [(at, at ^ step) for at in range(count)])


def add_pair(keep, send, plane, core):
    got = swap(send, "col", plane * core, 1)
    return (keep.astype(F32) + got.astype(F32)).astype(BF16)


def plane_pieces(total, plane, core):
    return [total[0]] + [swap(total[step], "col", plane * core, step * core) for step in range(1, plane)]


def last_sums(pieces, row_parts):
    parts, size, channels = pieces[0].shape
    held = sum(piece.astype(F32) for piece in pieces).astype(BF16)
    held = held.reshape(parts, row_parts, size // row_parts, channels)
    result = held[:, 0].astype(F32)
    for step in range(1, row_parts):
        result = result + swap(held[:, step], "row", row_parts, step).astype(F32)
    return result


def body(row_parts, col_parts, field, cotangent, gains, weights):
    high, wide, channels = field.shape
    core = 2
    plane = col_parts // core
    rows = high // col_parts
    cols = wide // row_parts
    tokens = high * wide
    height = high * row_parts
    length = wide * col_parts
    width = channels // HEADS
    together = min(cols, max(1, 256 // height))
    devices = row_parts * col_parts
    my_row = lax.axis_index("row")

    flat, triple = ((tokens, channels), False), ((tokens, 3 * channels), False)
    leaving = ((tokens, channels), True)
    packed = (plane, 4, channels // col_parts, channels)
    square = pltpu.VMEM((tokens, channels), BF16)
    copies = pltpu.SemaphoreType.DMA
    assert channels == tokens
    turns = [
        ((rows, col_parts, row_parts, cols), (2, 1, 0, 3), {}, 0),
        ((row_parts, col_parts, rows, cols), (2, 1, 0, 3), {}, 0),
        ((height, cols), (1, 0), {}, 0),
        ((cols, height), (1, 0), {}, 0),
        ((row_parts, high, cols), (2, 0, 1), {0: "row"}, 0),
        ((cols, row_parts, high), (1, 2, 0), {1: "row"}, 0),
        ((row_parts, plane, core, channels // devices), (2, 1, 0, 3), {0: "row", 1: "plane", 2: "core"}, 1),
    ]

    def all_to_all(item):
        item = item.reshape(devices, rows * cols, channels)
        return lax.all_to_all(item, ("row", "col"), 0, 0, tiled=True).reshape(tokens, channels)

    x = lax.all_to_all(field.reshape(col_parts, rows, wide, channels), "col", 0, 0, tiled=True)
    cots = []
    for step in range(row_parts):
        piece = lax.dynamic_slice_in_dim(cotangent, (my_row ^ step) * cols, cols, axis=1)
        piece = piece if step == 0 else swap(piece, "row", row_parts, step)
        cots.append(piece.reshape(high * cols, channels))
    weights, turn = call(
        functools.partial(set_up, turns), [(weights, True)],
        [(weights.shape, False), ((len(turns), tokens, channels), False)], [copies], 5,
    )

    sizes = (rows, length, width)
    probs = ((rows * HEADS, length, length), False)
    mid, *saved = call(
        functools.partial(row_forward, sizes),
        [(x, False), (gains, False), (weights, False), (turn, False)],
        [leaving] + [flat] * 5 + [probs], [square, copies((4,))], 6,
    )
    cots[0], _ = lax.optimization_barrier((cots[0], mid))
    cot, d_att = call(
        functools.partial(column_first, row_parts),
        [(item, False) for item in cots] + [(weights, False), (turn, False)], [flat, flat], [], 2,
    )
    mid = all_to_all(mid)

    count = together * height
    d_mid, *kept = call(
        functools.partial(column_main, (height, cols, width, together)),
        [(item, False) for item in (mid, cot, d_att, gains, weights, turn)],
        [leaving] + [flat] * 3 + [triple],
        [square] * 4 + [pltpu.VMEM((cols // together * HEADS, count, count), BF16), copies((4,))], 14,
    )
    d_mid = all_to_all(d_mid)
    *outs, keep_b, send_b = call(
        functools.partial(column_last, row_parts),
        [(item, False) for item in (cot, *kept, weights, turn)],
        [((high * cols, channels), True)] * row_parts + [(packed, False), (packed, True)],
        [square, pltpu.VMEM(packed, BF16), copies((4,)), copies((row_parts,))], 5,
    )
    sum_b = add_pair(keep_b, send_b, plane, core)
    d_mid, sum_b, outs = lax.optimization_barrier((d_mid, sum_b, outs))
    pieces_b = plane_pieces(sum_b, plane, core)
    pieces_out = [piece if step == 0 else swap(piece, "row", row_parts, step) for step, piece in enumerate(outs)]

    d_mid, dqkv_a, keep_a, send_a = call(
        functools.partial(row_back, sizes),
        [(item, False) for item in (d_mid, weights, turn, *saved)],
        [flat, triple, (packed, False), (packed, True)],
        [square, pltpu.VMEM(packed, BF16), copies((4,))], 10,
    )
    field_grad, = call(
        functools.partial(field_back, rows),
        [(item, False) for item in (x, d_mid, dqkv_a, gains, weights)],
        [((col_parts, rows, wide, channels), True)],
        [pltpu.VMEM((col_parts, rows, wide, channels), BF16), copies], 4,
    )
    keep_a, field_grad = lax.optimization_barrier((keep_a, field_grad))
    sum_a = add_pair(keep_a, send_a, plane, core)
    sum_a, field_grad, pieces_b, pieces_out = lax.optimization_barrier((sum_a, field_grad, pieces_b, pieces_out))
    pieces_a = plane_pieces(sum_a, plane, core)
    field_grad = lax.all_to_all(field_grad, "col", 0, 0, tiled=True).reshape(high, wide, channels)
    grads_b = last_sums(pieces_b, row_parts)
    grads_a = last_sums(pieces_a, row_parts)
    output = jnp.zeros((high, wide, channels), BF16)
    for step, piece in enumerate(pieces_out):
        piece = piece.reshape(high, cols, channels)
        output = lax.dynamic_update_slice_in_dim(output, piece, (my_row ^ step) * cols, axis=1)
    return output, field_grad, jnp.concatenate([grads_a, grads_b], axis=0)


def solution(mesh):
    return jax.shard_map(
        functools.partial(body, mesh.shape["row"], mesh.shape["col"]),
        mesh=mesh,
        in_specs=(P("row", "col", None), P("row", "col", None), P(), P()),
        out_specs=(P("row", "col", None), P("row", "col", None), P(None, ("row", "col"), None)),
        check_vma=False,
    )
```

time: 162 us -> 170 us (1.049)
  local copies, waits for them, and re-layouts: 6.96 us -> 34.8 us
  Pallas kernels: 54.1 us -> 36.3 us
  other arithmetic: 10.5 us -> 4.81 us
  waiting for transfers between devices: 46.5 us -> 50.3 us
    unnamed x49 -> x63, local copies, waits for them, and re-layouts: 4.02 us -> 30.3 us
    pallas_call x6 -> x7, Pallas kernels: 54.1 us -> 36.3 us  [call(): pl.pallas_call(kernel, in_specs=[spec(far) for _, far in ins], out_specs=...]
    ppermute x20, waiting for transfers between devices: 23.7 us -> 33.8 us  [swap(): return lax.ppermute(item, axis, [(at, at ^ step) for at in range(count)])]
    all_to_all x2, waiting for transfers between devices: 20.3 us -> 12.8 us  [all_to_all(): lax.all_to_all(item, ('row', 'col'), 0, 0, tiled=True)]
    convert_element_type x7 -> x2, other arithmetic: 6.6 us -> 0.27 us  [last_sums(): held = sum((piece.astype(F32) for piece in pieces)).astype(BF16)]
    dynamic_update_slice x4, local copies, waits for them, and re-layouts: 0.06 us -> 2.78 us  [body(): lax.dynamic_update_slice_in_dim(output, piece, (my_row ^ step) * cols, ax...]
    all_to_all x2, starting transfers between devices: 7.33 us -> 9.34 us  [all_to_all(): lax.all_to_all(item, ('row', 'col'), 0, 0, tiled=True)]
    ppermute x20, starting transfers between devices: 25.8 us -> 24 us  [swap(): return lax.ppermute(item, axis, [(at, at ^ step) for at in range(count)])]
  transfers between devices with their start and end apart: 24 -> 24, of which waited for: 8 -> 9; matrix products, arithmetic and copies ran while one was open for 8% -> 5% of each run, Pallas kernels for 12% -> 3%
where the time goes in v3:
time: 170 us; the launch traced here: 169 us
  waiting for transfers between devices  50.3 us (30%)
  starting transfers between devices  42 us (25%)
  Pallas kernels  36.3 us (21%)
  local copies, waits for them, and re-layouts  34.8 us (20%)
  other arithmetic  4.81 us (3%)
    pallas_call x7, Pallas kernels, call(): pl.pallas_call(kernel, in_specs=[spec(far) for _, far in ins], out_specs=...  36.3 us
    ppermute x20, waiting for transfers between devices, swap(): return lax.ppermute(item, axis, [(at, at ^ step) for at in range(count)])  33.8 us
    unnamed x63, local copies, waits for them, and re-layouts  30.3 us
    ppermute x20, starting transfers between devices, swap(): return lax.ppermute(item, axis, [(at, at ^ step) for at in range(count)])  24 us
    all_to_all x2, waiting for transfers between devices, all_to_all(): lax.all_to_all(item, ('row', 'col'), 0, 0, tiled=True)  12.8 us
    all_to_all x2, starting transfers between devices, all_to_all(): lax.all_to_all(item, ('row', 'col'), 0, 0, tiled=True)  9.34 us
    all_to_all x1, starting transfers between devices, body(): lax.all_to_all(field.reshape(col_parts, rows, wide, channels), 'col', 0,...  5.18 us
    all_to_all x1, waiting for transfers between devices, body(): lax.all_to_all(field.reshape(col_parts, rows, wide, channels), 'col', 0,...  3.67 us
  transfers between devices with their start and end apart: 24, of which 9 were waited for; matrix products, arithmetic and copies ran while one was open for 5% of the time, Pallas kernels for 3%

profile of v3, /device:TPU:0, one launch (start us, length us, event | category | flops | bytes accessed | tf_op | source)
XLA Modules:
  0.0 169.2 jit_solution(4117726381518270789)
XLA Ops:
  0.6 5.2 %all-to-all-start = ((bf16[8,2,32,512]{3,2,1,0:T(8,128)(2,1)}), bf16[8,2,32,512]{3,2,1,0:T(8,128)(2,1)S(1)}, u32[]{:S(2)}, u32[]{:S(2)}) async-start(bf16[8,2,32,512]{3,2,1,0:T(8,128)(2,1)} %bitcast.86), calls=%async_computation | async-start | bytes 1048576 | tf_op jit(solution)/shard_map/all_to_all | solution.py:363
  5.8 2.2 %shard_map.67 = (bf16[2,4,512,512]{3,2,1,0:T(8,128)(2,1)S(1)}, bf16[7,512,512]{2,1,0:T(8,128)(2,1)S(1)}) custom-call(bf16[2,4,512,512]{3,2,1,0:T(8,128)(2,1)} %w_hbm.1), custom_call_target="tpu_custom_call" | custom-call | flops 5500000256 | bytes 1048576 | tf_op jit(solution)/shard_map/pallas_call | solution.py:295
  11.9 3.7 %all-to-all-done.x_ref = bf16[8,2,32,512]{3,2,1,0:T(8,128)(2,1)S(1)} async-done(((bf16[8,2,32,512]{3,2,1,0:T(8,128)(2,1)}), bf16[8,2,32,512]{3,2,1,0:T(8,128)(2,1)S(1)}, u32[]{:S(2)}, u32[]{:S(2)}) %all-to-all-start) | async-done | bytes 524320 | tf_op jit(solution)/shard_map/all_to_all | solution.py:363
  15.6 2.2 %copy-done.1 = bf16[2,4,512,512]{3,2,1,0:T(8,128)(2,1)S(1)} copy-done((bf16[2,4,512,512]{3,2,1,0:T(8,128)(2,1)S(1)}, bf16[2,4,512,512]{3,2,1,0:T(8,128)(2,1)}, u32[]{:S(2)}) %copy-start.1) | copy-done | bytes 4194328
  19.8 6.9 %shard_map.68 = (bf16[512,512]{1,0:T(8,128)(2,1)}, bf16[512,512]{1,0:T(8,128)(2,1)S(1)}, bf16[512,512]{1,0:T(8,128)(2,1)S(1)}, bf16[512,512]{1,0:T(8,128)(2,1)S(...) custom-call(bf16[8,2,32,512]{3,2,1,0:T(8,128)(2,1)S(1)} %all-to-all-done.x_ref, ...), custom_call_target="tpu_custom_call" | custom-call | flops 6600000000 | bytes 1048576 | tf_op jit(solution)/shard_map/pallas_call | solution.py:295
  29.7 4.0 %all-to-all-start.1 = ((bf16[32,16,512]{2,1,0:T(8,128)(2,1)}), bf16[32,16,512]{2,1,0:T(8,128)(2,1)S(1)}, u32[]{:S(2)}, u32[]{:S(2)}) async-start(bf16[32,16,512]{2,1,0:T(8,128)(2,1)} %bitcast.87), calls=%async_computation.1 | async-start | bytes 1048576 | tf_op jit(solution)/shard_map/all_to_all | solution.py:361
  35.6 2.4 %collective-permute-start.1 = (bf16[16,8,512]{2,1,0:T(8,128)(2,1)S(1)}, bf16[16,8,512]{2,1,0:T(8,128)(2,1)S(1)}, u32[]{:S(2)}, u32[]{:S(2)}) collective-permute-start(bf16[16,8,512]{2,1,0:T(8,128)(2,1)S(1)} %get-tuple-element.103), channel_id=1, source_target_pairs={{0,16},{8,24},{16,0},{24,8},{1,17},{9,25},{17,1},{25,9},{2,18},{10... | collective-permute-start | bytes 393224 | tf_op jit(solution)/shard_map/ppermute | solution.py:307
  38.2 8.4 %collective-permute-done = bf16[16,8,512]{2,1,0:T(8,128)(2,1)S(1)} collective-permute-done((bf16[16,8,512]{2,1,0:T(8,128)(2,1)S(1)}, bf16[16,8,512]{2,1,0:T(8,128)(2,1)S(1)}, u32[]{:S(2)}, u32[]{:S(2)}) %collective-permute-start) | collective-permute-done | bytes 131104 | tf_op jit(solution)/shard_map/ppermute | solution.py:307
  46.6 11.0 %collective-permute-done.1 = bf16[16,8,512]{2,1,0:T(8,128)(2,1)S(1)} collective-permute-done((bf16[16,8,512]{2,1,0:T(8,128)(2,1)S(1)}, bf16[16,8,512]{2,1,0:T(8,128)(2,1)S(1)}, u32[]{:S(2)}, u32[]{:S(2)}) %collective-permute-start.1) | collective-permute-done | bytes 131104 | tf_op jit(solution)/shard_map/ppermute | solution.py:307
  57.6 2.2 %copy-done.2 = bf16[2,4,512,512]{3,2,1,0:T(8,128)(2,1)S(1)} copy-done((bf16[2,4,512,512]{3,2,1,0:T(8,128)(2,1)S(1)}, bf16[2,4,512,512]{3,2,1,0:T(8,128)(2,1)}, u32[]{:S(2)}) %copy-start.2) | copy-done | bytes 4194328
  66.7 12.8 %shard_map.70 = (bf16[512,512]{1,0:T(8,128)(2,1)}, bf16[512,512]{1,0:T(8,128)(2,1)S(1)}, bf16[512,512]{1,0:T(8,128)(2,1)S(1)}, bf16[512,512]{1,0:T(8,128)(2,1)S(1)}, bf16[512,1536]{1,0:T(8,128)(2,1)S(1)}) custom-call(bf16[512,512]{1,0:T(8,128)(2,1)S(1)} %bitcast.76, bf16[512,512]{1,0:T(8,128)(2,1)S(1)} %get-tuple-element.52.cot_ref, ...), custom_call_target="tpu_custom_call" | custom-call | flops 15399999488 | bytes 1048576 | tf_op jit(solution)/shard_map/pallas_call | solution.py:295
  79.6 3.3 %shard_map.71 = (bf16[128,512]{1,0:T(8,128)(2,1)}, bf16[128,512]{1,0:T(8,128)(2,1)}, bf16[128,512]{1,0:T(8,128)(2,1)}, bf16[128,512]{1,0:T(8,128)(2,1)}, bf16[4,...) custom-call(bf16[512,512]{1,0:T(8,128)(2,1)S(1)} %get-tuple-element.52.cot_ref, ...), custom_call_target="tpu_custom_call" | custom-call | flops 5500000256 | bytes 1048576 | tf_op jit(solution)/shard_map/pallas_call | solution.py:295
  83.0 5.4 %all-to-all-start.2 = ((bf16[32,16,512]{2,1,0:T(8,128)(2,1)}), bf16[32,16,512]{2,1,0:T(8,128)(2,1)S(1)}, u32[]{:S(2)}, u32[]{:S(2)}) async-start(bf16[32,16,512]{2,1,0:T(8,128)(2,1)} %bitcast.88), calls=%async_computation.2 | async-start | bytes 1048576 | tf_op jit(solution)/shard_map/all_to_all | solution.py:361
  88.4 2.5 %add_convert_fusion.1 = bf16[4,4,64,512]{3,2,1,0:T(8,128)(2,1)} fusion(bf16[4,4,64,512]{3,2,1,0:T(8,128)(2,1)} %collective-permute-done.3, bf16[4,4,64,512]{3,2,1,0:T(8,128)(2,1)S(1)} %get-tuple-element.59), kind=kLoop, calls=%fused_computation.1 | loop fusion | flops 2097152 | bytes 3145728 | tf_op jit(solution)/shard_map/convert_element_type | solution.py:312
  90.9 12.8 %all-to-all-done.2 = bf16[32,16,512]{2,1,0:T(8,128)(2,1)S(1)} async-done(((bf16[32,16,512]{2,1,0:T(8,128)(2,1)}), bf16[32,16,512]{2,1,0:T(8,128)(2,1)S(1)}, u32[]{:S(2)}, u32[]{:S(2)}) %all-to-all-start.2) | async-done | bytes 524320 | tf_op jit(solution)/shard_map/all_to_all | solution.py:361
  103.8 2.2 %copy-done.4 = bf16[2,4,512,512]{3,2,1,0:T(8,128)(2,1)S(1)} copy-done((bf16[2,4,512,512]{3,2,1,0:T(8,128)(2,1)S(1)}, bf16[2,4,512,512]{3,2,1,0:T(8,128)(2,1)}, u32[]{:S(2)}) %copy-start.4) | copy-done | bytes 4194328
  113.7 8.1 %shard_map.72 = (bf16[512,512]{1,0:T(8,128)(2,1)S(1)}, bf16[512,1536]{1,0:T(8,128)(2,1)S(1)}, bf16[4,4,64,512]{3,2,1,0:T(8,128)(2,1)S(1)}, bf16[4,4,64,512]{3,2,1,0:T(8,128)(2,1)}) custom-call(bf16[512,512]{1,0:T(8,128)(2,1)S(1)} %bitcast.77, bf16[2,4,512,512]{3,2,1,0:T(8,128)(2,1)S(1)} %copy-done.4, bf16[7,512,512]{2,1,0:T(8,128)(2,1)S(1)} %copy-done.9, ...), custom_call_target="tpu_custom_call" | custom-call | flops 11000000512 | bytes 1048576 | tf_op jit(solution)/shard_map/pallas_call | solution.py:295
  129.1 2.9 %collective-permute-done.10 = bf16[128,512]{1,0:T(8,128)(2,1)S(1)} collective-permute-done((bf16[128,512]{1,0:T(8,128)(2,1)S(1)}, bf16[128,512]{1,0:T(8,128)(2,1)S(1)}, u32[]{:S(2)}, u32[]{:S(2)}) %collective-permute-start.10) | collective-permute-done | bytes 131104 | tf_op jit(solution)/shard_map/ppermute | solution.py:307
  134.6 3.6 %collective-permute-done.8 = bf16[128,512]{1,0:T(8,128)(2,1)S(1)} collective-permute-done((bf16[128,512]{1,0:T(8,128)(2,1)S(1)}, bf16[128,512]{1,0:T(8,128)(2,1)S(1)}, u32[]{:S(2)}, u32[]{:S(2)}) %collective-permute-start.8) | collective-permute-done | bytes 131104 | tf_op jit(solution)/shard_map/ppermute | solution.py:307
  138.1 4.5 %collective-permute-done.9 = bf16[128,512]{1,0:T(8,128)(2,1)S(1)} collective-permute-done((bf16[128,512]{1,0:T(8,128)(2,1)S(1)}, bf16[128,512]{1,0:T(8,128)(2,1)S(1)}, u32[]{:S(2)}, u32[]{:S(2)}) %collective-permute-start.9) | collective-permute-done | bytes 131104 | tf_op jit(solution)/shard_map/ppermute | solution.py:307
  149.8 3.5 %all-to-all-start.3 = ((bf16[8,2,32,512]{3,2,1,0:T(8,128)(2,1)}), bf16[8,2,32,512]{3,2,1,0:T(8,128)(2,1)S(1)}, u32[]{:S(2)}, u32[]{:S(2)}) async-start(bf16[8,2,32,512]{3,2,1,0:T(8,128)(2,1)} %shard_map.73), calls=%async_computation.3 | async-start | bytes 1048576 | tf_op jit(solution)/shard_map/all_to_all | solution.py:423
  156.2 2.5 %collective-permute-start.19 = (bf16[4,16,512]{2,1,0:T(8,128)(2,1)}, bf16[4,16,512]{2,1,0:T(8,128)(2,1)S(1)}, u32[]{:S(2)}, u32[]{:S(2)}) collective-permute-start(bf16[4,16,512]{2,1,0:T(8,128)(2,1)} %get-tuple-element.109), channel_id=1, source_target_pairs={{0,24},{8,16},{16,8},{24,0},{1,25},{9,17},{17,9},{25,1},{2,26},{10... | collective-permute-start | bytes 196616 | tf_op jit(solution)/shard_map/ppermute | solution.py:307
  160.9 2.4 %collective-permute-start.16 = (bf16[4,16,512]{2,1,0:T(8,128)(2,1)S(1)}, bf16[4,16,512]{2,1,0:T(8,128)(2,1)S(1)}, u32[]{:S(2)}, u32[]{:S(2)}) collective-permute-start(bf16[4,16,512]{2,1,0:T(8,128)(2,1)S(1)} %get-tuple-element.106), channel_id=1, source_target_pairs={{0,24},{8,16},{16,8},{24,0},{1,25},{9,17},{17,9},{25,1},{2,26},{10... | collective-permute-start | bytes 196616 | tf_op jit(solution)/shard_map/ppermute | solution.py:307
  165.4 2.2 %collective-permute-done.15 = bf16[4,16,512]{2,1,0:T(8,128)(2,1)S(1)} collective-permute-done((bf16[4,16,512]{2,1,0:T(8,128)(2,1)S(1)}, bf16[4,16,512]{2,1,0:T(8,128)(2,1)S(1)}, u32[]{:S(2)}, u32[]{:S(2)}) %collective-permute-start.15) | collective-permute-done | bytes 65568 | tf_op jit(solution)/shard_map/ppermute | solution.py:307
  (111 shorter events, 51.3 us)
Async XLA Ops:
  0.6 14.9 %all-to-all-start = ((bf16[8,2,32,512]{3,2,1,0:T(8,128)(2,1)}), bf16[8,2,32,512]{3,2,1,0:T(8,128)(2,1)S(1)}, u32[]{:S(2)}, u32[]{:S(2)}) async-start(bf16[8,2,32,512]{3,2,1,0:T(8,128)(2,1)} %bitcast.86), calls=%async_computation | async-start | bytes 1048576 | tf_op jit(solution)/shard_map/all_to_all | solution.py:363
  29.7 32.8 %all-to-all-start.1 = ((bf16[32,16,512]{2,1,0:T(8,128)(2,1)}), bf16[32,16,512]{2,1,0:T(8,128)(2,1)S(1)}, u32[]{:S(2)}, u32[]{:S(2)}) async-start(bf16[32,16,512]{2,1,0:T(8,128)(2,1)} %bitcast.87), calls=%async_computation.1 | async-start | bytes 1048576 | tf_op jit(solution)/shard_map/all_to_all | solution.py:361
  33.7 12.9 %collective-permute-start = (bf16[16,8,512]{2,1,0:T(8,128)(2,1)S(1)}, bf16[16,8,512]{2,1,0:T(8,128)(2,1)S(1)}, u32[]{:S(2)}, u32[]{:S(2)}) collective-permute-start(bf16[16,8,512]{2,1,0:T(8,128)(2,1)S(1)} %get-tuple-element.101), channel_id=1, source_target_pairs={{0,8},{8,0},{16,24},{24,16},{1,9},{9,1},{17,25},{25,17},{2,10},{10... | collective-permute-start | bytes 393224 | tf_op jit(solution)/shard_map/ppermute | solution.py:307
  35.6 22.0 %collective-permute-start.1 = (bf16[16,8,512]{2,1,0:T(8,128)(2,1)S(1)}, bf16[16,8,512]{2,1,0:T(8,128)(2,1)S(1)}, u32[]{:S(2)}, u32[]{:S(2)}) collective-permute-start(bf16[16,8,512]{2,1,0:T(8,128)(2,1)S(1)} %get-tuple-element.103), channel_id=1, source_target_pairs={{0,16},{8,24},{16,0},{24,8},{1,17},{9,25},{17,1},{25,9},{2,18},{10... | collective-permute-start | bytes 393224 | tf_op jit(solution)/shard_map/ppermute | solution.py:307
  38.0 19.6 %collective-permute-start.2 = (bf16[16,8,512]{2,1,0:T(8,128)(2,1)S(1)}, bf16[16,8,512]{2,1,0:T(8,128)(2,1)S(1)}, u32[]{:S(2)}, u32[]{:S(2)}) collective-permute-start(bf16[16,8,512]{2,1,0:T(8,128)(2,1)S(1)} %get-tuple-element.100), channel_id=1, source_target_pairs={{0,24},{8,16},{16,8},{24,0},{1,25},{9,17},{17,9},{25,1},{2,26},{10... | collective-permute-start | bytes 393224 | tf_op jit(solution)/shard_map/ppermute | solution.py:307
  82.9 5.5 %collective-permute-start.3 = (bf16[4,4,64,512]{3,2,1,0:T(8,128)(2,1)}, bf16[4,4,64,512]{3,2,1,0:T(8,128)(2,1)}, u32[]{:S(2)}, u32[]{:S(2)}) collective-permute-start(bf16[4,4,64,512]{3,2,1,0:T(8,128)(2,1)} %get-tuple-element.60), channel_id=1, source_target_pairs={{0,1},{1,0},{2,3},{3,2},{4,5},{5,4},{6,7},{7,6},{8,9},{9,8},{10,11... | collective-permute-start | bytes 3145736 | tf_op jit(solution)/shard_map/ppermute | solution.py:307
  83.0 20.7 %all-to-all-start.2 = ((bf16[32,16,512]{2,1,0:T(8,128)(2,1)}), bf16[32,16,512]{2,1,0:T(8,128)(2,1)S(1)}, u32[]{:S(2)}, u32[]{:S(2)}) async-start(bf16[32,16,512]{2,1,0:T(8,128)(2,1)} %bitcast.88), calls=%async_computation.2 | async-start | bytes 1048576 | tf_op jit(solution)/shard_map/all_to_all | solution.py:361
  121.9 12.3 %collective-permute-start.4 = (bf16[4,4,64,512]{3,2,1,0:T(8,128)(2,1)}, bf16[4,4,64,512]{3,2,1,0:T(8,128)(2,1)S(1)}, u32[]{:S(2)}, u32[]{:S(2)}) collective-permute-start(bf16[4,4,64,512]{3,2,1,0:T(8,128)(2,1)} %get-tuple-element.76), channel_id=1, source_target_pairs={{0,1},{1,0},{2,3},{3,2},{4,5},{5,4},{6,7},{7,6},{8,9},{9,8},{10,11... | collective-permute-start | bytes 3145736 | tf_op jit(solution)/shard_map/ppermute | solution.py:307
  124.2 7.8 %collective-permute-start.10 = (bf16[128,512]{1,0:T(8,128)(2,1)S(1)}, bf16[128,512]{1,0:T(8,128)(2,1)S(1)}, u32[]{:S(2)}, u32[]{:S(2)}) collective-permute-start(bf16[128,512]{1,0:T(8,128)(2,1)S(1)} %copy-done.30), channel_id=1, source_target_pairs={{0,24},{8,16},{16,8},{24,0},{1,25},{9,17},{17,9},{25,1},{2,26},{10... | collective-permute-start | bytes 393224 | tf_op jit(solution)/shard_map/ppermute | solution.py:307
  125.5 17.1 %collective-permute-start.5 = (bf16[4,64,512]{2,1,0:T(8,128)(2,1)S(1)}, bf16[4,64,512]{2,1,0:T(8,128)(2,1)S(1)}, u32[]{:S(2)}, u32[]{:S(2)}) collective-permute-start(bf16[4,64,512]{2,1,0:T(8,128)(2,1)S(1)} %get-tuple-element.98), channel_id=1, source_target_pairs={{0,2},{1,3},{2,0},{3,1},{4,6},{5,7},{6,4},{7,5},{8,10},{9,11},{10,... | collective-permute-start | bytes 786440 | tf_op jit(solution)/shard_map/ppermute | solution.py:307
  126.8 15.8 %collective-permute-start.6 = (bf16[4,64,512]{2,1,0:T(8,128)(2,1)S(1)}, bf16[4,64,512]{2,1,0:T(8,128)(2,1)S(1)}, u32[]{:S(2)}, u32[]{:S(2)}) collective-permute-start(bf16[4,64,512]{2,1,0:T(8,128)(2,1)S(1)} %get-tuple-element.97), channel_id=1, source_target_pairs={{0,4},{1,5},{2,6},{3,7},{4,0},{5,1},{6,2},{7,3},{8,12},{9,13},{10,... | collective-permute-start | bytes 786440 | tf_op jit(solution)/shard_map/ppermute | solution.py:307
  128.2 14.4 %collective-permute-start.7 = (bf16[4,64,512]{2,1,0:T(8,128)(2,1)S(1)}, bf16[4,64,512]{2,1,0:T(8,128)(2,1)S(1)}, u32[]{:S(2)}, u32[]{:S(2)}) collective-permute-start(bf16[4,64,512]{2,1,0:T(8,128)(2,1)S(1)} %get-tuple-element.96), channel_id=1, source_target_pairs={{0,6},{1,7},{2,4},{3,5},{4,2},{5,3},{6,0},{7,1},{8,14},{9,15},{10,... | collective-permute-start | bytes 786440 | tf_op jit(solution)/shard_map/ppermute | solution.py:307
  132.0 6.1 %collective-permute-start.8 = (bf16[128,512]{1,0:T(8,128)(2,1)S(1)}, bf16[128,512]{1,0:T(8,128)(2,1)S(1)}, u32[]{:S(2)}, u32[]{:S(2)}) collective-permute-start(bf16[128,512]{1,0:T(8,128)(2,1)S(1)} %copy-done.29), channel_id=1, source_target_pairs={{0,8},{8,0},{16,24},{24,16},{1,9},{9,1},{17,25},{25,17},{2,10},{10... | collective-permute-start | bytes 393224 | tf_op jit(solution)/shard_map/ppermute | solution.py:307
  134.2 8.4 %collective-permute-start.9 = (bf16[128,512]{1,0:T(8,128)(2,1)S(1)}, bf16[128,512]{1,0:T(8,128)(2,1)S(1)}, u32[]{:S(2)}, u32[]{:S(2)}) collective-permute-start(bf16[128,512]{1,0:T(8,128)(2,1)S(1)} %copy-done.28), channel_id=1, source_target_pairs={{0,16},{8,24},{16,0},{24,8},{1,17},{9,25},{17,1},{25,9},{2,18},{10... | collective-permute-start | bytes 393224 | tf_op jit(solution)/shard_map/ppermute | solution.py:307
  143.5 12.7 %collective-permute-start.11 = (bf16[4,64,512]{2,1,0:T(8,128)(2,1)}, bf16[4,64,512]{2,1,0:T(8,128)(2,1)S(1)}, u32[]{:S(2)}, u32[]{:S(2)}) collective-permute-start(bf16[4,64,512]{2,1,0:T(8,128)(2,1)} %get-tuple-element.93), channel_id=1, source_target_pairs={{0,2},{1,3},{2,0},{3,1},{4,6},{5,7},{6,4},{7,5},{8,10},{9,11},{10,... | collective-permute-start | bytes 786440 | tf_op jit(solution)/shard_map/ppermute | solution.py:307
  143.6 15.1 %collective-permute-start.12 = (bf16[4,64,512]{2,1,0:T(8,128)(2,1)}, bf16[4,64,512]{2,1,0:T(8,128)(2,1)S(1)}, u32[]{:S(2)}, u32[]{:S(2)}) collective-permute-start(bf16[4,64,512]{2,1,0:T(8,128)(2,1)} %get-tuple-element.95), channel_id=1, source_target_pairs={{0,4},{1,5},{2,6},{3,7},{4,0},{5,1},{6,2},{7,3},{8,12},{9,13},{10,... | collective-permute-start | bytes 786440 | tf_op jit(solution)/shard_map/ppermute | solution.py:307
  145.0 13.7 %collective-permute-start.13 = (bf16[4,64,512]{2,1,0:T(8,128)(2,1)S(1)}, bf16[4,64,512]{2,1,0:T(8,128)(2,1)S(1)}, u32[]{:S(2)}, u32[]{:S(2)}) collective-permute-start(bf16[4,64,512]{2,1,0:T(8,128)(2,1)S(1)} %get-tuple-element.94), channel_id=1, source_target_pairs={{0,6},{1,7},{2,4},{3,5},{4,2},{5,3},{6,0},{7,1},{8,14},{9,15},{10,... | collective-permute-start | bytes 786440 | tf_op jit(solution)/shard_map/ppermute | solution.py:307
  147.8 13.1 %collective-permute-start.17 = (bf16[4,16,512]{2,1,0:T(8,128)(2,1)}, bf16[4,16,512]{2,1,0:T(8,128)(2,1)}, u32[]{:S(2)}, u32[]{:S(2)}) collective-permute-start(bf16[4,16,512]{2,1,0:T(8,128)(2,1)} %get-tuple-element.107), channel_id=1, source_target_pairs={{0,8},{8,0},{16,24},{24,16},{1,9},{9,1},{17,25},{25,17},{2,10},{10... | collective-permute-start | bytes 196616 | tf_op jit(solution)/shard_map/ppermute | solution.py:307
  147.8 15.5 %collective-permute-start.18 = (bf16[4,16,512]{2,1,0:T(8,128)(2,1)}, bf16[4,16,512]{2,1,0:T(8,128)(2,1)}, u32[]{:S(2)}, u32[]{:S(2)}) collective-permute-start(bf16[4,16,512]{2,1,0:T(8,128)(2,1)} %get-tuple-element.108), channel_id=1, source_target_pairs={{0,16},{8,24},{16,0},{24,8},{1,17},{9,25},{17,1},{25,9},{2,18},{10... | collective-permute-start | bytes 196616 | tf_op jit(solution)/shard_map/ppermute | solution.py:307
  149.8 18.6 %all-to-all-start.3 = ((bf16[8,2,32,512]{3,2,1,0:T(8,128)(2,1)}), bf16[8,2,32,512]{3,2,1,0:T(8,128)(2,1)S(1)}, u32[]{:S(2)}, u32[]{:S(2)}) async-start(bf16[8,2,32,512]{3,2,1,0:T(8,128)(2,1)} %shard_map.73), calls=%async_computation.3 | async-start | bytes 1048576 | tf_op jit(solution)/shard_map/all_to_all | solution.py:423
  156.2 7.1 %collective-permute-start.19 = (bf16[4,16,512]{2,1,0:T(8,128)(2,1)}, bf16[4,16,512]{2,1,0:T(8,128)(2,1)S(1)}, u32[]{:S(2)}, u32[]{:S(2)}) collective-permute-start(bf16[4,16,512]{2,1,0:T(8,128)(2,1)} %get-tuple-element.109), channel_id=1, source_target_pairs={{0,24},{8,16},{16,8},{24,0},{1,25},{9,17},{17,9},{25,1},{2,26},{10... | collective-permute-start | bytes 196616 | tf_op jit(solution)/shard_map/ppermute | solution.py:307
  158.8 6.6 %collective-permute-start.14 = (bf16[4,16,512]{2,1,0:T(8,128)(2,1)S(1)}, bf16[4,16,512]{2,1,0:T(8,128)(2,1)S(1)}, u32[]{:S(2)}, u32[]{:S(2)}) collective-permute-start(bf16[4,16,512]{2,1,0:T(8,128)(2,1)S(1)} %get-tuple-element.104), channel_id=1, source_target_pairs={{0,8},{8,0},{16,24},{24,16},{1,9},{9,1},{17,25},{25,17},{2,10},{10... | collective-permute-start | bytes 196616 | tf_op jit(solution)/shard_map/ppermute | solution.py:307
  158.9 8.7 %collective-permute-start.15 = (bf16[4,16,512]{2,1,0:T(8,128)(2,1)S(1)}, bf16[4,16,512]{2,1,0:T(8,128)(2,1)S(1)}, u32[]{:S(2)}, u32[]{:S(2)}) collective-permute-start(bf16[4,16,512]{2,1,0:T(8,128)(2,1)S(1)} %get-tuple-element.105), channel_id=1, source_target_pairs={{0,16},{8,24},{16,0},{24,8},{1,17},{9,25},{17,1},{25,9},{2,18},{10... | collective-permute-start | bytes 196616 | tf_op jit(solution)/shard_map/ppermute | solution.py:307
  160.9 6.7 %collective-permute-start.16 = (bf16[4,16,512]{2,1,0:T(8,128)(2,1)S(1)}, bf16[4,16,512]{2,1,0:T(8,128)(2,1)S(1)}, u32[]{:S(2)}, u32[]{:S(2)}) collective-permute-start(bf16[4,16,512]{2,1,0:T(8,128)(2,1)S(1)} %get-tuple-element.106), channel_id=1, source_target_pairs={{0,24},{8,16},{16,8},{24,0},{1,25},{9,17},{17,9},{25,1},{2,26},{10... | collective-permute-start | bytes 196616 | tf_op jit(solution)/shard_map/ppermute | solution.py:307
  (31 other events, 181.3 us)

commit v4 on v3

--- a/solution.py
+++ b/solution.py
@@ -153,33 +153,31 @@
         copy.wait()
 
 
-def set_up(turns, w_hbm, w_ref, turn_ref, sem):
-    copy = start(w_hbm, w_ref, sem)
+def set_up(turns, turn_hbm, turn_ref, sems):
     my_row, my_col = lax.axis_index("row"), lax.axis_index("col")
+    places = {"row": my_row, "plane": my_col >> 1, "core": my_col & 1}
+    going = []
     for at, (sizes, order, me, lead) in enumerate(turns):
-        places = {"row": my_row, "plane": my_col >> 1, "core": my_col & 1}
         turn_ref[at] = one_hot(sizes, order, {axis: places[name] for axis, name in me.items()}, lead)
-    copy.wait()
-
-
-def weight_grads(normed, attended, dqkv_ref, d_top, turn, keep_ref, send_ref, send_hbm, sems):
-    channels = normed.shape[-1]
+        going.append(start(turn_ref.at[at], turn_hbm.at[at], sems.at[at]))
+    finish(going)
+
+
+def weight_grad(at, left, right, keep_ref, send_ref, keep_hbm, send_hbm, keep_sem, send_sem):
     plane, _, size, _ = keep_ref.shape
-    normed = dot(normed, turn).astype(BF16)
-    attended = dot(attended, turn).astype(BF16)
-    going = []
-    for part in (3, 0, 1, 2):
-        if part < 3:
-            whole = dot_tn(normed, dqkv_ref[:, part * channels : (part + 1) * channels])
-        else:
-            whole = dot_tn(attended, d_top)
-        whole = whole.astype(BF16)
-        for group in range(plane):
-            at = plane + group
-            send_ref[group, part] = whole[at * size : (at + 1) * size]
-            keep_ref[group, part] = whole[group * size : (group + 1) * size]
-        going.append(start(send_ref.at[:, part], send_hbm.at[:, part], sems.at[part]))
-    return going
+    whole = dot_tn(left, right).astype(BF16)
+    for group in range(plane):
+        send_ref[group, at] = whole[(plane + group) * size : (plane + group + 1) * size]
+        keep_ref[group, at] = whole[group * size : (group + 1) * size]
+    return [
+        start(send_ref.at[:, at], send_hbm.at[:, at], send_sem),
+        start(keep_ref.at[:, at], keep_hbm.at[:, at], keep_sem),
+    ]
+
+
+def third(ref, part):
+    channels = ref.shape[-1] // 3
+    return ref[:, part * channels : (part + 1) * channels]
 
 
 def send_turned(turn_ref, values, stage_ref, targets, sems):
@@ -197,110 +195,193 @@
     return [ref.at[pl.ds(at * size, size)] for at in range(4)]
 
 
-def input_back(dqkv_ref, w_ref):
-    channels = w_ref.shape[-1]
-    total = dot_nt(dqkv_ref[:, :channels], w_ref[0])
-    total += dot_nt(dqkv_ref[:, channels : 2 * channels], w_ref[1])
-    total += dot_nt(dqkv_ref[:, 2 * channels :], w_ref[2])
+def input_back(dqkv_ref, w_refs):
+    total = dot_nt(third(dqkv_ref, 0), w_refs[0][...])
+    total += dot_nt(third(dqkv_ref, 1), w_refs[1][...])
+    total += dot_nt(third(dqkv_ref, 2), w_refs[2][...])
     return total.astype(BF16).astype(F32)
 
 
-def row_forward(sizes, x_ref, g_ref, w_ref, turn_ref, mid_hbm, n_ref, q_ref, k_ref, v_ref, att_ref, p_ref,
-                mid_ref, sems):
+def rows_of(x_ref):
+    _, rows, _, channels = x_ref.shape
+    length = x_ref.shape[0] * x_ref.shape[2]
+    pieces = [x_ref[:, i].reshape(length, channels) for i in range(rows)]
+    return jnp.concatenate(pieces, axis=0).astype(F32)
+
+
+def row_forward(sizes, x_ref, g_ref, w_hbm, turn_hbm, mid_hbm, n_hbm, q_hbm, k_hbm, v_hbm, att_hbm, p_hbm,
+                w_ref, turn_ref, mid_ref, n_ref, q_ref, k_ref, v_ref, att_ref, p_ref, in_sems, out_sems, sems):
     rows, length, width = sizes
-    channels = x_ref.shape[-1]
-    field = jnp.concatenate([x_ref[:, i].reshape(length, channels) for i in range(rows)], axis=0)
-    field = field.astype(F32)
-    centred, inverse = statistics(field)
+    coming = [start(w_hbm.at[0, part], w_ref.at[part], in_sems.at[part]) for part in range(4)]
+    coming.append(start(turn_hbm.at[0], turn_ref, in_sems.at[4]))
+    centred, inverse = statistics(rows_of(x_ref))
     normed = (centred * inverse * g_ref[0:1]).astype(BF16)
     n_ref[...] = normed
-    for part, ref in enumerate((q_ref, k_ref, v_ref)):
-        ref[...] = dot(normed, w_ref[0, part]).astype(BF16)
+    going = [start(n_ref, n_hbm, out_sems.at[0])]
+    for part, (ref, hbm) in enumerate(((q_ref, q_hbm), (k_ref, k_hbm), (v_ref, v_hbm))):
+        coming[part].wait()
+        ref[...] = dot(normed, w_ref[part]).astype(BF16)
+        going.append(start(ref, hbm, out_sems.at[1 + part]))
     attention_forward(q_ref, k_ref, v_ref, att_ref, p_ref, rows, length, width, length)
-    field = jnp.concatenate([x_ref[:, i].reshape(length, channels) for i in range(rows)], axis=0)
-    middle = (field.astype(F32) + dot(att_ref[...], w_ref[0, 3])).astype(BF16)
-    finish(send_turned(turn_ref.at[0], middle, mid_ref, quarters(mid_hbm), sems))
-
-
-def row_back(sizes, d_ref, w_ref, turn_ref, n_ref, q_ref, k_ref, v_ref, att_ref, p_ref,
-             dm_ref, dqkv_ref, keep_ref, send_hbm, da_ref, send_ref, sems):
+    going.append(start(p_ref, p_hbm, out_sems.at[5]))
+    going.append(start(att_ref, att_hbm, out_sems.at[4]))
+    coming[3].wait()
+    middle = (rows_of(x_ref) + dot(att_ref[...], w_ref[3])).astype(BF16)
+    coming[4].wait()
+    finish(going + send_turned(turn_ref, middle, mid_ref, quarters(mid_hbm), sems))
+
+
+def row_back_first(d_ref, w_hbm, turn_hbm, att_hbm, dm_ref, da_ref, keep_hbm, send_hbm,
+                   w_ref, turn_ref, att_ref, keep_ref, send_ref, sems):
+    coming = [
+        start(turn_hbm.at[1], turn_ref.at[0], sems.at[0]),
+        start(att_hbm, att_ref, sems.at[1]),
+        start(turn_hbm.at[6], turn_ref.at[1], sems.at[2]),
+        start(w_hbm.at[0, 3], w_ref, sems.at[3]),
+    ]
+    coming[0].wait()
+    d_middle = dot(turn_ref[0], d_ref[...]).astype(BF16)
+    dm_ref[...] = d_middle
+    finish(coming[1:3])
+    attended = dot(att_ref[...], turn_ref[1]).astype(BF16)
+    going = weight_grad(
+        0, attended, d_middle, keep_ref, send_ref, keep_hbm, send_hbm, sems.at[4], sems.at[5]
+    )
+    coming[3].wait()
+    da_ref[...] = dot_nt(d_middle, w_ref[...]).astype(BF16)
+    finish(going)
+
+
+def row_back(sizes, da_ref, turn_hbm, n_hbm, q_hbm, k_hbm, v_hbm, p_hbm, dqkv_hbm, keep_hbm, send_hbm,
+             turn_ref, n_ref, q_ref, k_ref, v_ref, p_ref, dqkv_ref, keep_ref, send_ref, sems):
     rows, length, width = sizes
-    d_middle = dot(turn_ref[1], d_ref[...]).astype(BF16)
-    dm_ref[...] = d_middle
-    da_ref[...] = dot_nt(d_middle, w_ref[0, 3]).astype(BF16)
+    half = p_ref.shape[0] // 2
+    coming = [
+        start(v_hbm, v_ref, sems.at[0]), start(k_hbm, k_ref, sems.at[1]), start(q_hbm, q_ref, sems.at[2]),
+        start(p_hbm.at[pl.ds(0, half)], p_ref.at[pl.ds(0, half)], sems.at[3]),
+        start(p_hbm.at[pl.ds(half, half)], p_ref.at[pl.ds(half, half)], sems.at[4]),
+        start(turn_hbm.at[6], turn_ref, sems.at[5]), start(n_hbm, n_ref, sems.at[6]),
+    ]
+    finish(coming[:5])
     attention_back(q_ref, k_ref, v_ref, p_ref, da_ref, dqkv_ref, rows, length, width)
-    finish(weight_grads(
-        n_ref[...], att_ref[...], dqkv_ref, d_middle, turn_ref[6], keep_ref, send_ref, send_hbm, sems
-    ))
-
-
-def field_back(rows, x_ref, dm_ref, dqkv_ref, g_ref, w_ref, fg_hbm, fg_ref, sem):
-    channels = x_ref.shape[-1]
-    length = dm_ref.shape[0] // rows
-    field = jnp.concatenate([x_ref[:, i].reshape(length, channels) for i in range(rows)], axis=0)
-    d_normed = input_back(dqkv_ref, w_ref.at[0])
-    result = dm_ref[...].astype(F32) + norm_back(field.astype(F32), g_ref[0:1], d_normed)
+    going = [start(dqkv_ref, dqkv_hbm, sems.at[7])]
+    finish(coming[5:])
+    normed = dot(n_ref[...], turn_ref[...]).astype(BF16)
+    for part in range(3):
+        going += weight_grad(
+            part, normed, third(dqkv_ref, part), keep_ref, send_ref, keep_hbm, send_hbm,
+            sems.at[8 + part], sems.at[11 + part],
+        )
+    finish(going)
+
+
+def field_back(x_ref, dm_ref, g_ref, dqkv_hbm, w_hbm, fg_hbm, dqkv_ref, w_ref, fg_ref, sems):
+    coming = [start(dqkv_hbm, dqkv_ref, sems.at[0]), start(w_hbm.at[0, 0:3], w_ref, sems.at[1])]
+    _, rows, _, channels = x_ref.shape
+    length = x_ref.shape[0] * x_ref.shape[2]
+    finish(coming)
+    d_normed = input_back(dqkv_ref, [w_ref.at[part] for part in range(3)])
+    result = dm_ref[...].astype(F32) + norm_back(rows_of(x_ref), g_ref[0:1], d_normed)
     result = result.astype(BF16)
     for i in range(rows):
         piece = result[i * length : (i + 1) * length]
         fg_ref[:, i] = piece.reshape(fg_ref.shape[0], fg_ref.shape[2], channels)
-    start(fg_ref, fg_hbm, sem).wait()
+    start(fg_ref, fg_hbm, sems.at[2]).wait()
 
 
 def column_first(parts, *refs):
-    c_refs, (w_ref, turn_ref, cot_ref, da_ref) = refs[:parts], refs[parts:]
+    c_refs, (w_hbm, turn_hbm, cot_ref, da_ref, early_ref, w_ref, turn_ref, sems) = refs[:parts], refs[parts:]
+    coming = [
+        start(turn_hbm.at[4], turn_ref, sems.at[0]), start(w_hbm.at[1, 3], w_ref, sems.at[1]),
+        start(turn_hbm.at[2], early_ref.at[0], sems.at[2]), start(w_hbm.at[1, 0], early_ref.at[1], sems.at[3]),
+    ]
     cotangent = jnp.concatenate([ref[...] for ref in c_refs], axis=0)
-    cotangent = dot(turn_ref[4], cotangent).astype(BF16)
+    coming[0].wait()
+    cotangent = dot(turn_ref[...], cotangent).astype(BF16)
     cot_ref[...] = cotangent
-    da_ref[...] = dot_nt(cotangent, w_ref[1, 3]).astype(BF16)
-
-
-def column_main(sizes, m_ref, cot_ref, da_ref, g_ref, w_ref, turn_ref,
-                dm_hbm, mid_ref, n_ref, att_ref, dqkv_ref, dm_ref, q_ref, k_ref, v_ref, p_ref, sems):
+    coming[1].wait()
+    da_ref[...] = dot_nt(cotangent, w_ref[...]).astype(BF16)
+    finish(coming[2:])
+
+
+def column_main(sizes, m_ref, cot_ref, da_ref, early_ref, g_ref, w_hbm, turn_hbm,
+                dm_hbm, mid_hbm, n_hbm, att_hbm, dqkv_hbm,
+                w_ref, turn_ref, dm_ref, mid_ref, n_ref, att_ref, dqkv_ref, q_ref, k_ref, v_ref, p_ref, sems):
     height, cols, width, together = sizes
-    middle = dot(turn_ref[2], m_ref[...])
+    coming = [
+        start(w_hbm.at[1, 1], w_ref.at[0], sems.at[0]), start(w_hbm.at[1, 2], w_ref.at[1], sems.at[1]),
+        start(turn_hbm.at[3], turn_ref, sems.at[2]),
+    ]
+    middle = dot(early_ref[0], m_ref[...])
     mid_ref[...] = middle.astype(BF16)
+    going = [start(mid_ref, mid_hbm, sems.at[3])]
     centred, inverse = statistics(middle)
     normed = (centred * inverse * g_ref[1:2]).astype(BF16)
     n_ref[...] = normed
-    for part, ref in enumerate((q_ref, k_ref, v_ref)):
-        ref[...] = dot(normed, w_ref[1, part]).astype(BF16)
+    going.append(start(n_ref, n_hbm, sems.at[4]))
+    q_ref[...] = dot(normed, early_ref[1]).astype(BF16)
+    coming[0].wait()
+    k_ref[...] = dot(normed, w_ref[0]).astype(BF16)
+    coming[1].wait()
+    v_ref[...] = dot(normed, w_ref[1]).astype(BF16)
     count = together * height
     groups = cols // together
     attention_forward(q_ref, k_ref, v_ref, att_ref, p_ref, groups, count, width, height)
+    going.append(start(att_ref, att_hbm, sems.at[5]))
     attention_back(q_ref, k_ref, v_ref, p_ref, da_ref, dqkv_ref, groups, count, width)
-    d_normed = input_back(dqkv_ref, w_ref.at[1])
+    going.append(start(dqkv_ref, dqkv_hbm, sems.at[6]))
+    d_normed = input_back(dqkv_ref, [early_ref.at[1], w_ref.at[0], w_ref.at[1]])
     middle = mid_ref[...].astype(F32)
     d_middle = cot_ref[...].astype(F32) + norm_back(middle, g_ref[1:2], d_normed)
-    finish(send_turned(turn_ref.at[3], d_middle.astype(BF16), dm_ref, quarters(dm_hbm), sems))
-
-
-def column_last(parts, cot_ref, mid_ref, n_ref, att_ref, dqkv_ref, w_ref, turn_ref, *refs):
-    out_hbms, (keep_ref, send_hbm, out_ref, send_ref, sems, out_sems) = refs[:parts], refs[parts:]
-    going = weight_grads(
-        n_ref[...], att_ref[...], dqkv_ref, cot_ref[...], turn_ref[6], keep_ref, send_ref, send_hbm, sems
-    )
-    output = (mid_ref[...].astype(F32) + dot(att_ref[...], w_ref[1, 3])).astype(BF16)
-    going += send_turned(turn_ref.at[5], output, out_ref, out_hbms, out_sems)
-    finish(going)
-
-
-def call(kernel, ins, outs, scratch, micros):
-    def spec(far):
-        return pl.BlockSpec(memory_space=pltpu.HBM if far else pltpu.VMEM)
-
-    def place(item, far):
-        return pltpu.with_memory_space_constraint(item, pltpu.HBM if far else pltpu.VMEM)
+    coming[2].wait()
+    finish(going + send_turned(turn_ref, d_middle.astype(BF16), dm_ref, quarters(dm_hbm), sems.at[pl.ds(7, 4)]))
+
+
+def column_last(parts, cot_hbm, mid_hbm, n_hbm, att_hbm, dqkv_hbm, w_hbm, turn_hbm, *refs):
+    out_hbms, refs = refs[:parts], refs[parts:]
+    keep_hbm, send_hbm, out_ref, keep_ref, send_ref, w_ref, turn_ref, flat_ref, dqkv_ref, sems = refs
+    coming = [
+        start(turn_hbm.at[6], turn_ref.at[0], sems.at[0]), start(n_hbm, flat_ref.at[0], sems.at[1]),
+        start(dqkv_hbm, dqkv_ref, sems.at[2]), start(att_hbm, flat_ref.at[1], sems.at[3]),
+        start(cot_hbm, flat_ref.at[2], sems.at[4]), start(mid_hbm, flat_ref.at[3], sems.at[5]),
+        start(w_hbm.at[1, 3], w_ref, sems.at[6]), start(turn_hbm.at[5], turn_ref.at[1], sems.at[7]),
+    ]
+    finish(coming[:3])
+    going = []
+    normed = dot(flat_ref[0], turn_ref[0]).astype(BF16)
+    for part in range(3):
+        going += weight_grad(
+            part, normed, third(dqkv_ref, part), keep_ref, send_ref, keep_hbm, send_hbm,
+            sems.at[8 + part], sems.at[12 + part],
+        )
+    finish(coming[3:])
+    attended = dot(flat_ref[1], turn_ref[0]).astype(BF16)
+    going += weight_grad(
+        3, attended, flat_ref[2], keep_ref, send_ref, keep_hbm, send_hbm, sems.at[11], sems.at[15]
+    )
+    output = (flat_ref[3].astype(F32) + dot(flat_ref[1], w_ref[...])).astype(BF16)
+    finish(going + send_turned(turn_ref.at[1], output, out_ref, out_hbms, sems.at[pl.ds(16, parts)]))
+
+
+NEAR, FAR, ANY = pltpu.VMEM, pltpu.HBM, None
+
+
+def call(kernel, ins, outs, scratch):
+    def spec(where):
+        return pl.BlockSpec(memory_space=pltpu.HBM if where is FAR else pltpu.VMEM)
+
+    def place(item, where):
+        return item if where is ANY else pltpu.with_memory_space_constraint(item, where)
 
     return pl.pallas_call(
         kernel,
-        in_specs=[spec(far) for _, far in ins],
-        out_specs=[spec(far) for _, far in outs],
-        out_shape=[(pltpu.HBM if far else pltpu.VMEM)(shape, BF16) for shape, far in outs],
+        in_specs=[spec(where) for _, where in ins],
+        out_specs=[spec(where) for _, where in outs],
+        out_shape=[jax.ShapeDtypeStruct(shape, BF16) if where is ANY else where(shape, BF16) for shape, where in outs],
         scratch_shapes=scratch,
-        compiler_params=pltpu.CompilerParams(vmem_limit_bytes=20 * 1024 * 1024),
-        cost_estimate=pl.CostEstimate(flops=int(micros * 1.1e9), bytes_accessed=1 << 20, transcendentals=0),
-    )(*[place(item, far) for item, far in ins])
+        compiler_params=pltpu.CompilerParams(vmem_limit_bytes=48 * 1024 * 1024),
+        cost_estimate=pl.CostEstimate(flops=1 << 20, bytes_accessed=1 << 10, transcendentals=0),
+    )(*[place(item, where) for item, where in ins])
 
 
 def swap(item, axis, count, step):
@@ -340,10 +421,20 @@
     devices = row_parts * col_parts
     my_row = lax.axis_index("row")
 
-    flat, triple = ((tokens, channels), False), ((tokens, 3 * channels), False)
-    leaving = ((tokens, channels), True)
-    packed = (plane, 4, channels // col_parts, channels)
-    square = pltpu.VMEM((tokens, channels), BF16)
+    flat, triple = (tokens, channels), (tokens, 3 * channels)
+    probs = (rows * HEADS, length, length)
+    size = channels // col_parts
+
+    def packed(parts):
+        return (plane, parts, size, channels)
+
+    def scratch(*shape):
+        return pltpu.VMEM(shape, BF16)
+
+    def at(where, *items):
+        return [(item, where) for item in items]
+
+    square = scratch(*flat)
     copies = pltpu.SemaphoreType.DMA
     assert channels == tokens
     turns = [
@@ -366,59 +457,62 @@
         piece = lax.dynamic_slice_in_dim(cotangent, (my_row ^ step) * cols, cols, axis=1)
         piece = piece if step == 0 else swap(piece, "row", row_parts, step)
         cots.append(piece.reshape(high * cols, channels))
-    weights, turn = call(
-        functools.partial(set_up, turns), [(weights, True)],
-        [(weights.shape, False), ((len(turns), tokens, channels), False)], [copies], 5,
+    turn, = call(
+        functools.partial(set_up, turns), [], at(FAR, (len(turns), *flat)),
+        [scratch(len(turns), *flat), copies((len(turns),))],
     )
 
     sizes = (rows, length, width)
-    probs = ((rows * HEADS, length, length), False)
-    mid, *saved = call(
+    mid, normed, query, key, value, attended, prob = call(
         functools.partial(row_forward, sizes),
-        [(x, False), (gains, False), (weights, False), (turn, False)],
-        [leaving] + [flat] * 5 + [probs], [square, copies((4,))], 6,
+        at(ANY, x, gains) + at(FAR, weights, turn), at(FAR, *[flat] * 6, probs),
+        [scratch(4, *flat)] + [square] * 7 + [scratch(*probs), copies((5,)), copies((6,)), copies((4,))],
     )
     cots[0], _ = lax.optimization_barrier((cots[0], mid))
-    cot, d_att = call(
+    cot, d_att, early = call(
         functools.partial(column_first, row_parts),
-        [(item, False) for item in cots] + [(weights, False), (turn, False)], [flat, flat], [], 2,
+        at(ANY, *cots) + at(FAR, weights, turn), at(NEAR, flat, flat, (2, *flat)), [square, square, copies((4,))],
     )
     mid = all_to_all(mid)
 
     count = together * height
     d_mid, *kept = call(
         functools.partial(column_main, (height, cols, width, together)),
-        [(item, False) for item in (mid, cot, d_att, gains, weights, turn)],
-        [leaving] + [flat] * 3 + [triple],
-        [square] * 4 + [pltpu.VMEM((cols // together * HEADS, count, count), BF16), copies((4,))], 14,
+        at(ANY, mid) + at(NEAR, cot, d_att, early) + at(ANY, gains) + at(FAR, weights, turn),
+        at(FAR, flat, flat, flat, flat, triple),
+        [scratch(2, *flat)] + [square] * 5 + [scratch(*triple)] + [square] * 3
+        + [scratch(cols // together * HEADS, count, count), copies((11,))],
     )
     d_mid = all_to_all(d_mid)
     *outs, keep_b, send_b = call(
         functools.partial(column_last, row_parts),
-        [(item, False) for item in (cot, *kept, weights, turn)],
-        [((high * cols, channels), True)] * row_parts + [(packed, False), (packed, True)],
-        [square, pltpu.VMEM(packed, BF16), copies((4,)), copies((row_parts,))], 5,
-    )
+        at(FAR, cot, *kept, weights, turn), at(FAR, *[(high * cols, channels)] * row_parts, packed(4), packed(4)),
+        [square, scratch(*packed(4)), scratch(*packed(4)), square, scratch(2, *flat), scratch(4, *flat),
+         scratch(*triple), copies((16 + row_parts,))],
+    )
+    d_mid, outs, keep_b, send_b = lax.optimization_barrier((d_mid, outs, keep_b, send_b))
     sum_b = add_pair(keep_b, send_b, plane, core)
-    d_mid, sum_b, outs = lax.optimization_barrier((d_mid, sum_b, outs))
-    pieces_b = plane_pieces(sum_b, plane, core)
+    d_mid, d_att, keep_o, send_o = call(
+        row_back_first,
+        at(ANY, d_mid) + at(FAR, weights, turn, attended), at(ANY, flat, flat) + at(FAR, packed(1), packed(1)),
+        [square, scratch(2, *flat), square, scratch(*packed(1)), scratch(*packed(1)), copies((6,))],
+    )
+    sum_o = add_pair(keep_o, send_o, plane, core)
+    d_att, sum_b, sum_o, outs = lax.optimization_barrier((d_att, sum_b, sum_o, outs))
+    pieces_b = plane_pieces(jnp.concatenate([sum_o, sum_b], axis=1), plane, core)
     pieces_out = [piece if step == 0 else swap(piece, "row", row_parts, step) for step, piece in enumerate(outs)]
 
-    d_mid, dqkv_a, keep_a, send_a = call(
+    dqkv, keep_a, send_a = call(
         functools.partial(row_back, sizes),
-        [(item, False) for item in (d_mid, weights, turn, *saved)],
-        [flat, triple, (packed, False), (packed, True)],
-        [square, pltpu.VMEM(packed, BF16), copies((4,))], 10,
+        at(ANY, d_att) + at(FAR, turn, normed, query, key, value, prob), at(FAR, triple, packed(3), packed(3)),
+        [square] * 5 + [scratch(*probs), scratch(*triple), scratch(*packed(3)), scratch(*packed(3)), copies((14,))],
     )
     field_grad, = call(
-        functools.partial(field_back, rows),
-        [(item, False) for item in (x, d_mid, dqkv_a, gains, weights)],
-        [((col_parts, rows, wide, channels), True)],
-        [pltpu.VMEM((col_parts, rows, wide, channels), BF16), copies], 4,
-    )
-    keep_a, field_grad = lax.optimization_barrier((keep_a, field_grad))
+        field_back, at(ANY, x, d_mid, gains) + at(FAR, dqkv, weights), at(FAR, x.shape),
+        [scratch(*triple), scratch(3, *flat), scratch(*x.shape), copies((3,))],
+    )
+    keep_a, field_grad, pieces_b, pieces_out = lax.optimization_barrier((keep_a, field_grad, pieces_b, pieces_out))
     sum_a = add_pair(keep_a, send_a, plane, core)
-    sum_a, field_grad, pieces_b, pieces_out = lax.optimization_barrier((sum_a, field_grad, pieces_b, pieces_out))
     pieces_a = plane_pieces(sum_a, plane, core)
     field_grad = lax.all_to_all(field_grad, "col", 0, 0, tiled=True).reshape(high, wide, channels)
     grads_b = last_sums(pieces_b, row_parts)

time: 170 us -> 156 us (0.918)
  local copies, waits for them, and re-layouts: 34.8 us -> 1.94 us
  Pallas kernels: 36.3 us -> 47.6 us
  waiting for transfers between devices: 50.3 us -> 59.7 us
    unnamed x63 -> x24, local copies, waits for them, and re-layouts: 30.3 us -> 0.86 us
    pallas_call x7 -> x8, Pallas kernels: 36.3 us -> 47.6 us  [call(): pl.pallas_call(kernel, in_specs=[spec(where) for _, where in ins], out_sp...]
    ppermute x20 -> x21, waiting for transfers between devices: 33.8 us -> 42.3 us  [swap(): return lax.ppermute(item, axis, [(at, at ^ step) for at in range(count)])]
    all_to_all x1, waiting for transfers between devices: 3.67 us -> 7.48 us  [body(): lax.all_to_all(field.reshape(col_parts, rows, wide, channels), 'col', 0,...]
    all_to_all x2, waiting for transfers between devices: 12.8 us -> 9.91 us  [all_to_all(): lax.all_to_all(item, ('row', 'col'), 0, 0, tiled=True)]
    dynamic_update_slice x4, local copies, waits for them, and re-layouts: 2.78 us -> 0.06 us  [body(): lax.dynamic_update_slice_in_dim(output, piece, (my_row ^ step) * cols, ax...]
    ppermute x20 -> x21, starting transfers between devices: 24 us -> 23.6 us  [swap(): return lax.ppermute(item, axis, [(at, at ^ step) for at in range(count)])]
  transfers between devices with their start and end apart: 24 -> 25, of which waited for: 9 -> 10; matrix products, arithmetic and copies ran while one was open for 5% -> 2% of each run, Pallas kernels for 3% -> 17%
where the time goes in v4:
time: 156 us; the launch traced here: 155 us
  waiting for transfers between devices  59.7 us (38%)
  Pallas kernels  47.6 us (31%)
  starting transfers between devices  41.5 us (27%)
  other arithmetic  3.52 us (2%)
  local copies, waits for them, and re-layouts  1.94 us (1%)
    pallas_call x8, Pallas kernels, call(): pl.pallas_call(kernel, in_specs=[spec(where) for _, where in ins], out_sp...  47.6 us
    ppermute x21, waiting for transfers between devices, swap(): return lax.ppermute(item, axis, [(at, at ^ step) for at in range(count)])  42.3 us
    ppermute x21, starting transfers between devices, swap(): return lax.ppermute(item, axis, [(at, at ^ step) for at in range(count)])  23.6 us
    all_to_all x2, waiting for transfers between devices, all_to_all(): lax.all_to_all(item, ('row', 'col'), 0, 0, tiled=True)  9.91 us
    all_to_all x2, starting transfers between devices, all_to_all(): lax.all_to_all(item, ('row', 'col'), 0, 0, tiled=True)  9.26 us
    all_to_all x1, waiting for transfers between devices, body(): lax.all_to_all(field.reshape(col_parts, rows, wide, channels), 'col', 0,...  7.48 us
    all_to_all x1, starting transfers between devices, body(): lax.all_to_all(field.reshape(col_parts, rows, wide, channels), 'col', 0,...  5.18 us
    all_to_all x1, starting transfers between devices, body(): lax.all_to_all(field_grad, 'col', 0, 0, tiled=True)  3.49 us
  transfers between devices with their start and end apart: 25, of which 10 were waited for; matrix products, arithmetic and copies ran while one was open for 2% of the time, Pallas kernels for 17%

profile of v4, /device:TPU:0, one launch (start us, length us, event | category | flops | bytes accessed | tf_op | source)
XLA Modules:
  0.0 155.4 jit_solution(14322526562865678501)
XLA Ops:
  0.6 5.2 %all-to-all-start = ((bf16[8,2,32,512]{3,2,1,0:T(8,128)(2,1)}), bf16[8,2,32,512]{3,2,1,0:T(8,128)(2,1)S(1)}, u32[]{:S(2)}, u32[]{:S(2)}) async-start(bf16[8,2,32,512]{3,2,1,0:T(8,128)(2,1)} %bitcast.88), calls=%async_computation | async-start | bytes 1048576 | tf_op jit(solution)/shard_map/all_to_all | solution.py:454
  5.8 2.2 %shard_map.67.turn_hbm.refs_5_ = bf16[7,512,512]{2,1,0:T(8,128)(2,1)} custom-call(), custom_call_target="tpu_custom_call" | custom-call | flops 1048576 | bytes 1024 | tf_op jit(solution)/shard_map/pallas_call | solution.py:376
  8.1 7.5 %all-to-all-done.x_ref = bf16[8,2,32,512]{3,2,1,0:T(8,128)(2,1)S(1)} async-done(((bf16[8,2,32,512]{3,2,1,0:T(8,128)(2,1)}), bf16[8,2,32,512]{3,2,1,0:T(8,128)(2,1)S(1)}, u32[]{:S(2)}, u32[]{:S(2)}) %all-to-all-start) | async-done | bytes 524320 | tf_op jit(solution)/shard_map/all_to_all | solution.py:454
  15.6 8.1 %shard_map.68 = (bf16[512,512]{1,0:T(8,128)(2,1)}, bf16[512,512]{1,0:T(8,128)(2,1)}, bf16[512,512]{1,0:T(8,128)(2,1)}, bf16[512,512]{1,0:T(8,128)(2,1)}, bf16[51...) custom-call(bf16[8,2,32,512]{3,2,1,0:T(8,128)(2,1)S(1)} %all-to-all-done.x_ref, ...), custom_call_target="tpu_custom_call" | custom-call | flops 1048576 | bytes 1024 | tf_op jit(solution)/shard_map/pallas_call | solution.py:376
  23.7 4.0 %all-to-all-start.1 = ((bf16[32,16,512]{2,1,0:T(8,128)(2,1)}), bf16[32,16,512]{2,1,0:T(8,128)(2,1)S(1)}, u32[]{:S(2)}, u32[]{:S(2)}) async-start(bf16[32,16,512]{2,1,0:T(8,128)(2,1)} %bitcast.89), calls=%async_computation.1 | async-start | bytes 1048576 | tf_op jit(solution)/shard_map/all_to_all | solution.py:452
  29.6 2.4 %collective-permute-start.1 = (bf16[16,8,512]{2,1,0:T(8,128)(2,1)S(1)}, bf16[16,8,512]{2,1,0:T(8,128)(2,1)S(1)}, u32[]{:S(2)}, u32[]{:S(2)}) collective-permute-start(bf16[16,8,512]{2,1,0:T(8,128)(2,1)S(1)} %get-tuple-element.119), channel_id=1, source_target_pairs={{0,16},{8,24},{16,0},{24,8},{1,17},{9,25},{17,1},{25,9},{2,18},{10... | collective-permute-start | bytes 393224 | tf_op jit(solution)/shard_map/ppermute | solution.py:388
  32.2 8.4 %collective-permute-done = bf16[16,8,512]{2,1,0:T(8,128)(2,1)S(1)} collective-permute-done((bf16[16,8,512]{2,1,0:T(8,128)(2,1)S(1)}, bf16[16,8,512]{2,1,0:T(8,128)(2,1)S(1)}, u32[]{:S(2)}, u32[]{:S(2)}) %collective-permute-start) | collective-permute-done | bytes 131104 | tf_op jit(solution)/shard_map/ppermute | solution.py:388
  40.6 11.0 %collective-permute-done.1 = bf16[16,8,512]{2,1,0:T(8,128)(2,1)S(1)} collective-permute-done((bf16[16,8,512]{2,1,0:T(8,128)(2,1)S(1)}, bf16[16,8,512]{2,1,0:T(8,128)(2,1)S(1)}, u32[]{:S(2)}, u32[]{:S(2)}) %collective-permute-start.1) | collective-permute-done | bytes 131104 | tf_op jit(solution)/shard_map/ppermute | solution.py:388
  51.6 2.0 %shard_map.69 = (bf16[512,512]{1,0:T(8,128)(2,1)S(1)}, bf16[512,512]{1,0:T(8,128)(2,1)S(1)}, bf16[2,512,512]{2,1,0:T(8,128)(2,1)S(1)}) custom-call(bf16[128,512]{1,0:T(8,128)(2,1)S(1)} %get-tuple-element.57.refs_0_, bf16[128,512]{1,0:T(8,128)(2,1)S(1)} %bitcast.80, bf16[128,512]{1,0:T(8,128)(2,1)S(1)} %bitcast.81, bf16[128,512]{1,0:T(8,128)(2,1)S(1)} %bitcast.82, ...), custom_call_target="tpu_custom_call" | custom-call | flops 1048576 | bytes 1024 | tf_op jit(solution)/shard_map/pallas_call | solution.py:376
  53.6 13.4 %shard_map.70 = (bf16[512,512]{1,0:T(8,128)(2,1)}, bf16[512,512]{1,0:T(8,128)(2,1)}, bf16[512,512]{1,0:T(8,128)(2,1)}, bf16[512,512]{1,0:T(8,128)(2,1)}, bf16[512,1536]{1,0:T(8,128)(2,1)}) custom-call(bf16[512,512]{1,0:T(8,128)(2,1)S(1)} %bitcast.78, bf16[512,512]{1,0:T(8,128)(2,1)S(1)} %get-tuple-element.58.cot_ref.cot_hbm, ...), custom_call_target="tpu_custom_call" | custom-call | flops 1048576 | bytes 1024 | tf_op jit(solution)/shard_map/pallas_call | solution.py:376
  67.0 5.3 %all-to-all-start.2 = ((bf16[32,16,512]{2,1,0:T(8,128)(2,1)}), bf16[32,16,512]{2,1,0:T(8,128)(2,1)S(1)}, u32[]{:S(2)}, u32[]{:S(2)}) async-start(bf16[32,16,512]{2,1,0:T(8,128)(2,1)} %bitcast.90), calls=%async_computation.2 | async-start | bytes 1048576 | tf_op jit(solution)/shard_map/all_to_all | solution.py:452
  72.3 5.5 %shard_map.71 = (bf16[128,512]{1,0:T(8,128)(2,1)}, bf16[128,512]{1,0:T(8,128)(2,1)}, bf16[128,512]{1,0:T(8,128)(2,1)}, bf16[128,512]{1,0:T(8,128)(2,1)}, bf16[4,...) custom-call(bf16[512,512]{1,0:T(8,128)(2,1)} %copy-done, bf16[512,512]{1,0:T(8,128)(2,1)} %get-tuple-element.62.mid_hbm, ...), custom_call_target="tpu_custom_call" | custom-call | flops 1048576 | bytes 1024 | tf_op jit(solution)/shard_map/pallas_call | solution.py:376
  77.8 9.9 %all-to-all-done.2 = bf16[32,16,512]{2,1,0:T(8,128)(2,1)S(1)} async-done(((bf16[32,16,512]{2,1,0:T(8,128)(2,1)}), bf16[32,16,512]{2,1,0:T(8,128)(2,1)S(1)}, u32[]{:S(2)}, u32[]{:S(2)}) %all-to-all-start.2) | async-done | bytes 524320 | tf_op jit(solution)/shard_map/all_to_all | solution.py:452
  87.7 3.2 %shard_map.72 = (bf16[512,512]{1,0:T(8,128)(2,1)S(1)}, bf16[512,512]{1,0:T(8,128)(2,1)S(1)}, bf16[4,1,64,512]{3,2,1,0:T(8,128)(2,1)}, bf16[4,1,64,512]{3,2,1,0:T(8,128)(2,1)}) custom-call(bf16[512,512]{1,0:T(8,128)(2,1)S(1)} %bitcast.79, bf16[2,4,512,512]{3,2,1,0:T(8,128)(2,1)} %w_hbm.9, bf16[7,512,512]{2,1,0:T(8,128)(2,1)} %shard_map.67.turn_hbm.refs_5_, ...), custom_call_target="tpu_custom_call" | custom-call | flops 1048576 | bytes 1024 | tf_op jit(solution)/shard_map/pallas_call | solution.py:376
  100.0 6.3 %collective-permute-done.10 = bf16[128,512]{1,0:T(8,128)(2,1)S(1)} collective-permute-done((bf16[128,512]{1,0:T(8,128)(2,1)S(1)}, bf16[128,512]{1,0:T(8,128)(2,1)S(1)}, u32[]{:S(2)}, u32[]{:S(2)}) %collective-permute-start.10) | collective-permute-done | bytes 131104 | tf_op jit(solution)/shard_map/ppermute | solution.py:388
  106.9 9.1 %shard_map.73 = (bf16[512,1536]{1,0:T(8,128)(2,1)}, bf16[4,3,64,512]{3,2,1,0:T(8,128)(2,1)}, bf16[4,3,64,512]{3,2,1,0:T(8,128)(2,1)}) custom-call(bf16[512,512]{1,0:T(8,128)(2,1)S(1)} %get-tuple-element.83.da_ref, bf16[7,512,512]{2,1,0:T(8,128)(2,1)} %shard_map.67.turn_hbm.refs_5_, bf16[512,512]{1,0:T(8,128)(2,1)} %get-tuple-element.84.n_hbm, ...), custom_call_target="tpu_custom_call" | custom-call | flops 1048576 | bytes 1024 | tf_op jit(solution)/shard_map/pallas_call | solution.py:376
  116.0 4.1 %shard_map.74 = bf16[8,2,32,512]{3,2,1,0:T(8,128)(2,1)} custom-call(bf16[8,2,32,512]{3,2,1,0:T(8,128)(2,1)S(1)} %all-to-all-done.x_ref, bf16[512,512]{1,0:T(8,128)(2,1)S(1)} %get-tuple-element.90.dm_ref, f32[2,512]{1,0:T(2,128)S(1)} %copy-done.1, bf16[512,1536]{1,0:T(8,128)(2,1)} %get-tuple-element.91.dqkv_hbm, bf16[2,4,512,512]{3,2,1,0:T(8,128)(2,1)} %w_hbm.9), custom_call_target="tpu_custom_call" | custom-call | flops 1048576 | bytes 1024 | tf_op jit(solution)/shard_map/pallas_call | solution.py:376
  122.1 2.1 %collective-permute-start.19 = (bf16[5,16,512]{2,1,0:T(8,128)(2,1)}, bf16[5,16,512]{2,1,0:T(8,128)(2,1)}, u32[]{:S(2)}, u32[]{:S(2)}) collective-permute-start(bf16[5,16,512]{2,1,0:T(8,128)(2,1)} %get-tuple-element.121), channel_id=1, source_target_pairs={{0,16},{8,24},{16,0},{24,8},{1,17},{9,25},{17,1},{25,9},{2,18},{10... | collective-permute-start | bytes 245768 | tf_op jit(solution)/shard_map/ppermute | solution.py:388
  124.2 3.5 %all-to-all-start.3 = ((bf16[8,2,32,512]{3,2,1,0:T(8,128)(2,1)}), bf16[8,2,32,512]{3,2,1,0:T(8,128)(2,1)S(1)}, u32[]{:S(2)}, u32[]{:S(2)}) async-start(bf16[8,2,32,512]{3,2,1,0:T(8,128)(2,1)} %shard_map.74), calls=%async_computation.3 | async-start | bytes 1048576 | tf_op jit(solution)/shard_map/all_to_all | solution.py:517
  128.1 2.0 %collective-permute-start.12 = (bf16[3,64,512]{2,1,0:T(8,128)(2,1)S(1)}, bf16[3,64,512]{2,1,0:T(8,128)(2,1)S(1)}, u32[]{:S(2)}, u32[]{:S(2)}) collective-permute-start(bf16[3,64,512]{2,1,0:T(8,128)(2,1)S(1)} %get-tuple-element.113), channel_id=1, source_target_pairs={{0,2},{1,3},{2,0},{3,1},{4,6},{5,7},{6,4},{7,5},{8,10},{9,11},{10,... | collective-permute-start | bytes 589832 | tf_op jit(solution)/shard_map/ppermute | solution.py:388
  131.7 9.4 %collective-permute-done.12 = bf16[3,64,512]{2,1,0:T(8,128)(2,1)S(1)} collective-permute-done((bf16[3,64,512]{2,1,0:T(8,128)(2,1)S(1)}, bf16[3,64,512]{2,1,0:T(8,128)(2,1)S(1)}, u32[]{:S(2)}, u32[]{:S(2)}) %collective-permute-start.12) | collective-permute-done | bytes 196640 | tf_op jit(solution)/shard_map/ppermute | solution.py:388
  142.4 3.4 %collective-permute-done.14 = bf16[3,64,512]{2,1,0:T(8,128)(2,1)S(1)} collective-permute-done((bf16[3,64,512]{2,1,0:T(8,128)(2,1)S(1)}, bf16[3,64,512]{2,1,0:T(8,128)(2,1)S(1)}, u32[]{:S(2)}, u32[]{:S(2)}) %collective-permute-start.14) | collective-permute-done | bytes 196640 | tf_op jit(solution)/shard_map/ppermute | solution.py:388
  147.8 2.6 %collective-permute-start.17 = (bf16[3,16,512]{2,1,0:T(8,128)(2,1)S(1)}, bf16[3,16,512]{2,1,0:T(8,128)(2,1)S(1)}, u32[]{:S(2)}, u32[]{:S(2)}) collective-permute-start(bf16[3,16,512]{2,1,0:T(8,128)(2,1)S(1)} %get-tuple-element.125), channel_id=1, source_target_pairs={{0,24},{8,16},{16,8},{24,0},{1,25},{9,17},{17,9},{25,1},{2,26},{10... | collective-permute-start | bytes 147464 | tf_op jit(solution)/shard_map/ppermute | solution.py:388
  151.3 1.9 %collective-permute-done.16 = bf16[3,16,512]{2,1,0:T(8,128)(2,1)S(1)} collective-permute-done((bf16[3,16,512]{2,1,0:T(8,128)(2,1)S(1)}, bf16[3,16,512]{2,1,0:T(8,128)(2,1)S(1)}, u32[]{:S(2)}, u32[]{:S(2)}) %collective-permute-start.16) | collective-permute-done | bytes 49184 | tf_op jit(solution)/shard_map/ppermute | solution.py:388
  (77 shorter events, 22.0 us)
Async XLA Ops:
  0.6 14.9 %all-to-all-start = ((bf16[8,2,32,512]{3,2,1,0:T(8,128)(2,1)}), bf16[8,2,32,512]{3,2,1,0:T(8,128)(2,1)S(1)}, u32[]{:S(2)}, u32[]{:S(2)}) async-start(bf16[8,2,32,512]{3,2,1,0:T(8,128)(2,1)} %bitcast.88), calls=%async_computation | async-start | bytes 1048576 | tf_op jit(solution)/shard_map/all_to_all | solution.py:454
  23.7 29.9 %all-to-all-start.1 = ((bf16[32,16,512]{2,1,0:T(8,128)(2,1)}), bf16[32,16,512]{2,1,0:T(8,128)(2,1)S(1)}, u32[]{:S(2)}, u32[]{:S(2)}) async-start(bf16[32,16,512]{2,1,0:T(8,128)(2,1)} %bitcast.89), calls=%async_computation.1 | async-start | bytes 1048576 | tf_op jit(solution)/shard_map/all_to_all | solution.py:452
  27.7 12.9 %collective-permute-start = (bf16[16,8,512]{2,1,0:T(8,128)(2,1)S(1)}, bf16[16,8,512]{2,1,0:T(8,128)(2,1)S(1)}, u32[]{:S(2)}, u32[]{:S(2)}) collective-permute-start(bf16[16,8,512]{2,1,0:T(8,128)(2,1)S(1)} %get-tuple-element.117), channel_id=1, source_target_pairs={{0,8},{8,0},{16,24},{24,16},{1,9},{9,1},{17,25},{25,17},{2,10},{10... | collective-permute-start | bytes 393224 | tf_op jit(solution)/shard_map/ppermute | solution.py:388
  29.6 22.0 %collective-permute-start.1 = (bf16[16,8,512]{2,1,0:T(8,128)(2,1)S(1)}, bf16[16,8,512]{2,1,0:T(8,128)(2,1)S(1)}, u32[]{:S(2)}, u32[]{:S(2)}) collective-permute-start(bf16[16,8,512]{2,1,0:T(8,128)(2,1)S(1)} %get-tuple-element.119), channel_id=1, source_target_pairs={{0,16},{8,24},{16,0},{24,8},{1,17},{9,25},{17,1},{25,9},{2,18},{10... | collective-permute-start | bytes 393224 | tf_op jit(solution)/shard_map/ppermute | solution.py:388
  32.0 19.6 %collective-permute-start.2 = (bf16[16,8,512]{2,1,0:T(8,128)(2,1)S(1)}, bf16[16,8,512]{2,1,0:T(8,128)(2,1)S(1)}, u32[]{:S(2)}, u32[]{:S(2)}) collective-permute-start(bf16[16,8,512]{2,1,0:T(8,128)(2,1)S(1)} %get-tuple-element.116), channel_id=1, source_target_pairs={{0,24},{8,16},{16,8},{24,0},{1,25},{9,17},{17,9},{25,1},{2,26},{10... | collective-permute-start | bytes 393224 | tf_op jit(solution)/shard_map/ppermute | solution.py:388
  67.0 20.7 %all-to-all-start.2 = ((bf16[32,16,512]{2,1,0:T(8,128)(2,1)}), bf16[32,16,512]{2,1,0:T(8,128)(2,1)S(1)}, u32[]{:S(2)}, u32[]{:S(2)}) async-start(bf16[32,16,512]{2,1,0:T(8,128)(2,1)} %bitcast.90), calls=%async_computation.2 | async-start | bytes 1048576 | tf_op jit(solution)/shard_map/all_to_all | solution.py:452
  87.7 6.2 %collective-permute-start.3 = (bf16[4,4,64,512]{3,2,1,0:T(8,128)(2,1)}, bf16[4,4,64,512]{3,2,1,0:T(8,128)(2,1)S(1)}, u32[]{:S(2)}, u32[]{:S(2)}) collective-permute-start(bf16[4,4,64,512]{3,2,1,0:T(8,128)(2,1)} %get-tuple-element.76), channel_id=1, source_target_pairs={{0,1},{1,0},{2,3},{3,2},{4,5},{5,4},{6,7},{7,6},{8,9},{9,8},{10,11... | collective-permute-start | bytes 3145736 | tf_op jit(solution)/shard_map/ppermute | solution.py:388
  94.5 25.6 %collective-permute-start.5 = (bf16[5,64,512]{2,1,0:T(8,128)(2,1)S(1)}, bf16[5,64,512]{2,1,0:T(8,128)(2,1)S(1)}, u32[]{:S(2)}, u32[]{:S(2)}) collective-permute-start(bf16[5,64,512]{2,1,0:T(8,128)(2,1)S(1)} %get-tuple-element.111), channel_id=1, source_target_pairs={{0,2},{1,3},{2,0},{3,1},{4,6},{5,7},{6,4},{7,5},{8,10},{9,11},{10,... | collective-permute-start | bytes 983048 | tf_op jit(solution)/shard_map/ppermute | solution.py:388
  95.8 24.4 %collective-permute-start.6 = (bf16[5,64,512]{2,1,0:T(8,128)(2,1)S(1)}, bf16[5,64,512]{2,1,0:T(8,128)(2,1)S(1)}, u32[]{:S(2)}, u32[]{:S(2)}) collective-permute-start(bf16[5,64,512]{2,1,0:T(8,128)(2,1)S(1)} %get-tuple-element.110), channel_id=1, source_target_pairs={{0,4},{1,5},{2,6},{3,7},{4,0},{5,1},{6,2},{7,3},{8,12},{9,13},{10,... | collective-permute-start | bytes 983048 | tf_op jit(solution)/shard_map/ppermute | solution.py:388
  97.0 23.2 %collective-permute-start.7 = (bf16[5,64,512]{2,1,0:T(8,128)(2,1)S(1)}, bf16[5,64,512]{2,1,0:T(8,128)(2,1)S(1)}, u32[]{:S(2)}, u32[]{:S(2)}) collective-permute-start(bf16[5,64,512]{2,1,0:T(8,128)(2,1)S(1)} %get-tuple-element.109), channel_id=1, source_target_pairs={{0,6},{1,7},{2,4},{3,5},{4,2},{5,3},{6,0},{7,1},{8,14},{9,15},{10,... | collective-permute-start | bytes 983048 | tf_op jit(solution)/shard_map/ppermute | solution.py:388
  98.1 8.2 %collective-permute-start.10 = (bf16[128,512]{1,0:T(8,128)(2,1)S(1)}, bf16[128,512]{1,0:T(8,128)(2,1)S(1)}, u32[]{:S(2)}, u32[]{:S(2)}) collective-permute-start(bf16[128,512]{1,0:T(8,128)(2,1)S(1)} %copy-done.10), channel_id=1, source_target_pairs={{0,24},{8,16},{16,8},{24,0},{1,25},{9,17},{17,9},{25,1},{2,26},{10... | collective-permute-start | bytes 393224 | tf_op jit(solution)/shard_map/ppermute | solution.py:388
  99.2 20.8 %collective-permute-start.8 = (bf16[128,512]{1,0:T(8,128)(2,1)S(1)}, bf16[128,512]{1,0:T(8,128)(2,1)S(1)}, u32[]{:S(2)}, u32[]{:S(2)}) collective-permute-start(bf16[128,512]{1,0:T(8,128)(2,1)S(1)} %copy-done.9), channel_id=1, source_target_pairs={{0,8},{8,0},{16,24},{24,16},{1,9},{9,1},{17,25},{25,17},{2,10},{10... | collective-permute-start | bytes 393224 | tf_op jit(solution)/shard_map/ppermute | solution.py:388
  106.3 13.9 %collective-permute-start.9 = (bf16[128,512]{1,0:T(8,128)(2,1)S(1)}, bf16[128,512]{1,0:T(8,128)(2,1)S(1)}, u32[]{:S(2)}, u32[]{:S(2)}) collective-permute-start(bf16[128,512]{1,0:T(8,128)(2,1)S(1)} %copy-done.8), channel_id=1, source_target_pairs={{0,16},{8,24},{16,0},{24,8},{1,17},{9,25},{17,1},{25,9},{2,18},{10... | collective-permute-start | bytes 393224 | tf_op jit(solution)/shard_map/ppermute | solution.py:388
  120.0 7.8 %collective-permute-start.11 = (bf16[4,3,64,512]{3,2,1,0:T(8,128)(2,1)}, bf16[4,3,64,512]{3,2,1,0:T(8,128)(2,1)S(1)}, u32[]{:S(2)}, u32[]{:S(2)}) collective-permute-start(bf16[4,3,64,512]{3,2,1,0:T(8,128)(2,1)} %get-tuple-element.104), channel_id=1, source_target_pairs={{0,1},{1,0},{2,3},{3,2},{4,5},{5,4},{6,7},{7,6},{8,9},{9,8},{10,11... | collective-permute-start | bytes 2359304 | tf_op jit(solution)/shard_map/ppermute | solution.py:388
  121.1 26.8 %collective-permute-start.18 = (bf16[5,16,512]{2,1,0:T(8,128)(2,1)}, bf16[5,16,512]{2,1,0:T(8,128)(2,1)S(1)}, u32[]{:S(2)}, u32[]{:S(2)}) collective-permute-start(bf16[5,16,512]{2,1,0:T(8,128)(2,1)} %get-tuple-element.120), channel_id=1, source_target_pairs={{0,8},{8,0},{16,24},{24,16},{1,9},{9,1},{17,25},{25,17},{2,10},{10... | collective-permute-start | bytes 245768 | tf_op jit(solution)/shard_map/ppermute | solution.py:388
  122.1 28.3 %collective-permute-start.19 = (bf16[5,16,512]{2,1,0:T(8,128)(2,1)}, bf16[5,16,512]{2,1,0:T(8,128)(2,1)}, u32[]{:S(2)}, u32[]{:S(2)}) collective-permute-start(bf16[5,16,512]{2,1,0:T(8,128)(2,1)} %get-tuple-element.121), channel_id=1, source_target_pairs={{0,16},{8,24},{16,0},{24,8},{1,17},{9,25},{17,1},{25,9},{2,18},{10... | collective-permute-start | bytes 245768 | tf_op jit(solution)/shard_map/ppermute | solution.py:388
  124.2 27.1 %all-to-all-start.3 = ((bf16[8,2,32,512]{3,2,1,0:T(8,128)(2,1)}), bf16[8,2,32,512]{3,2,1,0:T(8,128)(2,1)S(1)}, u32[]{:S(2)}, u32[]{:S(2)}) async-start(bf16[8,2,32,512]{3,2,1,0:T(8,128)(2,1)} %shard_map.74), calls=%async_computation.3 | async-start | bytes 1048576 | tf_op jit(solution)/shard_map/all_to_all | solution.py:517
  128.1 13.0 %collective-permute-start.12 = (bf16[3,64,512]{2,1,0:T(8,128)(2,1)S(1)}, bf16[3,64,512]{2,1,0:T(8,128)(2,1)S(1)}, u32[]{:S(2)}, u32[]{:S(2)}) collective-permute-start(bf16[3,64,512]{2,1,0:T(8,128)(2,1)S(1)} %get-tuple-element.113), channel_id=1, source_target_pairs={{0,2},{1,3},{2,0},{3,1},{4,6},{5,7},{6,4},{7,5},{8,10},{9,11},{10,... | collective-permute-start | bytes 589832 | tf_op jit(solution)/shard_map/ppermute | solution.py:388
  130.1 12.3 %collective-permute-start.13 = (bf16[3,64,512]{2,1,0:T(8,128)(2,1)S(1)}, bf16[3,64,512]{2,1,0:T(8,128)(2,1)S(1)}, u32[]{:S(2)}, u32[]{:S(2)}) collective-permute-start(bf16[3,64,512]{2,1,0:T(8,128)(2,1)S(1)} %get-tuple-element.115), channel_id=1, source_target_pairs={{0,4},{1,5},{2,6},{3,7},{4,0},{5,1},{6,2},{7,3},{8,12},{9,13},{10,... | collective-permute-start | bytes 589832 | tf_op jit(solution)/shard_map/ppermute | solution.py:388
  131.6 14.2 %collective-permute-start.14 = (bf16[3,64,512]{2,1,0:T(8,128)(2,1)S(1)}, bf16[3,64,512]{2,1,0:T(8,128)(2,1)S(1)}, u32[]{:S(2)}, u32[]{:S(2)}) collective-permute-start(bf16[3,64,512]{2,1,0:T(8,128)(2,1)S(1)} %get-tuple-element.114), channel_id=1, source_target_pairs={{0,6},{1,7},{2,4},{3,5},{4,2},{5,3},{6,0},{7,1},{8,14},{9,15},{10,... | collective-permute-start | bytes 589832 | tf_op jit(solution)/shard_map/ppermute | solution.py:388
  141.1 9.3 %collective-permute-start.20 = (bf16[5,16,512]{2,1,0:T(8,128)(2,1)S(1)}, bf16[5,16,512]{2,1,0:T(8,128)(2,1)S(1)}, u32[]{:S(2)}, u32[]{:S(2)}) collective-permute-start(bf16[5,16,512]{2,1,0:T(8,128)(2,1)S(1)} %copy-done.7), channel_id=1, source_target_pairs={{0,24},{8,16},{16,8},{24,0},{1,25},{9,17},{17,9},{25,1},{2,26},{10... | collective-permute-start | bytes 245768 | tf_op jit(solution)/shard_map/ppermute | solution.py:388
  145.9 5.4 %collective-permute-start.15 = (bf16[3,16,512]{2,1,0:T(8,128)(2,1)S(1)}, bf16[3,16,512]{2,1,0:T(8,128)(2,1)S(1)}, u32[]{:S(2)}, u32[]{:S(2)}) collective-permute-start(bf16[3,16,512]{2,1,0:T(8,128)(2,1)S(1)} %get-tuple-element.123), channel_id=1, source_target_pairs={{0,8},{8,0},{16,24},{24,16},{1,9},{9,1},{17,25},{25,17},{2,10},{10... | collective-permute-start | bytes 147464 | tf_op jit(solution)/shard_map/ppermute | solution.py:388
  147.2 6.0 %collective-permute-start.16 = (bf16[3,16,512]{2,1,0:T(8,128)(2,1)S(1)}, bf16[3,16,512]{2,1,0:T(8,128)(2,1)S(1)}, u32[]{:S(2)}, u32[]{:S(2)}) collective-permute-start(bf16[3,16,512]{2,1,0:T(8,128)(2,1)S(1)} %get-tuple-element.124), channel_id=1, source_target_pairs={{0,16},{8,24},{16,0},{24,8},{1,17},{9,25},{17,1},{25,9},{2,18},{10... | collective-permute-start | bytes 147464 | tf_op jit(solution)/shard_map/ppermute | solution.py:388
  147.8 6.0 %collective-permute-start.17 = (bf16[3,16,512]{2,1,0:T(8,128)(2,1)S(1)}, bf16[3,16,512]{2,1,0:T(8,128)(2,1)S(1)}, u32[]{:S(2)}, u32[]{:S(2)}) collective-permute-start(bf16[3,16,512]{2,1,0:T(8,128)(2,1)S(1)} %get-tuple-element.125), channel_id=1, source_target_pairs={{0,24},{8,16},{16,8},{24,0},{1,25},{9,17},{17,9},{25,1},{2,26},{10... | collective-permute-start | bytes 147464 | tf_op jit(solution)/shard_map/ppermute | solution.py:388
  (12 other events, 123.4 us)

commit v5 on v4

--- a/solution.py
+++ b/solution.py
@@ -388,9 +388,8 @@
     return lax.ppermute(item, axis, [(at, at ^ step) for at in range(count)])
 
 
-def add_pair(keep, send, plane, core):
-    got = swap(send, "col", plane * core, 1)
-    return (keep.astype(F32) + got.astype(F32)).astype(BF16)
+def add(left, right):
+    return (left.astype(F32) + right.astype(F32)).astype(BF16)
 
 
 def plane_pieces(total, plane, core):
@@ -468,7 +467,7 @@
         at(ANY, x, gains) + at(FAR, weights, turn), at(FAR, *[flat] * 6, probs),
         [scratch(4, *flat)] + [square] * 7 + [scratch(*probs), copies((5,)), copies((6,)), copies((4,))],
     )
-    cots[0], _ = lax.optimization_barrier((cots[0], mid))
+    mid, cots = lax.optimization_barrier((mid, cots))
     cot, d_att, early = call(
         functools.partial(column_first, row_parts),
         at(ANY, *cots) + at(FAR, weights, turn), at(NEAR, flat, flat, (2, *flat)), [square, square, copies((4,))],
@@ -491,16 +490,17 @@
          scratch(*triple), copies((16 + row_parts,))],
     )
     d_mid, outs, keep_b, send_b = lax.optimization_barrier((d_mid, outs, keep_b, send_b))
-    sum_b = add_pair(keep_b, send_b, plane, core)
+    sum_b = add(keep_b, swap(send_b, "col", col_parts, 1))
     d_mid, d_att, keep_o, send_o = call(
         row_back_first,
         at(ANY, d_mid) + at(FAR, weights, turn, attended), at(ANY, flat, flat) + at(FAR, packed(1), packed(1)),
         [square, scratch(2, *flat), square, scratch(*packed(1)), scratch(*packed(1)), copies((6,))],
     )
-    sum_o = add_pair(keep_o, send_o, plane, core)
+    sum_o = add(keep_o, swap(send_o, "col", col_parts, 1))
+    outs[1] = swap(outs[1], "row", row_parts, 1)
     d_att, sum_b, sum_o, outs = lax.optimization_barrier((d_att, sum_b, sum_o, outs))
     pieces_b = plane_pieces(jnp.concatenate([sum_o, sum_b], axis=1), plane, core)
-    pieces_out = [piece if step == 0 else swap(piece, "row", row_parts, step) for step, piece in enumerate(outs)]
+    pieces_out = [piece if step < 2 else swap(piece, "row", row_parts, step) for step, piece in enumerate(outs)]
 
     dqkv, keep_a, send_a = call(
         functools.partial(row_back, sizes),
@@ -511,8 +511,12 @@
         field_back, at(ANY, x, d_mid, gains) + at(FAR, dqkv, weights), at(FAR, x.shape),
         [scratch(*triple), scratch(3, *flat), scratch(*x.shape), copies((3,))],
     )
-    keep_a, field_grad, pieces_b, pieces_out = lax.optimization_barrier((keep_a, field_grad, pieces_b, pieces_out))
-    sum_a = add_pair(keep_a, send_a, plane, core)
+    got_a = swap(send_a, "col", col_parts, 1)
+    keep_a, got_a, field_grad, pieces_b, pieces_out = lax.optimization_barrier(
+        (keep_a, got_a, field_grad, pieces_b, pieces_out)
+    )
+    sum_a = add(keep_a, got_a)
+    sum_a, field_grad, pieces_b, pieces_out = lax.optimization_barrier((sum_a, field_grad, pieces_b, pieces_out))
     pieces_a = plane_pieces(sum_a, plane, core)
     field_grad = lax.all_to_all(field_grad, "col", 0, 0, tiled=True).reshape(high, wide, channels)
     grads_b = last_sums(pieces_b, row_parts)

time: 156 us -> 141 us (0.904)
  waiting for transfers between devices: 59.7 us -> 39 us
  local copies, waits for them, and re-layouts: 1.94 us -> 7.65 us
    ppermute x21, waiting for transfers between devices: 42.3 us -> 14.6 us  [swap(): return lax.ppermute(item, axis, [(at, at ^ step) for at in range(count)])]
    all_to_all x2, waiting for transfers between devices: 9.91 us -> 22.5 us  [all_to_all(): lax.all_to_all(item, ('row', 'col'), 0, 0, tiled=True)]
    all_to_all x1, waiting for transfers between devices: 7.48 us -> 1.93 us  [body(): lax.all_to_all(field.reshape(col_parts, rows, wide, channels), 'col', 0,...]
    dynamic_update_slice x4, local copies, waits for them, and re-layouts: 0.06 us -> 2.78 us  [body(): lax.dynamic_update_slice_in_dim(output, piece, (my_row ^ step) * cols, ax...]
    unnamed x24 -> x32, local copies, waits for them, and re-layouts: 0.86 us -> 2.73 us
    all_to_all x2, starting transfers between devices: 9.26 us -> 7.69 us  [all_to_all(): lax.all_to_all(item, ('row', 'col'), 0, 0, tiled=True)]
  transfers between devices with their start and end apart: 25 -> 25, of which waited for: 10 -> 10; matrix products, arithmetic and copies ran while one was open for 2% -> 6% of each run, Pallas kernels for 17% -> 18%
where the time goes in v5:
time: 141 us; the launch traced here: 140 us
  Pallas kernels  47.7 us (34%)
  starting transfers between devices  41 us (29%)
  waiting for transfers between devices  39 us (28%)
  local copies, waits for them, and re-layouts  7.65 us (5%)
  other arithmetic  3.64 us (3%)
    pallas_call x8, Pallas kernels, call(): pl.pallas_call(kernel, in_specs=[spec(where) for _, where in ins], out_sp...  47.7 us
    ppermute x21, starting transfers between devices, swap(): return lax.ppermute(item, axis, [(at, at ^ step) for at in range(count)])  24.6 us
    all_to_all x2, waiting for transfers between devices, all_to_all(): lax.all_to_all(item, ('row', 'col'), 0, 0, tiled=True)  22.5 us
    ppermute x21, waiting for transfers between devices, swap(): return lax.ppermute(item, axis, [(at, at ^ step) for at in range(count)])  14.6 us
    all_to_all x2, starting transfers between devices, all_to_all(): lax.all_to_all(item, ('row', 'col'), 0, 0, tiled=True)  7.69 us
    all_to_all x1, starting transfers between devices, body(): lax.all_to_all(field.reshape(col_parts, rows, wide, channels), 'col', 0,...  5.18 us
    all_to_all x1, starting transfers between devices, body(): lax.all_to_all(field_grad, 'col', 0, 0, tiled=True)  3.49 us
  transfers between devices with their start and end apart: 25, of which 10 were waited for; matrix products, arithmetic and copies ran while one was open for 6% of the time, Pallas kernels for 18%

profile of v5, /device:TPU:0, one launch (start us, length us, event | category | flops | bytes accessed | tf_op | source)
XLA Modules:
  0.0 140.0 jit_solution(427890909162447550)
XLA Ops:
  0.6 5.2 %all-to-all-start = ((bf16[8,2,32,512]{3,2,1,0:T(8,128)(2,1)}), bf16[8,2,32,512]{3,2,1,0:T(8,128)(2,1)S(1)}, u32[]{:S(2)}, u32[]{:S(2)}) async-start(bf16[8,2,32,512]{3,2,1,0:T(8,128)(2,1)} %bitcast.86), calls=%async_computation | async-start | bytes 1048576 | tf_op jit(solution)/shard_map/all_to_all | solution.py:453
  6.9 1.6 %collective-permute-start = (bf16[16,8,512]{2,1,0:T(8,128)(2,1)S(1)}, bf16[16,8,512]{2,1,0:T(8,128)(2,1)S(1)}, u32[]{:S(2)}, u32[]{:S(2)}) collective-permute-start(bf16[16,8,512]{2,1,0:T(8,128)(2,1)S(1)} %get-tuple-element.147), channel_id=1, source_target_pairs={{0,8},{8,0},{16,24},{24,16},{1,9},{9,1},{17,25},{25,17},{2,10},{10... | collective-permute-start | bytes 393224 | tf_op jit(solution)/shard_map/ppermute | solution.py:388
  8.6 2.6 %collective-permute-start.1 = (bf16[16,8,512]{2,1,0:T(8,128)(2,1)S(1)}, bf16[16,8,512]{2,1,0:T(8,128)(2,1)S(1)}, u32[]{:S(2)}, u32[]{:S(2)}) collective-permute-start(bf16[16,8,512]{2,1,0:T(8,128)(2,1)S(1)} %get-tuple-element.149), channel_id=1, source_target_pairs={{0,16},{8,24},{16,0},{24,8},{1,17},{9,25},{17,1},{25,9},{2,18},{10... | collective-permute-start | bytes 393224 | tf_op jit(solution)/shard_map/ppermute | solution.py:388
  11.4 2.2 %shard_map.67.turn_hbm.refs_5_ = bf16[7,512,512]{2,1,0:T(8,128)(2,1)} custom-call(), custom_call_target="tpu_custom_call" | custom-call | flops 1048576 | bytes 1024 | tf_op jit(solution)/shard_map/pallas_call | solution.py:376
  13.6 1.9 %all-to-all-done.x_ref = bf16[8,2,32,512]{3,2,1,0:T(8,128)(2,1)S(1)} async-done(((bf16[8,2,32,512]{3,2,1,0:T(8,128)(2,1)}), bf16[8,2,32,512]{3,2,1,0:T(8,128)(2,1)S(1)}, u32[]{:S(2)}, u32[]{:S(2)}) %all-to-all-start) | async-done | bytes 524320 | tf_op jit(solution)/shard_map/all_to_all | solution.py:453
  15.6 8.2 %shard_map.68 = (bf16[512,512]{1,0:T(8,128)(2,1)}, bf16[512,512]{1,0:T(8,128)(2,1)}, bf16[512,512]{1,0:T(8,128)(2,1)}, bf16[512,512]{1,0:T(8,128)(2,1)}, bf16[51...) custom-call(bf16[8,2,32,512]{3,2,1,0:T(8,128)(2,1)S(1)} %all-to-all-done.x_ref, ...), custom_call_target="tpu_custom_call" | custom-call | flops 1048576 | bytes 1024 | tf_op jit(solution)/shard_map/pallas_call | solution.py:376
  24.4 4.4 %all-to-all-start.1 = ((bf16[32,16,512]{2,1,0:T(8,128)(2,1)}), bf16[32,16,512]{2,1,0:T(8,128)(2,1)S(1)}, u32[]{:S(2)}, u32[]{:S(2)}) async-start(bf16[32,16,512]{2,1,0:T(8,128)(2,1)} %bitcast.87), calls=%async_computation.1 | async-start | bytes 1048576 | tf_op jit(solution)/shard_map/all_to_all | solution.py:451
  29.7 2.0 %shard_map.69 = (bf16[512,512]{1,0:T(8,128)(2,1)S(1)}, bf16[512,512]{1,0:T(8,128)(2,1)S(1)}, bf16[2,512,512]{2,1,0:T(8,128)(2,1)S(1)}) custom-call(bf16[128,512]{1,0:T(8,128)(2,1)S(1)} %get-tuple-element.73.refs_0_, bf16[128,512]{1,0:T(8,128)(2,1)S(1)} %bitcast.78, bf16[128,512]{1,0:T(8,128)(2,1)S(1)} %bitcast.79, bf16[128,512]{1,0:T(8,128)(2,1)S(1)} %bitcast.80, ...), custom_call_target="tpu_custom_call" | custom-call | flops 1048576 | bytes 1024 | tf_op jit(solution)/shard_map/pallas_call | solution.py:376
  31.8 12.6 %all-to-all-done.1 = bf16[32,16,512]{2,1,0:T(8,128)(2,1)S(1)} async-done(((bf16[32,16,512]{2,1,0:T(8,128)(2,1)}), bf16[32,16,512]{2,1,0:T(8,128)(2,1)S(1)}, u32[]{:S(2)}, u32[]{:S(2)}) %all-to-all-start.1) | async-done | bytes 524320 | tf_op jit(solution)/shard_map/all_to_all | solution.py:451
  44.4 13.3 %shard_map.70 = (bf16[512,512]{1,0:T(8,128)(2,1)}, bf16[512,512]{1,0:T(8,128)(2,1)}, bf16[512,512]{1,0:T(8,128)(2,1)}, bf16[512,512]{1,0:T(8,128)(2,1)}, bf16[512,1536]{1,0:T(8,128)(2,1)}) custom-call(bf16[512,512]{1,0:T(8,128)(2,1)S(1)} %bitcast.77, bf16[512,512]{1,0:T(8,128)(2,1)S(1)} %get-tuple-element.77.cot_ref.cot_hbm, ...), custom_call_target="tpu_custom_call" | custom-call | flops 1048576 | bytes 1024 | tf_op jit(solution)/shard_map/pallas_call | solution.py:376
  57.7 3.3 %all-to-all-start.2 = ((bf16[32,16,512]{2,1,0:T(8,128)(2,1)}), bf16[32,16,512]{2,1,0:T(8,128)(2,1)S(1)}, u32[]{:S(2)}, u32[]{:S(2)}) async-start(bf16[32,16,512]{2,1,0:T(8,128)(2,1)} %bitcast.88), calls=%async_computation.2 | async-start | bytes 1048576 | tf_op jit(solution)/shard_map/all_to_all | solution.py:451
  61.0 5.4 %shard_map.71 = (bf16[128,512]{1,0:T(8,128)(2,1)}, bf16[128,512]{1,0:T(8,128)(2,1)}, bf16[128,512]{1,0:T(8,128)(2,1)}, bf16[128,512]{1,0:T(8,128)(2,1)}, bf16[4,...) custom-call(bf16[512,512]{1,0:T(8,128)(2,1)} %copy-done, bf16[512,512]{1,0:T(8,128)(2,1)} %get-tuple-element.81.mid_hbm, ...), custom_call_target="tpu_custom_call" | custom-call | flops 1048576 | bytes 1024 | tf_op jit(solution)/shard_map/pallas_call | solution.py:376
  66.5 9.9 %all-to-all-done.2 = bf16[32,16,512]{2,1,0:T(8,128)(2,1)S(1)} async-done(((bf16[32,16,512]{2,1,0:T(8,128)(2,1)}), bf16[32,16,512]{2,1,0:T(8,128)(2,1)S(1)}, u32[]{:S(2)}, u32[]{:S(2)}) %all-to-all-start.2) | async-done | bytes 524320 | tf_op jit(solution)/shard_map/all_to_all | solution.py:451
  76.4 3.3 %shard_map.72 = (bf16[512,512]{1,0:T(8,128)(2,1)S(1)}, bf16[512,512]{1,0:T(8,128)(2,1)S(1)}, bf16[4,1,64,512]{3,2,1,0:T(8,128)(2,1)}, bf16[4,1,64,512]{3,2,1,0:T(8,128)(2,1)}) custom-call(bf16[512,512]{1,0:T(8,128)(2,1)S(1)} %bitcast.76, bf16[2,4,512,512]{3,2,1,0:T(8,128)(2,1)} %w_hbm.9, bf16[7,512,512]{2,1,0:T(8,128)(2,1)} %shard_map.67.turn_hbm.refs_5_, ...), custom_call_target="tpu_custom_call" | custom-call | flops 1048576 | bytes 1024 | tf_op jit(solution)/shard_map/pallas_call | solution.py:376
  83.0 2.7 %collective-permute-done.5 = bf16[128,512]{1,0:T(8,128)(2,1)S(1)} collective-permute-done((bf16[128,512]{1,0:T(8,128)(2,1)S(1)}, bf16[128,512]{1,0:T(8,128)(2,1)S(1)}, u32[]{:S(2)}, u32[]{:S(2)}) %collective-permute-start.5) | collective-permute-done | bytes 131104 | tf_op jit(solution)/shard_map/ppermute | solution.py:388
  85.7 9.1 %shard_map.73 = (bf16[512,1536]{1,0:T(8,128)(2,1)}, bf16[4,3,64,512]{3,2,1,0:T(8,128)(2,1)}, bf16[4,3,64,512]{3,2,1,0:T(8,128)(2,1)}) custom-call(bf16[512,512]{1,0:T(8,128)(2,1)S(1)} %get-tuple-element.102.da_ref, bf16[7,512,512]{2,1,0:T(8,128)(2,1)} %shard_map.67.turn_hbm.refs_5_, bf16[512,512]{1,0:T(8,128)(2,1)} %get-tuple-element.103.n_hbm, ...), custom_call_target="tpu_custom_call" | custom-call | flops 1048576 | bytes 1024 | tf_op jit(solution)/shard_map/pallas_call | solution.py:376
  100.1 7.6 %collective-permute-done.10 = bf16[128,512]{1,0:T(8,128)(2,1)S(1)} collective-permute-done((bf16[128,512]{1,0:T(8,128)(2,1)S(1)}, bf16[128,512]{1,0:T(8,128)(2,1)S(1)}, u32[]{:S(2)}, u32[]{:S(2)}) %collective-permute-start.10) | collective-permute-done | bytes 131104 | tf_op jit(solution)/shard_map/ppermute | solution.py:388
  108.7 4.2 %shard_map.74 = bf16[8,2,32,512]{3,2,1,0:T(8,128)(2,1)} custom-call(bf16[8,2,32,512]{3,2,1,0:T(8,128)(2,1)S(1)} %all-to-all-done.x_ref, bf16[512,512]{1,0:T(8,128)(2,1)S(1)} %get-tuple-element.110.dm_ref, f32[2,512]{1,0:T(2,128)S(1)} %copy-done.3, bf16[512,1536]{1,0:T(8,128)(2,1)} %get-tuple-element.111.dqkv_hbm, bf16[2,4,512,512]{3,2,1,0:T(8,128)(2,1)} %w_hbm.9), custom_call_target="tpu_custom_call" | custom-call | flops 1048576 | bytes 1024 | tf_op jit(solution)/shard_map/pallas_call | solution.py:376
  112.8 1.7 %collective-permute-done.11 = bf16[128,512]{1,0:T(8,128)(2,1)S(1)} collective-permute-done((bf16[128,512]{1,0:T(8,128)(2,1)S(1)}, bf16[128,512]{1,0:T(8,128)(2,1)S(1)}, u32[]{:S(2)}, u32[]{:S(2)}) %collective-permute-start.11) | collective-permute-done | bytes 131104 | tf_op jit(solution)/shard_map/ppermute | solution.py:388
  119.6 1.8 %collective-permute-start.19 = (bf16[5,16,512]{2,1,0:T(8,128)(2,1)}, bf16[5,16,512]{2,1,0:T(8,128)(2,1)}, u32[]{:S(2)}, u32[]{:S(2)}) collective-permute-start(bf16[5,16,512]{2,1,0:T(8,128)(2,1)} %get-tuple-element.151), channel_id=1, source_target_pairs={{0,16},{8,24},{16,0},{24,8},{1,17},{9,25},{17,1},{25,9},{2,18},{10... | collective-permute-start | bytes 245768 | tf_op jit(solution)/shard_map/ppermute | solution.py:388
  121.4 3.5 %all-to-all-start.3 = ((bf16[8,2,32,512]{3,2,1,0:T(8,128)(2,1)}), bf16[8,2,32,512]{3,2,1,0:T(8,128)(2,1)S(1)}, u32[]{:S(2)}, u32[]{:S(2)}) async-start(bf16[8,2,32,512]{3,2,1,0:T(8,128)(2,1)} %shard_map.74), calls=%async_computation.3 | async-start | bytes 1048576 | tf_op jit(solution)/shard_map/all_to_all | solution.py:521
  127.8 2.7 %collective-permute-start.20 = (bf16[5,16,512]{2,1,0:T(8,128)(2,1)S(1)}, bf16[5,16,512]{2,1,0:T(8,128)(2,1)S(1)}, u32[]{:S(2)}, u32[]{:S(2)}) collective-permute-start(bf16[5,16,512]{2,1,0:T(8,128)(2,1)S(1)} %copy-done.11), channel_id=1, source_target_pairs={{0,24},{8,16},{16,8},{24,0},{1,25},{9,17},{17,9},{25,1},{2,26},{10... | collective-permute-start | bytes 245768 | tf_op jit(solution)/shard_map/ppermute | solution.py:388
  130.7 1.8 %collective-permute-start.16 = (bf16[3,16,512]{2,1,0:T(8,128)(2,1)S(1)}, bf16[3,16,512]{2,1,0:T(8,128)(2,1)S(1)}, u32[]{:S(2)}, u32[]{:S(2)}) collective-permute-start(bf16[3,16,512]{2,1,0:T(8,128)(2,1)S(1)} %get-tuple-element.154), channel_id=1, source_target_pairs={{0,16},{8,24},{16,0},{24,8},{1,17},{9,25},{17,1},{25,9},{2,18},{10... | collective-permute-start | bytes 147464 | tf_op jit(solution)/shard_map/ppermute | solution.py:388
  132.5 2.6 %collective-permute-start.17 = (bf16[3,16,512]{2,1,0:T(8,128)(2,1)S(1)}, bf16[3,16,512]{2,1,0:T(8,128)(2,1)S(1)}, u32[]{:S(2)}, u32[]{:S(2)}) collective-permute-start(bf16[3,16,512]{2,1,0:T(8,128)(2,1)S(1)} %get-tuple-element.155), channel_id=1, source_target_pairs={{0,24},{8,16},{16,8},{24,0},{1,25},{9,17},{17,9},{25,1},{2,26},{10... | collective-permute-start | bytes 147464 | tf_op jit(solution)/shard_map/ppermute | solution.py:388
  (85 shorter events, 25.3 us)
Async XLA Ops:
  0.6 14.9 %all-to-all-start = ((bf16[8,2,32,512]{3,2,1,0:T(8,128)(2,1)}), bf16[8,2,32,512]{3,2,1,0:T(8,128)(2,1)S(1)}, u32[]{:S(2)}, u32[]{:S(2)}) async-start(bf16[8,2,32,512]{3,2,1,0:T(8,128)(2,1)} %bitcast.86), calls=%async_computation | async-start | bytes 1048576 | tf_op jit(solution)/shard_map/all_to_all | solution.py:453
  6.9 16.8 %collective-permute-start = (bf16[16,8,512]{2,1,0:T(8,128)(2,1)S(1)}, bf16[16,8,512]{2,1,0:T(8,128)(2,1)S(1)}, u32[]{:S(2)}, u32[]{:S(2)}) collective-permute-start(bf16[16,8,512]{2,1,0:T(8,128)(2,1)S(1)} %get-tuple-element.147), channel_id=1, source_target_pairs={{0,8},{8,0},{16,24},{24,16},{1,9},{9,1},{17,25},{25,17},{2,10},{10... | collective-permute-start | bytes 393224 | tf_op jit(solution)/shard_map/ppermute | solution.py:388
  8.6 15.1 %collective-permute-start.1 = (bf16[16,8,512]{2,1,0:T(8,128)(2,1)S(1)}, bf16[16,8,512]{2,1,0:T(8,128)(2,1)S(1)}, u32[]{:S(2)}, u32[]{:S(2)}) collective-permute-start(bf16[16,8,512]{2,1,0:T(8,128)(2,1)S(1)} %get-tuple-element.149), channel_id=1, source_target_pairs={{0,16},{8,24},{16,0},{24,8},{1,17},{9,25},{17,1},{25,9},{2,18},{10... | collective-permute-start | bytes 393224 | tf_op jit(solution)/shard_map/ppermute | solution.py:388
  11.2 12.6 %collective-permute-start.2 = (bf16[16,8,512]{2,1,0:T(8,128)(2,1)S(1)}, bf16[16,8,512]{2,1,0:T(8,128)(2,1)S(1)}, u32[]{:S(2)}, u32[]{:S(2)}) collective-permute-start(bf16[16,8,512]{2,1,0:T(8,128)(2,1)S(1)} %get-tuple-element.146), channel_id=1, source_target_pairs={{0,24},{8,16},{16,8},{24,0},{1,25},{9,17},{17,9},{25,1},{2,26},{10... | collective-permute-start | bytes 393224 | tf_op jit(solution)/shard_map/ppermute | solution.py:388
  24.4 20.0 %all-to-all-start.1 = ((bf16[32,16,512]{2,1,0:T(8,128)(2,1)}), bf16[32,16,512]{2,1,0:T(8,128)(2,1)S(1)}, u32[]{:S(2)}, u32[]{:S(2)}) async-start(bf16[32,16,512]{2,1,0:T(8,128)(2,1)} %bitcast.87), calls=%async_computation.1 | async-start | bytes 1048576 | tf_op jit(solution)/shard_map/all_to_all | solution.py:451
  57.7 18.6 %all-to-all-start.2 = ((bf16[32,16,512]{2,1,0:T(8,128)(2,1)}), bf16[32,16,512]{2,1,0:T(8,128)(2,1)S(1)}, u32[]{:S(2)}, u32[]{:S(2)}) async-start(bf16[32,16,512]{2,1,0:T(8,128)(2,1)} %bitcast.88), calls=%async_computation.2 | async-start | bytes 1048576 | tf_op jit(solution)/shard_map/all_to_all | solution.py:451
  76.4 6.3 %collective-permute-start.3 = (bf16[4,4,64,512]{3,2,1,0:T(8,128)(2,1)}, bf16[4,4,64,512]{3,2,1,0:T(8,128)(2,1)S(1)}, u32[]{:S(2)}, u32[]{:S(2)}) collective-permute-start(bf16[4,4,64,512]{3,2,1,0:T(8,128)(2,1)} %get-tuple-element.95), channel_id=1, source_target_pairs={{0,1},{1,0},{2,3},{3,2},{4,5},{5,4},{6,7},{7,6},{8,9},{9,8},{10,11... | collective-permute-start | bytes 3145736 | tf_op jit(solution)/shard_map/ppermute | solution.py:388
  80.2 5.5 %collective-permute-start.5 = (bf16[128,512]{1,0:T(8,128)(2,1)S(1)}, bf16[128,512]{1,0:T(8,128)(2,1)S(1)}, u32[]{:S(2)}, u32[]{:S(2)}) collective-permute-start(bf16[128,512]{1,0:T(8,128)(2,1)S(1)} %copy-done.14), channel_id=1, source_target_pairs={{0,8},{8,0},{16,24},{24,16},{1,9},{9,1},{17,25},{25,17},{2,10},{10... | collective-permute-start | bytes 393224 | tf_op jit(solution)/shard_map/ppermute | solution.py:388
  94.9 19.7 %collective-permute-start.6 = (bf16[4,3,64,512]{3,2,1,0:T(8,128)(2,1)}, bf16[4,3,64,512]{3,2,1,0:T(8,128)(2,1)S(1)}, u32[]{:S(2)}, u32[]{:S(2)}) collective-permute-start(bf16[4,3,64,512]{3,2,1,0:T(8,128)(2,1)} %get-tuple-element.109), channel_id=1, source_target_pairs={{0,1},{1,0},{2,3},{3,2},{4,5},{5,4},{6,7},{7,6},{8,9},{9,8},{10,11... | collective-permute-start | bytes 2359304 | tf_op jit(solution)/shard_map/ppermute | solution.py:388
  95.2 19.4 %collective-permute-start.7 = (bf16[5,64,512]{2,1,0:T(8,128)(2,1)S(1)}, bf16[5,64,512]{2,1,0:T(8,128)(2,1)S(1)}, u32[]{:S(2)}, u32[]{:S(2)}) collective-permute-start(bf16[5,64,512]{2,1,0:T(8,128)(2,1)S(1)} %get-tuple-element.141), channel_id=1, source_target_pairs={{0,2},{1,3},{2,0},{3,1},{4,6},{5,7},{6,4},{7,5},{8,10},{9,11},{10,... | collective-permute-start | bytes 983048 | tf_op jit(solution)/shard_map/ppermute | solution.py:388
  96.5 18.1 %collective-permute-start.8 = (bf16[5,64,512]{2,1,0:T(8,128)(2,1)S(1)}, bf16[5,64,512]{2,1,0:T(8,128)(2,1)S(1)}, u32[]{:S(2)}, u32[]{:S(2)}) collective-permute-start(bf16[5,64,512]{2,1,0:T(8,128)(2,1)S(1)} %get-tuple-element.140), channel_id=1, source_target_pairs={{0,4},{1,5},{2,6},{3,7},{4,0},{5,1},{6,2},{7,3},{8,12},{9,13},{10,... | collective-permute-start | bytes 983048 | tf_op jit(solution)/shard_map/ppermute | solution.py:388
  97.7 16.9 %collective-permute-start.9 = (bf16[5,64,512]{2,1,0:T(8,128)(2,1)S(1)}, bf16[5,64,512]{2,1,0:T(8,128)(2,1)S(1)}, u32[]{:S(2)}, u32[]{:S(2)}) collective-permute-start(bf16[5,64,512]{2,1,0:T(8,128)(2,1)S(1)} %get-tuple-element.139), channel_id=1, source_target_pairs={{0,6},{1,7},{2,4},{3,5},{4,2},{5,3},{6,0},{7,1},{8,14},{9,15},{10,... | collective-permute-start | bytes 983048 | tf_op jit(solution)/shard_map/ppermute | solution.py:388
  98.8 9.0 %collective-permute-start.10 = (bf16[128,512]{1,0:T(8,128)(2,1)S(1)}, bf16[128,512]{1,0:T(8,128)(2,1)S(1)}, u32[]{:S(2)}, u32[]{:S(2)}) collective-permute-start(bf16[128,512]{1,0:T(8,128)(2,1)S(1)} %copy-done.13), channel_id=1, source_target_pairs={{0,16},{8,24},{16,0},{24,8},{1,17},{9,25},{17,1},{25,9},{2,18},{10... | collective-permute-start | bytes 393224 | tf_op jit(solution)/shard_map/ppermute | solution.py:388
  107.8 6.8 %collective-permute-start.11 = (bf16[128,512]{1,0:T(8,128)(2,1)S(1)}, bf16[128,512]{1,0:T(8,128)(2,1)S(1)}, u32[]{:S(2)}, u32[]{:S(2)}) collective-permute-start(bf16[128,512]{1,0:T(8,128)(2,1)S(1)} %copy-done.12), channel_id=1, source_target_pairs={{0,24},{8,16},{16,8},{24,0},{1,25},{9,17},{17,9},{25,1},{2,26},{10... | collective-permute-start | bytes 393224 | tf_op jit(solution)/shard_map/ppermute | solution.py:388
  115.2 12.6 %collective-permute-start.12 = (bf16[3,64,512]{2,1,0:T(8,128)(2,1)S(1)}, bf16[3,64,512]{2,1,0:T(8,128)(2,1)S(1)}, u32[]{:S(2)}, u32[]{:S(2)}) collective-permute-start(bf16[3,64,512]{2,1,0:T(8,128)(2,1)S(1)} %get-tuple-element.143), channel_id=1, source_target_pairs={{0,2},{1,3},{2,0},{3,1},{4,6},{5,7},{6,4},{7,5},{8,10},{9,11},{10,... | collective-permute-start | bytes 589832 | tf_op jit(solution)/shard_map/ppermute | solution.py:388
  116.4 14.1 %collective-permute-start.13 = (bf16[3,64,512]{2,1,0:T(8,128)(2,1)S(1)}, bf16[3,64,512]{2,1,0:T(8,128)(2,1)S(1)}, u32[]{:S(2)}, u32[]{:S(2)}) collective-permute-start(bf16[3,64,512]{2,1,0:T(8,128)(2,1)S(1)} %get-tuple-element.145), channel_id=1, source_target_pairs={{0,4},{1,5},{2,6},{3,7},{4,0},{5,1},{6,2},{7,3},{8,12},{9,13},{10,... | collective-permute-start | bytes 589832 | tf_op jit(solution)/shard_map/ppermute | solution.py:388
  117.5 13.0 %collective-permute-start.14 = (bf16[3,64,512]{2,1,0:T(8,128)(2,1)S(1)}, bf16[3,64,512]{2,1,0:T(8,128)(2,1)S(1)}, u32[]{:S(2)}, u32[]{:S(2)}) collective-permute-start(bf16[3,64,512]{2,1,0:T(8,128)(2,1)S(1)} %get-tuple-element.144), channel_id=1, source_target_pairs={{0,6},{1,7},{2,4},{3,5},{4,2},{5,3},{6,0},{7,1},{8,14},{9,15},{10,... | collective-permute-start | bytes 589832 | tf_op jit(solution)/shard_map/ppermute | solution.py:388
  119.6 12.9 %collective-permute-start.18 = (bf16[5,16,512]{2,1,0:T(8,128)(2,1)}, bf16[5,16,512]{2,1,0:T(8,128)(2,1)}, u32[]{:S(2)}, u32[]{:S(2)}) collective-permute-start(bf16[5,16,512]{2,1,0:T(8,128)(2,1)} %get-tuple-element.150), channel_id=1, source_target_pairs={{0,8},{8,0},{16,24},{24,16},{1,9},{9,1},{17,25},{25,17},{2,10},{10... | collective-permute-start | bytes 245768 | tf_op jit(solution)/shard_map/ppermute | solution.py:388
  119.6 15.5 %collective-permute-start.19 = (bf16[5,16,512]{2,1,0:T(8,128)(2,1)}, bf16[5,16,512]{2,1,0:T(8,128)(2,1)}, u32[]{:S(2)}, u32[]{:S(2)}) collective-permute-start(bf16[5,16,512]{2,1,0:T(8,128)(2,1)} %get-tuple-element.151), channel_id=1, source_target_pairs={{0,16},{8,24},{16,0},{24,8},{1,17},{9,25},{17,1},{25,9},{2,18},{10... | collective-permute-start | bytes 245768 | tf_op jit(solution)/shard_map/ppermute | solution.py:388
  121.4 17.8 %all-to-all-start.3 = ((bf16[8,2,32,512]{3,2,1,0:T(8,128)(2,1)}), bf16[8,2,32,512]{3,2,1,0:T(8,128)(2,1)S(1)}, u32[]{:S(2)}, u32[]{:S(2)}) async-start(bf16[8,2,32,512]{3,2,1,0:T(8,128)(2,1)} %shard_map.74), calls=%async_computation.3 | async-start | bytes 1048576 | tf_op jit(solution)/shard_map/all_to_all | solution.py:521
  127.8 7.3 %collective-permute-start.20 = (bf16[5,16,512]{2,1,0:T(8,128)(2,1)S(1)}, bf16[5,16,512]{2,1,0:T(8,128)(2,1)S(1)}, u32[]{:S(2)}, u32[]{:S(2)}) collective-permute-start(bf16[5,16,512]{2,1,0:T(8,128)(2,1)S(1)} %copy-done.11), channel_id=1, source_target_pairs={{0,24},{8,16},{16,8},{24,0},{1,25},{9,17},{17,9},{25,1},{2,26},{10... | collective-permute-start | bytes 245768 | tf_op jit(solution)/shard_map/ppermute | solution.py:388
  130.6 5.8 %collective-permute-start.15 = (bf16[3,16,512]{2,1,0:T(8,128)(2,1)S(1)}, bf16[3,16,512]{2,1,0:T(8,128)(2,1)S(1)}, u32[]{:S(2)}, u32[]{:S(2)}) collective-permute-start(bf16[3,16,512]{2,1,0:T(8,128)(2,1)S(1)} %get-tuple-element.153), channel_id=1, source_target_pairs={{0,8},{8,0},{16,24},{24,16},{1,9},{9,1},{17,25},{25,17},{2,10},{10... | collective-permute-start | bytes 147464 | tf_op jit(solution)/shard_map/ppermute | solution.py:388
  130.7 7.1 %collective-permute-start.16 = (bf16[3,16,512]{2,1,0:T(8,128)(2,1)S(1)}, bf16[3,16,512]{2,1,0:T(8,128)(2,1)S(1)}, u32[]{:S(2)}, u32[]{:S(2)}) collective-permute-start(bf16[3,16,512]{2,1,0:T(8,128)(2,1)S(1)} %get-tuple-element.154), channel_id=1, source_target_pairs={{0,16},{8,24},{16,0},{24,8},{1,17},{9,25},{17,1},{25,9},{2,18},{10... | collective-permute-start | bytes 147464 | tf_op jit(solution)/shard_map/ppermute | solution.py:388
  132.5 5.9 %collective-permute-start.17 = (bf16[3,16,512]{2,1,0:T(8,128)(2,1)S(1)}, bf16[3,16,512]{2,1,0:T(8,128)(2,1)S(1)}, u32[]{:S(2)}, u32[]{:S(2)}) collective-permute-start(bf16[3,16,512]{2,1,0:T(8,128)(2,1)S(1)} %get-tuple-element.155), channel_id=1, source_target_pairs={{0,24},{8,16},{16,8},{24,0},{1,25},{9,17},{17,9},{25,1},{2,26},{10... | collective-permute-start | bytes 147464 | tf_op jit(solution)/shard_map/ppermute | solution.py:388
  (16 other events, 99.5 us)

commit v6 on v5

--- a/solution.py
+++ b/solution.py
@@ -163,16 +163,18 @@
     finish(going)
 
 
-def weight_grad(at, left, right, keep_ref, send_ref, keep_hbm, send_hbm, keep_sem, send_sem):
+def weight_grad(part, left, right, keep_ref, send_ref):
     plane, _, size, _ = keep_ref.shape
     whole = dot_tn(left, right).astype(BF16)
     for group in range(plane):
-        send_ref[group, at] = whole[(plane + group) * size : (plane + group + 1) * size]
-        keep_ref[group, at] = whole[group * size : (group + 1) * size]
-    return [
-        start(send_ref.at[:, at], send_hbm.at[:, at], send_sem),
-        start(keep_ref.at[:, at], keep_hbm.at[:, at], keep_sem),
-    ]
+        send_ref[group, part] = whole[(plane + group) * size : (plane + group + 1) * size]
+        keep_ref[group, part] = whole[group * size : (group + 1) * size]
+
+
+def send_grads(keep_ref, send_ref, keep_hbms, send_hbms, sems):
+    plane = keep_ref.shape[0]
+    going = [start(send_ref.at[at], send_hbms[at], sems.at[at]) for at in range(plane)]
+    return going + [start(keep_ref.at[at], keep_hbms[at], sems.at[plane + at]) for at in range(plane)]
 
 
 def third(ref, part):
@@ -231,48 +233,35 @@
     finish(going + send_turned(turn_ref, middle, mid_ref, quarters(mid_hbm), sems))
 
 
-def row_back_first(d_ref, w_hbm, turn_hbm, att_hbm, dm_ref, da_ref, keep_hbm, send_hbm,
-                   w_ref, turn_ref, att_ref, keep_ref, send_ref, sems):
+def row_back(sizes, d_ref, w_hbm, turn_hbm, n_hbm, q_hbm, k_hbm, v_hbm, att_hbm, p_hbm, *refs):
+    rows, length, width, plane = sizes
+    dm_ref, dqkv_hbm, keep_hbms, send_hbms = refs[0], refs[1], refs[2 : 2 + plane], refs[2 + plane : 2 + 2 * plane]
+    w_ref, turn_ref, n_ref, q_ref, k_ref, v_ref, att_ref, p_ref, da_ref, dqkv_ref = refs[2 + 2 * plane : -4]
+    keep_ref, send_ref, sems, out_sems = refs[-4:]
+    half = p_ref.shape[0] // 2
     coming = [
-        start(turn_hbm.at[1], turn_ref.at[0], sems.at[0]),
-        start(att_hbm, att_ref, sems.at[1]),
-        start(turn_hbm.at[6], turn_ref.at[1], sems.at[2]),
-        start(w_hbm.at[0, 3], w_ref, sems.at[3]),
+        start(turn_hbm.at[1], turn_ref.at[0], sems.at[0]), start(w_hbm.at[0, 3], w_ref, sems.at[1]),
+        start(v_hbm, v_ref, sems.at[2]), start(k_hbm, k_ref, sems.at[3]), start(q_hbm, q_ref, sems.at[4]),
+        start(p_hbm.at[pl.ds(0, half)], p_ref.at[pl.ds(0, half)], sems.at[5]),
+        start(p_hbm.at[pl.ds(half, half)], p_ref.at[pl.ds(half, half)], sems.at[6]),
+        start(turn_hbm.at[6], turn_ref.at[1], sems.at[7]), start(att_hbm, att_ref, sems.at[8]),
+        start(n_hbm, n_ref, sems.at[9]),
     ]
     coming[0].wait()
     d_middle = dot(turn_ref[0], d_ref[...]).astype(BF16)
     dm_ref[...] = d_middle
-    finish(coming[1:3])
+    coming[1].wait()
+    da_ref[...] = dot_nt(d_middle, w_ref[...]).astype(BF16)
+    finish(coming[2:7])
+    attention_back(q_ref, k_ref, v_ref, p_ref, da_ref, dqkv_ref, rows, length, width)
+    going = [start(dqkv_ref, dqkv_hbm, sems.at[10])]
+    finish(coming[7:])
+    normed = dot(n_ref[...], turn_ref[1]).astype(BF16)
+    for part in range(3):
+        weight_grad(part, normed, third(dqkv_ref, part), keep_ref, send_ref)
     attended = dot(att_ref[...], turn_ref[1]).astype(BF16)
-    going = weight_grad(
-        0, attended, d_middle, keep_ref, send_ref, keep_hbm, send_hbm, sems.at[4], sems.at[5]
-    )
-    coming[3].wait()
-    da_ref[...] = dot_nt(d_middle, w_ref[...]).astype(BF16)
-    finish(going)
-
-
-def row_back(sizes, da_ref, turn_hbm, n_hbm, q_hbm, k_hbm, v_hbm, p_hbm, dqkv_hbm, keep_hbm, send_hbm,
-             turn_ref, n_ref, q_ref, k_ref, v_ref, p_ref, dqkv_ref, keep_ref, send_ref, sems):
-    rows, length, width = sizes
-    half = p_ref.shape[0] // 2
-    coming = [
-        start(v_hbm, v_ref, sems.at[0]), start(k_hbm, k_ref, sems.at[1]), start(q_hbm, q_ref, sems.at[2]),
-        start(p_hbm.at[pl.ds(0, half)], p_ref.at[pl.ds(0, half)], sems.at[3]),
-        start(p_hbm.at[pl.ds(half, half)], p_ref.at[pl.ds(half, half)], sems.at[4]),
-        start(turn_hbm.at[6], turn_ref, sems.at[5]), start(n_hbm, n_ref, sems.at[6]),
-    ]
-    finish(coming[:5])
-    attention_back(q_ref, k_ref, v_ref, p_ref, da_ref, dqkv_ref, rows, length, width)
-    going = [start(dqkv_ref, dqkv_hbm, sems.at[7])]
-    finish(coming[5:])
-    normed = dot(n_ref[...], turn_ref[...]).astype(BF16)
-    for part in range(3):
-        going += weight_grad(
-            part, normed, third(dqkv_ref, part), keep_ref, send_ref, keep_hbm, send_hbm,
-            sems.at[8 + part], sems.at[11 + part],
-        )
-    finish(going)
+    weight_grad(3, attended, dm_ref[...], keep_ref, send_ref)
+    finish(going + send_grads(keep_ref, send_ref, keep_hbms, send_hbms, out_sems))
 
 
 def field_back(x_ref, dm_ref, g_ref, dqkv_hbm, w_hbm, fg_hbm, dqkv_ref, w_ref, fg_ref, sems):
@@ -337,9 +326,9 @@
     finish(going + send_turned(turn_ref, d_middle.astype(BF16), dm_ref, quarters(dm_hbm), sems.at[pl.ds(7, 4)]))
 
 
-def column_last(parts, cot_hbm, mid_hbm, n_hbm, att_hbm, dqkv_hbm, w_hbm, turn_hbm, *refs):
-    out_hbms, refs = refs[:parts], refs[parts:]
-    keep_hbm, send_hbm, out_ref, keep_ref, send_ref, w_ref, turn_ref, flat_ref, dqkv_ref, sems = refs
+def column_last(plane, cot_hbm, mid_hbm, n_hbm, att_hbm, dqkv_hbm, w_hbm, turn_hbm, out_hbm, *refs):
+    keep_hbms, send_hbms, refs = refs[:plane], refs[plane : 2 * plane], refs[2 * plane :]
+    out_ref, keep_ref, send_ref, w_ref, turn_ref, flat_ref, dqkv_ref, sems, out_sems = refs
     coming = [
         start(turn_hbm.at[6], turn_ref.at[0], sems.at[0]), start(n_hbm, flat_ref.at[0], sems.at[1]),
         start(dqkv_hbm, dqkv_ref, sems.at[2]), start(att_hbm, flat_ref.at[1], sems.at[3]),
@@ -347,20 +336,15 @@
         start(w_hbm.at[1, 3], w_ref, sems.at[6]), start(turn_hbm.at[5], turn_ref.at[1], sems.at[7]),
     ]
     finish(coming[:3])
-    going = []
     normed = dot(flat_ref[0], turn_ref[0]).astype(BF16)
     for part in range(3):
-        going += weight_grad(
-            part, normed, third(dqkv_ref, part), keep_ref, send_ref, keep_hbm, send_hbm,
-            sems.at[8 + part], sems.at[12 + part],
-        )
+        weight_grad(part, normed, third(dqkv_ref, part), keep_ref, send_ref)
     finish(coming[3:])
     attended = dot(flat_ref[1], turn_ref[0]).astype(BF16)
-    going += weight_grad(
-        3, attended, flat_ref[2], keep_ref, send_ref, keep_hbm, send_hbm, sems.at[11], sems.at[15]
-    )
+    weight_grad(3, attended, flat_ref[2], keep_ref, send_ref)
+    going = send_grads(keep_ref, send_ref, keep_hbms, send_hbms, out_sems)
     output = (flat_ref[3].astype(F32) + dot(flat_ref[1], w_ref[...])).astype(BF16)
-    finish(going + send_turned(turn_ref.at[1], output, out_ref, out_hbms, sems.at[pl.ds(16, parts)]))
+    finish(going + send_turned(turn_ref.at[1], output, out_ref, [out_hbm], sems.at[pl.ds(8, 1)]))
 
 
 NEAR, FAR, ANY = pltpu.VMEM, pltpu.HBM, None
@@ -392,8 +376,8 @@
     return (left.astype(F32) + right.astype(F32)).astype(BF16)
 
 
-def plane_pieces(total, plane, core):
-    return [total[0]] + [swap(total[step], "col", plane * core, step * core) for step in range(1, plane)]
+def plane_pieces(sums, plane, core):
+    return [item if step == 0 else swap(item, "col", plane * core, step * core) for step, item in enumerate(sums)]
 
 
 def last_sums(pieces, row_parts):
@@ -422,10 +406,7 @@
 
     flat, triple = (tokens, channels), (tokens, 3 * channels)
     probs = (rows * HEADS, length, length)
-    size = channels // col_parts
-
-    def packed(parts):
-        return (plane, parts, size, channels)
+    packed = (4, channels // col_parts, channels)
 
     def scratch(*shape):
         return pltpu.VMEM(shape, BF16)
@@ -442,7 +423,7 @@
         ((height, cols), (1, 0), {}, 0),
         ((cols, height), (1, 0), {}, 0),
         ((row_parts, high, cols), (2, 0, 1), {0: "row"}, 0),
-        ((cols, row_parts, high), (1, 2, 0), {1: "row"}, 0),
+        ((cols, row_parts, high), (1, 2, 0), {}, 0),
         ((row_parts, plane, core, channels // devices), (2, 1, 0, 3), {0: "row", 1: "plane", 2: "core"}, 1),
     ]
 
@@ -483,48 +464,37 @@
         + [scratch(cols // together * HEADS, count, count), copies((11,))],
     )
     d_mid = all_to_all(d_mid)
-    *outs, keep_b, send_b = call(
-        functools.partial(column_last, row_parts),
-        at(FAR, cot, *kept, weights, turn), at(FAR, *[(high * cols, channels)] * row_parts, packed(4), packed(4)),
-        [square, scratch(*packed(4)), scratch(*packed(4)), square, scratch(2, *flat), scratch(4, *flat),
-         scratch(*triple), copies((16 + row_parts,))],
-    )
-    d_mid, outs, keep_b, send_b = lax.optimization_barrier((d_mid, outs, keep_b, send_b))
-    sum_b = add(keep_b, swap(send_b, "col", col_parts, 1))
-    d_mid, d_att, keep_o, send_o = call(
-        row_back_first,
-        at(ANY, d_mid) + at(FAR, weights, turn, attended), at(ANY, flat, flat) + at(FAR, packed(1), packed(1)),
-        [square, scratch(2, *flat), square, scratch(*packed(1)), scratch(*packed(1)), copies((6,))],
-    )
-    sum_o = add(keep_o, swap(send_o, "col", col_parts, 1))
-    outs[1] = swap(outs[1], "row", row_parts, 1)
-    d_att, sum_b, sum_o, outs = lax.optimization_barrier((d_att, sum_b, sum_o, outs))
-    pieces_b = plane_pieces(jnp.concatenate([sum_o, sum_b], axis=1), plane, core)
-    pieces_out = [piece if step < 2 else swap(piece, "row", row_parts, step) for step, piece in enumerate(outs)]
-
-    dqkv, keep_a, send_a = call(
-        functools.partial(row_back, sizes),
-        at(ANY, d_att) + at(FAR, turn, normed, query, key, value, prob), at(FAR, triple, packed(3), packed(3)),
-        [square] * 5 + [scratch(*probs), scratch(*triple), scratch(*packed(3)), scratch(*packed(3)), copies((14,))],
-    )
+    out, *grads = call(
+        functools.partial(column_last, plane),
+        at(FAR, cot, *kept, weights, turn), at(FAR, flat, *[packed] * (2 * plane)),
+        [square, scratch(plane, *packed), scratch(plane, *packed), square, scratch(2, *flat), scratch(4, *flat),
+         scratch(*triple), copies((9,)), copies((2 * plane,))],
+    )
+    sums_b = [add(keep, swap(send, "col", col_parts, 1)) for keep, send in zip(grads[:plane], grads[plane:])]
+    pieces_b = plane_pieces(sums_b, plane, core)
+    d_mid, sums_b, out = lax.optimization_barrier((d_mid, sums_b, out))
+    out = lax.all_to_all(out.reshape(row_parts, high, cols, channels), "row", 0, 0, tiled=True)
+    d_mid, dqkv, *grads = call(
+        functools.partial(row_back, (rows, length, width, plane)),
+        at(ANY, d_mid) + at(FAR, weights, turn, normed, query, key, value, attended, prob),
+        at(ANY, flat) + at(FAR, triple, *[packed] * (2 * plane)),
+        [square, scratch(2, *flat)] + [square] * 5 + [scratch(*probs), square, scratch(*triple)]
+        + [scratch(plane, *packed), scratch(plane, *packed), copies((11,)), copies((2 * plane,))],
+    )
+    keeps, got = grads[:plane], [swap(send, "col", col_parts, 1) for send in grads[plane:]]
+    dqkv, pieces_b = lax.optimization_barrier((dqkv, pieces_b))
     field_grad, = call(
         field_back, at(ANY, x, d_mid, gains) + at(FAR, dqkv, weights), at(FAR, x.shape),
         [scratch(*triple), scratch(3, *flat), scratch(*x.shape), copies((3,))],
     )
-    got_a = swap(send_a, "col", col_parts, 1)
-    keep_a, got_a, field_grad, pieces_b, pieces_out = lax.optimization_barrier(
-        (keep_a, got_a, field_grad, pieces_b, pieces_out)
-    )
-    sum_a = add(keep_a, got_a)
-    sum_a, field_grad, pieces_b, pieces_out = lax.optimization_barrier((sum_a, field_grad, pieces_b, pieces_out))
-    pieces_a = plane_pieces(sum_a, plane, core)
+    field_grad, keeps, got, pieces_b = lax.optimization_barrier((field_grad, keeps, got, pieces_b))
+    sums_a = [add(keep, other) for keep, other in zip(keeps, got)]
+    field_grad, sums_a, pieces_b = lax.optimization_barrier((field_grad, sums_a, pieces_b))
+    pieces_a = plane_pieces(sums_a, plane, core)
+    grads_b = last_sums(pieces_b, row_parts)
     field_grad = lax.all_to_all(field_grad, "col", 0, 0, tiled=True).reshape(high, wide, channels)
-    grads_b = last_sums(pieces_b, row_parts)
     grads_a = last_sums(pieces_a, row_parts)
-    output = jnp.zeros((high, wide, channels), BF16)
-    for step, piece in enumerate(pieces_out):
-        piece = piece.reshape(high, cols, channels)
-        output = lax.dynamic_update_slice_in_dim(output, piece, (my_row ^ step) * cols, axis=1)
+    output = out.transpose(1, 0, 2, 3).reshape(high, wide, channels)
     return output, field_grad, jnp.concatenate([grads_a, grads_b], axis=0)
 
 

time: 141 us -> 149 us (1.057)
  waiting for transfers between devices: 39 us -> 52.4 us
  local copies, waits for them, and re-layouts: 7.65 us -> 4.39 us
  Pallas kernels: 47.7 us -> 45.8 us
    ppermute x21 -> x23, waiting for transfers between devices: 14.6 us -> 29 us  [swap(): return lax.ppermute(item, axis, [(at, at ^ step) for at in range(count)])]
    ppermute x21 -> x23, starting transfers between devices: 24.6 us -> 21.1 us  [swap(): return lax.ppermute(item, axis, [(at, at ^ step) for at in range(count)])]
    all_to_all x0 -> x1, starting transfers between devices: none -> 3.48 us  [body(): lax.all_to_all(out.reshape(row_parts, high, cols, channels), 'row', 0, 0,...]
    dynamic_update_slice x4 -> x0, local copies, waits for them, and re-layouts: 2.78 us -> none  [body(): lax.dynamic_update_slice_in_dim(output, piece, (my_row ^ step) * cols, ax...]
    pallas_call x8 -> x7, Pallas kernels: 47.7 us -> 45.8 us  [call(): pl.pallas_call(kernel, in_specs=[spec(where) for _, where in ins], out_sp...]
  transfers between devices with their start and end apart: 25 -> 28, of which waited for: 10 -> 7; matrix products, arithmetic and copies ran while one was open for 6% -> 3% of each run, Pallas kernels for 18% -> 18%
where the time goes in v6:
time: 149 us; the launch traced here: 148 us
  waiting for transfers between devices  52.4 us (35%)
  Pallas kernels  45.8 us (31%)
  starting transfers between devices  41 us (28%)
  local copies, waits for them, and re-layouts  4.39 us (3%)
  other arithmetic  3.51 us (2%)
    pallas_call x7, Pallas kernels, call(): pl.pallas_call(kernel, in_specs=[spec(where) for _, where in ins], out_sp...  45.8 us
    ppermute x23, waiting for transfers between devices, swap(): return lax.ppermute(item, axis, [(at, at ^ step) for at in range(count)])  29 us
    all_to_all x2, waiting for transfers between devices, all_to_all(): lax.all_to_all(item, ('row', 'col'), 0, 0, tiled=True)  21.5 us
    ppermute x23, starting transfers between devices, swap(): return lax.ppermute(item, axis, [(at, at ^ step) for at in range(count)])  21.1 us
    all_to_all x2, starting transfers between devices, all_to_all(): lax.all_to_all(item, ('row', 'col'), 0, 0, tiled=True)  7.79 us
    all_to_all x1, starting transfers between devices, body(): lax.all_to_all(field.reshape(col_parts, rows, wide, channels), 'col', 0,...  5.18 us
    all_to_all x1, starting transfers between devices, body(): lax.all_to_all(field_grad, 'col', 0, 0, tiled=True)  3.51 us
    all_to_all x1, starting transfers between devices, body(): lax.all_to_all(out.reshape(row_parts, high, cols, channels), 'row', 0, 0,...  3.48 us
  transfers between devices with their start and end apart: 28, of which 7 were waited for; matrix products, arithmetic and copies ran while one was open for 3% of the time, Pallas kernels for 18%

profile of v6, /device:TPU:0, one launch (start us, length us, event | category | flops | bytes accessed | tf_op | source)
XLA Modules:
  0.0 148.2 jit_solution(12576001434556515610)
XLA Ops:
  0.6 5.2 %all-to-all-start = ((bf16[8,2,32,512]{3,2,1,0:T(8,128)(2,1)}), bf16[8,2,32,512]{3,2,1,0:T(8,128)(2,1)S(1)}, u32[]{:S(2)}, u32[]{:S(2)}) async-start(bf16[8,2,32,512]{3,2,1,0:T(8,128)(2,1)} %bitcast.67), calls=%async_computation | async-start | bytes 1048576 | tf_op jit(solution)/shard_map/all_to_all | solution.py:434
  7.0 3.7 %collective-permute-start.2 = (bf16[16,8,512]{2,1,0:T(8,128)(2,1)S(1)}, bf16[16,8,512]{2,1,0:T(8,128)(2,1)S(1)}, u32[]{:S(2)}, u32[]{:S(2)}) collective-permute-start(bf16[16,8,512]{2,1,0:T(8,128)(2,1)S(1)} %get-tuple-element.139), channel_id=1, source_target_pairs={{0,24},{8,16},{16,8},{24,0},{1,25},{9,17},{17,9},{25,1},{2,26},{10... | collective-permute-start | bytes 393224 | tf_op jit(solution)/shard_map/ppermute | solution.py:372
  11.4 2.2 %shard_map.67.turn_hbm.refs_5_ = bf16[7,512,512]{2,1,0:T(8,128)(2,1)} custom-call(), custom_call_target="tpu_custom_call" | custom-call | flops 1048576 | bytes 1024 | tf_op jit(solution)/shard_map/pallas_call | solution.py:360
  13.7 1.9 %all-to-all-done.x_ref = bf16[8,2,32,512]{3,2,1,0:T(8,128)(2,1)S(1)} async-done(((bf16[8,2,32,512]{3,2,1,0:T(8,128)(2,1)}), bf16[8,2,32,512]{3,2,1,0:T(8,128)(2,1)S(1)}, u32[]{:S(2)}, u32[]{:S(2)}) %all-to-all-start) | async-done | bytes 524320 | tf_op jit(solution)/shard_map/all_to_all | solution.py:434
  15.6 8.1 %shard_map.68 = (bf16[512,512]{1,0:T(8,128)(2,1)}, bf16[512,512]{1,0:T(8,128)(2,1)}, bf16[512,512]{1,0:T(8,128)(2,1)}, bf16[512,512]{1,0:T(8,128)(2,1)}, bf16[51...) custom-call(bf16[8,2,32,512]{3,2,1,0:T(8,128)(2,1)S(1)} %all-to-all-done.x_ref, ...), custom_call_target="tpu_custom_call" | custom-call | flops 1048576 | bytes 1024 | tf_op jit(solution)/shard_map/pallas_call | solution.py:360
  24.4 4.4 %all-to-all-start.1 = ((bf16[32,16,512]{2,1,0:T(8,128)(2,1)}), bf16[32,16,512]{2,1,0:T(8,128)(2,1)S(1)}, u32[]{:S(2)}, u32[]{:S(2)}) async-start(bf16[32,16,512]{2,1,0:T(8,128)(2,1)} %bitcast.68), calls=%async_computation.1 | async-start | bytes 1048576 | tf_op jit(solution)/shard_map/all_to_all | solution.py:432
  29.7 2.0 %shard_map.69 = (bf16[512,512]{1,0:T(8,128)(2,1)S(1)}, bf16[512,512]{1,0:T(8,128)(2,1)S(1)}, bf16[2,512,512]{2,1,0:T(8,128)(2,1)S(1)}) custom-call(bf16[128,512]{1,0:T(8,128)(2,1)S(1)} %get-tuple-element.73.refs_0_, bf16[128,512]{1,0:T(8,128)(2,1)S(1)} %bitcast.60, bf16[128,512]{1,0:T(8,128)(2,1)S(1)} %bitcast.61, bf16[128,512]{1,0:T(8,128)(2,1)S(1)} %bitcast.59, ...), custom_call_target="tpu_custom_call" | custom-call | flops 1048576 | bytes 1024 | tf_op jit(solution)/shard_map/pallas_call | solution.py:360
  31.7 12.6 %all-to-all-done.1 = bf16[32,16,512]{2,1,0:T(8,128)(2,1)S(1)} async-done(((bf16[32,16,512]{2,1,0:T(8,128)(2,1)}), bf16[32,16,512]{2,1,0:T(8,128)(2,1)S(1)}, u32[]{:S(2)}, u32[]{:S(2)}) %all-to-all-start.1) | async-done | bytes 524320 | tf_op jit(solution)/shard_map/all_to_all | solution.py:432
  44.3 13.2 %shard_map.70 = (bf16[512,512]{1,0:T(8,128)(2,1)}, bf16[512,512]{1,0:T(8,128)(2,1)}, bf16[512,512]{1,0:T(8,128)(2,1)}, bf16[512,512]{1,0:T(8,128)(2,1)}, bf16[512,1536]{1,0:T(8,128)(2,1)}) custom-call(bf16[512,512]{1,0:T(8,128)(2,1)S(1)} %bitcast.58, bf16[512,512]{1,0:T(8,128)(2,1)S(1)} %get-tuple-element.77.cot_ref.cot_hbm, ...), custom_call_target="tpu_custom_call" | custom-call | flops 1048576 | bytes 1024 | tf_op jit(solution)/shard_map/pallas_call | solution.py:360
  57.6 5.6 %shard_map.71 = (bf16[512,512]{1,0:T(8,128)(2,1)}, bf16[4,64,512]{2,1,0:T(8,128)(2,1)}, bf16[4,64,512]{2,1,0:T(8,128)(2,1)}, bf16[4,64,512]{2,1,0:T(8,128)(2,1)}...) custom-call(bf16[512,512]{1,0:T(8,128)(2,1)} %copy-done, ...), custom_call_target="tpu_custom_call" | custom-call | flops 1048576 | bytes 1024 | tf_op jit(solution)/shard_map/pallas_call | solution.py:360
  63.3 3.4 %all-to-all-start.2 = ((bf16[32,16,512]{2,1,0:T(8,128)(2,1)}), bf16[32,16,512]{2,1,0:T(8,128)(2,1)S(1)}, u32[]{:S(2)}, u32[]{:S(2)}) async-start(bf16[32,16,512]{2,1,0:T(8,128)(2,1)} %bitcast.7), calls=%async_computation.2 | async-start | bytes 1048576 | tf_op jit(solution)/shard_map/all_to_all | solution.py:432
  68.3 1.7 %collective-permute-start.7 = (bf16[4,64,512]{2,1,0:T(8,128)(2,1)S(1)}, bf16[4,64,512]{2,1,0:T(8,128)(2,1)S(1)}, u32[]{:S(2)}, u32[]{:S(2)}) collective-permute-start(bf16[4,64,512]{2,1,0:T(8,128)(2,1)S(1)} %add_convert_fusion.8), channel_id=1, source_target_pairs={{0,2},{1,3},{2,0},{3,1},{4,6},{5,7},{6,4},{7,5},{8,10},{9,11},{10,... | collective-permute-start | bytes 786440 | tf_op jit(solution)/shard_map/ppermute | solution.py:372
  73.2 8.8 %all-to-all-done.2 = bf16[32,16,512]{2,1,0:T(8,128)(2,1)S(1)} async-done(((bf16[32,16,512]{2,1,0:T(8,128)(2,1)}), bf16[32,16,512]{2,1,0:T(8,128)(2,1)S(1)}, u32[]{:S(2)}, u32[]{:S(2)}) %all-to-all-start.2) | async-done | bytes 524320 | tf_op jit(solution)/shard_map/all_to_all | solution.py:432
  82.0 10.6 %shard_map.72 = (bf16[512,512]{1,0:T(8,128)(2,1)S(1)}, bf16[512,1536]{1,0:T(8,128)(2,1)}, bf16[4,64,512]{2,1,0:T(8,128)(2,1)}, bf16[4,64,512]{2,1,0:T(8,128)(2,1...) custom-call(bf16[512,512]{1,0:T(8,128)(2,1)S(1)} %bitcast.57, ...), custom_call_target="tpu_custom_call" | custom-call | flops 1048576 | bytes 1024 | tf_op jit(solution)/shard_map/pallas_call | solution.py:360
  93.7 4.2 %shard_map.73 = bf16[8,2,32,512]{3,2,1,0:T(8,128)(2,1)} custom-call(bf16[8,2,32,512]{3,2,1,0:T(8,128)(2,1)S(1)} %all-to-all-done.x_ref, bf16[512,512]{1,0:T(8,128)(2,1)S(1)} %get-tuple-element.102.dm_ref, f32[2,512]{1,0:T(2,128)S(1)} %copy-done.3, bf16[512,1536]{1,0:T(8,128)(2,1)} %get-tuple-element.104.dqkv_hbm, bf16[2,4,512,512]{3,2,1,0:T(8,128)(2,1)} %w_hbm.9), custom_call_target="tpu_custom_call" | custom-call | flops 1048576 | bytes 1024 | tf_op jit(solution)/shard_map/pallas_call | solution.py:360
  98.3 3.5 %all-to-all-start.4 = ((bf16[8,2,32,512]{3,2,1,0:T(8,128)(2,1)}), bf16[8,2,32,512]{3,2,1,0:T(8,128)(2,1)S(1)}, u32[]{:S(2)}, u32[]{:S(2)}) async-start(bf16[8,2,32,512]{3,2,1,0:T(8,128)(2,1)} %shard_map.73), calls=%async_computation.4 | async-start | bytes 1048576 | tf_op jit(solution)/shard_map/all_to_all | solution.py:495
  101.8 1.9 %collective-permute-start.14 = (bf16[4,64,512]{2,1,0:T(8,128)(2,1)S(1)}, bf16[4,64,512]{2,1,0:T(8,128)(2,1)S(1)}, u32[]{:S(2)}, u32[]{:S(2)}) collective-permute-start(bf16[4,64,512]{2,1,0:T(8,128)(2,1)S(1)} %get-tuple-element.132), channel_id=1, source_target_pairs={{0,2},{1,3},{2,0},{3,1},{4,6},{5,7},{6,4},{7,5},{8,10},{9,11},{10,... | collective-permute-start | bytes 786440 | tf_op jit(solution)/shard_map/ppermute | solution.py:372
  107.3 9.3 %collective-permute-done.14 = bf16[4,64,512]{2,1,0:T(8,128)(2,1)S(1)} collective-permute-done((bf16[4,64,512]{2,1,0:T(8,128)(2,1)S(1)}, bf16[4,64,512]{2,1,0:T(8,128)(2,1)S(1)}, u32[]{:S(2)}, u32[]{:S(2)}) %collective-permute-start.14) | collective-permute-done | bytes 262176 | tf_op jit(solution)/shard_map/ppermute | solution.py:372
  117.8 4.8 %collective-permute-done.16 = bf16[4,64,512]{2,1,0:T(8,128)(2,1)S(1)} collective-permute-done((bf16[4,64,512]{2,1,0:T(8,128)(2,1)S(1)}, bf16[4,64,512]{2,1,0:T(8,128)(2,1)S(1)}, u32[]{:S(2)}, u32[]{:S(2)}) %collective-permute-start.16) | collective-permute-done | bytes 262176 | tf_op jit(solution)/shard_map/ppermute | solution.py:372
  122.8 3.5 %all-to-all-start.3 = ((bf16[4,16,8,512]{3,2,1,0:T(8,128)(2,1)}), bf16[4,16,8,512]{3,2,1,0:T(8,128)(2,1)S(1)}, u32[]{:S(2)}, u32[]{:S(2)}) async-start(bf16[4,16,8,512]{3,2,1,0:T(8,128)(2,1)} %bitcast.9), calls=%async_computation.3 | async-start | bytes 1048576 | tf_op jit(solution)/shard_map/all_to_all | solution.py:476
  126.3 2.0 %collective-permute-start.17 = (bf16[4,16,512]{2,1,0:T(8,128)(2,1)S(1)}, bf16[4,16,512]{2,1,0:T(8,128)(2,1)S(1)}, u32[]{:S(2)}, u32[]{:S(2)}) collective-permute-start(bf16[4,16,512]{2,1,0:T(8,128)(2,1)S(1)} %get-tuple-element.143), channel_id=1, source_target_pairs={{0,8},{8,0},{16,24},{24,16},{1,9},{9,1},{17,25},{25,17},{2,10},{10... | collective-permute-start | bytes 196616 | tf_op jit(solution)/shard_map/ppermute | solution.py:372
  128.4 2.4 %collective-permute-start.18 = (bf16[4,16,512]{2,1,0:T(8,128)(2,1)S(1)}, bf16[4,16,512]{2,1,0:T(8,128)(2,1)S(1)}, u32[]{:S(2)}, u32[]{:S(2)}) collective-permute-start(bf16[4,16,512]{2,1,0:T(8,128)(2,1)S(1)} %get-tuple-element.144), channel_id=1, source_target_pairs={{0,16},{8,24},{16,0},{24,8},{1,17},{9,25},{17,1},{25,9},{2,18},{10... | collective-permute-start | bytes 196616 | tf_op jit(solution)/shard_map/ppermute | solution.py:372
  130.9 6.6 %collective-permute-done.17 = bf16[4,16,512]{2,1,0:T(8,128)(2,1)S(1)} collective-permute-done((bf16[4,16,512]{2,1,0:T(8,128)(2,1)S(1)}, bf16[4,16,512]{2,1,0:T(8,128)(2,1)S(1)}, u32[]{:S(2)}, u32[]{:S(2)}) %collective-permute-start.17) | collective-permute-done | bytes 65568 | tf_op jit(solution)/shard_map/ppermute | solution.py:372
  137.5 8.3 %collective-permute-done.18 = bf16[4,16,512]{2,1,0:T(8,128)(2,1)S(1)} collective-permute-done((bf16[4,16,512]{2,1,0:T(8,128)(2,1)S(1)}, bf16[4,16,512]{2,1,0:T(8,128)(2,1)S(1)}, u32[]{:S(2)}, u32[]{:S(2)}) %collective-permute-start.18) | collective-permute-done | bytes 65568 | tf_op jit(solution)/shard_map/ppermute | solution.py:372
  (75 shorter events, 17.3 us)
Async XLA Ops:
  0.6 14.9 %all-to-all-start = ((bf16[8,2,32,512]{3,2,1,0:T(8,128)(2,1)}), bf16[8,2,32,512]{3,2,1,0:T(8,128)(2,1)S(1)}, u32[]{:S(2)}, u32[]{:S(2)}) async-start(bf16[8,2,32,512]{3,2,1,0:T(8,128)(2,1)} %bitcast.67), calls=%async_computation | async-start | bytes 1048576 | tf_op jit(solution)/shard_map/all_to_all | solution.py:434
  7.0 16.7 %collective-permute-start.2 = (bf16[16,8,512]{2,1,0:T(8,128)(2,1)S(1)}, bf16[16,8,512]{2,1,0:T(8,128)(2,1)S(1)}, u32[]{:S(2)}, u32[]{:S(2)}) collective-permute-start(bf16[16,8,512]{2,1,0:T(8,128)(2,1)S(1)} %get-tuple-element.139), channel_id=1, source_target_pairs={{0,24},{8,16},{16,8},{24,0},{1,25},{9,17},{17,9},{25,1},{2,26},{10... | collective-permute-start | bytes 393224 | tf_op jit(solution)/shard_map/ppermute | solution.py:372
  10.6 13.1 %collective-permute-start = (bf16[16,8,512]{2,1,0:T(8,128)(2,1)S(1)}, bf16[16,8,512]{2,1,0:T(8,128)(2,1)S(1)}, u32[]{:S(2)}, u32[]{:S(2)}) collective-permute-start(bf16[16,8,512]{2,1,0:T(8,128)(2,1)S(1)} %get-tuple-element.140), channel_id=1, source_target_pairs={{0,8},{8,0},{16,24},{24,16},{1,9},{9,1},{17,25},{25,17},{2,10},{10... | collective-permute-start | bytes 393224 | tf_op jit(solution)/shard_map/ppermute | solution.py:372
  10.6 13.1 %collective-permute-start.1 = (bf16[16,8,512]{2,1,0:T(8,128)(2,1)S(1)}, bf16[16,8,512]{2,1,0:T(8,128)(2,1)S(1)}, u32[]{:S(2)}, u32[]{:S(2)}) collective-permute-start(bf16[16,8,512]{2,1,0:T(8,128)(2,1)S(1)} %get-tuple-element.142), channel_id=1, source_target_pairs={{0,16},{8,24},{16,0},{24,8},{1,17},{9,25},{17,1},{25,9},{2,18},{10... | collective-permute-start | bytes 393224 | tf_op jit(solution)/shard_map/ppermute | solution.py:372
  24.4 20.0 %all-to-all-start.1 = ((bf16[32,16,512]{2,1,0:T(8,128)(2,1)}), bf16[32,16,512]{2,1,0:T(8,128)(2,1)S(1)}, u32[]{:S(2)}, u32[]{:S(2)}) async-start(bf16[32,16,512]{2,1,0:T(8,128)(2,1)} %bitcast.68), calls=%async_computation.1 | async-start | bytes 1048576 | tf_op jit(solution)/shard_map/all_to_all | solution.py:432
  63.3 18.7 %all-to-all-start.2 = ((bf16[32,16,512]{2,1,0:T(8,128)(2,1)}), bf16[32,16,512]{2,1,0:T(8,128)(2,1)S(1)}, u32[]{:S(2)}, u32[]{:S(2)}) async-start(bf16[32,16,512]{2,1,0:T(8,128)(2,1)} %bitcast.7), calls=%async_computation.2 | async-start | bytes 1048576 | tf_op jit(solution)/shard_map/all_to_all | solution.py:432
  66.8 6.3 %collective-permute-start.3 = (bf16[4,64,512]{2,1,0:T(8,128)(2,1)}, bf16[4,64,512]{2,1,0:T(8,128)(2,1)S(1)}, u32[]{:S(2)}, u32[]{:S(2)}) collective-permute-start(bf16[4,64,512]{2,1,0:T(8,128)(2,1)} %get-tuple-element.86), channel_id=1, source_target_pairs={{0,1},{1,0},{2,3},{3,2},{4,5},{5,4},{6,7},{7,6},{8,9},{9,8},{10,11... | collective-permute-start | bytes 786440 | tf_op jit(solution)/shard_map/ppermute | solution.py:372
  67.2 5.4 %collective-permute-start.6 = (bf16[4,64,512]{2,1,0:T(8,128)(2,1)}, bf16[4,64,512]{2,1,0:T(8,128)(2,1)S(1)}, u32[]{:S(2)}, u32[]{:S(2)}) collective-permute-start(bf16[4,64,512]{2,1,0:T(8,128)(2,1)} %get-tuple-element.92), channel_id=1, source_target_pairs={{0,1},{1,0},{2,3},{3,2},{4,5},{5,4},{6,7},{7,6},{8,9},{9,8},{10,11... | collective-permute-start | bytes 786440 | tf_op jit(solution)/shard_map/ppermute | solution.py:372
  68.3 24.8 %collective-permute-start.7 = (bf16[4,64,512]{2,1,0:T(8,128)(2,1)S(1)}, bf16[4,64,512]{2,1,0:T(8,128)(2,1)S(1)}, u32[]{:S(2)}, u32[]{:S(2)}) collective-permute-start(bf16[4,64,512]{2,1,0:T(8,128)(2,1)S(1)} %add_convert_fusion.8), channel_id=1, source_target_pairs={{0,2},{1,3},{2,0},{3,1},{4,6},{5,7},{6,4},{7,5},{8,10},{9,11},{10,... | collective-permute-start | bytes 786440 | tf_op jit(solution)/shard_map/ppermute | solution.py:372
  71.1 22.2 %collective-permute-start.8 = (bf16[4,64,512]{2,1,0:T(8,128)(2,1)S(1)}, bf16[4,64,512]{2,1,0:T(8,128)(2,1)S(1)}, u32[]{:S(2)}, u32[]{:S(2)}) collective-permute-start(bf16[4,64,512]{2,1,0:T(8,128)(2,1)S(1)} %add_convert_fusion.7), channel_id=1, source_target_pairs={{0,4},{1,5},{2,6},{3,7},{4,0},{5,1},{6,2},{7,3},{8,12},{9,13},{10,... | collective-permute-start | bytes 786440 | tf_op jit(solution)/shard_map/ppermute | solution.py:372
  72.7 21.0 %collective-permute-start.9 = (bf16[4,64,512]{2,1,0:T(8,128)(2,1)S(1)}, bf16[4,64,512]{2,1,0:T(8,128)(2,1)S(1)}, u32[]{:S(2)}, u32[]{:S(2)}) collective-permute-start(bf16[4,64,512]{2,1,0:T(8,128)(2,1)S(1)} %add_convert_fusion.6), channel_id=1, source_target_pairs={{0,6},{1,7},{2,4},{3,5},{4,2},{5,3},{6,0},{7,1},{8,14},{9,15},{10,... | collective-permute-start | bytes 786440 | tf_op jit(solution)/shard_map/ppermute | solution.py:372
  92.6 5.3 %collective-permute-start.10 = (bf16[4,64,512]{2,1,0:T(8,128)(2,1)}, bf16[4,64,512]{2,1,0:T(8,128)(2,1)S(1)}, u32[]{:S(2)}, u32[]{:S(2)}) collective-permute-start(bf16[4,64,512]{2,1,0:T(8,128)(2,1)} %get-tuple-element.109), channel_id=1, source_target_pairs={{0,1},{1,0},{2,3},{3,2},{4,5},{5,4},{6,7},{7,6},{8,9},{9,8},{10,11... | collective-permute-start | bytes 786440 | tf_op jit(solution)/shard_map/ppermute | solution.py:372
  92.7 5.2 %collective-permute-start.11 = (bf16[4,64,512]{2,1,0:T(8,128)(2,1)}, bf16[4,64,512]{2,1,0:T(8,128)(2,1)S(1)}, u32[]{:S(2)}, u32[]{:S(2)}) collective-permute-start(bf16[4,64,512]{2,1,0:T(8,128)(2,1)} %get-tuple-element.110), channel_id=1, source_target_pairs={{0,1},{1,0},{2,3},{3,2},{4,5},{5,4},{6,7},{7,6},{8,9},{9,8},{10,11... | collective-permute-start | bytes 786440 | tf_op jit(solution)/shard_map/ppermute | solution.py:372
  98.3 24.6 %all-to-all-start.4 = ((bf16[8,2,32,512]{3,2,1,0:T(8,128)(2,1)}), bf16[8,2,32,512]{3,2,1,0:T(8,128)(2,1)S(1)}, u32[]{:S(2)}, u32[]{:S(2)}) async-start(bf16[8,2,32,512]{3,2,1,0:T(8,128)(2,1)} %shard_map.73), calls=%async_computation.4 | async-start | bytes 1048576 | tf_op jit(solution)/shard_map/all_to_all | solution.py:495
  101.8 14.8 %collective-permute-start.14 = (bf16[4,64,512]{2,1,0:T(8,128)(2,1)S(1)}, bf16[4,64,512]{2,1,0:T(8,128)(2,1)S(1)}, u32[]{:S(2)}, u32[]{:S(2)}) collective-permute-start(bf16[4,64,512]{2,1,0:T(8,128)(2,1)S(1)} %get-tuple-element.132), channel_id=1, source_target_pairs={{0,2},{1,3},{2,0},{3,1},{4,6},{5,7},{6,4},{7,5},{8,10},{9,11},{10,... | collective-permute-start | bytes 786440 | tf_op jit(solution)/shard_map/ppermute | solution.py:372
  103.7 14.1 %collective-permute-start.15 = (bf16[4,64,512]{2,1,0:T(8,128)(2,1)S(1)}, bf16[4,64,512]{2,1,0:T(8,128)(2,1)S(1)}, u32[]{:S(2)}, u32[]{:S(2)}) collective-permute-start(bf16[4,64,512]{2,1,0:T(8,128)(2,1)S(1)} %get-tuple-element.133), channel_id=1, source_target_pairs={{0,4},{1,5},{2,6},{3,7},{4,0},{5,1},{6,2},{7,3},{8,12},{9,13},{10,... | collective-permute-start | bytes 786440 | tf_op jit(solution)/shard_map/ppermute | solution.py:372
  105.2 17.5 %collective-permute-start.16 = (bf16[4,64,512]{2,1,0:T(8,128)(2,1)S(1)}, bf16[4,64,512]{2,1,0:T(8,128)(2,1)S(1)}, u32[]{:S(2)}, u32[]{:S(2)}) collective-permute-start(bf16[4,64,512]{2,1,0:T(8,128)(2,1)S(1)} %get-tuple-element.134), channel_id=1, source_target_pairs={{0,6},{1,7},{2,4},{3,5},{4,2},{5,3},{6,0},{7,1},{8,14},{9,15},{10,... | collective-permute-start | bytes 786440 | tf_op jit(solution)/shard_map/ppermute | solution.py:372
  105.5 25.3 %collective-permute-start.20 = (bf16[4,16,512]{2,1,0:T(8,128)(2,1)S(1)}, bf16[4,16,512]{2,1,0:T(8,128)(2,1)S(1)}, u32[]{:S(2)}, u32[]{:S(2)}) collective-permute-start(bf16[4,16,512]{2,1,0:T(8,128)(2,1)S(1)} %get-tuple-element.146), channel_id=1, source_target_pairs={{0,8},{8,0},{16,24},{24,16},{1,9},{9,1},{17,25},{25,17},{2,10},{10... | collective-permute-start | bytes 196616 | tf_op jit(solution)/shard_map/ppermute | solution.py:372
  106.8 24.0 %collective-permute-start.21 = (bf16[4,16,512]{2,1,0:T(8,128)(2,1)S(1)}, bf16[4,16,512]{2,1,0:T(8,128)(2,1)S(1)}, u32[]{:S(2)}, u32[]{:S(2)}) collective-permute-start(bf16[4,16,512]{2,1,0:T(8,128)(2,1)S(1)} %get-tuple-element.147), channel_id=1, source_target_pairs={{0,16},{8,24},{16,0},{24,8},{1,17},{9,25},{17,1},{25,9},{2,18},{10... | collective-permute-start | bytes 196616 | tf_op jit(solution)/shard_map/ppermute | solution.py:372
  116.6 14.2 %collective-permute-start.22 = (bf16[4,16,512]{2,1,0:T(8,128)(2,1)S(1)}, bf16[4,16,512]{2,1,0:T(8,128)(2,1)S(1)}, u32[]{:S(2)}, u32[]{:S(2)}) collective-permute-start(bf16[4,16,512]{2,1,0:T(8,128)(2,1)S(1)} %get-tuple-element.148), channel_id=1, source_target_pairs={{0,24},{8,16},{16,8},{24,0},{1,25},{9,17},{17,9},{25,1},{2,26},{10... | collective-permute-start | bytes 196616 | tf_op jit(solution)/shard_map/ppermute | solution.py:372
  122.8 23.7 %all-to-all-start.3 = ((bf16[4,16,8,512]{3,2,1,0:T(8,128)(2,1)}), bf16[4,16,8,512]{3,2,1,0:T(8,128)(2,1)S(1)}, u32[]{:S(2)}, u32[]{:S(2)}) async-start(bf16[4,16,8,512]{3,2,1,0:T(8,128)(2,1)} %bitcast.9), calls=%async_computation.3 | async-start | bytes 1048576 | tf_op jit(solution)/shard_map/all_to_all | solution.py:476
  126.3 11.1 %collective-permute-start.17 = (bf16[4,16,512]{2,1,0:T(8,128)(2,1)S(1)}, bf16[4,16,512]{2,1,0:T(8,128)(2,1)S(1)}, u32[]{:S(2)}, u32[]{:S(2)}) collective-permute-start(bf16[4,16,512]{2,1,0:T(8,128)(2,1)S(1)} %get-tuple-element.143), channel_id=1, source_target_pairs={{0,8},{8,0},{16,24},{24,16},{1,9},{9,1},{17,25},{25,17},{2,10},{10... | collective-permute-start | bytes 196616 | tf_op jit(solution)/shard_map/ppermute | solution.py:372
  128.4 17.4 %collective-permute-start.18 = (bf16[4,16,512]{2,1,0:T(8,128)(2,1)S(1)}, bf16[4,16,512]{2,1,0:T(8,128)(2,1)S(1)}, u32[]{:S(2)}, u32[]{:S(2)}) collective-permute-start(bf16[4,16,512]{2,1,0:T(8,128)(2,1)S(1)} %get-tuple-element.144), channel_id=1, source_target_pairs={{0,16},{8,24},{16,0},{24,8},{1,17},{9,25},{17,1},{25,9},{2,18},{10... | collective-permute-start | bytes 196616 | tf_op jit(solution)/shard_map/ppermute | solution.py:372
  130.8 15.0 %collective-permute-start.19 = (bf16[4,16,512]{2,1,0:T(8,128)(2,1)S(1)}, bf16[4,16,512]{2,1,0:T(8,128)(2,1)S(1)}, u32[]{:S(2)}, u32[]{:S(2)}) collective-permute-start(bf16[4,16,512]{2,1,0:T(8,128)(2,1)S(1)} %get-tuple-element.145), channel_id=1, source_target_pairs={{0,24},{8,16},{16,8},{24,0},{1,25},{9,17},{17,9},{25,1},{2,26},{10... | collective-permute-start | bytes 196616 | tf_op jit(solution)/shard_map/ppermute | solution.py:372
  (14 other events, 89.6 us)

commit v7 on v6

--- a/solution.py
+++ b/solution.py
@@ -347,6 +347,12 @@
     finish(going + send_turned(turn_ref.at[1], output, out_ref, [out_hbm], sems.at[pl.ds(8, 1)]))
 
 
+def add_pairs(*refs):
+    count = len(refs) // 3
+    for left, right, target in zip(refs[:count], refs[count : 2 * count], refs[2 * count :]):
+        target[...] = (left[...].astype(F32) + right[...].astype(F32)).astype(BF16)
+
+
 NEAR, FAR, ANY = pltpu.VMEM, pltpu.HBM, None
 
 
@@ -372,8 +378,9 @@
     return lax.ppermute(item, axis, [(at, at ^ step) for at in range(count)])
 
 
-def add(left, right):
-    return (left.astype(F32) + right.astype(F32)).astype(BF16)
+def chip_sums(keeps, sends, col_parts):
+    got = [swap(send, "col", col_parts, 1) for send in sends]
+    return call(add_pairs, [(item, ANY) for item in keeps + got], [(item.shape, ANY) for item in keeps], [])
 
 
 def plane_pieces(sums, plane, core):
@@ -470,10 +477,8 @@
         [square, scratch(plane, *packed), scratch(plane, *packed), square, scratch(2, *flat), scratch(4, *flat),
          scratch(*triple), copies((9,)), copies((2 * plane,))],
     )
-    sums_b = [add(keep, swap(send, "col", col_parts, 1)) for keep, send in zip(grads[:plane], grads[plane:])]
-    pieces_b = plane_pieces(sums_b, plane, core)
-    d_mid, sums_b, out = lax.optimization_barrier((d_mid, sums_b, out))
-    out = lax.all_to_all(out.reshape(row_parts, high, cols, channels), "row", 0, 0, tiled=True)
+    pieces_b = plane_pieces(chip_sums(grads[:plane], grads[plane:], col_parts), plane, core)
+    d_mid, out = lax.optimization_barrier((d_mid, out))
     d_mid, dqkv, *grads = call(
         functools.partial(row_back, (rows, length, width, plane)),
         at(ANY, d_mid) + at(FAR, weights, turn, normed, query, key, value, attended, prob),
@@ -481,17 +486,16 @@
         [square, scratch(2, *flat)] + [square] * 5 + [scratch(*probs), square, scratch(*triple)]
         + [scratch(plane, *packed), scratch(plane, *packed), copies((11,)), copies((2 * plane,))],
     )
-    keeps, got = grads[:plane], [swap(send, "col", col_parts, 1) for send in grads[plane:]]
-    dqkv, pieces_b = lax.optimization_barrier((dqkv, pieces_b))
+    out, d_mid = lax.optimization_barrier((out, d_mid))
+    out = lax.all_to_all(out.reshape(row_parts, high, cols, channels), "row", 0, 0, tiled=True)
+    pieces_a = plane_pieces(chip_sums(grads[:plane], grads[plane:], col_parts), plane, core)
+    dqkv, pieces_b, out = lax.optimization_barrier((dqkv, pieces_b, out))
+    grads_b = last_sums(pieces_b, row_parts)
     field_grad, = call(
         field_back, at(ANY, x, d_mid, gains) + at(FAR, dqkv, weights), at(FAR, x.shape),
         [scratch(*triple), scratch(3, *flat), scratch(*x.shape), copies((3,))],
     )
-    field_grad, keeps, got, pieces_b = lax.optimization_barrier((field_grad, keeps, got, pieces_b))
-    sums_a = [add(keep, other) for keep, other in zip(keeps, got)]
-    field_grad, sums_a, pieces_b = lax.optimization_barrier((field_grad, sums_a, pieces_b))
-    pieces_a = plane_pieces(sums_a, plane, core)
-    grads_b = last_sums(pieces_b, row_parts)
+    field_grad, pieces_a = lax.optimization_barrier((field_grad, pieces_a))
     field_grad = lax.all_to_all(field_grad, "col", 0, 0, tiled=True).reshape(high, wide, channels)
     grads_a = last_sums(pieces_a, row_parts)
     output = out.transpose(1, 0, 2, 3).reshape(high, wide, channels)

time: 149 us -> 145 us (0.973)
  waiting for transfers between devices: 52.4 us -> 42.6 us
  local copies, waits for them, and re-layouts: 4.39 us -> 7.16 us
  starting transfers between devices: 41 us -> 43.5 us
  Pallas kernels: 45.8 us -> 47.5 us
    ppermute x23, waiting for transfers between devices: 29 us -> 18.4 us  [swap(): return lax.ppermute(item, axis, [(at, at ^ step) for at in range(count)])]
    convert_element_type x6 -> x0, other arithmetic: 2.45 us -> none  [add(): return (left.astype(F32) + right.astype(F32)).astype(BF16)]
    convert_element_type x2, other arithmetic: 0.27 us -> 2.23 us  [last_sums(): held = sum((piece.astype(F32) for piece in pieces)).astype(BF16)]
    ppermute x23, starting transfers between devices: 21.1 us -> 22.8 us  [swap(): return lax.ppermute(item, axis, [(at, at ^ step) for at in range(count)])]
    unnamed x21 -> x35, local copies, waits for them, and re-layouts: 2.38 us -> 4.05 us
    pallas_call x7 -> x9, Pallas kernels: 45.8 us -> 47.5 us  [call(): pl.pallas_call(kernel, in_specs=[spec(where) for _, where in ins], out_sp...]
  transfers between devices with their start and end apart: 28 -> 28, of which waited for: 7 -> 13; matrix products, arithmetic and copies ran while one was open for 3% -> 4% of each run, Pallas kernels for 18% -> 24%
where the time goes in v7:
time: 145 us
  Pallas kernels  47.5 us (33%)
  starting transfers between devices  43.5 us (30%)
  waiting for transfers between devices  42.6 us (29%)
  local copies, waits for them, and re-layouts  7.16 us (5%)
  other arithmetic  3.02 us (2%)
    pallas_call x9, Pallas kernels, call(): pl.pallas_call(kernel, in_specs=[spec(where) for _, where in ins], out_sp...  47.5 us
    ppermute x23, starting transfers between devices, swap(): return lax.ppermute(item, axis, [(at, at ^ step) for at in range(count)])  22.8 us
    all_to_all x2, waiting for transfers between devices, all_to_all(): lax.all_to_all(item, ('row', 'col'), 0, 0, tiled=True)  22.2 us
    ppermute x23, waiting for transfers between devices, swap(): return lax.ppermute(item, axis, [(at, at ^ step) for at in range(count)])  18.4 us
    all_to_all x2, starting transfers between devices, all_to_all(): lax.all_to_all(item, ('row', 'col'), 0, 0, tiled=True)  7.68 us
    all_to_all x1, starting transfers between devices, body(): lax.all_to_all(field.reshape(col_parts, rows, wide, channels), 'col', 0,...  5.18 us
    all_to_all x1, starting transfers between devices, body(): lax.all_to_all(out.reshape(row_parts, high, cols, channels), 'row', 0, 0,...  4.29 us
    unnamed x35, local copies, waits for them, and re-layouts  4.05 us
  transfers between devices with their start and end apart: 28, of which 13 were waited for; matrix products, arithmetic and copies ran while one was open for 4% of the time, Pallas kernels for 24%

profile of v7, /device:TPU:0, one launch (start us, length us, event | category | flops | bytes accessed | tf_op | source)
XLA Modules:
  0.0 144.7 jit_solution(7565898106421166047)
XLA Ops:
  0.6 5.2 %all-to-all-start = ((bf16[8,2,32,512]{3,2,1,0:T(8,128)(2,1)}), bf16[8,2,32,512]{3,2,1,0:T(8,128)(2,1)S(1)}, u32[]{:S(2)}, u32[]{:S(2)}) async-start(bf16[8,2,32,512]{3,2,1,0:T(8,128)(2,1)} %bitcast.67), calls=%async_computation | async-start | bytes 1048576 | tf_op jit(solution)/shard_map/all_to_all | solution.py:441
  7.0 3.7 %collective-permute-start.2 = (bf16[16,8,512]{2,1,0:T(8,128)(2,1)S(1)}, bf16[16,8,512]{2,1,0:T(8,128)(2,1)S(1)}, u32[]{:S(2)}, u32[]{:S(2)}) collective-permute-start(bf16[16,8,512]{2,1,0:T(8,128)(2,1)S(1)} %get-tuple-element.127), channel_id=1, source_target_pairs={{0,24},{8,16},{16,8},{24,0},{1,25},{9,17},{17,9},{25,1},{2,26},{10... | collective-permute-start | bytes 393224 | tf_op jit(solution)/shard_map/ppermute | solution.py:378
  11.4 2.2 %shard_map.67.turn_hbm.refs_5_ = bf16[7,512,512]{2,1,0:T(8,128)(2,1)} custom-call(), custom_call_target="tpu_custom_call" | custom-call | flops 1048576 | bytes 1024 | tf_op jit(solution)/shard_map/pallas_call | solution.py:366
  13.6 1.9 %all-to-all-done.x_ref = bf16[8,2,32,512]{3,2,1,0:T(8,128)(2,1)S(1)} async-done(((bf16[8,2,32,512]{3,2,1,0:T(8,128)(2,1)}), bf16[8,2,32,512]{3,2,1,0:T(8,128)(2,1)S(1)}, u32[]{:S(2)}, u32[]{:S(2)}) %all-to-all-start) | async-done | bytes 524320 | tf_op jit(solution)/shard_map/all_to_all | solution.py:441
  15.6 8.2 %shard_map.68 = (bf16[512,512]{1,0:T(8,128)(2,1)}, bf16[512,512]{1,0:T(8,128)(2,1)}, bf16[512,512]{1,0:T(8,128)(2,1)}, bf16[512,512]{1,0:T(8,128)(2,1)}, bf16[51...) custom-call(bf16[8,2,32,512]{3,2,1,0:T(8,128)(2,1)S(1)} %all-to-all-done.x_ref, ...), custom_call_target="tpu_custom_call" | custom-call | flops 1048576 | bytes 1024 | tf_op jit(solution)/shard_map/pallas_call | solution.py:366
  24.4 4.4 %all-to-all-start.1 = ((bf16[32,16,512]{2,1,0:T(8,128)(2,1)}), bf16[32,16,512]{2,1,0:T(8,128)(2,1)S(1)}, u32[]{:S(2)}, u32[]{:S(2)}) async-start(bf16[32,16,512]{2,1,0:T(8,128)(2,1)} %bitcast.69), calls=%async_computation.1 | async-start | bytes 1048576 | tf_op jit(solution)/shard_map/all_to_all | solution.py:439
  29.7 2.0 %shard_map.69 = (bf16[512,512]{1,0:T(8,128)(2,1)S(1)}, bf16[512,512]{1,0:T(8,128)(2,1)S(1)}, bf16[2,512,512]{2,1,0:T(8,128)(2,1)S(1)}) custom-call(bf16[128,512]{1,0:T(8,128)(2,1)S(1)} %get-tuple-element.67.refs_0_, bf16[128,512]{1,0:T(8,128)(2,1)S(1)} %bitcast.60, bf16[128,512]{1,0:T(8,128)(2,1)S(1)} %bitcast.61, bf16[128,512]{1,0:T(8,128)(2,1)S(1)} %bitcast.59, ...), custom_call_target="tpu_custom_call" | custom-call | flops 1048576 | bytes 1024 | tf_op jit(solution)/shard_map/pallas_call | solution.py:366
  31.7 12.6 %all-to-all-done.1 = bf16[32,16,512]{2,1,0:T(8,128)(2,1)S(1)} async-done(((bf16[32,16,512]{2,1,0:T(8,128)(2,1)}), bf16[32,16,512]{2,1,0:T(8,128)(2,1)S(1)}, u32[]{:S(2)}, u32[]{:S(2)}) %all-to-all-start.1) | async-done | bytes 524320 | tf_op jit(solution)/shard_map/all_to_all | solution.py:439
  44.4 13.3 %shard_map.70 = (bf16[512,512]{1,0:T(8,128)(2,1)}, bf16[512,512]{1,0:T(8,128)(2,1)}, bf16[512,512]{1,0:T(8,128)(2,1)}, bf16[512,512]{1,0:T(8,128)(2,1)}, bf16[512,1536]{1,0:T(8,128)(2,1)}) custom-call(bf16[512,512]{1,0:T(8,128)(2,1)S(1)} %bitcast.58, bf16[512,512]{1,0:T(8,128)(2,1)S(1)} %get-tuple-element.71.cot_ref.cot_hbm, ...), custom_call_target="tpu_custom_call" | custom-call | flops 1048576 | bytes 1024 | tf_op jit(solution)/shard_map/pallas_call | solution.py:366
  57.7 3.3 %all-to-all-start.2 = ((bf16[32,16,512]{2,1,0:T(8,128)(2,1)}), bf16[32,16,512]{2,1,0:T(8,128)(2,1)S(1)}, u32[]{:S(2)}, u32[]{:S(2)}) async-start(bf16[32,16,512]{2,1,0:T(8,128)(2,1)} %bitcast.70), calls=%async_computation.2 | async-start | bytes 1048576 | tf_op jit(solution)/shard_map/all_to_all | solution.py:439
  61.0 5.6 %shard_map.71 = (bf16[512,512]{1,0:T(8,128)(2,1)}, bf16[4,64,512]{2,1,0:T(8,128)(2,1)}, bf16[4,64,512]{2,1,0:T(8,128)(2,1)}, bf16[4,64,512]{2,1,0:T(8,128)(2,1)}...) custom-call(bf16[512,512]{1,0:T(8,128)(2,1)} %copy-done, ...), custom_call_target="tpu_custom_call" | custom-call | flops 1048576 | bytes 1024 | tf_op jit(solution)/shard_map/pallas_call | solution.py:366
  66.8 9.6 %all-to-all-done.2 = bf16[32,16,512]{2,1,0:T(8,128)(2,1)S(1)} async-done(((bf16[32,16,512]{2,1,0:T(8,128)(2,1)}), bf16[32,16,512]{2,1,0:T(8,128)(2,1)S(1)}, u32[]{:S(2)}, u32[]{:S(2)}) %all-to-all-start.2) | async-done | bytes 524320 | tf_op jit(solution)/shard_map/all_to_all | solution.py:439
  76.4 10.7 %shard_map.72 = (bf16[512,512]{1,0:T(8,128)(2,1)S(1)}, bf16[512,1536]{1,0:T(8,128)(2,1)}, bf16[4,64,512]{2,1,0:T(8,128)(2,1)}, bf16[4,64,512]{2,1,0:T(8,128)(2,1...) custom-call(bf16[512,512]{1,0:T(8,128)(2,1)S(1)} %bitcast.57, ...), custom_call_target="tpu_custom_call" | custom-call | flops 1048576 | bytes 1024 | tf_op jit(solution)/shard_map/pallas_call | solution.py:366
  87.1 4.3 %all-to-all-start.3 = ((bf16[4,16,8,512]{3,2,1,0:T(8,128)(2,1)}), bf16[4,16,8,512]{3,2,1,0:T(8,128)(2,1)}, u32[]{:S(2)}, u32[]{:S(2)}) async-start(bf16[4,16,8,512]{3,2,1,0:T(8,128)(2,1)} %bitcast.68), calls=%async_computation.3 | async-start | bytes 1048576 | tf_op jit(solution)/shard_map/all_to_all | solution.py:490
  102.6 2.9 %collective-permute-done.7 = bf16[4,64,512]{2,1,0:T(8,128)(2,1)S(1)} collective-permute-done((bf16[4,64,512]{2,1,0:T(8,128)(2,1)S(1)}, bf16[4,64,512]{2,1,0:T(8,128)(2,1)S(1)}, u32[]{:S(2)}, u32[]{:S(2)}) %collective-permute-start.7) | collective-permute-done | bytes 262176 | tf_op jit(solution)/shard_map/ppermute | solution.py:378
  107.4 4.7 %collective-permute-done.8 = bf16[4,64,512]{2,1,0:T(8,128)(2,1)S(1)} collective-permute-done((bf16[4,64,512]{2,1,0:T(8,128)(2,1)S(1)}, bf16[4,64,512]{2,1,0:T(8,128)(2,1)S(1)}, u32[]{:S(2)}, u32[]{:S(2)}) %collective-permute-start.8) | collective-permute-done | bytes 262176 | tf_op jit(solution)/shard_map/ppermute | solution.py:378
  112.8 4.1 %shard_map.74 = bf16[8,2,32,512]{3,2,1,0:T(8,128)(2,1)} custom-call(bf16[8,2,32,512]{3,2,1,0:T(8,128)(2,1)S(1)} %all-to-all-done.x_ref, bf16[512,512]{1,0:T(8,128)(2,1)S(1)} %get-tuple-element.104.dm_ref, f32[2,512]{1,0:T(2,128)S(1)} %copy-done.11, bf16[512,1536]{1,0:T(8,128)(2,1)} %get-tuple-element.105.dqkv_hbm, bf16[2,4,512,512]{3,2,1,0:T(8,128)(2,1)} %w_hbm.9), custom_call_target="tpu_custom_call" | custom-call | flops 1048576 | bytes 1024 | tf_op jit(solution)/shard_map/pallas_call | solution.py:366
  116.9 1.9 %copy_bitcast_fusion = bf16[16,32,512]{2,1,0:T(8,128)(2,1)} fusion(bf16[4,16,8,512]{3,2,1,0:T(8,128)(2,1)} %all-to-all-done.3), kind=kLoop, calls=%fused_computation | loop fusion | bytes 1048576 | tf_op jit(solution)/shard_map/reshape | solution.py:501
  118.9 3.6 %collective-permute-done.15 = bf16[4,64,512]{2,1,0:T(8,128)(2,1)S(1)} collective-permute-done((bf16[4,64,512]{2,1,0:T(8,128)(2,1)S(1)}, bf16[4,64,512]{2,1,0:T(8,128)(2,1)S(1)}, u32[]{:S(2)}, u32[]{:S(2)}) %collective-permute-start.15) | collective-permute-done | bytes 262176 | tf_op jit(solution)/shard_map/ppermute | solution.py:378
  122.5 3.5 %all-to-all-start.4 = ((bf16[8,2,32,512]{3,2,1,0:T(8,128)(2,1)}), bf16[8,2,32,512]{3,2,1,0:T(8,128)(2,1)S(1)}, u32[]{:S(2)}, u32[]{:S(2)}) async-start(bf16[8,2,32,512]{3,2,1,0:T(8,128)(2,1)} %shard_map.74), calls=%async_computation.4 | async-start | bytes 1048576 | tf_op jit(solution)/shard_map/all_to_all | solution.py:499
  127.1 1.9 %collective-permute-start.17 = (bf16[4,16,512]{2,1,0:T(8,128)(2,1)S(1)}, bf16[4,16,512]{2,1,0:T(8,128)(2,1)S(1)}, u32[]{:S(2)}, u32[]{:S(2)}) collective-permute-start(bf16[4,16,512]{2,1,0:T(8,128)(2,1)S(1)} %get-tuple-element.131), channel_id=1, source_target_pairs={{0,8},{8,0},{16,24},{24,16},{1,9},{9,1},{17,25},{25,17},{2,10},{10... | collective-permute-start | bytes 196616 | tf_op jit(solution)/shard_map/ppermute | solution.py:378
  129.0 2.4 %collective-permute-start.18 = (bf16[4,16,512]{2,1,0:T(8,128)(2,1)S(1)}, bf16[4,16,512]{2,1,0:T(8,128)(2,1)S(1)}, u32[]{:S(2)}, u32[]{:S(2)}) collective-permute-start(bf16[4,16,512]{2,1,0:T(8,128)(2,1)S(1)} %get-tuple-element.132), channel_id=1, source_target_pairs={{0,16},{8,24},{16,0},{24,8},{1,17},{9,25},{17,1},{25,9},{2,18},{10... | collective-permute-start | bytes 196616 | tf_op jit(solution)/shard_map/ppermute | solution.py:378
  133.7 3.3 %collective-permute-start.21 = (bf16[4,16,512]{2,1,0:T(8,128)(2,1)S(1)}, bf16[4,16,512]{2,1,0:T(8,128)(2,1)S(1)}, u32[]{:S(2)}, u32[]{:S(2)}) collective-permute-start(bf16[4,16,512]{2,1,0:T(8,128)(2,1)S(1)} %get-tuple-element.135), channel_id=1, source_target_pairs={{0,16},{8,24},{16,0},{24,8},{1,17},{9,25},{17,1},{25,9},{2,18},{10... | collective-permute-start | bytes 196616 | tf_op jit(solution)/shard_map/ppermute | solution.py:378
  138.6 3.7 %collective-permute-done.21 = bf16[4,16,512]{2,1,0:T(8,128)(2,1)S(1)} collective-permute-done((bf16[4,16,512]{2,1,0:T(8,128)(2,1)S(1)}, bf16[4,16,512]{2,1,0:T(8,128)(2,1)S(1)}, u32[]{:S(2)}, u32[]{:S(2)}) %collective-permute-start.21) | collective-permute-done | bytes 65568 | tf_op jit(solution)/shard_map/ppermute | solution.py:378
  (85 shorter events, 24.9 us)
Async XLA Ops:
  0.6 14.9 %all-to-all-start = ((bf16[8,2,32,512]{3,2,1,0:T(8,128)(2,1)}), bf16[8,2,32,512]{3,2,1,0:T(8,128)(2,1)S(1)}, u32[]{:S(2)}, u32[]{:S(2)}) async-start(bf16[8,2,32,512]{3,2,1,0:T(8,128)(2,1)} %bitcast.67), calls=%async_computation | async-start | bytes 1048576 | tf_op jit(solution)/shard_map/all_to_all | solution.py:441
  7.0 16.8 %collective-permute-start.2 = (bf16[16,8,512]{2,1,0:T(8,128)(2,1)S(1)}, bf16[16,8,512]{2,1,0:T(8,128)(2,1)S(1)}, u32[]{:S(2)}, u32[]{:S(2)}) collective-permute-start(bf16[16,8,512]{2,1,0:T(8,128)(2,1)S(1)} %get-tuple-element.127), channel_id=1, source_target_pairs={{0,24},{8,16},{16,8},{24,0},{1,25},{9,17},{17,9},{25,1},{2,26},{10... | collective-permute-start | bytes 393224 | tf_op jit(solution)/shard_map/ppermute | solution.py:378
  10.6 13.1 %collective-permute-start = (bf16[16,8,512]{2,1,0:T(8,128)(2,1)S(1)}, bf16[16,8,512]{2,1,0:T(8,128)(2,1)S(1)}, u32[]{:S(2)}, u32[]{:S(2)}) collective-permute-start(bf16[16,8,512]{2,1,0:T(8,128)(2,1)S(1)} %get-tuple-element.128), channel_id=1, source_target_pairs={{0,8},{8,0},{16,24},{24,16},{1,9},{9,1},{17,25},{25,17},{2,10},{10... | collective-permute-start | bytes 393224 | tf_op jit(solution)/shard_map/ppermute | solution.py:378
  10.6 13.1 %collective-permute-start.1 = (bf16[16,8,512]{2,1,0:T(8,128)(2,1)S(1)}, bf16[16,8,512]{2,1,0:T(8,128)(2,1)S(1)}, u32[]{:S(2)}, u32[]{:S(2)}) collective-permute-start(bf16[16,8,512]{2,1,0:T(8,128)(2,1)S(1)} %get-tuple-element.130), channel_id=1, source_target_pairs={{0,16},{8,24},{16,0},{24,8},{1,17},{9,25},{17,1},{25,9},{2,18},{10... | collective-permute-start | bytes 393224 | tf_op jit(solution)/shard_map/ppermute | solution.py:378
  24.4 20.0 %all-to-all-start.1 = ((bf16[32,16,512]{2,1,0:T(8,128)(2,1)}), bf16[32,16,512]{2,1,0:T(8,128)(2,1)S(1)}, u32[]{:S(2)}, u32[]{:S(2)}) async-start(bf16[32,16,512]{2,1,0:T(8,128)(2,1)} %bitcast.69), calls=%async_computation.1 | async-start | bytes 1048576 | tf_op jit(solution)/shard_map/all_to_all | solution.py:439
  57.7 18.6 %all-to-all-start.2 = ((bf16[32,16,512]{2,1,0:T(8,128)(2,1)}), bf16[32,16,512]{2,1,0:T(8,128)(2,1)S(1)}, u32[]{:S(2)}, u32[]{:S(2)}) async-start(bf16[32,16,512]{2,1,0:T(8,128)(2,1)} %bitcast.70), calls=%async_computation.2 | async-start | bytes 1048576 | tf_op jit(solution)/shard_map/all_to_all | solution.py:439
  66.6 25.9 %collective-permute-start.3 = (bf16[4,64,512]{2,1,0:T(8,128)(2,1)}, bf16[4,64,512]{2,1,0:T(8,128)(2,1)}, u32[]{:S(2)}, u32[]{:S(2)}) collective-permute-start(bf16[4,64,512]{2,1,0:T(8,128)(2,1)} %get-tuple-element.92), channel_id=1, source_target_pairs={{0,1},{1,0},{2,3},{3,2},{4,5},{5,4},{6,7},{7,6},{8,9},{9,8},{10,11... | collective-permute-start | bytes 786440 | tf_op jit(solution)/shard_map/ppermute | solution.py:378
  87.1 25.7 %all-to-all-start.3 = ((bf16[4,16,8,512]{3,2,1,0:T(8,128)(2,1)}), bf16[4,16,8,512]{3,2,1,0:T(8,128)(2,1)}, u32[]{:S(2)}, u32[]{:S(2)}) async-start(bf16[4,16,8,512]{3,2,1,0:T(8,128)(2,1)} %bitcast.68), calls=%async_computation.3 | async-start | bytes 1048576 | tf_op jit(solution)/shard_map/all_to_all | solution.py:490
  92.5 6.3 %collective-permute-start.11 = (bf16[4,64,512]{2,1,0:T(8,128)(2,1)}, bf16[4,64,512]{2,1,0:T(8,128)(2,1)S(1)}, u32[]{:S(2)}, u32[]{:S(2)}) collective-permute-start(bf16[4,64,512]{2,1,0:T(8,128)(2,1)} %get-tuple-element.111), channel_id=1, source_target_pairs={{0,1},{1,0},{2,3},{3,2},{4,5},{5,4},{6,7},{7,6},{8,9},{9,8},{10,11... | collective-permute-start | bytes 786440 | tf_op jit(solution)/shard_map/ppermute | solution.py:378
  93.2 6.7 %collective-permute-start.12 = (bf16[4,64,512]{2,1,0:T(8,128)(2,1)}, bf16[4,64,512]{2,1,0:T(8,128)(2,1)S(1)}, u32[]{:S(2)}, u32[]{:S(2)}) collective-permute-start(bf16[4,64,512]{2,1,0:T(8,128)(2,1)} %get-tuple-element.112), channel_id=1, source_target_pairs={{0,1},{1,0},{2,3},{3,2},{4,5},{5,4},{6,7},{7,6},{8,9},{9,8},{10,11... | collective-permute-start | bytes 786440 | tf_op jit(solution)/shard_map/ppermute | solution.py:378
  93.6 6.3 %collective-permute-start.13 = (bf16[4,64,512]{2,1,0:T(8,128)(2,1)}, bf16[4,64,512]{2,1,0:T(8,128)(2,1)S(1)}, u32[]{:S(2)}, u32[]{:S(2)}) collective-permute-start(bf16[4,64,512]{2,1,0:T(8,128)(2,1)} %get-tuple-element.113), channel_id=1, source_target_pairs={{0,1},{1,0},{2,3},{3,2},{4,5},{5,4},{6,7},{7,6},{8,9},{9,8},{10,11... | collective-permute-start | bytes 786440 | tf_op jit(solution)/shard_map/ppermute | solution.py:378
  96.3 9.2 %collective-permute-start.7 = (bf16[4,64,512]{2,1,0:T(8,128)(2,1)S(1)}, bf16[4,64,512]{2,1,0:T(8,128)(2,1)S(1)}, u32[]{:S(2)}, u32[]{:S(2)}) collective-permute-start(bf16[4,64,512]{2,1,0:T(8,128)(2,1)S(1)} %get-tuple-element.97), channel_id=1, source_target_pairs={{0,2},{1,3},{2,0},{3,1},{4,6},{5,7},{6,4},{7,5},{8,10},{9,11},{10,... | collective-permute-start | bytes 786440 | tf_op jit(solution)/shard_map/ppermute | solution.py:378
  97.3 14.8 %collective-permute-start.8 = (bf16[4,64,512]{2,1,0:T(8,128)(2,1)S(1)}, bf16[4,64,512]{2,1,0:T(8,128)(2,1)S(1)}, u32[]{:S(2)}, u32[]{:S(2)}) collective-permute-start(bf16[4,64,512]{2,1,0:T(8,128)(2,1)S(1)} %get-tuple-element.98), channel_id=1, source_target_pairs={{0,4},{1,5},{2,6},{3,7},{4,0},{5,1},{6,2},{7,3},{8,12},{9,13},{10,... | collective-permute-start | bytes 786440 | tf_op jit(solution)/shard_map/ppermute | solution.py:378
  98.8 14.0 %collective-permute-start.9 = (bf16[4,64,512]{2,1,0:T(8,128)(2,1)S(1)}, bf16[4,64,512]{2,1,0:T(8,128)(2,1)}, u32[]{:S(2)}, u32[]{:S(2)}) collective-permute-start(bf16[4,64,512]{2,1,0:T(8,128)(2,1)S(1)} %get-tuple-element.99), channel_id=1, source_target_pairs={{0,6},{1,7},{2,4},{3,5},{4,2},{5,3},{6,0},{7,1},{8,14},{9,15},{10,... | collective-permute-start | bytes 786440 | tf_op jit(solution)/shard_map/ppermute | solution.py:378
  100.1 18.7 %collective-permute-start.14 = (bf16[4,64,512]{2,1,0:T(8,128)(2,1)S(1)}, bf16[4,64,512]{2,1,0:T(8,128)(2,1)S(1)}, u32[]{:S(2)}, u32[]{:S(2)}) collective-permute-start(bf16[4,64,512]{2,1,0:T(8,128)(2,1)S(1)} %get-tuple-element.115), channel_id=1, source_target_pairs={{0,2},{1,3},{2,0},{3,1},{4,6},{5,7},{6,4},{7,5},{8,10},{9,11},{10,... | collective-permute-start | bytes 786440 | tf_op jit(solution)/shard_map/ppermute | solution.py:378
  101.2 21.3 %collective-permute-start.15 = (bf16[4,64,512]{2,1,0:T(8,128)(2,1)S(1)}, bf16[4,64,512]{2,1,0:T(8,128)(2,1)S(1)}, u32[]{:S(2)}, u32[]{:S(2)}) collective-permute-start(bf16[4,64,512]{2,1,0:T(8,128)(2,1)S(1)} %get-tuple-element.116), channel_id=1, source_target_pairs={{0,4},{1,5},{2,6},{3,7},{4,0},{5,1},{6,2},{7,3},{8,12},{9,13},{10,... | collective-permute-start | bytes 786440 | tf_op jit(solution)/shard_map/ppermute | solution.py:378
  105.5 17.0 %collective-permute-start.16 = (bf16[4,64,512]{2,1,0:T(8,128)(2,1)S(1)}, bf16[4,64,512]{2,1,0:T(8,128)(2,1)}, u32[]{:S(2)}, u32[]{:S(2)}) collective-permute-start(bf16[4,64,512]{2,1,0:T(8,128)(2,1)S(1)} %get-tuple-element.117), channel_id=1, source_target_pairs={{0,6},{1,7},{2,4},{3,5},{4,2},{5,3},{6,0},{7,1},{8,14},{9,15},{10,... | collective-permute-start | bytes 786440 | tf_op jit(solution)/shard_map/ppermute | solution.py:378
  122.5 21.4 %all-to-all-start.4 = ((bf16[8,2,32,512]{3,2,1,0:T(8,128)(2,1)}), bf16[8,2,32,512]{3,2,1,0:T(8,128)(2,1)S(1)}, u32[]{:S(2)}, u32[]{:S(2)}) async-start(bf16[8,2,32,512]{3,2,1,0:T(8,128)(2,1)} %shard_map.74), calls=%async_computation.4 | async-start | bytes 1048576 | tf_op jit(solution)/shard_map/all_to_all | solution.py:499
  127.1 9.8 %collective-permute-start.17 = (bf16[4,16,512]{2,1,0:T(8,128)(2,1)S(1)}, bf16[4,16,512]{2,1,0:T(8,128)(2,1)S(1)}, u32[]{:S(2)}, u32[]{:S(2)}) collective-permute-start(bf16[4,16,512]{2,1,0:T(8,128)(2,1)S(1)} %get-tuple-element.131), channel_id=1, source_target_pairs={{0,8},{8,0},{16,24},{24,16},{1,9},{9,1},{17,25},{25,17},{2,10},{10... | collective-permute-start | bytes 196616 | tf_op jit(solution)/shard_map/ppermute | solution.py:378
  129.0 8.2 %collective-permute-start.18 = (bf16[4,16,512]{2,1,0:T(8,128)(2,1)S(1)}, bf16[4,16,512]{2,1,0:T(8,128)(2,1)S(1)}, u32[]{:S(2)}, u32[]{:S(2)}) collective-permute-start(bf16[4,16,512]{2,1,0:T(8,128)(2,1)S(1)} %get-tuple-element.132), channel_id=1, source_target_pairs={{0,16},{8,24},{16,0},{24,8},{1,17},{9,25},{17,1},{25,9},{2,18},{10... | collective-permute-start | bytes 196616 | tf_op jit(solution)/shard_map/ppermute | solution.py:378
  131.4 6.7 %collective-permute-start.19 = (bf16[4,16,512]{2,1,0:T(8,128)(2,1)S(1)}, bf16[4,16,512]{2,1,0:T(8,128)(2,1)S(1)}, u32[]{:S(2)}, u32[]{:S(2)}) collective-permute-start(bf16[4,16,512]{2,1,0:T(8,128)(2,1)S(1)} %get-tuple-element.133), channel_id=1, source_target_pairs={{0,24},{8,16},{16,8},{24,0},{1,25},{9,17},{17,9},{25,1},{2,26},{10... | collective-permute-start | bytes 196616 | tf_op jit(solution)/shard_map/ppermute | solution.py:378
  132.7 5.8 %collective-permute-start.20 = (bf16[4,16,512]{2,1,0:T(8,128)(2,1)S(1)}, bf16[4,16,512]{2,1,0:T(8,128)(2,1)S(1)}, u32[]{:S(2)}, u32[]{:S(2)}) collective-permute-start(bf16[4,16,512]{2,1,0:T(8,128)(2,1)S(1)} %get-tuple-element.134), channel_id=1, source_target_pairs={{0,8},{8,0},{16,24},{24,16},{1,9},{9,1},{17,25},{25,17},{2,10},{10... | collective-permute-start | bytes 196616 | tf_op jit(solution)/shard_map/ppermute | solution.py:378
  133.7 8.6 %collective-permute-start.21 = (bf16[4,16,512]{2,1,0:T(8,128)(2,1)S(1)}, bf16[4,16,512]{2,1,0:T(8,128)(2,1)S(1)}, u32[]{:S(2)}, u32[]{:S(2)}) collective-permute-start(bf16[4,16,512]{2,1,0:T(8,128)(2,1)S(1)} %get-tuple-element.135), channel_id=1, source_target_pairs={{0,16},{8,24},{16,0},{24,8},{1,17},{9,25},{17,1},{25,9},{2,18},{10... | collective-permute-start | bytes 196616 | tf_op jit(solution)/shard_map/ppermute | solution.py:378
  137.0 6.2 %collective-permute-start.22 = (bf16[4,16,512]{2,1,0:T(8,128)(2,1)S(1)}, bf16[4,16,512]{2,1,0:T(8,128)(2,1)S(1)}, u32[]{:S(2)}, u32[]{:S(2)}) collective-permute-start(bf16[4,16,512]{2,1,0:T(8,128)(2,1)S(1)} %get-tuple-element.136), channel_id=1, source_target_pairs={{0,24},{8,16},{16,8},{24,0},{1,25},{9,17},{17,9},{25,1},{2,26},{10... | collective-permute-start | bytes 196616 | tf_op jit(solution)/shard_map/ppermute | solution.py:378
  (21 other events, 205.2 us)

commit v8 on v7

--- a/solution.py
+++ b/solution.py
@@ -326,7 +326,8 @@
     finish(going + send_turned(turn_ref, d_middle.astype(BF16), dm_ref, quarters(dm_hbm), sems.at[pl.ds(7, 4)]))
 
 
-def column_last(plane, cot_hbm, mid_hbm, n_hbm, att_hbm, dqkv_hbm, w_hbm, turn_hbm, out_hbm, *refs):
+def column_last(parts, plane, cot_hbm, mid_hbm, n_hbm, att_hbm, dqkv_hbm, w_hbm, turn_hbm, *refs):
+    out_hbms, refs = refs[:parts], refs[parts:]
     keep_hbms, send_hbms, refs = refs[:plane], refs[plane : 2 * plane], refs[2 * plane :]
     out_ref, keep_ref, send_ref, w_ref, turn_ref, flat_ref, dqkv_ref, sems, out_sems = refs
     coming = [
@@ -344,7 +345,7 @@
     weight_grad(3, attended, flat_ref[2], keep_ref, send_ref)
     going = send_grads(keep_ref, send_ref, keep_hbms, send_hbms, out_sems)
     output = (flat_ref[3].astype(F32) + dot(flat_ref[1], w_ref[...])).astype(BF16)
-    finish(going + send_turned(turn_ref.at[1], output, out_ref, [out_hbm], sems.at[pl.ds(8, 1)]))
+    finish(going + send_turned(turn_ref.at[1], output, out_ref, out_hbms, sems.at[pl.ds(8, parts)]))
 
 
 def add_pairs(*refs):
@@ -380,7 +381,7 @@
 
 def chip_sums(keeps, sends, col_parts):
     got = [swap(send, "col", col_parts, 1) for send in sends]
-    return call(add_pairs, [(item, ANY) for item in keeps + got], [(item.shape, ANY) for item in keeps], [])
+    return call(add_pairs, [(item, ANY) for item in (*keeps, *got)], [(item.shape, ANY) for item in keeps], [])
 
 
 def plane_pieces(sums, plane, core):
@@ -430,7 +431,7 @@
         ((height, cols), (1, 0), {}, 0),
         ((cols, height), (1, 0), {}, 0),
         ((row_parts, high, cols), (2, 0, 1), {0: "row"}, 0),
-        ((cols, row_parts, high), (1, 2, 0), {}, 0),
+        ((cols, row_parts, high), (1, 2, 0), {1: "row"}, 0),
         ((row_parts, plane, core, channels // devices), (2, 1, 0, 3), {0: "row", 1: "plane", 2: "core"}, 1),
     ]
 
@@ -471,34 +472,39 @@
         + [scratch(cols // together * HEADS, count, count), copies((11,))],
     )
     d_mid = all_to_all(d_mid)
-    out, *grads = call(
-        functools.partial(column_last, plane),
-        at(FAR, cot, *kept, weights, turn), at(FAR, flat, *[packed] * (2 * plane)),
+    results = call(
+        functools.partial(column_last, row_parts, plane),
+        at(FAR, cot, *kept, weights, turn), at(FAR, *[(high * cols, channels)] * row_parts, *[packed] * (2 * plane)),
         [square, scratch(plane, *packed), scratch(plane, *packed), square, scratch(2, *flat), scratch(4, *flat),
-         scratch(*triple), copies((9,)), copies((2 * plane,))],
-    )
-    pieces_b = plane_pieces(chip_sums(grads[:plane], grads[plane:], col_parts), plane, core)
-    d_mid, out = lax.optimization_barrier((d_mid, out))
-    d_mid, dqkv, *grads = call(
+         scratch(*triple), copies((8 + row_parts,)), copies((2 * plane,))],
+    )
+    outs, grads = results[:row_parts], results[row_parts:]
+    sums_b = chip_sums(grads[:plane], grads[plane:], col_parts)
+    pieces_b = plane_pieces(sums_b, plane, core)
+    d_mid, outs, _ = lax.optimization_barrier((d_mid, outs, sums_b))
+    early = [item if step == 0 else swap(item, "row", row_parts, step) for step, item in enumerate(outs[:3])]
+    results = call(
         functools.partial(row_back, (rows, length, width, plane)),
         at(ANY, d_mid) + at(FAR, weights, turn, normed, query, key, value, attended, prob),
         at(ANY, flat) + at(FAR, triple, *[packed] * (2 * plane)),
         [square, scratch(2, *flat)] + [square] * 5 + [scratch(*probs), square, scratch(*triple)]
         + [scratch(plane, *packed), scratch(plane, *packed), copies((11,)), copies((2 * plane,))],
     )
-    out, d_mid = lax.optimization_barrier((out, d_mid))
-    out = lax.all_to_all(out.reshape(row_parts, high, cols, channels), "row", 0, 0, tiled=True)
+    (d_mid, dqkv, *grads), pieces_b, early, late = lax.optimization_barrier((results, pieces_b, early, outs[3:]))
     pieces_a = plane_pieces(chip_sums(grads[:plane], grads[plane:], col_parts), plane, core)
-    dqkv, pieces_b, out = lax.optimization_barrier((dqkv, pieces_b, out))
+    pieces_out = [*early] + [swap(item, "row", row_parts, 3 + step) for step, item in enumerate(late)]
     grads_b = last_sums(pieces_b, row_parts)
     field_grad, = call(
         field_back, at(ANY, x, d_mid, gains) + at(FAR, dqkv, weights), at(FAR, x.shape),
         [scratch(*triple), scratch(3, *flat), scratch(*x.shape), copies((3,))],
     )
-    field_grad, pieces_a = lax.optimization_barrier((field_grad, pieces_a))
+    field_grad, pieces_a, grads_b, pieces_out = lax.optimization_barrier((field_grad, pieces_a, grads_b, pieces_out))
     field_grad = lax.all_to_all(field_grad, "col", 0, 0, tiled=True).reshape(high, wide, channels)
+    output = jnp.zeros((high, wide, channels), BF16)
+    for step, piece in enumerate(pieces_out):
+        piece = piece.reshape(high, cols, channels)
+        output = lax.dynamic_update_slice_in_dim(output, piece, (my_row ^ step) * cols, axis=1)
     grads_a = last_sums(pieces_a, row_parts)
-    output = out.transpose(1, 0, 2, 3).reshape(high, wide, channels)
     return output, field_grad, jnp.concatenate([grads_a, grads_b], axis=0)
 
 

time: 145 us -> 137 us (0.945)
  waiting for transfers between devices: 42.6 us -> 31.5 us
  local copies, waits for them, and re-layouts: 7.16 us -> 11.2 us
  other arithmetic: 3.02 us -> 1.14 us
    ppermute x23 -> x26, waiting for transfers between devices: 18.4 us -> 8.23 us  [swap(): return lax.ppermute(item, axis, [(at, at ^ step) for at in range(count)])]
    all_to_all x2, waiting for transfers between devices: 22.2 us -> 12.6 us  [all_to_all(): lax.all_to_all(item, ('row', 'col'), 0, 0, tiled=True)]
    all_to_all x1, waiting for transfers between devices: 0.01 us -> 8.71 us  [body(): lax.all_to_all(field_grad, 'col', 0, 0, tiled=True)]
    unnamed x35, local copies, waits for them, and re-layouts: 4.05 us -> 9.97 us
    ppermute x23 -> x26, starting transfers between devices: 22.8 us -> 27.2 us  [swap(): return lax.ppermute(item, axis, [(at, at ^ step) for at in range(count)])]
    all_to_all x1 -> x0, starting transfers between devices: 4.29 us -> none  [body(): lax.all_to_all(out.reshape(row_parts, high, cols, channels), 'row', 0, 0,...]
    convert_element_type x2, other arithmetic: 2.23 us -> 0.27 us  [last_sums(): held = sum((piece.astype(F32) for piece in pieces)).astype(BF16)]
    reshape x1 -> x0, local copies, waits for them, and re-layouts: 1.95 us -> none  [body(): output = out.transpose(1, 0, 2, 3).reshape(high, wide, channels)]
  transfers between devices with their start and end apart: 28 -> 30, of which waited for: 13 -> 8; matrix products, arithmetic and copies ran while one was open for 4% -> 2% of each run, Pallas kernels for 24% -> 25%
where the time goes in v8:
time: 137 us; the launch traced here: 136 us
  Pallas kernels  46.6 us (34%)
  starting transfers between devices  44.3 us (32%)
  waiting for transfers between devices  31.5 us (23%)
  local copies, waits for them, and re-layouts  11.2 us (8%)
    pallas_call x9, Pallas kernels, call(): pl.pallas_call(kernel, in_specs=[spec(where) for _, where in ins], out_sp...  46.6 us
    ppermute x26, starting transfers between devices, swap(): return lax.ppermute(item, axis, [(at, at ^ step) for at in range(count)])  27.2 us
    all_to_all x2, waiting for transfers between devices, all_to_all(): lax.all_to_all(item, ('row', 'col'), 0, 0, tiled=True)  12.6 us
    unnamed x35, local copies, waits for them, and re-layouts  9.97 us
    all_to_all x1, waiting for transfers between devices, body(): lax.all_to_all(field_grad, 'col', 0, 0, tiled=True)  8.71 us
    ppermute x26, waiting for transfers between devices, swap(): return lax.ppermute(item, axis, [(at, at ^ step) for at in range(count)])  8.23 us
    all_to_all x2, starting transfers between devices, all_to_all(): lax.all_to_all(item, ('row', 'col'), 0, 0, tiled=True)  7.72 us
    all_to_all x1, starting transfers between devices, body(): lax.all_to_all(field.reshape(col_parts, rows, wide, channels), 'col', 0,...  5.18 us
  transfers between devices with their start and end apart: 30, of which 8 were waited for; matrix products, arithmetic and copies ran while one was open for 2% of the time, Pallas kernels for 25%

profile of v8, /device:TPU:0, one launch (start us, length us, event | category | flops | bytes accessed | tf_op | source)
XLA Modules:
  0.0 135.8 jit_solution(14502575791207655317)
XLA Ops:
  0.6 5.2 %all-to-all-start = ((bf16[8,2,32,512]{3,2,1,0:T(8,128)(2,1)}), bf16[8,2,32,512]{3,2,1,0:T(8,128)(2,1)S(1)}, u32[]{:S(2)}, u32[]{:S(2)}) async-start(bf16[8,2,32,512]{3,2,1,0:T(8,128)(2,1)} %bitcast.69), calls=%async_computation | async-start | bytes 1048576 | tf_op jit(solution)/shard_map/all_to_all | solution.py:442
  7.0 1.6 %collective-permute-start = (bf16[16,8,512]{2,1,0:T(8,128)(2,1)S(1)}, bf16[16,8,512]{2,1,0:T(8,128)(2,1)S(1)}, u32[]{:S(2)}, u32[]{:S(2)}) collective-permute-start(bf16[16,8,512]{2,1,0:T(8,128)(2,1)S(1)} %get-tuple-element.170), channel_id=1, source_target_pairs={{0,8},{8,0},{16,24},{24,16},{1,9},{9,1},{17,25},{25,17},{2,10},{10... | collective-permute-start | bytes 393224 | tf_op jit(solution)/shard_map/ppermute | solution.py:379
  8.6 2.6 %collective-permute-start.1 = (bf16[16,8,512]{2,1,0:T(8,128)(2,1)S(1)}, bf16[16,8,512]{2,1,0:T(8,128)(2,1)S(1)}, u32[]{:S(2)}, u32[]{:S(2)}) collective-permute-start(bf16[16,8,512]{2,1,0:T(8,128)(2,1)S(1)} %get-tuple-element.172), channel_id=1, source_target_pairs={{0,16},{8,24},{16,0},{24,8},{1,17},{9,25},{17,1},{25,9},{2,18},{10... | collective-permute-start | bytes 393224 | tf_op jit(solution)/shard_map/ppermute | solution.py:379
  11.4 2.2 %shard_map.67.turn_hbm.refs_5_ = bf16[7,512,512]{2,1,0:T(8,128)(2,1)} custom-call(), custom_call_target="tpu_custom_call" | custom-call | flops 1048576 | bytes 1024 | tf_op jit(solution)/shard_map/pallas_call | solution.py:367
  13.6 1.9 %all-to-all-done.x_ref = bf16[8,2,32,512]{3,2,1,0:T(8,128)(2,1)S(1)} async-done(((bf16[8,2,32,512]{3,2,1,0:T(8,128)(2,1)}), bf16[8,2,32,512]{3,2,1,0:T(8,128)(2,1)S(1)}, u32[]{:S(2)}, u32[]{:S(2)}) %all-to-all-start) | async-done | bytes 524320 | tf_op jit(solution)/shard_map/all_to_all | solution.py:442
  15.6 8.2 %shard_map.68 = (bf16[512,512]{1,0:T(8,128)(2,1)}, bf16[512,512]{1,0:T(8,128)(2,1)}, bf16[512,512]{1,0:T(8,128)(2,1)}, bf16[512,512]{1,0:T(8,128)(2,1)}, bf16[51...) custom-call(bf16[8,2,32,512]{3,2,1,0:T(8,128)(2,1)S(1)} %all-to-all-done.x_ref, ...), custom_call_target="tpu_custom_call" | custom-call | flops 1048576 | bytes 1024 | tf_op jit(solution)/shard_map/pallas_call | solution.py:367
  24.4 4.4 %all-to-all-start.1 = ((bf16[32,16,512]{2,1,0:T(8,128)(2,1)}), bf16[32,16,512]{2,1,0:T(8,128)(2,1)S(1)}, u32[]{:S(2)}, u32[]{:S(2)}) async-start(bf16[32,16,512]{2,1,0:T(8,128)(2,1)} %bitcast.71), calls=%async_computation.1 | async-start | bytes 1048576 | tf_op jit(solution)/shard_map/all_to_all | solution.py:440
  29.8 2.0 %shard_map.69 = (bf16[512,512]{1,0:T(8,128)(2,1)S(1)}, bf16[512,512]{1,0:T(8,128)(2,1)S(1)}, bf16[2,512,512]{2,1,0:T(8,128)(2,1)S(1)}) custom-call(bf16[128,512]{1,0:T(8,128)(2,1)S(1)} %get-tuple-element.88.refs_0_, bf16[128,512]{1,0:T(8,128)(2,1)S(1)} %bitcast.61, bf16[128,512]{1,0:T(8,128)(2,1)S(1)} %bitcast.62, bf16[128,512]{1,0:T(8,128)(2,1)S(1)} %bitcast.63, ...), custom_call_target="tpu_custom_call" | custom-call | flops 1048576 | bytes 1024 | tf_op jit(solution)/shard_map/pallas_call | solution.py:367
  31.8 12.6 %all-to-all-done.1 = bf16[32,16,512]{2,1,0:T(8,128)(2,1)S(1)} async-done(((bf16[32,16,512]{2,1,0:T(8,128)(2,1)}), bf16[32,16,512]{2,1,0:T(8,128)(2,1)S(1)}, u32[]{:S(2)}, u32[]{:S(2)}) %all-to-all-start.1) | async-done | bytes 524320 | tf_op jit(solution)/shard_map/all_to_all | solution.py:440
  44.4 13.3 %shard_map.70 = (bf16[512,512]{1,0:T(8,128)(2,1)}, bf16[512,512]{1,0:T(8,128)(2,1)}, bf16[512,512]{1,0:T(8,128)(2,1)}, bf16[512,512]{1,0:T(8,128)(2,1)}, bf16[512,1536]{1,0:T(8,128)(2,1)}) custom-call(bf16[512,512]{1,0:T(8,128)(2,1)S(1)} %bitcast.60, bf16[512,512]{1,0:T(8,128)(2,1)S(1)} %get-tuple-element.92.cot_ref.cot_hbm, ...), custom_call_target="tpu_custom_call" | custom-call | flops 1048576 | bytes 1024 | tf_op jit(solution)/shard_map/pallas_call | solution.py:367
  57.7 3.3 %all-to-all-start.2 = ((bf16[32,16,512]{2,1,0:T(8,128)(2,1)}), bf16[32,16,512]{2,1,0:T(8,128)(2,1)S(1)}, u32[]{:S(2)}, u32[]{:S(2)}) async-start(bf16[32,16,512]{2,1,0:T(8,128)(2,1)} %bitcast.70), calls=%async_computation.2 | async-start | bytes 1048576 | tf_op jit(solution)/shard_map/all_to_all | solution.py:440
  61.0 5.8 %shard_map.71 = (bf16[128,512]{1,0:T(8,128)(2,1)}, bf16[128,512]{1,0:T(8,128)(2,1)}, bf16[128,512]{1,0:T(8,128)(2,1)}, bf16[128,512]{1,0:T(8,128)(2,1)}, bf16[4,...) custom-call(bf16[512,512]{1,0:T(8,128)(2,1)} %copy-done, ...), custom_call_target="tpu_custom_call" | custom-call | flops 1048576 | bytes 1024 | tf_op jit(solution)/shard_map/pallas_call | solution.py:367
  73.8 1.7 %collective-permute-start.7 = (bf16[4,64,512]{2,1,0:T(8,128)(2,1)S(1)}, bf16[4,64,512]{2,1,0:T(8,128)(2,1)S(1)}, u32[]{:S(2)}, u32[]{:S(2)}) collective-permute-start(bf16[4,64,512]{2,1,0:T(8,128)(2,1)S(1)} %get-tuple-element.113), channel_id=1, source_target_pairs={{0,2},{1,3},{2,0},{3,1},{4,6},{5,7},{6,4},{7,5},{8,10},{9,11},{10,... | collective-permute-start | bytes 786440 | tf_op jit(solution)/shard_map/ppermute | solution.py:379
  77.3 1.6 %collective-permute-start.10 = (bf16[128,512]{1,0:T(8,128)(2,1)S(1)}, bf16[128,512]{1,0:T(8,128)(2,1)S(1)}, u32[]{:S(2)}, u32[]{:S(2)}) collective-permute-start(bf16[128,512]{1,0:T(8,128)(2,1)S(1)} %copy-done.16), channel_id=1, source_target_pairs={{0,8},{8,0},{16,24},{24,16},{1,9},{9,1},{17,25},{25,17},{2,10},{10... | collective-permute-start | bytes 393224 | tf_op jit(solution)/shard_map/ppermute | solution.py:379
  78.9 2.4 %collective-permute-start.11 = (bf16[128,512]{1,0:T(8,128)(2,1)S(1)}, bf16[128,512]{1,0:T(8,128)(2,1)S(1)}, u32[]{:S(2)}, u32[]{:S(2)}) collective-permute-start(bf16[128,512]{1,0:T(8,128)(2,1)S(1)} %copy-done.15), channel_id=1, source_target_pairs={{0,16},{8,24},{16,0},{24,8},{1,17},{9,25},{17,1},{25,9},{2,18},{10... | collective-permute-start | bytes 393224 | tf_op jit(solution)/shard_map/ppermute | solution.py:379
  81.3 10.6 %shard_map.73 = (bf16[512,512]{1,0:T(8,128)(2,1)S(1)}, bf16[512,1536]{1,0:T(8,128)(2,1)}, bf16[4,64,512]{2,1,0:T(8,128)(2,1)}, bf16[4,64,512]{2,1,0:T(8,128)(2,1...) custom-call(bf16[512,512]{1,0:T(8,128)(2,1)S(1)} %bitcast.59, ...), custom_call_target="tpu_custom_call" | custom-call | flops 1048576 | bytes 1024 | tf_op jit(solution)/shard_map/pallas_call | solution.py:367
  94.4 3.4 %collective-permute-start.21 = (bf16[4,16,512]{2,1,0:T(8,128)(2,1)S(1)}, bf16[4,16,512]{2,1,0:T(8,128)(2,1)S(1)}, u32[]{:S(2)}, u32[]{:S(2)}) collective-permute-start(bf16[4,16,512]{2,1,0:T(8,128)(2,1)S(1)} %get-tuple-element.178), channel_id=1, source_target_pairs={{0,24},{8,16},{16,8},{24,0},{1,25},{9,17},{17,9},{25,1},{2,26},{10... | collective-permute-start | bytes 196616 | tf_op jit(solution)/shard_map/ppermute | solution.py:379
  101.8 1.6 %collective-permute-start.16 = (bf16[4,64,512]{2,1,0:T(8,128)(2,1)S(1)}, bf16[4,64,512]{2,1,0:T(8,128)(2,1)S(1)}, u32[]{:S(2)}, u32[]{:S(2)}) collective-permute-start(bf16[4,64,512]{2,1,0:T(8,128)(2,1)S(1)} %get-tuple-element.148), channel_id=1, source_target_pairs={{0,2},{1,3},{2,0},{3,1},{4,6},{5,7},{6,4},{7,5},{8,10},{9,11},{10,... | collective-permute-start | bytes 786440 | tf_op jit(solution)/shard_map/ppermute | solution.py:379
  103.3 1.5 %collective-permute-start.17 = (bf16[4,64,512]{2,1,0:T(8,128)(2,1)S(1)}, bf16[4,64,512]{2,1,0:T(8,128)(2,1)S(1)}, u32[]{:S(2)}, u32[]{:S(2)}) collective-permute-start(bf16[4,64,512]{2,1,0:T(8,128)(2,1)S(1)} %get-tuple-element.149), channel_id=1, source_target_pairs={{0,4},{1,5},{2,6},{3,7},{4,0},{5,1},{6,2},{7,3},{8,12},{9,13},{10,... | collective-permute-start | bytes 786440 | tf_op jit(solution)/shard_map/ppermute | solution.py:379
  105.3 4.1 %shard_map.74 = bf16[8,2,32,512]{3,2,1,0:T(8,128)(2,1)} custom-call(bf16[8,2,32,512]{3,2,1,0:T(8,128)(2,1)S(1)} %all-to-all-done.x_ref, bf16[512,512]{1,0:T(8,128)(2,1)S(1)} %get-tuple-element.137.dm_ref, f32[2,512]{1,0:T(2,128)S(1)} %copy-done.11, bf16[512,1536]{1,0:T(8,128)(2,1)} %get-tuple-element.138.dqkv_hbm, bf16[2,4,512,512]{3,2,1,0:T(8,128)(2,1)} %w_hbm.9), custom_call_target="tpu_custom_call" | custom-call | flops 1048576 | bytes 1024 | tf_op jit(solution)/shard_map/pallas_call | solution.py:367
  110.0 6.3 %collective-permute-done.22 = bf16[128,512]{1,0:T(8,128)(2,1)S(1)} collective-permute-done((bf16[128,512]{1,0:T(8,128)(2,1)S(1)}, bf16[128,512]{1,0:T(8,128)(2,1)S(1)}, u32[]{:S(2)}, u32[]{:S(2)}) %collective-permute-start.22) | collective-permute-done | bytes 131104 | tf_op jit(solution)/shard_map/ppermute | solution.py:379
  117.8 3.2 %collective-permute-start.25 = (bf16[4,16,512]{2,1,0:T(8,128)(2,1)S(1)}, bf16[4,16,512]{2,1,0:T(8,128)(2,1)S(1)}, u32[]{:S(2)}, u32[]{:S(2)}) collective-permute-start(bf16[4,16,512]{2,1,0:T(8,128)(2,1)S(1)} %get-tuple-element.175), channel_id=1, source_target_pairs={{0,24},{8,16},{16,8},{24,0},{1,25},{9,17},{17,9},{25,1},{2,26},{10... | collective-permute-start | bytes 196616 | tf_op jit(solution)/shard_map/ppermute | solution.py:379
  121.0 4.2 %all-to-all-start.3 = ((bf16[8,2,32,512]{3,2,1,0:T(8,128)(2,1)}), bf16[8,2,32,512]{3,2,1,0:T(8,128)(2,1)S(1)}, u32[]{:S(2)}, u32[]{:S(2)}) async-start(bf16[8,2,32,512]{3,2,1,0:T(8,128)(2,1)} %shard_map.74), calls=%async_computation.3 | async-start | bytes 1048576 | tf_op jit(solution)/shard_map/all_to_all | solution.py:502
  126.3 8.7 %all-to-all-done.3 = bf16[8,2,32,512]{3,2,1,0:T(8,128)(2,1)S(1)} async-done(((bf16[8,2,32,512]{3,2,1,0:T(8,128)(2,1)}), bf16[8,2,32,512]{3,2,1,0:T(8,128)(2,1)S(1)}, u32[]{:S(2)}, u32[]{:S(2)}) %all-to-all-start.3) | async-done | bytes 524320 | tf_op jit(solution)/shard_map/all_to_all | solution.py:502
  (93 shorter events, 22.5 us)
Async XLA Ops:
  0.6 14.9 %all-to-all-start = ((bf16[8,2,32,512]{3,2,1,0:T(8,128)(2,1)}), bf16[8,2,32,512]{3,2,1,0:T(8,128)(2,1)S(1)}, u32[]{:S(2)}, u32[]{:S(2)}) async-start(bf16[8,2,32,512]{3,2,1,0:T(8,128)(2,1)} %bitcast.69), calls=%async_computation | async-start | bytes 1048576 | tf_op jit(solution)/shard_map/all_to_all | solution.py:442
  7.0 16.8 %collective-permute-start = (bf16[16,8,512]{2,1,0:T(8,128)(2,1)S(1)}, bf16[16,8,512]{2,1,0:T(8,128)(2,1)S(1)}, u32[]{:S(2)}, u32[]{:S(2)}) collective-permute-start(bf16[16,8,512]{2,1,0:T(8,128)(2,1)S(1)} %get-tuple-element.170), channel_id=1, source_target_pairs={{0,8},{8,0},{16,24},{24,16},{1,9},{9,1},{17,25},{25,17},{2,10},{10... | collective-permute-start | bytes 393224 | tf_op jit(solution)/shard_map/ppermute | solution.py:379
  8.6 15.1 %collective-permute-start.1 = (bf16[16,8,512]{2,1,0:T(8,128)(2,1)S(1)}, bf16[16,8,512]{2,1,0:T(8,128)(2,1)S(1)}, u32[]{:S(2)}, u32[]{:S(2)}) collective-permute-start(bf16[16,8,512]{2,1,0:T(8,128)(2,1)S(1)} %get-tuple-element.172), channel_id=1, source_target_pairs={{0,16},{8,24},{16,0},{24,8},{1,17},{9,25},{17,1},{25,9},{2,18},{10... | collective-permute-start | bytes 393224 | tf_op jit(solution)/shard_map/ppermute | solution.py:379
  11.2 12.6 %collective-permute-start.2 = (bf16[16,8,512]{2,1,0:T(8,128)(2,1)S(1)}, bf16[16,8,512]{2,1,0:T(8,128)(2,1)S(1)}, u32[]{:S(2)}, u32[]{:S(2)}) collective-permute-start(bf16[16,8,512]{2,1,0:T(8,128)(2,1)S(1)} %get-tuple-element.169), channel_id=1, source_target_pairs={{0,24},{8,16},{16,8},{24,0},{1,25},{9,17},{17,9},{25,1},{2,26},{10... | collective-permute-start | bytes 393224 | tf_op jit(solution)/shard_map/ppermute | solution.py:379
  24.4 20.0 %all-to-all-start.1 = ((bf16[32,16,512]{2,1,0:T(8,128)(2,1)}), bf16[32,16,512]{2,1,0:T(8,128)(2,1)S(1)}, u32[]{:S(2)}, u32[]{:S(2)}) async-start(bf16[32,16,512]{2,1,0:T(8,128)(2,1)} %bitcast.71), calls=%async_computation.1 | async-start | bytes 1048576 | tf_op jit(solution)/shard_map/all_to_all | solution.py:440
  57.7 19.6 %all-to-all-start.2 = ((bf16[32,16,512]{2,1,0:T(8,128)(2,1)}), bf16[32,16,512]{2,1,0:T(8,128)(2,1)S(1)}, u32[]{:S(2)}, u32[]{:S(2)}) async-start(bf16[32,16,512]{2,1,0:T(8,128)(2,1)} %bitcast.70), calls=%async_computation.2 | async-start | bytes 1048576 | tf_op jit(solution)/shard_map/all_to_all | solution.py:440
  73.8 18.2 %collective-permute-start.7 = (bf16[4,64,512]{2,1,0:T(8,128)(2,1)S(1)}, bf16[4,64,512]{2,1,0:T(8,128)(2,1)S(1)}, u32[]{:S(2)}, u32[]{:S(2)}) collective-permute-start(bf16[4,64,512]{2,1,0:T(8,128)(2,1)S(1)} %get-tuple-element.113), channel_id=1, source_target_pairs={{0,2},{1,3},{2,0},{3,1},{4,6},{5,7},{6,4},{7,5},{8,10},{9,11},{10,... | collective-permute-start | bytes 786440 | tf_op jit(solution)/shard_map/ppermute | solution.py:379
  75.4 16.5 %collective-permute-start.8 = (bf16[4,64,512]{2,1,0:T(8,128)(2,1)S(1)}, bf16[4,64,512]{2,1,0:T(8,128)(2,1)S(1)}, u32[]{:S(2)}, u32[]{:S(2)}) collective-permute-start(bf16[4,64,512]{2,1,0:T(8,128)(2,1)S(1)} %get-tuple-element.114), channel_id=1, source_target_pairs={{0,4},{1,5},{2,6},{3,7},{4,0},{5,1},{6,2},{7,3},{8,12},{9,13},{10,... | collective-permute-start | bytes 786440 | tf_op jit(solution)/shard_map/ppermute | solution.py:379
  76.9 15.1 %collective-permute-start.9 = (bf16[4,64,512]{2,1,0:T(8,128)(2,1)S(1)}, bf16[4,64,512]{2,1,0:T(8,128)(2,1)S(1)}, u32[]{:S(2)}, u32[]{:S(2)}) collective-permute-start(bf16[4,64,512]{2,1,0:T(8,128)(2,1)S(1)} %get-tuple-element.115), channel_id=1, source_target_pairs={{0,6},{1,7},{2,4},{3,5},{4,2},{5,3},{6,0},{7,1},{8,14},{9,15},{10,... | collective-permute-start | bytes 786440 | tf_op jit(solution)/shard_map/ppermute | solution.py:379
  77.3 14.7 %collective-permute-start.10 = (bf16[128,512]{1,0:T(8,128)(2,1)S(1)}, bf16[128,512]{1,0:T(8,128)(2,1)S(1)}, u32[]{:S(2)}, u32[]{:S(2)}) collective-permute-start(bf16[128,512]{1,0:T(8,128)(2,1)S(1)} %copy-done.16), channel_id=1, source_target_pairs={{0,8},{8,0},{16,24},{24,16},{1,9},{9,1},{17,25},{25,17},{2,10},{10... | collective-permute-start | bytes 393224 | tf_op jit(solution)/shard_map/ppermute | solution.py:379
  78.9 13.1 %collective-permute-start.11 = (bf16[128,512]{1,0:T(8,128)(2,1)S(1)}, bf16[128,512]{1,0:T(8,128)(2,1)S(1)}, u32[]{:S(2)}, u32[]{:S(2)}) collective-permute-start(bf16[128,512]{1,0:T(8,128)(2,1)S(1)} %copy-done.15), channel_id=1, source_target_pairs={{0,16},{8,24},{16,0},{24,8},{1,17},{9,25},{17,1},{25,9},{2,18},{10... | collective-permute-start | bytes 393224 | tf_op jit(solution)/shard_map/ppermute | solution.py:379
  92.6 5.1 %collective-permute-start.14 = (bf16[4,64,512]{2,1,0:T(8,128)(2,1)}, bf16[4,64,512]{2,1,0:T(8,128)(2,1)S(1)}, u32[]{:S(2)}, u32[]{:S(2)}) collective-permute-start(bf16[4,64,512]{2,1,0:T(8,128)(2,1)} %get-tuple-element.145), channel_id=1, source_target_pairs={{0,1},{1,0},{2,3},{3,2},{4,5},{5,4},{6,7},{7,6},{8,9},{9,8},{10,11... | collective-permute-start | bytes 786440 | tf_op jit(solution)/shard_map/ppermute | solution.py:379
  92.7 5.1 %collective-permute-start.15 = (bf16[4,64,512]{2,1,0:T(8,128)(2,1)}, bf16[4,64,512]{2,1,0:T(8,128)(2,1)S(1)}, u32[]{:S(2)}, u32[]{:S(2)}) collective-permute-start(bf16[4,64,512]{2,1,0:T(8,128)(2,1)} %get-tuple-element.146), channel_id=1, source_target_pairs={{0,1},{1,0},{2,3},{3,2},{4,5},{5,4},{6,7},{7,6},{8,9},{9,8},{10,11... | collective-permute-start | bytes 786440 | tf_op jit(solution)/shard_map/ppermute | solution.py:379
  93.3 11.6 %collective-permute-start.19 = (bf16[4,16,512]{2,1,0:T(8,128)(2,1)S(1)}, bf16[4,16,512]{2,1,0:T(8,128)(2,1)S(1)}, u32[]{:S(2)}, u32[]{:S(2)}) collective-permute-start(bf16[4,16,512]{2,1,0:T(8,128)(2,1)S(1)} %get-tuple-element.176), channel_id=1, source_target_pairs={{0,8},{8,0},{16,24},{24,16},{1,9},{9,1},{17,25},{25,17},{2,10},{10... | collective-permute-start | bytes 196616 | tf_op jit(solution)/shard_map/ppermute | solution.py:379
  93.8 15.6 %collective-permute-start.20 = (bf16[4,16,512]{2,1,0:T(8,128)(2,1)S(1)}, bf16[4,16,512]{2,1,0:T(8,128)(2,1)S(1)}, u32[]{:S(2)}, u32[]{:S(2)}) collective-permute-start(bf16[4,16,512]{2,1,0:T(8,128)(2,1)S(1)} %get-tuple-element.177), channel_id=1, source_target_pairs={{0,16},{8,24},{16,0},{24,8},{1,17},{9,25},{17,1},{25,9},{2,18},{10... | collective-permute-start | bytes 196616 | tf_op jit(solution)/shard_map/ppermute | solution.py:379
  94.4 15.6 %collective-permute-start.21 = (bf16[4,16,512]{2,1,0:T(8,128)(2,1)S(1)}, bf16[4,16,512]{2,1,0:T(8,128)(2,1)S(1)}, u32[]{:S(2)}, u32[]{:S(2)}) collective-permute-start(bf16[4,16,512]{2,1,0:T(8,128)(2,1)S(1)} %get-tuple-element.178), channel_id=1, source_target_pairs={{0,24},{8,16},{16,8},{24,0},{1,25},{9,17},{17,9},{25,1},{2,26},{10... | collective-permute-start | bytes 196616 | tf_op jit(solution)/shard_map/ppermute | solution.py:379
  101.8 14.6 %collective-permute-start.16 = (bf16[4,64,512]{2,1,0:T(8,128)(2,1)S(1)}, bf16[4,64,512]{2,1,0:T(8,128)(2,1)S(1)}, u32[]{:S(2)}, u32[]{:S(2)}) collective-permute-start(bf16[4,64,512]{2,1,0:T(8,128)(2,1)S(1)} %get-tuple-element.148), channel_id=1, source_target_pairs={{0,2},{1,3},{2,0},{3,1},{4,6},{5,7},{6,4},{7,5},{8,10},{9,11},{10,... | collective-permute-start | bytes 786440 | tf_op jit(solution)/shard_map/ppermute | solution.py:379
  103.3 13.0 %collective-permute-start.17 = (bf16[4,64,512]{2,1,0:T(8,128)(2,1)S(1)}, bf16[4,64,512]{2,1,0:T(8,128)(2,1)S(1)}, u32[]{:S(2)}, u32[]{:S(2)}) collective-permute-start(bf16[4,64,512]{2,1,0:T(8,128)(2,1)S(1)} %get-tuple-element.149), channel_id=1, source_target_pairs={{0,4},{1,5},{2,6},{3,7},{4,0},{5,1},{6,2},{7,3},{8,12},{9,13},{10,... | collective-permute-start | bytes 786440 | tf_op jit(solution)/shard_map/ppermute | solution.py:379
  104.8 11.5 %collective-permute-start.18 = (bf16[4,64,512]{2,1,0:T(8,128)(2,1)S(1)}, bf16[4,64,512]{2,1,0:T(8,128)(2,1)S(1)}, u32[]{:S(2)}, u32[]{:S(2)}) collective-permute-start(bf16[4,64,512]{2,1,0:T(8,128)(2,1)S(1)} %get-tuple-element.150), channel_id=1, source_target_pairs={{0,6},{1,7},{2,4},{3,5},{4,2},{5,3},{6,0},{7,1},{8,14},{9,15},{10,... | collective-permute-start | bytes 786440 | tf_op jit(solution)/shard_map/ppermute | solution.py:379
  109.4 6.9 %collective-permute-start.22 = (bf16[128,512]{1,0:T(8,128)(2,1)S(1)}, bf16[128,512]{1,0:T(8,128)(2,1)S(1)}, u32[]{:S(2)}, u32[]{:S(2)}) collective-permute-start(bf16[128,512]{1,0:T(8,128)(2,1)S(1)} %copy-done.14), channel_id=1, source_target_pairs={{0,24},{8,16},{16,8},{24,0},{1,25},{9,17},{17,9},{25,1},{2,26},{10... | collective-permute-start | bytes 393224 | tf_op jit(solution)/shard_map/ppermute | solution.py:379
  116.5 8.9 %collective-permute-start.23 = (bf16[4,16,512]{2,1,0:T(8,128)(2,1)S(1)}, bf16[4,16,512]{2,1,0:T(8,128)(2,1)S(1)}, u32[]{:S(2)}, u32[]{:S(2)}) collective-permute-start(bf16[4,16,512]{2,1,0:T(8,128)(2,1)S(1)} %get-tuple-element.173), channel_id=1, source_target_pairs={{0,8},{8,0},{16,24},{24,16},{1,9},{9,1},{17,25},{25,17},{2,10},{10... | collective-permute-start | bytes 196616 | tf_op jit(solution)/shard_map/ppermute | solution.py:379
  116.6 8.8 %collective-permute-start.24 = (bf16[4,16,512]{2,1,0:T(8,128)(2,1)S(1)}, bf16[4,16,512]{2,1,0:T(8,128)(2,1)S(1)}, u32[]{:S(2)}, u32[]{:S(2)}) collective-permute-start(bf16[4,16,512]{2,1,0:T(8,128)(2,1)S(1)} %get-tuple-element.174), channel_id=1, source_target_pairs={{0,16},{8,24},{16,0},{24,8},{1,17},{9,25},{17,1},{25,9},{2,18},{10... | collective-permute-start | bytes 196616 | tf_op jit(solution)/shard_map/ppermute | solution.py:379
  117.8 7.6 %collective-permute-start.25 = (bf16[4,16,512]{2,1,0:T(8,128)(2,1)S(1)}, bf16[4,16,512]{2,1,0:T(8,128)(2,1)S(1)}, u32[]{:S(2)}, u32[]{:S(2)}) collective-permute-start(bf16[4,16,512]{2,1,0:T(8,128)(2,1)S(1)} %get-tuple-element.175), channel_id=1, source_target_pairs={{0,24},{8,16},{16,8},{24,0},{1,25},{9,17},{17,9},{25,1},{2,26},{10... | collective-permute-start | bytes 196616 | tf_op jit(solution)/shard_map/ppermute | solution.py:379
  121.0 14.0 %all-to-all-start.3 = ((bf16[8,2,32,512]{3,2,1,0:T(8,128)(2,1)}), bf16[8,2,32,512]{3,2,1,0:T(8,128)(2,1)S(1)}, u32[]{:S(2)}, u32[]{:S(2)}) async-start(bf16[8,2,32,512]{3,2,1,0:T(8,128)(2,1)} %shard_map.74), calls=%async_computation.3 | async-start | bytes 1048576 | tf_op jit(solution)/shard_map/all_to_all | solution.py:502
  (23 other events, 96.1 us)

commit v9 on v8

--- a/solution.py
+++ b/solution.py
@@ -348,10 +348,14 @@
     finish(going + send_turned(turn_ref.at[1], output, out_ref, out_hbms, sems.at[pl.ds(8, parts)]))
 
 
-def add_pairs(*refs):
-    count = len(refs) // 3
-    for left, right, target in zip(refs[:count], refs[count : 2 * count], refs[2 * count :]):
-        target[...] = (left[...].astype(F32) + right[...].astype(F32)).astype(BF16)
+def add_pairs(count, *refs):
+    keep_hbms, got_refs, sum_refs, (keep_ref, sems) = (
+        refs[:count], refs[count : 2 * count], refs[2 * count : 3 * count], refs[3 * count :]
+    )
+    coming = [start(hbm, keep_ref.at[at], sems.at[at]) for at, hbm in enumerate(keep_hbms)]
+    for at, copy in enumerate(coming):
+        copy.wait()
+        sum_refs[at][...] = (keep_ref[at].astype(F32) + got_refs[at][...].astype(F32)).astype(BF16)
 
 
 NEAR, FAR, ANY = pltpu.VMEM, pltpu.HBM, None
@@ -381,7 +385,12 @@
 
 def chip_sums(keeps, sends, col_parts):
     got = [swap(send, "col", col_parts, 1) for send in sends]
-    return call(add_pairs, [(item, ANY) for item in (*keeps, *got)], [(item.shape, ANY) for item in keeps], [])
+    count, shape = len(keeps), keeps[0].shape
+    return call(
+        functools.partial(add_pairs, count),
+        [(item, FAR) for item in keeps] + [(item, ANY) for item in got], [(shape, ANY)] * count,
+        [pltpu.VMEM((count, *shape), BF16), pltpu.SemaphoreType.DMA((count,))],
+    )
 
 
 def plane_pieces(sums, plane, core):
@@ -481,8 +490,8 @@
     outs, grads = results[:row_parts], results[row_parts:]
     sums_b = chip_sums(grads[:plane], grads[plane:], col_parts)
     pieces_b = plane_pieces(sums_b, plane, core)
-    d_mid, outs, _ = lax.optimization_barrier((d_mid, outs, sums_b))
-    early = [item if step == 0 else swap(item, "row", row_parts, step) for step, item in enumerate(outs[:3])]
+    near, far = [outs[0], swap(outs[1], "row", row_parts, 1)], outs[2:]
+    d_mid, near, far, _ = lax.optimization_barrier((d_mid, near, far, sums_b))
     results = call(
         functools.partial(row_back, (rows, length, width, plane)),
         at(ANY, d_mid) + at(FAR, weights, turn, normed, query, key, value, attended, prob),
@@ -490,19 +499,20 @@
         [square, scratch(2, *flat)] + [square] * 5 + [scratch(*probs), square, scratch(*triple)]
         + [scratch(plane, *packed), scratch(plane, *packed), copies((11,)), copies((2 * plane,))],
     )
-    (d_mid, dqkv, *grads), pieces_b, early, late = lax.optimization_barrier((results, pieces_b, early, outs[3:]))
-    pieces_a = plane_pieces(chip_sums(grads[:plane], grads[plane:], col_parts), plane, core)
-    pieces_out = [*early] + [swap(item, "row", row_parts, 3 + step) for step, item in enumerate(late)]
-    grads_b = last_sums(pieces_b, row_parts)
+    (d_mid, dqkv, *grads), pieces_b, far = lax.optimization_barrier((results, pieces_b, far))
+    sums_a = chip_sums(grads[:plane], grads[plane:], col_parts)
+    pieces_a = plane_pieces(sums_a, plane, core)
+    dqkv, pieces_b, far, _ = lax.optimization_barrier((dqkv, pieces_b, far, sums_a))
     field_grad, = call(
         field_back, at(ANY, x, d_mid, gains) + at(FAR, dqkv, weights), at(FAR, x.shape),
         [scratch(*triple), scratch(3, *flat), scratch(*x.shape), copies((3,))],
     )
-    field_grad, pieces_a, grads_b, pieces_out = lax.optimization_barrier((field_grad, pieces_a, grads_b, pieces_out))
+    field_grad, pieces_a[1] = lax.optimization_barrier((field_grad, pieces_a[1]))
     field_grad = lax.all_to_all(field_grad, "col", 0, 0, tiled=True).reshape(high, wide, channels)
+    grads_b = last_sums(pieces_b, row_parts)
     output = jnp.zeros((high, wide, channels), BF16)
-    for step, piece in enumerate(pieces_out):
-        piece = piece.reshape(high, cols, channels)
+    for step, piece in enumerate((*near, *far)):
+        piece = (piece if step < 2 else swap(piece, "row", row_parts, step)).reshape(high, cols, channels)
         output = lax.dynamic_update_slice_in_dim(output, piece, (my_row ^ step) * cols, axis=1)
     grads_a = last_sums(pieces_a, row_parts)
     return output, field_grad, jnp.concatenate([grads_a, grads_b], axis=0)

time: 137 us -> 138 us (level)
  local copies, waits for them, and re-layouts: 11.2 us -> 3.64 us
  waiting for transfers between devices: 31.5 us -> 38.2 us
  Pallas kernels: 46.6 us -> 48.8 us
    unnamed x35 -> x19, local copies, waits for them, and re-layouts: 9.97 us -> 2.38 us
    ppermute x26, waiting for transfers between devices: 8.23 us -> 15.5 us  [swap(): return lax.ppermute(item, axis, [(at, at ^ step) for at in range(count)])]
    pallas_call x9, Pallas kernels: 46.6 us -> 48.8 us  [call(): pl.pallas_call(kernel, in_specs=[spec(where) for _, where in ins], out_sp...]
  transfers between devices with their start and end apart: 30 -> 30, of which waited for: 8 -> 14; matrix products, arithmetic and copies ran while one was open for 2% -> 2% of each run, Pallas kernels for 25% -> 25%
where the time goes in v9:
time: 138 us; the launch traced here: 137 us
  Pallas kernels  48.8 us (35%)
  starting transfers between devices  44.4 us (32%)
  waiting for transfers between devices  38.2 us (28%)
  local copies, waits for them, and re-layouts  3.64 us (3%)
    pallas_call x9, Pallas kernels, call(): pl.pallas_call(kernel, in_specs=[spec(where) for _, where in ins], out_sp...  48.8 us
    ppermute x26, starting transfers between devices, swap(): return lax.ppermute(item, axis, [(at, at ^ step) for at in range(count)])  27.8 us
    ppermute x26, waiting for transfers between devices, swap(): return lax.ppermute(item, axis, [(at, at ^ step) for at in range(count)])  15.5 us
    all_to_all x2, waiting for transfers between devices, all_to_all(): lax.all_to_all(item, ('row', 'col'), 0, 0, tiled=True)  12.6 us
    all_to_all x1, waiting for transfers between devices, body(): lax.all_to_all(field_grad, 'col', 0, 0, tiled=True)  8.22 us
    all_to_all x2, starting transfers between devices, all_to_all(): lax.all_to_all(item, ('row', 'col'), 0, 0, tiled=True)  7.7 us
    all_to_all x1, starting transfers between devices, body(): lax.all_to_all(field.reshape(col_parts, rows, wide, channels), 'col', 0,...  5.18 us
    all_to_all x1, starting transfers between devices, body(): lax.all_to_all(field_grad, 'col', 0, 0, tiled=True)  3.7 us
  transfers between devices with their start and end apart: 30, of which 14 were waited for; matrix products, arithmetic and copies ran while one was open for 2% of the time, Pallas kernels for 25%

profile of v9, /device:TPU:0, one launch (start us, length us, event | category | flops | bytes accessed | tf_op | source)
XLA Modules:
  0.0 137.2 jit_solution(6636608598436085610)
XLA Ops:
  0.6 5.2 %all-to-all-start = ((bf16[8,2,32,512]{3,2,1,0:T(8,128)(2,1)}), bf16[8,2,32,512]{3,2,1,0:T(8,128)(2,1)S(1)}, u32[]{:S(2)}, u32[]{:S(2)}) async-start(bf16[8,2,32,512]{3,2,1,0:T(8,128)(2,1)} %bitcast.69), calls=%async_computation | async-start | bytes 1048576 | tf_op jit(solution)/shard_map/all_to_all | solution.py:451
  7.0 1.6 %collective-permute-start = (bf16[16,8,512]{2,1,0:T(8,128)(2,1)S(1)}, bf16[16,8,512]{2,1,0:T(8,128)(2,1)S(1)}, u32[]{:S(2)}, u32[]{:S(2)}) collective-permute-start(bf16[16,8,512]{2,1,0:T(8,128)(2,1)S(1)} %get-tuple-element.164), channel_id=1, source_target_pairs={{0,8},{8,0},{16,24},{24,16},{1,9},{9,1},{17,25},{25,17},{2,10},{10... | collective-permute-start | bytes 393224 | tf_op jit(solution)/shard_map/ppermute | solution.py:383
  8.6 2.6 %collective-permute-start.1 = (bf16[16,8,512]{2,1,0:T(8,128)(2,1)S(1)}, bf16[16,8,512]{2,1,0:T(8,128)(2,1)S(1)}, u32[]{:S(2)}, u32[]{:S(2)}) collective-permute-start(bf16[16,8,512]{2,1,0:T(8,128)(2,1)S(1)} %get-tuple-element.166), channel_id=1, source_target_pairs={{0,16},{8,24},{16,0},{24,8},{1,17},{9,25},{17,1},{25,9},{2,18},{10... | collective-permute-start | bytes 393224 | tf_op jit(solution)/shard_map/ppermute | solution.py:383
  11.4 2.2 %shard_map.67.turn_hbm.refs_5_ = bf16[7,512,512]{2,1,0:T(8,128)(2,1)} custom-call(), custom_call_target="tpu_custom_call" | custom-call | flops 1048576 | bytes 1024 | tf_op jit(solution)/shard_map/pallas_call | solution.py:371
  13.6 1.9 %all-to-all-done.x_ref = bf16[8,2,32,512]{3,2,1,0:T(8,128)(2,1)S(1)} async-done(((bf16[8,2,32,512]{3,2,1,0:T(8,128)(2,1)}), bf16[8,2,32,512]{3,2,1,0:T(8,128)(2,1)S(1)}, u32[]{:S(2)}, u32[]{:S(2)}) %all-to-all-start) | async-done | bytes 524320 | tf_op jit(solution)/shard_map/all_to_all | solution.py:451
  15.6 8.2 %shard_map.68 = (bf16[512,512]{1,0:T(8,128)(2,1)}, bf16[512,512]{1,0:T(8,128)(2,1)}, bf16[512,512]{1,0:T(8,128)(2,1)}, bf16[512,512]{1,0:T(8,128)(2,1)}, bf16[51...) custom-call(bf16[8,2,32,512]{3,2,1,0:T(8,128)(2,1)S(1)} %all-to-all-done.x_ref, ...), custom_call_target="tpu_custom_call" | custom-call | flops 1048576 | bytes 1024 | tf_op jit(solution)/shard_map/pallas_call | solution.py:371
  24.4 4.4 %all-to-all-start.1 = ((bf16[32,16,512]{2,1,0:T(8,128)(2,1)}), bf16[32,16,512]{2,1,0:T(8,128)(2,1)S(1)}, u32[]{:S(2)}, u32[]{:S(2)}) async-start(bf16[32,16,512]{2,1,0:T(8,128)(2,1)} %bitcast.71), calls=%async_computation.1 | async-start | bytes 1048576 | tf_op jit(solution)/shard_map/all_to_all | solution.py:449
  29.8 2.0 %shard_map.69 = (bf16[512,512]{1,0:T(8,128)(2,1)S(1)}, bf16[512,512]{1,0:T(8,128)(2,1)S(1)}, bf16[2,512,512]{2,1,0:T(8,128)(2,1)S(1)}) custom-call(bf16[128,512]{1,0:T(8,128)(2,1)S(1)} %get-tuple-element.85.refs_0_, bf16[128,512]{1,0:T(8,128)(2,1)S(1)} %bitcast.61, bf16[128,512]{1,0:T(8,128)(2,1)S(1)} %bitcast.62, bf16[128,512]{1,0:T(8,128)(2,1)S(1)} %bitcast.63, ...), custom_call_target="tpu_custom_call" | custom-call | flops 1048576 | bytes 1024 | tf_op jit(solution)/shard_map/pallas_call | solution.py:371
  31.8 12.6 %all-to-all-done.1 = bf16[32,16,512]{2,1,0:T(8,128)(2,1)S(1)} async-done(((bf16[32,16,512]{2,1,0:T(8,128)(2,1)}), bf16[32,16,512]{2,1,0:T(8,128)(2,1)S(1)}, u32[]{:S(2)}, u32[]{:S(2)}) %all-to-all-start.1) | async-done | bytes 524320 | tf_op jit(solution)/shard_map/all_to_all | solution.py:449
  44.4 13.3 %shard_map.70 = (bf16[512,512]{1,0:T(8,128)(2,1)}, bf16[512,512]{1,0:T(8,128)(2,1)}, bf16[512,512]{1,0:T(8,128)(2,1)}, bf16[512,512]{1,0:T(8,128)(2,1)}, bf16[512,1536]{1,0:T(8,128)(2,1)}) custom-call(bf16[512,512]{1,0:T(8,128)(2,1)S(1)} %bitcast.60, bf16[512,512]{1,0:T(8,128)(2,1)S(1)} %get-tuple-element.89.cot_ref.cot_hbm, ...), custom_call_target="tpu_custom_call" | custom-call | flops 1048576 | bytes 1024 | tf_op jit(solution)/shard_map/pallas_call | solution.py:371
  57.7 3.3 %all-to-all-start.2 = ((bf16[32,16,512]{2,1,0:T(8,128)(2,1)}), bf16[32,16,512]{2,1,0:T(8,128)(2,1)S(1)}, u32[]{:S(2)}, u32[]{:S(2)}) async-start(bf16[32,16,512]{2,1,0:T(8,128)(2,1)} %bitcast.70), calls=%async_computation.2 | async-start | bytes 1048576 | tf_op jit(solution)/shard_map/all_to_all | solution.py:449
  61.0 5.7 %shard_map.71 = (bf16[128,512]{1,0:T(8,128)(2,1)}, bf16[128,512]{1,0:T(8,128)(2,1)}, bf16[128,512]{1,0:T(8,128)(2,1)}, bf16[128,512]{1,0:T(8,128)(2,1)}, bf16[4,...) custom-call(bf16[512,512]{1,0:T(8,128)(2,1)} %copy-done, ...), custom_call_target="tpu_custom_call" | custom-call | flops 1048576 | bytes 1024 | tf_op jit(solution)/shard_map/pallas_call | solution.py:371
  71.0 2.6 %collective-permute-start.10 = (bf16[4,64,512]{2,1,0:T(8,128)(2,1)S(1)}, bf16[4,64,512]{2,1,0:T(8,128)(2,1)S(1)}, u32[]{:S(2)}, u32[]{:S(2)}) collective-permute-start(bf16[4,64,512]{2,1,0:T(8,128)(2,1)S(1)} %get-tuple-element.112), channel_id=1, source_target_pairs={{0,6},{1,7},{2,4},{3,5},{4,2},{5,3},{6,0},{7,1},{8,14},{9,15},{10,... | collective-permute-start | bytes 786440 | tf_op jit(solution)/shard_map/ppermute | solution.py:383
  76.2 3.4 %collective-permute-done.3 = bf16[128,512]{1,0:T(8,128)(2,1)S(1)} collective-permute-done((bf16[128,512]{1,0:T(8,128)(2,1)S(1)}, bf16[128,512]{1,0:T(8,128)(2,1)S(1)}, u32[]{:S(2)}, u32[]{:S(2)}) %collective-permute-start.3) | collective-permute-done | bytes 131104 | tf_op jit(solution)/shard_map/ppermute | solution.py:383
  79.6 10.6 %shard_map.73 = (bf16[512,512]{1,0:T(8,128)(2,1)S(1)}, bf16[512,1536]{1,0:T(8,128)(2,1)}, bf16[4,64,512]{2,1,0:T(8,128)(2,1)}, bf16[4,64,512]{2,1,0:T(8,128)(2,1...) custom-call(bf16[512,512]{1,0:T(8,128)(2,1)S(1)} %bitcast.59, ...), custom_call_target="tpu_custom_call" | custom-call | flops 1048576 | bytes 1024 | tf_op jit(solution)/shard_map/pallas_call | solution.py:371
  94.7 1.7 %collective-permute-start.23 = (bf16[4,16,512]{2,1,0:T(8,128)(2,1)S(1)}, bf16[4,16,512]{2,1,0:T(8,128)(2,1)S(1)}, u32[]{:S(2)}, u32[]{:S(2)}) collective-permute-start(bf16[4,16,512]{2,1,0:T(8,128)(2,1)S(1)} %get-tuple-element.170), channel_id=1, source_target_pairs={{0,8},{8,0},{16,24},{24,16},{1,9},{9,1},{17,25},{25,17},{2,10},{10... | collective-permute-start | bytes 196616 | tf_op jit(solution)/shard_map/ppermute | solution.py:383
  96.4 2.4 %collective-permute-start.24 = (bf16[4,16,512]{2,1,0:T(8,128)(2,1)S(1)}, bf16[4,16,512]{2,1,0:T(8,128)(2,1)S(1)}, u32[]{:S(2)}, u32[]{:S(2)}) collective-permute-start(bf16[4,16,512]{2,1,0:T(8,128)(2,1)S(1)} %get-tuple-element.171), channel_id=1, source_target_pairs={{0,16},{8,24},{16,0},{24,8},{1,17},{9,25},{17,1},{25,9},{2,18},{10... | collective-permute-start | bytes 196616 | tf_op jit(solution)/shard_map/ppermute | solution.py:383
  99.2 1.7 %collective-permute-start.17 = (bf16[4,64,512]{2,1,0:T(8,128)(2,1)S(1)}, bf16[4,64,512]{2,1,0:T(8,128)(2,1)S(1)}, u32[]{:S(2)}, u32[]{:S(2)}) collective-permute-start(bf16[4,64,512]{2,1,0:T(8,128)(2,1)S(1)} %get-tuple-element.150), channel_id=1, source_target_pairs={{0,2},{1,3},{2,0},{3,1},{4,6},{5,7},{6,4},{7,5},{8,10},{9,11},{10,... | collective-permute-start | bytes 786440 | tf_op jit(solution)/shard_map/ppermute | solution.py:383
  102.3 4.1 %shard_map.75 = bf16[8,2,32,512]{3,2,1,0:T(8,128)(2,1)} custom-call(bf16[8,2,32,512]{3,2,1,0:T(8,128)(2,1)S(1)} %all-to-all-done.x_ref, bf16[512,512]{1,0:T(8,128)(2,1)S(1)} %get-tuple-element.155.dm_ref, f32[2,512]{1,0:T(2,128)S(1)} %copy-done.3, bf16[512,1536]{1,0:T(8,128)(2,1)} %get-tuple-element.156.dqkv_hbm, bf16[2,4,512,512]{3,2,1,0:T(8,128)(2,1)} %w_hbm.9), custom_call_target="tpu_custom_call" | custom-call | flops 1048576 | bytes 1024 | tf_op jit(solution)/shard_map/pallas_call | solution.py:371
  108.5 1.9 %collective-permute-start.16 = (bf16[128,512]{1,0:T(8,128)(2,1)S(1)}, bf16[128,512]{1,0:T(8,128)(2,1)S(1)}, u32[]{:S(2)}, u32[]{:S(2)}) collective-permute-start(bf16[128,512]{1,0:T(8,128)(2,1)S(1)} %copy-done.6), channel_id=1, source_target_pairs={{0,24},{8,16},{16,8},{24,0},{1,25},{9,17},{17,9},{25,1},{2,26},{10... | collective-permute-start | bytes 393224 | tf_op jit(solution)/shard_map/ppermute | solution.py:383
  110.5 7.8 %collective-permute-done.15 = bf16[128,512]{1,0:T(8,128)(2,1)S(1)} collective-permute-done((bf16[128,512]{1,0:T(8,128)(2,1)S(1)}, bf16[128,512]{1,0:T(8,128)(2,1)S(1)}, u32[]{:S(2)}, u32[]{:S(2)}) %collective-permute-start.15) | collective-permute-done | bytes 131104 | tf_op jit(solution)/shard_map/ppermute | solution.py:383
  118.5 2.8 %collective-permute-start.21 = (bf16[4,16,512]{2,1,0:T(8,128)(2,1)S(1)}, bf16[4,16,512]{2,1,0:T(8,128)(2,1)S(1)}, u32[]{:S(2)}, u32[]{:S(2)}) collective-permute-start(bf16[4,16,512]{2,1,0:T(8,128)(2,1)S(1)} %get-tuple-element.168), channel_id=1, source_target_pairs={{0,16},{8,24},{16,0},{24,8},{1,17},{9,25},{17,1},{25,9},{2,18},{10... | collective-permute-start | bytes 196616 | tf_op jit(solution)/shard_map/ppermute | solution.py:383
  122.9 3.7 %all-to-all-start.3 = ((bf16[8,2,32,512]{3,2,1,0:T(8,128)(2,1)}), bf16[8,2,32,512]{3,2,1,0:T(8,128)(2,1)S(1)}, u32[]{:S(2)}, u32[]{:S(2)}) async-start(bf16[8,2,32,512]{3,2,1,0:T(8,128)(2,1)} %shard_map.75), calls=%async_computation.3 | async-start | bytes 1048576 | tf_op jit(solution)/shard_map/all_to_all | solution.py:511
  128.1 8.2 %all-to-all-done.3 = bf16[8,2,32,512]{3,2,1,0:T(8,128)(2,1)S(1)} async-done(((bf16[8,2,32,512]{3,2,1,0:T(8,128)(2,1)}), bf16[8,2,32,512]{3,2,1,0:T(8,128)(2,1)S(1)}, u32[]{:S(2)}, u32[]{:S(2)}) %all-to-all-start.3) | async-done | bytes 524320 | tf_op jit(solution)/shard_map/all_to_all | solution.py:511
  (77 shorter events, 22.3 us)
Async XLA Ops:
  0.6 14.9 %all-to-all-start = ((bf16[8,2,32,512]{3,2,1,0:T(8,128)(2,1)}), bf16[8,2,32,512]{3,2,1,0:T(8,128)(2,1)S(1)}, u32[]{:S(2)}, u32[]{:S(2)}) async-start(bf16[8,2,32,512]{3,2,1,0:T(8,128)(2,1)} %bitcast.69), calls=%async_computation | async-start | bytes 1048576 | tf_op jit(solution)/shard_map/all_to_all | solution.py:451
  7.0 16.8 %collective-permute-start = (bf16[16,8,512]{2,1,0:T(8,128)(2,1)S(1)}, bf16[16,8,512]{2,1,0:T(8,128)(2,1)S(1)}, u32[]{:S(2)}, u32[]{:S(2)}) collective-permute-start(bf16[16,8,512]{2,1,0:T(8,128)(2,1)S(1)} %get-tuple-element.164), channel_id=1, source_target_pairs={{0,8},{8,0},{16,24},{24,16},{1,9},{9,1},{17,25},{25,17},{2,10},{10... | collective-permute-start | bytes 393224 | tf_op jit(solution)/shard_map/ppermute | solution.py:383
  8.6 15.1 %collective-permute-start.1 = (bf16[16,8,512]{2,1,0:T(8,128)(2,1)S(1)}, bf16[16,8,512]{2,1,0:T(8,128)(2,1)S(1)}, u32[]{:S(2)}, u32[]{:S(2)}) collective-permute-start(bf16[16,8,512]{2,1,0:T(8,128)(2,1)S(1)} %get-tuple-element.166), channel_id=1, source_target_pairs={{0,16},{8,24},{16,0},{24,8},{1,17},{9,25},{17,1},{25,9},{2,18},{10... | collective-permute-start | bytes 393224 | tf_op jit(solution)/shard_map/ppermute | solution.py:383
  11.2 12.6 %collective-permute-start.2 = (bf16[16,8,512]{2,1,0:T(8,128)(2,1)S(1)}, bf16[16,8,512]{2,1,0:T(8,128)(2,1)S(1)}, u32[]{:S(2)}, u32[]{:S(2)}) collective-permute-start(bf16[16,8,512]{2,1,0:T(8,128)(2,1)S(1)} %get-tuple-element.163), channel_id=1, source_target_pairs={{0,24},{8,16},{16,8},{24,0},{1,25},{9,17},{17,9},{25,1},{2,26},{10... | collective-permute-start | bytes 393224 | tf_op jit(solution)/shard_map/ppermute | solution.py:383
  24.4 20.0 %all-to-all-start.1 = ((bf16[32,16,512]{2,1,0:T(8,128)(2,1)}), bf16[32,16,512]{2,1,0:T(8,128)(2,1)S(1)}, u32[]{:S(2)}, u32[]{:S(2)}) async-start(bf16[32,16,512]{2,1,0:T(8,128)(2,1)} %bitcast.71), calls=%async_computation.1 | async-start | bytes 1048576 | tf_op jit(solution)/shard_map/all_to_all | solution.py:449
  57.7 21.8 %all-to-all-start.2 = ((bf16[32,16,512]{2,1,0:T(8,128)(2,1)}), bf16[32,16,512]{2,1,0:T(8,128)(2,1)S(1)}, u32[]{:S(2)}, u32[]{:S(2)}) async-start(bf16[32,16,512]{2,1,0:T(8,128)(2,1)} %bitcast.70), calls=%async_computation.2 | async-start | bytes 1048576 | tf_op jit(solution)/shard_map/all_to_all | solution.py:449
  67.4 2.3 %collective-permute-start.7 = (bf16[4,64,512]{2,1,0:T(8,128)(2,1)}, bf16[4,64,512]{2,1,0:T(8,128)(2,1)S(1)}, u32[]{:S(2)}, u32[]{:S(2)}) collective-permute-start(bf16[4,64,512]{2,1,0:T(8,128)(2,1)} %get-tuple-element.108), channel_id=1, source_target_pairs={{0,1},{1,0},{2,3},{3,2},{4,5},{5,4},{6,7},{7,6},{8,9},{9,8},{10,11... | collective-permute-start | bytes 786440 | tf_op jit(solution)/shard_map/ppermute | solution.py:383
  71.0 19.2 %collective-permute-start.10 = (bf16[4,64,512]{2,1,0:T(8,128)(2,1)S(1)}, bf16[4,64,512]{2,1,0:T(8,128)(2,1)S(1)}, u32[]{:S(2)}, u32[]{:S(2)}) collective-permute-start(bf16[4,64,512]{2,1,0:T(8,128)(2,1)S(1)} %get-tuple-element.112), channel_id=1, source_target_pairs={{0,6},{1,7},{2,4},{3,5},{4,2},{5,3},{6,0},{7,1},{8,14},{9,15},{10,... | collective-permute-start | bytes 786440 | tf_op jit(solution)/shard_map/ppermute | solution.py:383
  73.6 16.6 %collective-permute-start.8 = (bf16[4,64,512]{2,1,0:T(8,128)(2,1)S(1)}, bf16[4,64,512]{2,1,0:T(8,128)(2,1)S(1)}, u32[]{:S(2)}, u32[]{:S(2)}) collective-permute-start(bf16[4,64,512]{2,1,0:T(8,128)(2,1)S(1)} %get-tuple-element.110), channel_id=1, source_target_pairs={{0,2},{1,3},{2,0},{3,1},{4,6},{5,7},{6,4},{7,5},{8,10},{9,11},{10,... | collective-permute-start | bytes 786440 | tf_op jit(solution)/shard_map/ppermute | solution.py:383
  74.2 16.1 %collective-permute-start.9 = (bf16[4,64,512]{2,1,0:T(8,128)(2,1)S(1)}, bf16[4,64,512]{2,1,0:T(8,128)(2,1)S(1)}, u32[]{:S(2)}, u32[]{:S(2)}) collective-permute-start(bf16[4,64,512]{2,1,0:T(8,128)(2,1)S(1)} %get-tuple-element.111), channel_id=1, source_target_pairs={{0,4},{1,5},{2,6},{3,7},{4,0},{5,1},{6,2},{7,3},{8,12},{9,13},{10,... | collective-permute-start | bytes 786440 | tf_op jit(solution)/shard_map/ppermute | solution.py:383
  74.6 5.0 %collective-permute-start.3 = (bf16[128,512]{1,0:T(8,128)(2,1)S(1)}, bf16[128,512]{1,0:T(8,128)(2,1)S(1)}, u32[]{:S(2)}, u32[]{:S(2)}) collective-permute-start(bf16[128,512]{1,0:T(8,128)(2,1)S(1)} %copy-done.8), channel_id=1, source_target_pairs={{0,8},{8,0},{16,24},{24,16},{1,9},{9,1},{17,25},{25,17},{2,10},{10... | collective-permute-start | bytes 393224 | tf_op jit(solution)/shard_map/ppermute | solution.py:383
  90.9 2.3 %collective-permute-start.14 = (bf16[4,64,512]{2,1,0:T(8,128)(2,1)}, bf16[4,64,512]{2,1,0:T(8,128)(2,1)S(1)}, u32[]{:S(2)}, u32[]{:S(2)}) collective-permute-start(bf16[4,64,512]{2,1,0:T(8,128)(2,1)} %get-tuple-element.148), channel_id=1, source_target_pairs={{0,1},{1,0},{2,3},{3,2},{4,5},{5,4},{6,7},{7,6},{8,9},{9,8},{10,11... | collective-permute-start | bytes 786440 | tf_op jit(solution)/shard_map/ppermute | solution.py:383
  94.7 11.7 %collective-permute-start.23 = (bf16[4,16,512]{2,1,0:T(8,128)(2,1)S(1)}, bf16[4,16,512]{2,1,0:T(8,128)(2,1)S(1)}, u32[]{:S(2)}, u32[]{:S(2)}) collective-permute-start(bf16[4,16,512]{2,1,0:T(8,128)(2,1)S(1)} %get-tuple-element.170), channel_id=1, source_target_pairs={{0,8},{8,0},{16,24},{24,16},{1,9},{9,1},{17,25},{25,17},{2,10},{10... | collective-permute-start | bytes 196616 | tf_op jit(solution)/shard_map/ppermute | solution.py:383
  96.4 10.5 %collective-permute-start.24 = (bf16[4,16,512]{2,1,0:T(8,128)(2,1)S(1)}, bf16[4,16,512]{2,1,0:T(8,128)(2,1)S(1)}, u32[]{:S(2)}, u32[]{:S(2)}) collective-permute-start(bf16[4,16,512]{2,1,0:T(8,128)(2,1)S(1)} %get-tuple-element.171), channel_id=1, source_target_pairs={{0,16},{8,24},{16,0},{24,8},{1,17},{9,25},{17,1},{25,9},{2,18},{10... | collective-permute-start | bytes 196616 | tf_op jit(solution)/shard_map/ppermute | solution.py:383
  98.8 9.7 %collective-permute-start.25 = (bf16[4,16,512]{2,1,0:T(8,128)(2,1)S(1)}, bf16[4,16,512]{2,1,0:T(8,128)(2,1)S(1)}, u32[]{:S(2)}, u32[]{:S(2)}) collective-permute-start(bf16[4,16,512]{2,1,0:T(8,128)(2,1)S(1)} %get-tuple-element.172), channel_id=1, source_target_pairs={{0,24},{8,16},{16,8},{24,0},{1,25},{9,17},{17,9},{25,1},{2,26},{10... | collective-permute-start | bytes 196616 | tf_op jit(solution)/shard_map/ppermute | solution.py:383
  99.2 19.1 %collective-permute-start.17 = (bf16[4,64,512]{2,1,0:T(8,128)(2,1)S(1)}, bf16[4,64,512]{2,1,0:T(8,128)(2,1)S(1)}, u32[]{:S(2)}, u32[]{:S(2)}) collective-permute-start(bf16[4,64,512]{2,1,0:T(8,128)(2,1)S(1)} %get-tuple-element.150), channel_id=1, source_target_pairs={{0,2},{1,3},{2,0},{3,1},{4,6},{5,7},{6,4},{7,5},{8,10},{9,11},{10,... | collective-permute-start | bytes 786440 | tf_op jit(solution)/shard_map/ppermute | solution.py:383
  100.8 17.4 %collective-permute-start.18 = (bf16[4,64,512]{2,1,0:T(8,128)(2,1)S(1)}, bf16[4,64,512]{2,1,0:T(8,128)(2,1)S(1)}, u32[]{:S(2)}, u32[]{:S(2)}) collective-permute-start(bf16[4,64,512]{2,1,0:T(8,128)(2,1)S(1)} %get-tuple-element.151), channel_id=1, source_target_pairs={{0,4},{1,5},{2,6},{3,7},{4,0},{5,1},{6,2},{7,3},{8,12},{9,13},{10,... | collective-permute-start | bytes 786440 | tf_op jit(solution)/shard_map/ppermute | solution.py:383
  106.4 11.9 %collective-permute-start.19 = (bf16[4,64,512]{2,1,0:T(8,128)(2,1)S(1)}, bf16[4,64,512]{2,1,0:T(8,128)(2,1)S(1)}, u32[]{:S(2)}, u32[]{:S(2)}) collective-permute-start(bf16[4,64,512]{2,1,0:T(8,128)(2,1)S(1)} %get-tuple-element.152), channel_id=1, source_target_pairs={{0,6},{1,7},{2,4},{3,5},{4,2},{5,3},{6,0},{7,1},{8,14},{9,15},{10,... | collective-permute-start | bytes 786440 | tf_op jit(solution)/shard_map/ppermute | solution.py:383
  106.9 11.3 %collective-permute-start.15 = (bf16[128,512]{1,0:T(8,128)(2,1)S(1)}, bf16[128,512]{1,0:T(8,128)(2,1)S(1)}, u32[]{:S(2)}, u32[]{:S(2)}) collective-permute-start(bf16[128,512]{1,0:T(8,128)(2,1)S(1)} %copy-done.7), channel_id=1, source_target_pairs={{0,16},{8,24},{16,0},{24,8},{1,17},{9,25},{17,1},{25,9},{2,18},{10... | collective-permute-start | bytes 393224 | tf_op jit(solution)/shard_map/ppermute | solution.py:383
  108.5 18.1 %collective-permute-start.16 = (bf16[128,512]{1,0:T(8,128)(2,1)S(1)}, bf16[128,512]{1,0:T(8,128)(2,1)S(1)}, u32[]{:S(2)}, u32[]{:S(2)}) collective-permute-start(bf16[128,512]{1,0:T(8,128)(2,1)S(1)} %copy-done.6), channel_id=1, source_target_pairs={{0,24},{8,16},{16,8},{24,0},{1,25},{9,17},{17,9},{25,1},{2,26},{10... | collective-permute-start | bytes 393224 | tf_op jit(solution)/shard_map/ppermute | solution.py:383
  118.5 8.2 %collective-permute-start.20 = (bf16[4,16,512]{2,1,0:T(8,128)(2,1)S(1)}, bf16[4,16,512]{2,1,0:T(8,128)(2,1)S(1)}, u32[]{:S(2)}, u32[]{:S(2)}) collective-permute-start(bf16[4,16,512]{2,1,0:T(8,128)(2,1)S(1)} %get-tuple-element.167), channel_id=1, source_target_pairs={{0,8},{8,0},{16,24},{24,16},{1,9},{9,1},{17,25},{25,17},{2,10},{10... | collective-permute-start | bytes 196616 | tf_op jit(solution)/shard_map/ppermute | solution.py:383
  118.5 8.1 %collective-permute-start.21 = (bf16[4,16,512]{2,1,0:T(8,128)(2,1)S(1)}, bf16[4,16,512]{2,1,0:T(8,128)(2,1)S(1)}, u32[]{:S(2)}, u32[]{:S(2)}) collective-permute-start(bf16[4,16,512]{2,1,0:T(8,128)(2,1)S(1)} %get-tuple-element.168), channel_id=1, source_target_pairs={{0,16},{8,24},{16,0},{24,8},{1,17},{9,25},{17,1},{25,9},{2,18},{10... | collective-permute-start | bytes 196616 | tf_op jit(solution)/shard_map/ppermute | solution.py:383
  121.3 6.1 %collective-permute-start.22 = (bf16[4,16,512]{2,1,0:T(8,128)(2,1)S(1)}, bf16[4,16,512]{2,1,0:T(8,128)(2,1)S(1)}, u32[]{:S(2)}, u32[]{:S(2)}) collective-permute-start(bf16[4,16,512]{2,1,0:T(8,128)(2,1)S(1)} %get-tuple-element.169), channel_id=1, source_target_pairs={{0,24},{8,16},{16,8},{24,0},{1,25},{9,17},{17,9},{25,1},{2,26},{10... | collective-permute-start | bytes 196616 | tf_op jit(solution)/shard_map/ppermute | solution.py:383
  122.9 13.4 %all-to-all-start.3 = ((bf16[8,2,32,512]{3,2,1,0:T(8,128)(2,1)}), bf16[8,2,32,512]{3,2,1,0:T(8,128)(2,1)S(1)}, u32[]{:S(2)}, u32[]{:S(2)}) async-start(bf16[8,2,32,512]{3,2,1,0:T(8,128)(2,1)} %shard_map.75), calls=%async_computation.3 | async-start | bytes 1048576 | tf_op jit(solution)/shard_map/all_to_all | solution.py:511
  (15 other events, 95.1 us)

commit v10 on v9

--- a/solution.py
+++ b/solution.py
@@ -491,7 +491,7 @@
     sums_b = chip_sums(grads[:plane], grads[plane:], col_parts)
     pieces_b = plane_pieces(sums_b, plane, core)
     near, far = [outs[0], swap(outs[1], "row", row_parts, 1)], outs[2:]
-    d_mid, near, far, _ = lax.optimization_barrier((d_mid, near, far, sums_b))
+    d_mid, far, _ = lax.optimization_barrier((d_mid, far, sums_b))
     results = call(
         functools.partial(row_back, (rows, length, width, plane)),
         at(ANY, d_mid) + at(FAR, weights, turn, normed, query, key, value, attended, prob),
@@ -499,21 +499,22 @@
         [square, scratch(2, *flat)] + [square] * 5 + [scratch(*probs), square, scratch(*triple)]
         + [scratch(plane, *packed), scratch(plane, *packed), copies((11,)), copies((2 * plane,))],
     )
-    (d_mid, dqkv, *grads), pieces_b, far = lax.optimization_barrier((results, pieces_b, far))
+    (d_mid, dqkv, *grads), pieces_b, near = lax.optimization_barrier((results, pieces_b, near))
     sums_a = chip_sums(grads[:plane], grads[plane:], col_parts)
     pieces_a = plane_pieces(sums_a, plane, core)
-    dqkv, pieces_b, far, _ = lax.optimization_barrier((dqkv, pieces_b, far, sums_a))
+    dqkv, _ = lax.optimization_barrier((dqkv, sums_a))
     field_grad, = call(
         field_back, at(ANY, x, d_mid, gains) + at(FAR, dqkv, weights), at(FAR, x.shape),
         [scratch(*triple), scratch(3, *flat), scratch(*x.shape), copies((3,))],
     )
-    field_grad, pieces_a[1] = lax.optimization_barrier((field_grad, pieces_a[1]))
-    field_grad = lax.all_to_all(field_grad, "col", 0, 0, tiled=True).reshape(high, wide, channels)
+    field_grad, pieces_a[1], pieces_b, far = lax.optimization_barrier((field_grad, pieces_a[1], pieces_b, far))
     grads_b = last_sums(pieces_b, row_parts)
     output = jnp.zeros((high, wide, channels), BF16)
     for step, piece in enumerate((*near, *far)):
         piece = (piece if step < 2 else swap(piece, "row", row_parts, step)).reshape(high, cols, channels)
         output = lax.dynamic_update_slice_in_dim(output, piece, (my_row ^ step) * cols, axis=1)
+    field_grad = lax.all_to_all(field_grad, "col", 0, 0, tiled=True).reshape(high, wide, channels)
+    field_grad, pieces_a = lax.optimization_barrier((field_grad, pieces_a))
     grads_a = last_sums(pieces_a, row_parts)
     return output, field_grad, jnp.concatenate([grads_a, grads_b], axis=0)
 

time: 138 us -> 135 us (0.978)
  waiting for transfers between devices: 38.2 us -> 35 us
    all_to_all x1, waiting for transfers between devices: 8.22 us -> 0.01 us  [body(): lax.all_to_all(field_grad, 'col', 0, 0, tiled=True)]
    ppermute x26, waiting for transfers between devices: 15.5 us -> 20.3 us  [swap(): return lax.ppermute(item, axis, [(at, at ^ step) for at in range(count)])]
  transfers between devices with their start and end apart: 30 -> 30, of which waited for: 14 -> 16; matrix products, arithmetic and copies ran while one was open for 2% -> 2% of each run, Pallas kernels for 25% -> 25%
where the time goes in v10:
time: 135 us; the launch traced here: 134 us
  Pallas kernels  48.8 us (36%)
  starting transfers between devices  43.9 us (33%)
  waiting for transfers between devices  35 us (26%)
  local copies, waits for them, and re-layouts  3.63 us (3%)
  other arithmetic  1.95 us (1%)
    pallas_call x9, Pallas kernels, call(): pl.pallas_call(kernel, in_specs=[spec(where) for _, where in ins], out_sp...  48.8 us
    ppermute x26, starting transfers between devices, swap(): return lax.ppermute(item, axis, [(at, at ^ step) for at in range(count)])  27.5 us
    ppermute x26, waiting for transfers between devices, swap(): return lax.ppermute(item, axis, [(at, at ^ step) for at in range(count)])  20.3 us
    all_to_all x2, waiting for transfers between devices, all_to_all(): lax.all_to_all(item, ('row', 'col'), 0, 0, tiled=True)  12.8 us
    all_to_all x2, starting transfers between devices, all_to_all(): lax.all_to_all(item, ('row', 'col'), 0, 0, tiled=True)  7.72 us
    all_to_all x1, starting transfers between devices, body(): lax.all_to_all(field.reshape(col_parts, rows, wide, channels), 'col', 0,...  5.18 us
    all_to_all x1, starting transfers between devices, body(): lax.all_to_all(field_grad, 'col', 0, 0, tiled=True)  3.49 us
  transfers between devices with their start and end apart: 30, of which 16 were waited for; matrix products, arithmetic and copies ran while one was open for 2% of the time, Pallas kernels for 25%

profile of v10, /device:TPU:0, one launch (start us, length us, event | category | flops | bytes accessed | tf_op | source)
XLA Modules:
  0.0 134.3 jit_solution(9729252326510863989)
XLA Ops:
  0.6 5.2 %all-to-all-start = ((bf16[8,2,32,512]{3,2,1,0:T(8,128)(2,1)}), bf16[8,2,32,512]{3,2,1,0:T(8,128)(2,1)S(1)}, u32[]{:S(2)}, u32[]{:S(2)}) async-start(bf16[8,2,32,512]{3,2,1,0:T(8,128)(2,1)} %bitcast.69), calls=%async_computation | async-start | bytes 1048576 | tf_op jit(solution)/shard_map/all_to_all | solution.py:451
  7.0 1.6 %collective-permute-start = (bf16[16,8,512]{2,1,0:T(8,128)(2,1)S(1)}, bf16[16,8,512]{2,1,0:T(8,128)(2,1)S(1)}, u32[]{:S(2)}, u32[]{:S(2)}) collective-permute-start(bf16[16,8,512]{2,1,0:T(8,128)(2,1)S(1)} %get-tuple-element.170), channel_id=1, source_target_pairs={{0,8},{8,0},{16,24},{24,16},{1,9},{9,1},{17,25},{25,17},{2,10},{10... | collective-permute-start | bytes 393224 | tf_op jit(solution)/shard_map/ppermute | solution.py:383
  8.6 2.6 %collective-permute-start.1 = (bf16[16,8,512]{2,1,0:T(8,128)(2,1)S(1)}, bf16[16,8,512]{2,1,0:T(8,128)(2,1)S(1)}, u32[]{:S(2)}, u32[]{:S(2)}) collective-permute-start(bf16[16,8,512]{2,1,0:T(8,128)(2,1)S(1)} %get-tuple-element.172), channel_id=1, source_target_pairs={{0,16},{8,24},{16,0},{24,8},{1,17},{9,25},{17,1},{25,9},{2,18},{10... | collective-permute-start | bytes 393224 | tf_op jit(solution)/shard_map/ppermute | solution.py:383
  11.4 2.2 %shard_map.67.turn_hbm.refs_5_ = bf16[7,512,512]{2,1,0:T(8,128)(2,1)} custom-call(), custom_call_target="tpu_custom_call" | custom-call | flops 1048576 | bytes 1024 | tf_op jit(solution)/shard_map/pallas_call | solution.py:371
  13.7 1.9 %all-to-all-done.x_ref = bf16[8,2,32,512]{3,2,1,0:T(8,128)(2,1)S(1)} async-done(((bf16[8,2,32,512]{3,2,1,0:T(8,128)(2,1)}), bf16[8,2,32,512]{3,2,1,0:T(8,128)(2,1)S(1)}, u32[]{:S(2)}, u32[]{:S(2)}) %all-to-all-start) | async-done | bytes 524320 | tf_op jit(solution)/shard_map/all_to_all | solution.py:451
  15.6 8.2 %shard_map.68 = (bf16[512,512]{1,0:T(8,128)(2,1)}, bf16[512,512]{1,0:T(8,128)(2,1)}, bf16[512,512]{1,0:T(8,128)(2,1)}, bf16[512,512]{1,0:T(8,128)(2,1)}, bf16[51...) custom-call(bf16[8,2,32,512]{3,2,1,0:T(8,128)(2,1)S(1)} %all-to-all-done.x_ref, ...), custom_call_target="tpu_custom_call" | custom-call | flops 1048576 | bytes 1024 | tf_op jit(solution)/shard_map/pallas_call | solution.py:371
  24.4 4.4 %all-to-all-start.1 = ((bf16[32,16,512]{2,1,0:T(8,128)(2,1)}), bf16[32,16,512]{2,1,0:T(8,128)(2,1)S(1)}, u32[]{:S(2)}, u32[]{:S(2)}) async-start(bf16[32,16,512]{2,1,0:T(8,128)(2,1)} %bitcast.71), calls=%async_computation.1 | async-start | bytes 1048576 | tf_op jit(solution)/shard_map/all_to_all | solution.py:449
  29.8 2.0 %shard_map.69 = (bf16[512,512]{1,0:T(8,128)(2,1)S(1)}, bf16[512,512]{1,0:T(8,128)(2,1)S(1)}, bf16[2,512,512]{2,1,0:T(8,128)(2,1)S(1)}) custom-call(bf16[128,512]{1,0:T(8,128)(2,1)S(1)} %get-tuple-element.88.refs_0_, bf16[128,512]{1,0:T(8,128)(2,1)S(1)} %bitcast.61, bf16[128,512]{1,0:T(8,128)(2,1)S(1)} %bitcast.62, bf16[128,512]{1,0:T(8,128)(2,1)S(1)} %bitcast.63, ...), custom_call_target="tpu_custom_call" | custom-call | flops 1048576 | bytes 1024 | tf_op jit(solution)/shard_map/pallas_call | solution.py:371
  31.8 12.6 %all-to-all-done.1 = bf16[32,16,512]{2,1,0:T(8,128)(2,1)S(1)} async-done(((bf16[32,16,512]{2,1,0:T(8,128)(2,1)}), bf16[32,16,512]{2,1,0:T(8,128)(2,1)S(1)}, u32[]{:S(2)}, u32[]{:S(2)}) %all-to-all-start.1) | async-done | bytes 524320 | tf_op jit(solution)/shard_map/all_to_all | solution.py:449
  44.4 13.3 %shard_map.70 = (bf16[512,512]{1,0:T(8,128)(2,1)}, bf16[512,512]{1,0:T(8,128)(2,1)}, bf16[512,512]{1,0:T(8,128)(2,1)}, bf16[512,512]{1,0:T(8,128)(2,1)}, bf16[512,1536]{1,0:T(8,128)(2,1)}) custom-call(bf16[512,512]{1,0:T(8,128)(2,1)S(1)} %bitcast.60, bf16[512,512]{1,0:T(8,128)(2,1)S(1)} %get-tuple-element.92.cot_ref.cot_hbm, ...), custom_call_target="tpu_custom_call" | custom-call | flops 1048576 | bytes 1024 | tf_op jit(solution)/shard_map/pallas_call | solution.py:371
  57.7 3.3 %all-to-all-start.2 = ((bf16[32,16,512]{2,1,0:T(8,128)(2,1)}), bf16[32,16,512]{2,1,0:T(8,128)(2,1)S(1)}, u32[]{:S(2)}, u32[]{:S(2)}) async-start(bf16[32,16,512]{2,1,0:T(8,128)(2,1)} %bitcast.70), calls=%async_computation.2 | async-start | bytes 1048576 | tf_op jit(solution)/shard_map/all_to_all | solution.py:449
  61.0 5.7 %shard_map.71 = (bf16[128,512]{1,0:T(8,128)(2,1)}, bf16[128,512]{1,0:T(8,128)(2,1)}, bf16[128,512]{1,0:T(8,128)(2,1)}, bf16[128,512]{1,0:T(8,128)(2,1)}, bf16[4,...) custom-call(bf16[512,512]{1,0:T(8,128)(2,1)} %copy-done, ...), custom_call_target="tpu_custom_call" | custom-call | flops 1048576 | bytes 1024 | tf_op jit(solution)/shard_map/pallas_call | solution.py:371
  71.1 1.7 %collective-permute-start.7 = (bf16[4,64,512]{2,1,0:T(8,128)(2,1)S(1)}, bf16[4,64,512]{2,1,0:T(8,128)(2,1)S(1)}, u32[]{:S(2)}, u32[]{:S(2)}) collective-permute-start(bf16[4,64,512]{2,1,0:T(8,128)(2,1)S(1)} %get-tuple-element.111), channel_id=1, source_target_pairs={{0,2},{1,3},{2,0},{3,1},{4,6},{5,7},{6,4},{7,5},{8,10},{9,11},{10,... | collective-permute-start | bytes 786440 | tf_op jit(solution)/shard_map/ppermute | solution.py:383
  72.7 1.5 %collective-permute-start.8 = (bf16[4,64,512]{2,1,0:T(8,128)(2,1)S(1)}, bf16[4,64,512]{2,1,0:T(8,128)(2,1)S(1)}, u32[]{:S(2)}, u32[]{:S(2)}) collective-permute-start(bf16[4,64,512]{2,1,0:T(8,128)(2,1)S(1)} %get-tuple-element.112), channel_id=1, source_target_pairs={{0,4},{1,5},{2,6},{3,7},{4,0},{5,1},{6,2},{7,3},{8,12},{9,13},{10,... | collective-permute-start | bytes 786440 | tf_op jit(solution)/shard_map/ppermute | solution.py:383
  74.6 1.6 %collective-permute-start.10 = (bf16[128,512]{1,0:T(8,128)(2,1)S(1)}, bf16[128,512]{1,0:T(8,128)(2,1)S(1)}, u32[]{:S(2)}, u32[]{:S(2)}) collective-permute-start(bf16[128,512]{1,0:T(8,128)(2,1)S(1)} %copy-done.7), channel_id=1, source_target_pairs={{0,8},{8,0},{16,24},{24,16},{1,9},{9,1},{17,25},{25,17},{2,10},{10... | collective-permute-start | bytes 393224 | tf_op jit(solution)/shard_map/ppermute | solution.py:383
  76.4 10.6 %shard_map.73 = (bf16[512,512]{1,0:T(8,128)(2,1)S(1)}, bf16[512,1536]{1,0:T(8,128)(2,1)}, bf16[4,64,512]{2,1,0:T(8,128)(2,1)}, bf16[4,64,512]{2,1,0:T(8,128)(2,1...) custom-call(bf16[512,512]{1,0:T(8,128)(2,1)S(1)} %bitcast.59, ...), custom_call_target="tpu_custom_call" | custom-call | flops 1048576 | bytes 1024 | tf_op jit(solution)/shard_map/pallas_call | solution.py:371
  92.8 4.1 %shard_map.75 = bf16[8,2,32,512]{3,2,1,0:T(8,128)(2,1)} custom-call(bf16[8,2,32,512]{3,2,1,0:T(8,128)(2,1)S(1)} %all-to-all-done.x_ref, bf16[512,512]{1,0:T(8,128)(2,1)S(1)} %get-tuple-element.135.dm_ref, f32[2,512]{1,0:T(2,128)S(1)} %copy-done.3, bf16[512,1536]{1,0:T(8,128)(2,1)} %get-tuple-element.149.dqkv_hbm, bf16[2,4,512,512]{3,2,1,0:T(8,128)(2,1)} %w_hbm.9), custom_call_target="tpu_custom_call" | custom-call | flops 1048576 | bytes 1024 | tf_op jit(solution)/shard_map/pallas_call | solution.py:371
  96.9 2.9 %collective-permute-done.15 = bf16[4,64,512]{2,1,0:T(8,128)(2,1)S(1)} collective-permute-done((bf16[4,64,512]{2,1,0:T(8,128)(2,1)S(1)}, bf16[4,64,512]{2,1,0:T(8,128)(2,1)S(1)}, u32[]{:S(2)}, u32[]{:S(2)}) %collective-permute-start.15) | collective-permute-done | bytes 262176 | tf_op jit(solution)/shard_map/ppermute | solution.py:383
  101.2 1.9 %collective-permute-start.24 = (bf16[4,16,512]{2,1,0:T(8,128)(2,1)S(1)}, bf16[4,16,512]{2,1,0:T(8,128)(2,1)S(1)}, u32[]{:S(2)}, u32[]{:S(2)}) collective-permute-start(bf16[4,16,512]{2,1,0:T(8,128)(2,1)S(1)} %get-tuple-element.177), channel_id=1, source_target_pairs={{0,16},{8,24},{16,0},{24,8},{1,17},{9,25},{17,1},{25,9},{2,18},{10... | collective-permute-start | bytes 196616 | tf_op jit(solution)/shard_map/ppermute | solution.py:383
  107.2 3.5 %all-to-all-start.3 = ((bf16[8,2,32,512]{3,2,1,0:T(8,128)(2,1)}), bf16[8,2,32,512]{3,2,1,0:T(8,128)(2,1)S(1)}, u32[]{:S(2)}, u32[]{:S(2)}) async-start(bf16[8,2,32,512]{3,2,1,0:T(8,128)(2,1)} %shard_map.75), calls=%async_computation.3 | async-start | bytes 1048576 | tf_op jit(solution)/shard_map/all_to_all | solution.py:516
  110.7 1.6 %collective-permute-start.16 = (bf16[128,512]{1,0:T(8,128)(2,1)}, bf16[128,512]{1,0:T(8,128)(2,1)S(1)}, u32[]{:S(2)}, u32[]{:S(2)}) collective-permute-start(bf16[128,512]{1,0:T(8,128)(2,1)} %get-tuple-element.156), channel_id=1, source_target_pairs={{0,16},{8,24},{16,0},{24,8},{1,17},{9,25},{17,1},{25,9},{2,18},{10... | collective-permute-start | bytes 393224 | tf_op jit(solution)/shard_map/ppermute | solution.py:383
  114.4 8.8 %collective-permute-done.16 = bf16[128,512]{1,0:T(8,128)(2,1)S(1)} collective-permute-done((bf16[128,512]{1,0:T(8,128)(2,1)}, bf16[128,512]{1,0:T(8,128)(2,1)S(1)}, u32[]{:S(2)}, u32[]{:S(2)}) %collective-permute-start.16) | collective-permute-done | bytes 131104 | tf_op jit(solution)/shard_map/ppermute | solution.py:383
  123.5 3.1 %collective-permute-start.21 = (bf16[4,16,512]{2,1,0:T(8,128)(2,1)S(1)}, bf16[4,16,512]{2,1,0:T(8,128)(2,1)S(1)}, u32[]{:S(2)}, u32[]{:S(2)}) collective-permute-start(bf16[4,16,512]{2,1,0:T(8,128)(2,1)S(1)} %get-tuple-element.174), channel_id=1, source_target_pairs={{0,16},{8,24},{16,0},{24,8},{1,17},{9,25},{17,1},{25,9},{2,18},{10... | collective-permute-start | bytes 196616 | tf_op jit(solution)/shard_map/ppermute | solution.py:383
  128.6 2.9 %collective-permute-done.21 = bf16[4,16,512]{2,1,0:T(8,128)(2,1)S(1)} collective-permute-done((bf16[4,16,512]{2,1,0:T(8,128)(2,1)S(1)}, bf16[4,16,512]{2,1,0:T(8,128)(2,1)S(1)}, u32[]{:S(2)}, u32[]{:S(2)}) %collective-permute-start.21) | collective-permute-done | bytes 65568 | tf_op jit(solution)/shard_map/ppermute | solution.py:383
  (75 shorter events, 26.1 us)
Async XLA Ops:
  0.6 14.9 %all-to-all-start = ((bf16[8,2,32,512]{3,2,1,0:T(8,128)(2,1)}), bf16[8,2,32,512]{3,2,1,0:T(8,128)(2,1)S(1)}, u32[]{:S(2)}, u32[]{:S(2)}) async-start(bf16[8,2,32,512]{3,2,1,0:T(8,128)(2,1)} %bitcast.69), calls=%async_computation | async-start | bytes 1048576 | tf_op jit(solution)/shard_map/all_to_all | solution.py:451
  7.0 16.8 %collective-permute-start = (bf16[16,8,512]{2,1,0:T(8,128)(2,1)S(1)}, bf16[16,8,512]{2,1,0:T(8,128)(2,1)S(1)}, u32[]{:S(2)}, u32[]{:S(2)}) collective-permute-start(bf16[16,8,512]{2,1,0:T(8,128)(2,1)S(1)} %get-tuple-element.170), channel_id=1, source_target_pairs={{0,8},{8,0},{16,24},{24,16},{1,9},{9,1},{17,25},{25,17},{2,10},{10... | collective-permute-start | bytes 393224 | tf_op jit(solution)/shard_map/ppermute | solution.py:383
  8.6 15.1 %collective-permute-start.1 = (bf16[16,8,512]{2,1,0:T(8,128)(2,1)S(1)}, bf16[16,8,512]{2,1,0:T(8,128)(2,1)S(1)}, u32[]{:S(2)}, u32[]{:S(2)}) collective-permute-start(bf16[16,8,512]{2,1,0:T(8,128)(2,1)S(1)} %get-tuple-element.172), channel_id=1, source_target_pairs={{0,16},{8,24},{16,0},{24,8},{1,17},{9,25},{17,1},{25,9},{2,18},{10... | collective-permute-start | bytes 393224 | tf_op jit(solution)/shard_map/ppermute | solution.py:383
  11.2 12.6 %collective-permute-start.2 = (bf16[16,8,512]{2,1,0:T(8,128)(2,1)S(1)}, bf16[16,8,512]{2,1,0:T(8,128)(2,1)S(1)}, u32[]{:S(2)}, u32[]{:S(2)}) collective-permute-start(bf16[16,8,512]{2,1,0:T(8,128)(2,1)S(1)} %get-tuple-element.169), channel_id=1, source_target_pairs={{0,24},{8,16},{16,8},{24,0},{1,25},{9,17},{17,9},{25,1},{2,26},{10... | collective-permute-start | bytes 393224 | tf_op jit(solution)/shard_map/ppermute | solution.py:383
  24.4 20.0 %all-to-all-start.1 = ((bf16[32,16,512]{2,1,0:T(8,128)(2,1)}), bf16[32,16,512]{2,1,0:T(8,128)(2,1)S(1)}, u32[]{:S(2)}, u32[]{:S(2)}) async-start(bf16[32,16,512]{2,1,0:T(8,128)(2,1)} %bitcast.71), calls=%async_computation.1 | async-start | bytes 1048576 | tf_op jit(solution)/shard_map/all_to_all | solution.py:449
  57.7 18.7 %all-to-all-start.2 = ((bf16[32,16,512]{2,1,0:T(8,128)(2,1)}), bf16[32,16,512]{2,1,0:T(8,128)(2,1)S(1)}, u32[]{:S(2)}, u32[]{:S(2)}) async-start(bf16[32,16,512]{2,1,0:T(8,128)(2,1)} %bitcast.70), calls=%async_computation.2 | async-start | bytes 1048576 | tf_op jit(solution)/shard_map/all_to_all | solution.py:449
  67.4 2.3 %collective-permute-start.6 = (bf16[4,64,512]{2,1,0:T(8,128)(2,1)}, bf16[4,64,512]{2,1,0:T(8,128)(2,1)S(1)}, u32[]{:S(2)}, u32[]{:S(2)}) collective-permute-start(bf16[4,64,512]{2,1,0:T(8,128)(2,1)} %get-tuple-element.109), channel_id=1, source_target_pairs={{0,1},{1,0},{2,3},{3,2},{4,5},{5,4},{6,7},{7,6},{8,9},{9,8},{10,11... | collective-permute-start | bytes 786440 | tf_op jit(solution)/shard_map/ppermute | solution.py:383
  71.1 16.0 %collective-permute-start.7 = (bf16[4,64,512]{2,1,0:T(8,128)(2,1)S(1)}, bf16[4,64,512]{2,1,0:T(8,128)(2,1)S(1)}, u32[]{:S(2)}, u32[]{:S(2)}) collective-permute-start(bf16[4,64,512]{2,1,0:T(8,128)(2,1)S(1)} %get-tuple-element.111), channel_id=1, source_target_pairs={{0,2},{1,3},{2,0},{3,1},{4,6},{5,7},{6,4},{7,5},{8,10},{9,11},{10,... | collective-permute-start | bytes 786440 | tf_op jit(solution)/shard_map/ppermute | solution.py:383
  72.7 14.3 %collective-permute-start.8 = (bf16[4,64,512]{2,1,0:T(8,128)(2,1)S(1)}, bf16[4,64,512]{2,1,0:T(8,128)(2,1)S(1)}, u32[]{:S(2)}, u32[]{:S(2)}) collective-permute-start(bf16[4,64,512]{2,1,0:T(8,128)(2,1)S(1)} %get-tuple-element.112), channel_id=1, source_target_pairs={{0,4},{1,5},{2,6},{3,7},{4,0},{5,1},{6,2},{7,3},{8,12},{9,13},{10,... | collective-permute-start | bytes 786440 | tf_op jit(solution)/shard_map/ppermute | solution.py:383
  74.2 12.9 %collective-permute-start.9 = (bf16[4,64,512]{2,1,0:T(8,128)(2,1)S(1)}, bf16[4,64,512]{2,1,0:T(8,128)(2,1)S(1)}, u32[]{:S(2)}, u32[]{:S(2)}) collective-permute-start(bf16[4,64,512]{2,1,0:T(8,128)(2,1)S(1)} %get-tuple-element.113), channel_id=1, source_target_pairs={{0,6},{1,7},{2,4},{3,5},{4,2},{5,3},{6,0},{7,1},{8,14},{9,15},{10,... | collective-permute-start | bytes 786440 | tf_op jit(solution)/shard_map/ppermute | solution.py:383
  74.6 12.4 %collective-permute-start.10 = (bf16[128,512]{1,0:T(8,128)(2,1)S(1)}, bf16[128,512]{1,0:T(8,128)(2,1)S(1)}, u32[]{:S(2)}, u32[]{:S(2)}) collective-permute-start(bf16[128,512]{1,0:T(8,128)(2,1)S(1)} %copy-done.7), channel_id=1, source_target_pairs={{0,8},{8,0},{16,24},{24,16},{1,9},{9,1},{17,25},{25,17},{2,10},{10... | collective-permute-start | bytes 393224 | tf_op jit(solution)/shard_map/ppermute | solution.py:383
  87.7 2.3 %collective-permute-start.14 = (bf16[4,64,512]{2,1,0:T(8,128)(2,1)}, bf16[4,64,512]{2,1,0:T(8,128)(2,1)S(1)}, u32[]{:S(2)}, u32[]{:S(2)}) collective-permute-start(bf16[4,64,512]{2,1,0:T(8,128)(2,1)} %get-tuple-element.144), channel_id=1, source_target_pairs={{0,1},{1,0},{2,3},{3,2},{4,5},{5,4},{6,7},{7,6},{8,9},{9,8},{10,11... | collective-permute-start | bytes 786440 | tf_op jit(solution)/shard_map/ppermute | solution.py:383
  91.3 8.4 %collective-permute-start.15 = (bf16[4,64,512]{2,1,0:T(8,128)(2,1)S(1)}, bf16[4,64,512]{2,1,0:T(8,128)(2,1)S(1)}, u32[]{:S(2)}, u32[]{:S(2)}) collective-permute-start(bf16[4,64,512]{2,1,0:T(8,128)(2,1)S(1)} %get-tuple-element.146), channel_id=1, source_target_pairs={{0,2},{1,3},{2,0},{3,1},{4,6},{5,7},{6,4},{7,5},{8,10},{9,11},{10,... | collective-permute-start | bytes 786440 | tf_op jit(solution)/shard_map/ppermute | solution.py:383
  99.9 10.8 %collective-permute-start.23 = (bf16[4,16,512]{2,1,0:T(8,128)(2,1)S(1)}, bf16[4,16,512]{2,1,0:T(8,128)(2,1)S(1)}, u32[]{:S(2)}, u32[]{:S(2)}) collective-permute-start(bf16[4,16,512]{2,1,0:T(8,128)(2,1)S(1)} %get-tuple-element.176), channel_id=1, source_target_pairs={{0,8},{8,0},{16,24},{24,16},{1,9},{9,1},{17,25},{25,17},{2,10},{10... | collective-permute-start | bytes 196616 | tf_op jit(solution)/shard_map/ppermute | solution.py:383
  101.2 11.1 %collective-permute-start.24 = (bf16[4,16,512]{2,1,0:T(8,128)(2,1)S(1)}, bf16[4,16,512]{2,1,0:T(8,128)(2,1)S(1)}, u32[]{:S(2)}, u32[]{:S(2)}) collective-permute-start(bf16[4,16,512]{2,1,0:T(8,128)(2,1)S(1)} %get-tuple-element.177), channel_id=1, source_target_pairs={{0,16},{8,24},{16,0},{24,8},{1,17},{9,25},{17,1},{25,9},{2,18},{10... | collective-permute-start | bytes 196616 | tf_op jit(solution)/shard_map/ppermute | solution.py:383
  103.2 10.3 %collective-permute-start.25 = (bf16[4,16,512]{2,1,0:T(8,128)(2,1)S(1)}, bf16[4,16,512]{2,1,0:T(8,128)(2,1)}, u32[]{:S(2)}, u32[]{:S(2)}) collective-permute-start(bf16[4,16,512]{2,1,0:T(8,128)(2,1)S(1)} %get-tuple-element.178), channel_id=1, source_target_pairs={{0,24},{8,16},{16,8},{24,0},{1,25},{9,17},{17,9},{25,1},{2,26},{10... | collective-permute-start | bytes 196616 | tf_op jit(solution)/shard_map/ppermute | solution.py:383
  104.4 18.8 %collective-permute-start.18 = (bf16[4,64,512]{2,1,0:T(8,128)(2,1)S(1)}, bf16[4,64,512]{2,1,0:T(8,128)(2,1)S(1)}, u32[]{:S(2)}, u32[]{:S(2)}) collective-permute-start(bf16[4,64,512]{2,1,0:T(8,128)(2,1)S(1)} %get-tuple-element.147), channel_id=1, source_target_pairs={{0,4},{1,5},{2,6},{3,7},{4,0},{5,1},{6,2},{7,3},{8,12},{9,13},{10,... | collective-permute-start | bytes 786440 | tf_op jit(solution)/shard_map/ppermute | solution.py:383
  105.7 17.5 %collective-permute-start.19 = (bf16[4,64,512]{2,1,0:T(8,128)(2,1)S(1)}, bf16[4,64,512]{2,1,0:T(8,128)(2,1)S(1)}, u32[]{:S(2)}, u32[]{:S(2)}) collective-permute-start(bf16[4,64,512]{2,1,0:T(8,128)(2,1)S(1)} %get-tuple-element.148), channel_id=1, source_target_pairs={{0,6},{1,7},{2,4},{3,5},{4,2},{5,3},{6,0},{7,1},{8,14},{9,15},{10,... | collective-permute-start | bytes 786440 | tf_op jit(solution)/shard_map/ppermute | solution.py:383
  107.2 16.0 %all-to-all-start.3 = ((bf16[8,2,32,512]{3,2,1,0:T(8,128)(2,1)}), bf16[8,2,32,512]{3,2,1,0:T(8,128)(2,1)S(1)}, u32[]{:S(2)}, u32[]{:S(2)}) async-start(bf16[8,2,32,512]{3,2,1,0:T(8,128)(2,1)} %shard_map.75), calls=%async_computation.3 | async-start | bytes 1048576 | tf_op jit(solution)/shard_map/all_to_all | solution.py:516
  110.7 12.5 %collective-permute-start.16 = (bf16[128,512]{1,0:T(8,128)(2,1)}, bf16[128,512]{1,0:T(8,128)(2,1)S(1)}, u32[]{:S(2)}, u32[]{:S(2)}) collective-permute-start(bf16[128,512]{1,0:T(8,128)(2,1)} %get-tuple-element.156), channel_id=1, source_target_pairs={{0,16},{8,24},{16,0},{24,8},{1,17},{9,25},{17,1},{25,9},{2,18},{10... | collective-permute-start | bytes 393224 | tf_op jit(solution)/shard_map/ppermute | solution.py:383
  112.3 15.6 %collective-permute-start.17 = (bf16[128,512]{1,0:T(8,128)(2,1)}, bf16[128,512]{1,0:T(8,128)(2,1)S(1)}, u32[]{:S(2)}, u32[]{:S(2)}) collective-permute-start(bf16[128,512]{1,0:T(8,128)(2,1)} %get-tuple-element.157), channel_id=1, source_target_pairs={{0,24},{8,16},{16,8},{24,0},{1,25},{9,17},{17,9},{25,1},{2,26},{10... | collective-permute-start | bytes 393224 | tf_op jit(solution)/shard_map/ppermute | solution.py:383
  123.4 5.2 %collective-permute-start.20 = (bf16[4,16,512]{2,1,0:T(8,128)(2,1)S(1)}, bf16[4,16,512]{2,1,0:T(8,128)(2,1)S(1)}, u32[]{:S(2)}, u32[]{:S(2)}) collective-permute-start(bf16[4,16,512]{2,1,0:T(8,128)(2,1)S(1)} %get-tuple-element.173), channel_id=1, source_target_pairs={{0,8},{8,0},{16,24},{24,16},{1,9},{9,1},{17,25},{25,17},{2,10},{10... | collective-permute-start | bytes 196616 | tf_op jit(solution)/shard_map/ppermute | solution.py:383
  123.5 8.0 %collective-permute-start.21 = (bf16[4,16,512]{2,1,0:T(8,128)(2,1)S(1)}, bf16[4,16,512]{2,1,0:T(8,128)(2,1)S(1)}, u32[]{:S(2)}, u32[]{:S(2)}) collective-permute-start(bf16[4,16,512]{2,1,0:T(8,128)(2,1)S(1)} %get-tuple-element.174), channel_id=1, source_target_pairs={{0,16},{8,24},{16,0},{24,8},{1,17},{9,25},{17,1},{25,9},{2,18},{10... | collective-permute-start | bytes 196616 | tf_op jit(solution)/shard_map/ppermute | solution.py:383
  126.6 6.2 %collective-permute-start.22 = (bf16[4,16,512]{2,1,0:T(8,128)(2,1)S(1)}, bf16[4,16,512]{2,1,0:T(8,128)(2,1)S(1)}, u32[]{:S(2)}, u32[]{:S(2)}) collective-permute-start(bf16[4,16,512]{2,1,0:T(8,128)(2,1)S(1)} %get-tuple-element.175), channel_id=1, source_target_pairs={{0,24},{8,16},{16,8},{24,0},{1,25},{9,17},{17,9},{25,1},{2,26},{10... | collective-permute-start | bytes 196616 | tf_op jit(solution)/shard_map/ppermute | solution.py:383
  (14 other events, 69.0 us)

commit v11 on v9

--- a/solution.py
+++ b/solution.py
@@ -331,7 +331,7 @@
     keep_hbms, send_hbms, refs = refs[:plane], refs[plane : 2 * plane], refs[2 * plane :]
     out_ref, keep_ref, send_ref, w_ref, turn_ref, flat_ref, dqkv_ref, sems, out_sems = refs
     coming = [
-        start(turn_hbm.at[6], turn_ref.at[0], sems.at[0]), start(n_hbm, flat_ref.at[0], sems.at[1]),
+        start(turn_hbm.at[7], turn_ref.at[0], sems.at[0]), start(n_hbm, flat_ref.at[0], sems.at[1]),
         start(dqkv_hbm, dqkv_ref, sems.at[2]), start(att_hbm, flat_ref.at[1], sems.at[3]),
         start(cot_hbm, flat_ref.at[2], sems.at[4]), start(mid_hbm, flat_ref.at[3], sems.at[5]),
         start(w_hbm.at[1, 3], w_ref, sems.at[6]), start(turn_hbm.at[5], turn_ref.at[1], sems.at[7]),
@@ -397,6 +397,14 @@
     return [item if step == 0 else swap(item, "col", plane * core, step * core) for step, item in enumerate(sums)]
 
 
+def last_sums_at_once(pieces, row_parts):
+    parts, size, channels = pieces[0].shape
+    held = sum(piece.astype(F32) for piece in pieces).astype(BF16)
+    held = held.reshape(parts, row_parts, size // row_parts, channels).transpose(1, 0, 2, 3)
+    got = lax.all_to_all(held, "row", 0, 0, tiled=True)
+    return jnp.sum(got.astype(F32), axis=0)
+
+
 def last_sums(pieces, row_parts):
     parts, size, channels = pieces[0].shape
     held = sum(piece.astype(F32) for piece in pieces).astype(BF16)
@@ -442,6 +450,7 @@
         ((row_parts, high, cols), (2, 0, 1), {0: "row"}, 0),
         ((cols, row_parts, high), (1, 2, 0), {1: "row"}, 0),
         ((row_parts, plane, core, channels // devices), (2, 1, 0, 3), {0: "row", 1: "plane", 2: "core"}, 1),
+        ((row_parts, plane, core, channels // devices), (2, 1, 0, 3), {1: "plane", 2: "core"}, 1),
     ]
 
     def all_to_all(item):
@@ -490,8 +499,9 @@
     outs, grads = results[:row_parts], results[row_parts:]
     sums_b = chip_sums(grads[:plane], grads[plane:], col_parts)
     pieces_b = plane_pieces(sums_b, plane, core)
-    near, far = [outs[0], swap(outs[1], "row", row_parts, 1)], outs[2:]
-    d_mid, near, far, _ = lax.optimization_barrier((d_mid, near, far, sums_b))
+    pieces_out = [outs[0], swap(outs[1], "row", row_parts, 1)]
+    d_mid, rest, _ = lax.optimization_barrier((d_mid, outs[2:], sums_b))
+    pieces_out += [swap(item, "row", row_parts, 2 + step) for step, item in enumerate(rest[:1])]
     results = call(
         functools.partial(row_back, (rows, length, width, plane)),
         at(ANY, d_mid) + at(FAR, weights, turn, normed, query, key, value, attended, prob),
@@ -499,20 +509,24 @@
         [square, scratch(2, *flat)] + [square] * 5 + [scratch(*probs), square, scratch(*triple)]
         + [scratch(plane, *packed), scratch(plane, *packed), copies((11,)), copies((2 * plane,))],
     )
-    (d_mid, dqkv, *grads), pieces_b, far = lax.optimization_barrier((results, pieces_b, far))
+    (d_mid, dqkv, *grads), pieces_b, pieces_out, rest = lax.optimization_barrier(
+        (results, pieces_b, pieces_out, rest[1:])
+    )
     sums_a = chip_sums(grads[:plane], grads[plane:], col_parts)
     pieces_a = plane_pieces(sums_a, plane, core)
-    dqkv, pieces_b, far, _ = lax.optimization_barrier((dqkv, pieces_b, far, sums_a))
+    dqkv, rest, _ = lax.optimization_barrier((dqkv, rest, sums_a))
+    pieces_out += [swap(item, "row", row_parts, 3 + step) for step, item in enumerate(rest)]
     field_grad, = call(
         field_back, at(ANY, x, d_mid, gains) + at(FAR, dqkv, weights), at(FAR, x.shape),
         [scratch(*triple), scratch(3, *flat), scratch(*x.shape), copies((3,))],
     )
-    field_grad, pieces_a[1] = lax.optimization_barrier((field_grad, pieces_a[1]))
+    field_grad, pieces_b = lax.optimization_barrier((field_grad, pieces_b))
+    grads_b = last_sums_at_once(pieces_b, row_parts)
+    field_grad, pieces_a = lax.optimization_barrier((field_grad, pieces_a))
     field_grad = lax.all_to_all(field_grad, "col", 0, 0, tiled=True).reshape(high, wide, channels)
-    grads_b = last_sums(pieces_b, row_parts)
     output = jnp.zeros((high, wide, channels), BF16)
-    for step, piece in enumerate((*near, *far)):
-        piece = (piece if step < 2 else swap(piece, "row", row_parts, step)).reshape(high, cols, channels)
+    for step, piece in enumerate(pieces_out):
+        piece = piece.reshape(high, cols, channels)
         output = lax.dynamic_update_slice_in_dim(output, piece, (my_row ^ step) * cols, axis=1)
     grads_a = last_sums(pieces_a, row_parts)
     return output, field_grad, jnp.concatenate([grads_a, grads_b], axis=0)

time: 138 us -> 136 us (0.986)
  waiting for transfers between devices: 38.2 us -> 32.8 us
  starting transfers between devices: 44.4 us -> 46 us
    ppermute x26 -> x23, waiting for transfers between devices: 15.5 us -> 6.94 us  [swap(): return lax.ppermute(item, axis, [(at, at ^ step) for at in range(count)])]
    all_to_all x0 -> x1, starting transfers between devices: none -> 3.41 us  [last_sums_at_once(): got = lax.all_to_all(held, 'row', 0, 0, tiled=True)]
    all_to_all x0 -> x1, waiting for transfers between devices: none -> 2.57 us  [last_sums_at_once(): got = lax.all_to_all(held, 'row', 0, 0, tiled=True)]
    ppermute x26 -> x23, starting transfers between devices: 27.8 us -> 25.8 us  [swap(): return lax.ppermute(item, axis, [(at, at ^ step) for at in range(count)])]
  transfers between devices with their start and end apart: 30 -> 28, of which waited for: 14 -> 15; matrix products, arithmetic and copies ran while one was open for 2% -> 3% of each run, Pallas kernels for 25% -> 25%
where the time goes in v11:
time: 136 us; the launch traced here: 135 us
  Pallas kernels  49 us (36%)
  starting transfers between devices  46 us (34%)
  waiting for transfers between devices  32.8 us (24%)
  local copies, waits for them, and re-layouts  4.35 us (3%)
  other arithmetic  2.14 us (2%)
    pallas_call x9, Pallas kernels, call(): pl.pallas_call(kernel, in_specs=[spec(where) for _, where in ins], out_sp...  49 us
    ppermute x23, starting transfers between devices, swap(): return lax.ppermute(item, axis, [(at, at ^ step) for at in range(count)])  25.8 us
    all_to_all x2, waiting for transfers between devices, all_to_all(): lax.all_to_all(item, ('row', 'col'), 0, 0, tiled=True)  12.8 us
    all_to_all x1, waiting for transfers between devices, body(): lax.all_to_all(field_grad, 'col', 0, 0, tiled=True)  8.79 us
    all_to_all x2, starting transfers between devices, all_to_all(): lax.all_to_all(item, ('row', 'col'), 0, 0, tiled=True)  7.89 us
    ppermute x23, waiting for transfers between devices, swap(): return lax.ppermute(item, axis, [(at, at ^ step) for at in range(count)])  6.94 us
    all_to_all x1, starting transfers between devices, body(): lax.all_to_all(field.reshape(col_parts, rows, wide, channels), 'col', 0,...  5.18 us
    all_to_all x1, starting transfers between devices, body(): lax.all_to_all(field_grad, 'col', 0, 0, tiled=True)  3.7 us
  transfers between devices with their start and end apart: 28, of which 15 were waited for; matrix products, arithmetic and copies ran while one was open for 3% of the time, Pallas kernels for 25%

profile of v11, /device:TPU:0, one launch (start us, length us, event | category | flops | bytes accessed | tf_op | source)
XLA Modules:
  0.0 135.2 jit_solution(8861341384263786671)
XLA Ops:
  0.6 5.2 %all-to-all-start = ((bf16[8,2,32,512]{3,2,1,0:T(8,128)(2,1)}), bf16[8,2,32,512]{3,2,1,0:T(8,128)(2,1)S(1)}, u32[]{:S(2)}, u32[]{:S(2)}) async-start(bf16[8,2,32,512]{3,2,1,0:T(8,128)(2,1)} %bitcast.52), calls=%async_computation | async-start | bytes 1048576 | tf_op jit(solution)/shard_map/all_to_all | solution.py:460
  6.9 1.6 %collective-permute-start = (bf16[16,8,512]{2,1,0:T(8,128)(2,1)S(1)}, bf16[16,8,512]{2,1,0:T(8,128)(2,1)S(1)}, u32[]{:S(2)}, u32[]{:S(2)}) collective-permute-start(bf16[16,8,512]{2,1,0:T(8,128)(2,1)S(1)} %get-tuple-element.170), channel_id=1, source_target_pairs={{0,8},{8,0},{16,24},{24,16},{1,9},{9,1},{17,25},{25,17},{2,10},{10... | collective-permute-start | bytes 393224 | tf_op jit(solution)/shard_map/ppermute | solution.py:383
  8.6 2.6 %collective-permute-start.1 = (bf16[16,8,512]{2,1,0:T(8,128)(2,1)S(1)}, bf16[16,8,512]{2,1,0:T(8,128)(2,1)S(1)}, u32[]{:S(2)}, u32[]{:S(2)}) collective-permute-start(bf16[16,8,512]{2,1,0:T(8,128)(2,1)S(1)} %get-tuple-element.172), channel_id=1, source_target_pairs={{0,16},{8,24},{16,0},{24,8},{1,17},{9,25},{17,1},{25,9},{2,18},{10... | collective-permute-start | bytes 393224 | tf_op jit(solution)/shard_map/ppermute | solution.py:383
  11.4 2.4 %shard_map.67.turn_hbm.refs_5_ = bf16[8,512,512]{2,1,0:T(8,128)(2,1)} custom-call(), custom_call_target="tpu_custom_call" | custom-call | flops 1048576 | bytes 1024 | tf_op jit(solution)/shard_map/pallas_call | solution.py:371
  13.8 1.7 %all-to-all-done.x_ref = bf16[8,2,32,512]{3,2,1,0:T(8,128)(2,1)S(1)} async-done(((bf16[8,2,32,512]{3,2,1,0:T(8,128)(2,1)}), bf16[8,2,32,512]{3,2,1,0:T(8,128)(2,1)S(1)}, u32[]{:S(2)}, u32[]{:S(2)}) %all-to-all-start) | async-done | bytes 524320 | tf_op jit(solution)/shard_map/all_to_all | solution.py:460
  15.6 8.2 %shard_map.68 = (bf16[512,512]{1,0:T(8,128)(2,1)}, bf16[512,512]{1,0:T(8,128)(2,1)}, bf16[512,512]{1,0:T(8,128)(2,1)}, bf16[512,512]{1,0:T(8,128)(2,1)}, bf16[51...) custom-call(bf16[8,2,32,512]{3,2,1,0:T(8,128)(2,1)S(1)} %all-to-all-done.x_ref, ...), custom_call_target="tpu_custom_call" | custom-call | flops 1048576 | bytes 1024 | tf_op jit(solution)/shard_map/pallas_call | solution.py:371
  24.4 4.6 %all-to-all-start.1 = ((bf16[32,16,512]{2,1,0:T(8,128)(2,1)}), bf16[32,16,512]{2,1,0:T(8,128)(2,1)S(1)}, u32[]{:S(2)}, u32[]{:S(2)}) async-start(bf16[32,16,512]{2,1,0:T(8,128)(2,1)} %bitcast.54), calls=%async_computation.1 | async-start | bytes 1048576 | tf_op jit(solution)/shard_map/all_to_all | solution.py:458
  29.9 2.0 %shard_map.69 = (bf16[512,512]{1,0:T(8,128)(2,1)S(1)}, bf16[512,512]{1,0:T(8,128)(2,1)S(1)}, bf16[2,512,512]{2,1,0:T(8,128)(2,1)S(1)}) custom-call(bf16[128,512]{1,0:T(8,128)(2,1)S(1)} %get-tuple-element.88.refs_0_, bf16[128,512]{1,0:T(8,128)(2,1)S(1)} %bitcast.45, bf16[128,512]{1,0:T(8,128)(2,1)S(1)} %bitcast.46, bf16[128,512]{1,0:T(8,128)(2,1)S(1)} %bitcast.47, ...), custom_call_target="tpu_custom_call" | custom-call | flops 1048576 | bytes 1024 | tf_op jit(solution)/shard_map/pallas_call | solution.py:371
  32.0 12.6 %all-to-all-done.1 = bf16[32,16,512]{2,1,0:T(8,128)(2,1)S(1)} async-done(((bf16[32,16,512]{2,1,0:T(8,128)(2,1)}), bf16[32,16,512]{2,1,0:T(8,128)(2,1)S(1)}, u32[]{:S(2)}, u32[]{:S(2)}) %all-to-all-start.1) | async-done | bytes 524320 | tf_op jit(solution)/shard_map/all_to_all | solution.py:458
  44.6 13.3 %shard_map.70 = (bf16[512,512]{1,0:T(8,128)(2,1)}, bf16[512,512]{1,0:T(8,128)(2,1)}, bf16[512,512]{1,0:T(8,128)(2,1)}, bf16[512,512]{1,0:T(8,128)(2,1)}, bf16[512,1536]{1,0:T(8,128)(2,1)}) custom-call(bf16[512,512]{1,0:T(8,128)(2,1)S(1)} %bitcast.43, bf16[512,512]{1,0:T(8,128)(2,1)S(1)} %get-tuple-element.92.cot_ref.cot_hbm, ...), custom_call_target="tpu_custom_call" | custom-call | flops 1048576 | bytes 1024 | tf_op jit(solution)/shard_map/pallas_call | solution.py:371
  57.9 3.3 %all-to-all-start.2 = ((bf16[32,16,512]{2,1,0:T(8,128)(2,1)}), bf16[32,16,512]{2,1,0:T(8,128)(2,1)S(1)}, u32[]{:S(2)}, u32[]{:S(2)}) async-start(bf16[32,16,512]{2,1,0:T(8,128)(2,1)} %bitcast.53), calls=%async_computation.2 | async-start | bytes 1048576 | tf_op jit(solution)/shard_map/all_to_all | solution.py:458
  61.2 5.7 %shard_map.71 = (bf16[128,512]{1,0:T(8,128)(2,1)}, bf16[128,512]{1,0:T(8,128)(2,1)}, bf16[128,512]{1,0:T(8,128)(2,1)}, bf16[128,512]{1,0:T(8,128)(2,1)}, bf16[4,...) custom-call(bf16[512,512]{1,0:T(8,128)(2,1)} %copy-done, ...), custom_call_target="tpu_custom_call" | custom-call | flops 1048576 | bytes 1024 | tf_op jit(solution)/shard_map/pallas_call | solution.py:371
  71.2 1.7 %collective-permute-start.7 = (bf16[4,64,512]{2,1,0:T(8,128)(2,1)S(1)}, bf16[4,64,512]{2,1,0:T(8,128)(2,1)S(1)}, u32[]{:S(2)}, u32[]{:S(2)}) collective-permute-start(bf16[4,64,512]{2,1,0:T(8,128)(2,1)S(1)} %get-tuple-element.111), channel_id=1, source_target_pairs={{0,2},{1,3},{2,0},{3,1},{4,6},{5,7},{6,4},{7,5},{8,10},{9,11},{10,... | collective-permute-start | bytes 786440 | tf_op jit(solution)/shard_map/ppermute | solution.py:383
  74.8 1.6 %collective-permute-start.10 = (bf16[128,512]{1,0:T(8,128)(2,1)S(1)}, bf16[128,512]{1,0:T(8,128)(2,1)S(1)}, u32[]{:S(2)}, u32[]{:S(2)}) collective-permute-start(bf16[128,512]{1,0:T(8,128)(2,1)S(1)} %copy-done.8), channel_id=1, source_target_pairs={{0,8},{8,0},{16,24},{24,16},{1,9},{9,1},{17,25},{25,17},{2,10},{10... | collective-permute-start | bytes 393224 | tf_op jit(solution)/shard_map/ppermute | solution.py:383
  76.6 2.2 %collective-permute-start.11 = (bf16[128,512]{1,0:T(8,128)(2,1)S(1)}, bf16[128,512]{1,0:T(8,128)(2,1)S(1)}, u32[]{:S(2)}, u32[]{:S(2)}) collective-permute-start(bf16[128,512]{1,0:T(8,128)(2,1)S(1)} %copy-done.7), channel_id=1, source_target_pairs={{0,16},{8,24},{16,0},{24,8},{1,17},{9,25},{17,1},{25,9},{2,18},{10... | collective-permute-start | bytes 393224 | tf_op jit(solution)/shard_map/ppermute | solution.py:383
  78.8 10.6 %shard_map.73 = (bf16[512,512]{1,0:T(8,128)(2,1)S(1)}, bf16[512,1536]{1,0:T(8,128)(2,1)}, bf16[4,64,512]{2,1,0:T(8,128)(2,1)}, bf16[4,64,512]{2,1,0:T(8,128)(2,1...) custom-call(bf16[512,512]{1,0:T(8,128)(2,1)S(1)} %bitcast.44, ...), custom_call_target="tpu_custom_call" | custom-call | flops 1048576 | bytes 1024 | tf_op jit(solution)/shard_map/pallas_call | solution.py:371
  97.3 4.1 %shard_map.75 = bf16[8,2,32,512]{3,2,1,0:T(8,128)(2,1)} custom-call(bf16[8,2,32,512]{3,2,1,0:T(8,128)(2,1)S(1)} %all-to-all-done.x_ref, bf16[512,512]{1,0:T(8,128)(2,1)S(1)} %get-tuple-element.153.dm_ref, f32[2,512]{1,0:T(2,128)S(1)} %copy-done.3, bf16[512,1536]{1,0:T(8,128)(2,1)} %get-tuple-element.154.dqkv_hbm, bf16[2,4,512,512]{3,2,1,0:T(8,128)(2,1)} %w_hbm.9), custom_call_target="tpu_custom_call" | custom-call | flops 1048576 | bytes 1024 | tf_op jit(solution)/shard_map/pallas_call | solution.py:371
  102.3 3.4 %all-to-all-start.4 = ((bf16[4,4,16,512]{3,2,1,0:T(8,128)(2,1)}), bf16[4,4,16,512]{3,2,1,0:T(8,128)(2,1)S(1)}, u32[]{:S(2)}, u32[]{:S(2)}) async-start(bf16[4,4,16,512]{3,2,1,0:T(8,128)(2,1)} %bitcast.42), calls=%async_computation.4 | async-start | bytes 524288 | tf_op jit(solution)/shard_map/all_to_all | solution.py:404
  105.7 3.8 %collective-permute-start.16 = (bf16[128,512]{1,0:T(8,128)(2,1)S(1)}, bf16[128,512]{1,0:T(8,128)(2,1)S(1)}, u32[]{:S(2)}, u32[]{:S(2)}) collective-permute-start(bf16[128,512]{1,0:T(8,128)(2,1)S(1)} %copy-done.6), channel_id=1, source_target_pairs={{0,24},{8,16},{16,8},{24,0},{1,25},{9,17},{17,9},{25,1},{2,26},{10... | collective-permute-start | bytes 393224 | tf_op jit(solution)/shard_map/ppermute | solution.py:383
  111.5 3.7 %collective-permute-start.22 = (bf16[4,16,512]{2,1,0:T(8,128)(2,1)S(1)}, bf16[4,16,512]{2,1,0:T(8,128)(2,1)S(1)}, u32[]{:S(2)}, u32[]{:S(2)}) collective-permute-start(bf16[4,16,512]{2,1,0:T(8,128)(2,1)S(1)} %get-tuple-element.175), channel_id=1, source_target_pairs={{0,24},{8,16},{16,8},{24,0},{1,25},{9,17},{17,9},{25,1},{2,26},{10... | collective-permute-start | bytes 196616 | tf_op jit(solution)/shard_map/ppermute | solution.py:383
  115.2 3.2 %collective-permute-done.16 = bf16[128,512]{1,0:T(8,128)(2,1)S(1)} collective-permute-done((bf16[128,512]{1,0:T(8,128)(2,1)S(1)}, bf16[128,512]{1,0:T(8,128)(2,1)S(1)}, u32[]{:S(2)}, u32[]{:S(2)}) %collective-permute-start.16) | collective-permute-done | bytes 131104 | tf_op jit(solution)/shard_map/ppermute | solution.py:383
  118.4 2.6 %all-to-all-done.4 = bf16[4,4,16,512]{3,2,1,0:T(8,128)(2,1)S(1)} async-done(((bf16[4,4,16,512]{3,2,1,0:T(8,128)(2,1)}), bf16[4,4,16,512]{3,2,1,0:T(8,128)(2,1)S(1)}, u32[]{:S(2)}, u32[]{:S(2)}) %all-to-all-start.4) | async-done | bytes 262176 | tf_op jit(solution)/shard_map/all_to_all | solution.py:404
  121.0 3.7 %all-to-all-start.3 = ((bf16[8,2,32,512]{3,2,1,0:T(8,128)(2,1)}), bf16[8,2,32,512]{3,2,1,0:T(8,128)(2,1)S(1)}, u32[]{:S(2)}, u32[]{:S(2)}) async-start(bf16[8,2,32,512]{3,2,1,0:T(8,128)(2,1)} %shard_map.75), calls=%async_computation.3 | async-start | bytes 1048576 | tf_op jit(solution)/shard_map/all_to_all | solution.py:526
  125.7 8.8 %all-to-all-done.3 = bf16[8,2,32,512]{3,2,1,0:T(8,128)(2,1)S(1)} async-done(((bf16[8,2,32,512]{3,2,1,0:T(8,128)(2,1)}), bf16[8,2,32,512]{3,2,1,0:T(8,128)(2,1)S(1)}, u32[]{:S(2)}, u32[]{:S(2)}) %all-to-all-start.3) | async-done | bytes 524320 | tf_op jit(solution)/shard_map/all_to_all | solution.py:526
  (73 shorter events, 21.7 us)
Async XLA Ops:
  0.6 14.9 %all-to-all-start = ((bf16[8,2,32,512]{3,2,1,0:T(8,128)(2,1)}), bf16[8,2,32,512]{3,2,1,0:T(8,128)(2,1)S(1)}, u32[]{:S(2)}, u32[]{:S(2)}) async-start(bf16[8,2,32,512]{3,2,1,0:T(8,128)(2,1)} %bitcast.52), calls=%async_computation | async-start | bytes 1048576 | tf_op jit(solution)/shard_map/all_to_all | solution.py:460
  6.9 16.8 %collective-permute-start = (bf16[16,8,512]{2,1,0:T(8,128)(2,1)S(1)}, bf16[16,8,512]{2,1,0:T(8,128)(2,1)S(1)}, u32[]{:S(2)}, u32[]{:S(2)}) collective-permute-start(bf16[16,8,512]{2,1,0:T(8,128)(2,1)S(1)} %get-tuple-element.170), channel_id=1, source_target_pairs={{0,8},{8,0},{16,24},{24,16},{1,9},{9,1},{17,25},{25,17},{2,10},{10... | collective-permute-start | bytes 393224 | tf_op jit(solution)/shard_map/ppermute | solution.py:383
  8.6 15.1 %collective-permute-start.1 = (bf16[16,8,512]{2,1,0:T(8,128)(2,1)S(1)}, bf16[16,8,512]{2,1,0:T(8,128)(2,1)S(1)}, u32[]{:S(2)}, u32[]{:S(2)}) collective-permute-start(bf16[16,8,512]{2,1,0:T(8,128)(2,1)S(1)} %get-tuple-element.172), channel_id=1, source_target_pairs={{0,16},{8,24},{16,0},{24,8},{1,17},{9,25},{17,1},{25,9},{2,18},{10... | collective-permute-start | bytes 393224 | tf_op jit(solution)/shard_map/ppermute | solution.py:383
  11.2 12.6 %collective-permute-start.2 = (bf16[16,8,512]{2,1,0:T(8,128)(2,1)S(1)}, bf16[16,8,512]{2,1,0:T(8,128)(2,1)S(1)}, u32[]{:S(2)}, u32[]{:S(2)}) collective-permute-start(bf16[16,8,512]{2,1,0:T(8,128)(2,1)S(1)} %get-tuple-element.169), channel_id=1, source_target_pairs={{0,24},{8,16},{16,8},{24,0},{1,25},{9,17},{17,9},{25,1},{2,26},{10... | collective-permute-start | bytes 393224 | tf_op jit(solution)/shard_map/ppermute | solution.py:383
  24.4 20.2 %all-to-all-start.1 = ((bf16[32,16,512]{2,1,0:T(8,128)(2,1)}), bf16[32,16,512]{2,1,0:T(8,128)(2,1)S(1)}, u32[]{:S(2)}, u32[]{:S(2)}) async-start(bf16[32,16,512]{2,1,0:T(8,128)(2,1)} %bitcast.54), calls=%async_computation.1 | async-start | bytes 1048576 | tf_op jit(solution)/shard_map/all_to_all | solution.py:458
  57.9 18.7 %all-to-all-start.2 = ((bf16[32,16,512]{2,1,0:T(8,128)(2,1)}), bf16[32,16,512]{2,1,0:T(8,128)(2,1)S(1)}, u32[]{:S(2)}, u32[]{:S(2)}) async-start(bf16[32,16,512]{2,1,0:T(8,128)(2,1)} %bitcast.53), calls=%async_computation.2 | async-start | bytes 1048576 | tf_op jit(solution)/shard_map/all_to_all | solution.py:458
  67.1 2.0 %collective-permute-start.4 = (bf16[4,64,512]{2,1,0:T(8,128)(2,1)}, bf16[4,64,512]{2,1,0:T(8,128)(2,1)S(1)}, u32[]{:S(2)}, u32[]{:S(2)}) collective-permute-start(bf16[4,64,512]{2,1,0:T(8,128)(2,1)} %get-tuple-element.107), channel_id=1, source_target_pairs={{0,1},{1,0},{2,3},{3,2},{4,5},{5,4},{6,7},{7,6},{8,9},{9,8},{10,11... | collective-permute-start | bytes 786440 | tf_op jit(solution)/shard_map/ppermute | solution.py:383
  67.6 2.3 %collective-permute-start.6 = (bf16[4,64,512]{2,1,0:T(8,128)(2,1)}, bf16[4,64,512]{2,1,0:T(8,128)(2,1)S(1)}, u32[]{:S(2)}, u32[]{:S(2)}) collective-permute-start(bf16[4,64,512]{2,1,0:T(8,128)(2,1)} %get-tuple-element.109), channel_id=1, source_target_pairs={{0,1},{1,0},{2,3},{3,2},{4,5},{5,4},{6,7},{7,6},{8,9},{9,8},{10,11... | collective-permute-start | bytes 786440 | tf_op jit(solution)/shard_map/ppermute | solution.py:383
  71.2 18.2 %collective-permute-start.7 = (bf16[4,64,512]{2,1,0:T(8,128)(2,1)S(1)}, bf16[4,64,512]{2,1,0:T(8,128)(2,1)S(1)}, u32[]{:S(2)}, u32[]{:S(2)}) collective-permute-start(bf16[4,64,512]{2,1,0:T(8,128)(2,1)S(1)} %get-tuple-element.111), channel_id=1, source_target_pairs={{0,2},{1,3},{2,0},{3,1},{4,6},{5,7},{6,4},{7,5},{8,10},{9,11},{10,... | collective-permute-start | bytes 786440 | tf_op jit(solution)/shard_map/ppermute | solution.py:383
  72.9 16.6 %collective-permute-start.8 = (bf16[4,64,512]{2,1,0:T(8,128)(2,1)S(1)}, bf16[4,64,512]{2,1,0:T(8,128)(2,1)S(1)}, u32[]{:S(2)}, u32[]{:S(2)}) collective-permute-start(bf16[4,64,512]{2,1,0:T(8,128)(2,1)S(1)} %get-tuple-element.112), channel_id=1, source_target_pairs={{0,4},{1,5},{2,6},{3,7},{4,0},{5,1},{6,2},{7,3},{8,12},{9,13},{10,... | collective-permute-start | bytes 786440 | tf_op jit(solution)/shard_map/ppermute | solution.py:383
  74.4 15.1 %collective-permute-start.9 = (bf16[4,64,512]{2,1,0:T(8,128)(2,1)S(1)}, bf16[4,64,512]{2,1,0:T(8,128)(2,1)S(1)}, u32[]{:S(2)}, u32[]{:S(2)}) collective-permute-start(bf16[4,64,512]{2,1,0:T(8,128)(2,1)S(1)} %get-tuple-element.113), channel_id=1, source_target_pairs={{0,6},{1,7},{2,4},{3,5},{4,2},{5,3},{6,0},{7,1},{8,14},{9,15},{10,... | collective-permute-start | bytes 786440 | tf_op jit(solution)/shard_map/ppermute | solution.py:383
  74.8 14.6 %collective-permute-start.10 = (bf16[128,512]{1,0:T(8,128)(2,1)S(1)}, bf16[128,512]{1,0:T(8,128)(2,1)S(1)}, u32[]{:S(2)}, u32[]{:S(2)}) collective-permute-start(bf16[128,512]{1,0:T(8,128)(2,1)S(1)} %copy-done.8), channel_id=1, source_target_pairs={{0,8},{8,0},{16,24},{24,16},{1,9},{9,1},{17,25},{25,17},{2,10},{10... | collective-permute-start | bytes 393224 | tf_op jit(solution)/shard_map/ppermute | solution.py:383
  76.6 12.9 %collective-permute-start.11 = (bf16[128,512]{1,0:T(8,128)(2,1)S(1)}, bf16[128,512]{1,0:T(8,128)(2,1)S(1)}, u32[]{:S(2)}, u32[]{:S(2)}) collective-permute-start(bf16[128,512]{1,0:T(8,128)(2,1)S(1)} %copy-done.7), channel_id=1, source_target_pairs={{0,16},{8,24},{16,0},{24,8},{1,17},{9,25},{17,1},{25,9},{2,18},{10... | collective-permute-start | bytes 393224 | tf_op jit(solution)/shard_map/ppermute | solution.py:383
  89.6 2.1 %collective-permute-start.13 = (bf16[4,64,512]{2,1,0:T(8,128)(2,1)}, bf16[4,64,512]{2,1,0:T(8,128)(2,1)S(1)}, u32[]{:S(2)}, u32[]{:S(2)}) collective-permute-start(bf16[4,64,512]{2,1,0:T(8,128)(2,1)} %get-tuple-element.145), channel_id=1, source_target_pairs={{0,1},{1,0},{2,3},{3,2},{4,5},{5,4},{6,7},{7,6},{8,9},{9,8},{10,11... | collective-permute-start | bytes 786440 | tf_op jit(solution)/shard_map/ppermute | solution.py:383
  90.2 2.3 %collective-permute-start.15 = (bf16[4,64,512]{2,1,0:T(8,128)(2,1)}, bf16[4,64,512]{2,1,0:T(8,128)(2,1)S(1)}, u32[]{:S(2)}, u32[]{:S(2)}) collective-permute-start(bf16[4,64,512]{2,1,0:T(8,128)(2,1)} %get-tuple-element.147), channel_id=1, source_target_pairs={{0,1},{1,0},{2,3},{3,2},{4,5},{5,4},{6,7},{7,6},{8,9},{9,8},{10,11... | collective-permute-start | bytes 786440 | tf_op jit(solution)/shard_map/ppermute | solution.py:383
  93.8 15.8 %collective-permute-start.17 = (bf16[4,64,512]{2,1,0:T(8,128)(2,1)S(1)}, bf16[4,64,512]{2,1,0:T(8,128)(2,1)S(1)}, u32[]{:S(2)}, u32[]{:S(2)}) collective-permute-start(bf16[4,64,512]{2,1,0:T(8,128)(2,1)S(1)} %get-tuple-element.149), channel_id=1, source_target_pairs={{0,2},{1,3},{2,0},{3,1},{4,6},{5,7},{6,4},{7,5},{8,10},{9,11},{10,... | collective-permute-start | bytes 786440 | tf_op jit(solution)/shard_map/ppermute | solution.py:383
  95.3 14.2 %collective-permute-start.18 = (bf16[4,64,512]{2,1,0:T(8,128)(2,1)S(1)}, bf16[4,64,512]{2,1,0:T(8,128)(2,1)}, u32[]{:S(2)}, u32[]{:S(2)}) collective-permute-start(bf16[4,64,512]{2,1,0:T(8,128)(2,1)S(1)} %get-tuple-element.150), channel_id=1, source_target_pairs={{0,4},{1,5},{2,6},{3,7},{4,0},{5,1},{6,2},{7,3},{8,12},{9,13},{10,... | collective-permute-start | bytes 786440 | tf_op jit(solution)/shard_map/ppermute | solution.py:383
  96.8 12.7 %collective-permute-start.19 = (bf16[4,64,512]{2,1,0:T(8,128)(2,1)S(1)}, bf16[4,64,512]{2,1,0:T(8,128)(2,1)}, u32[]{:S(2)}, u32[]{:S(2)}) collective-permute-start(bf16[4,64,512]{2,1,0:T(8,128)(2,1)S(1)} %get-tuple-element.151), channel_id=1, source_target_pairs={{0,6},{1,7},{2,4},{3,5},{4,2},{5,3},{6,0},{7,1},{8,14},{9,15},{10,... | collective-permute-start | bytes 786440 | tf_op jit(solution)/shard_map/ppermute | solution.py:383
  102.3 18.7 %all-to-all-start.4 = ((bf16[4,4,16,512]{3,2,1,0:T(8,128)(2,1)}), bf16[4,4,16,512]{3,2,1,0:T(8,128)(2,1)S(1)}, u32[]{:S(2)}, u32[]{:S(2)}) async-start(bf16[4,4,16,512]{3,2,1,0:T(8,128)(2,1)} %bitcast.42), calls=%async_computation.4 | async-start | bytes 524288 | tf_op jit(solution)/shard_map/all_to_all | solution.py:404
  105.7 12.7 %collective-permute-start.16 = (bf16[128,512]{1,0:T(8,128)(2,1)S(1)}, bf16[128,512]{1,0:T(8,128)(2,1)S(1)}, u32[]{:S(2)}, u32[]{:S(2)}) collective-permute-start(bf16[128,512]{1,0:T(8,128)(2,1)S(1)} %copy-done.6), channel_id=1, source_target_pairs={{0,24},{8,16},{16,8},{24,0},{1,25},{9,17},{17,9},{25,1},{2,26},{10... | collective-permute-start | bytes 393224 | tf_op jit(solution)/shard_map/ppermute | solution.py:383
  110.8 13.9 %collective-permute-start.20 = (bf16[4,16,512]{2,1,0:T(8,128)(2,1)S(1)}, bf16[4,16,512]{2,1,0:T(8,128)(2,1)S(1)}, u32[]{:S(2)}, u32[]{:S(2)}) collective-permute-start(bf16[4,16,512]{2,1,0:T(8,128)(2,1)S(1)} %get-tuple-element.173), channel_id=1, source_target_pairs={{0,8},{8,0},{16,24},{24,16},{1,9},{9,1},{17,25},{25,17},{2,10},{10... | collective-permute-start | bytes 196616 | tf_op jit(solution)/shard_map/ppermute | solution.py:383
  110.9 13.9 %collective-permute-start.21 = (bf16[4,16,512]{2,1,0:T(8,128)(2,1)S(1)}, bf16[4,16,512]{2,1,0:T(8,128)(2,1)S(1)}, u32[]{:S(2)}, u32[]{:S(2)}) collective-permute-start(bf16[4,16,512]{2,1,0:T(8,128)(2,1)S(1)} %get-tuple-element.174), channel_id=1, source_target_pairs={{0,16},{8,24},{16,0},{24,8},{1,17},{9,25},{17,1},{25,9},{2,18},{10... | collective-permute-start | bytes 196616 | tf_op jit(solution)/shard_map/ppermute | solution.py:383
  111.5 13.3 %collective-permute-start.22 = (bf16[4,16,512]{2,1,0:T(8,128)(2,1)S(1)}, bf16[4,16,512]{2,1,0:T(8,128)(2,1)S(1)}, u32[]{:S(2)}, u32[]{:S(2)}) collective-permute-start(bf16[4,16,512]{2,1,0:T(8,128)(2,1)S(1)} %get-tuple-element.175), channel_id=1, source_target_pairs={{0,24},{8,16},{16,8},{24,0},{1,25},{9,17},{17,9},{25,1},{2,26},{10... | collective-permute-start | bytes 196616 | tf_op jit(solution)/shard_map/ppermute | solution.py:383
  121.0 13.4 %all-to-all-start.3 = ((bf16[8,2,32,512]{3,2,1,0:T(8,128)(2,1)}), bf16[8,2,32,512]{3,2,1,0:T(8,128)(2,1)S(1)}, u32[]{:S(2)}, u32[]{:S(2)}) async-start(bf16[8,2,32,512]{3,2,1,0:T(8,128)(2,1)} %shard_map.75), calls=%async_computation.3 | async-start | bytes 1048576 | tf_op jit(solution)/shard_map/all_to_all | solution.py:526
  (13 other events, 89.9 us)

commit v12 on v11

--- a/solution.py
+++ b/solution.py
@@ -76,7 +76,7 @@
     return lax.broadcasted_iota(jnp.int32, (count, 2 * width), 1) < width
 
 
-def attention_forward(q_ref, k_ref, v_ref, att_ref, p_ref, groups, count, width, span):
+def attention_forward(q_ref, k_ref, v_ref, att_ref, p_ref, groups, count, width, span, unroll=2):
     first = head_lanes(count, width)
     pairs = HEADS // 2
     scale = width ** (-0.5)
@@ -104,10 +104,10 @@
         att_ref[rows, lanes] = total.astype(BF16)
         return carry
 
-    lax.fori_loop(0, groups * pairs, step, 0, unroll=2)
-
-
-def attention_back(q_ref, k_ref, v_ref, p_ref, da_ref, dqkv_ref, groups, count, width):
+    lax.fori_loop(0, groups * pairs, step, 0, unroll=unroll)
+
+
+def attention_back(q_ref, k_ref, v_ref, p_ref, da_ref, dqkv_ref, groups, count, width, unroll=2):
     first = head_lanes(count, width)
     pairs = HEADS // 2
     channels = HEADS * width
@@ -139,7 +139,7 @@
             dqkv_ref[rows, at] = item.astype(BF16)
         return carry
 
-    lax.fori_loop(0, groups * pairs, step, 0, unroll=2)
+    lax.fori_loop(0, groups * pairs, step, 0, unroll=unroll)
 
 
 def start(source, target, sem):
@@ -315,9 +315,9 @@
     v_ref[...] = dot(normed, w_ref[1]).astype(BF16)
     count = together * height
     groups = cols // together
-    attention_forward(q_ref, k_ref, v_ref, att_ref, p_ref, groups, count, width, height)
+    attention_forward(q_ref, k_ref, v_ref, att_ref, p_ref, groups, count, width, height, 4)
     going.append(start(att_ref, att_hbm, sems.at[5]))
-    attention_back(q_ref, k_ref, v_ref, p_ref, da_ref, dqkv_ref, groups, count, width)
+    attention_back(q_ref, k_ref, v_ref, p_ref, da_ref, dqkv_ref, groups, count, width, 4)
     going.append(start(dqkv_ref, dqkv_hbm, sems.at[6]))
     d_normed = input_back(dqkv_ref, [early_ref.at[1], w_ref.at[0], w_ref.at[1]])
     middle = mid_ref[...].astype(F32)
@@ -331,7 +331,7 @@
     keep_hbms, send_hbms, refs = refs[:plane], refs[plane : 2 * plane], refs[2 * plane :]
     out_ref, keep_ref, send_ref, w_ref, turn_ref, flat_ref, dqkv_ref, sems, out_sems = refs
     coming = [
-        start(turn_hbm.at[7], turn_ref.at[0], sems.at[0]), start(n_hbm, flat_ref.at[0], sems.at[1]),
+        start(turn_hbm.at[6], turn_ref.at[0], sems.at[0]), start(n_hbm, flat_ref.at[0], sems.at[1]),
         start(dqkv_hbm, dqkv_ref, sems.at[2]), start(att_hbm, flat_ref.at[1], sems.at[3]),
         start(cot_hbm, flat_ref.at[2], sems.at[4]), start(mid_hbm, flat_ref.at[3], sems.at[5]),
         start(w_hbm.at[1, 3], w_ref, sems.at[6]), start(turn_hbm.at[5], turn_ref.at[1], sems.at[7]),
@@ -397,14 +397,6 @@
     return [item if step == 0 else swap(item, "col", plane * core, step * core) for step, item in enumerate(sums)]
 
 
-def last_sums_at_once(pieces, row_parts):
-    parts, size, channels = pieces[0].shape
-    held = sum(piece.astype(F32) for piece in pieces).astype(BF16)
-    held = held.reshape(parts, row_parts, size // row_parts, channels).transpose(1, 0, 2, 3)
-    got = lax.all_to_all(held, "row", 0, 0, tiled=True)
-    return jnp.sum(got.astype(F32), axis=0)
-
-
 def last_sums(pieces, row_parts):
     parts, size, channels = pieces[0].shape
     held = sum(piece.astype(F32) for piece in pieces).astype(BF16)
@@ -425,7 +417,7 @@
     height = high * row_parts
     length = wide * col_parts
     width = channels // HEADS
-    together = min(cols, max(1, 256 // height))
+    together = min(cols, max(1, 128 // height))
     devices = row_parts * col_parts
     my_row = lax.axis_index("row")
 
@@ -450,7 +442,6 @@
         ((row_parts, high, cols), (2, 0, 1), {0: "row"}, 0),
         ((cols, row_parts, high), (1, 2, 0), {1: "row"}, 0),
         ((row_parts, plane, core, channels // devices), (2, 1, 0, 3), {0: "row", 1: "plane", 2: "core"}, 1),
-        ((row_parts, plane, core, channels // devices), (2, 1, 0, 3), {1: "plane", 2: "core"}, 1),
     ]
 
     def all_to_all(item):
@@ -514,16 +505,16 @@
     )
     sums_a = chip_sums(grads[:plane], grads[plane:], col_parts)
     pieces_a = plane_pieces(sums_a, plane, core)
-    dqkv, rest, _ = lax.optimization_barrier((dqkv, rest, sums_a))
-    pieces_out += [swap(item, "row", row_parts, 3 + step) for step, item in enumerate(rest)]
+    dqkv, _ = lax.optimization_barrier((dqkv, sums_a))
     field_grad, = call(
         field_back, at(ANY, x, d_mid, gains) + at(FAR, dqkv, weights), at(FAR, x.shape),
         [scratch(*triple), scratch(3, *flat), scratch(*x.shape), copies((3,))],
     )
     field_grad, pieces_b = lax.optimization_barrier((field_grad, pieces_b))
-    grads_b = last_sums_at_once(pieces_b, row_parts)
-    field_grad, pieces_a = lax.optimization_barrier((field_grad, pieces_a))
+    grads_b = last_sums(pieces_b, row_parts)
+    field_grad, pieces_a, rest = lax.optimization_barrier((field_grad, pieces_a, rest))
     field_grad = lax.all_to_all(field_grad, "col", 0, 0, tiled=True).reshape(high, wide, channels)
+    pieces_out += [swap(item, "row", row_parts, 3 + step) for step, item in enumerate(rest)]
     output = jnp.zeros((high, wide, channels), BF16)
     for step, piece in enumerate(pieces_out):
         piece = piece.reshape(high, cols, channels)

time: 136 us -> 130 us (0.956)
  waiting for transfers between devices: 32.8 us -> 30.1 us
  starting transfers between devices: 46 us -> 43.4 us
  Pallas kernels: 49 us -> 50.4 us
    all_to_all x1 -> x0, starting transfers between devices: 3.41 us -> none  [last_sums_at_once(): got = lax.all_to_all(held, 'row', 0, 0, tiled=True)]
    all_to_all x1, waiting for transfers between devices: 8.79 us -> 6.01 us  [body(): lax.all_to_all(field_grad, 'col', 0, 0, tiled=True)]
    all_to_all x1 -> x0, waiting for transfers between devices: 2.57 us -> none  [last_sums_at_once(): got = lax.all_to_all(held, 'row', 0, 0, tiled=True)]
    ppermute x23 -> x26, waiting for transfers between devices: 6.94 us -> 9.4 us  [swap(): return lax.ppermute(item, axis, [(at, at ^ step) for at in range(count)])]
    pallas_call x9, Pallas kernels: 49 us -> 50.4 us  [call(): pl.pallas_call(kernel, in_specs=[spec(where) for _, where in ins], out_sp...]
    ppermute x23 -> x26, starting transfers between devices: 25.8 us -> 27 us  [swap(): return lax.ppermute(item, axis, [(at, at ^ step) for at in range(count)])]
  transfers between devices with their start and end apart: 28 -> 30, of which waited for: 15 -> 14; matrix products, arithmetic and copies ran while one was open for 3% -> 2% of each run, Pallas kernels for 25% -> 26%
where the time goes in v12:
time: 130 us
  Pallas kernels  50.4 us (39%)
  starting transfers between devices  43.4 us (33%)
  waiting for transfers between devices  30.1 us (23%)
  local copies, waits for them, and re-layouts  3.65 us (3%)
    pallas_call x9, Pallas kernels, call(): pl.pallas_call(kernel, in_specs=[spec(where) for _, where in ins], out_sp...  50.4 us
    ppermute x26, starting transfers between devices, swap(): return lax.ppermute(item, axis, [(at, at ^ step) for at in range(count)])  27 us
    all_to_all x2, waiting for transfers between devices, all_to_all(): lax.all_to_all(item, ('row', 'col'), 0, 0, tiled=True)  12.8 us
    ppermute x26, waiting for transfers between devices, swap(): return lax.ppermute(item, axis, [(at, at ^ step) for at in range(count)])  9.4 us
    all_to_all x2, starting transfers between devices, all_to_all(): lax.all_to_all(item, ('row', 'col'), 0, 0, tiled=True)  7.68 us
    all_to_all x1, waiting for transfers between devices, body(): lax.all_to_all(field_grad, 'col', 0, 0, tiled=True)  6.01 us
    all_to_all x1, starting transfers between devices, body(): lax.all_to_all(field.reshape(col_parts, rows, wide, channels), 'col', 0,...  5.18 us
    all_to_all x1, starting transfers between devices, body(): lax.all_to_all(field_grad, 'col', 0, 0, tiled=True)  3.49 us
  transfers between devices with their start and end apart: 30, of which 14 were waited for; matrix products, arithmetic and copies ran while one was open for 2% of the time, Pallas kernels for 26%

profile of v12, /device:TPU:0, one launch (start us, length us, event | category | flops | bytes accessed | tf_op | source)
XLA Modules:
  0.0 129.6 jit_solution(444698814092894764)
XLA Ops:
  0.6 5.2 %all-to-all-start = ((bf16[8,2,32,512]{3,2,1,0:T(8,128)(2,1)}), bf16[8,2,32,512]{3,2,1,0:T(8,128)(2,1)S(1)}, u32[]{:S(2)}, u32[]{:S(2)}) async-start(bf16[8,2,32,512]{3,2,1,0:T(8,128)(2,1)} %bitcast.69), calls=%async_computation | async-start | bytes 1048576 | tf_op jit(solution)/shard_map/all_to_all | solution.py:451
  7.0 1.6 %collective-permute-start = (bf16[16,8,512]{2,1,0:T(8,128)(2,1)S(1)}, bf16[16,8,512]{2,1,0:T(8,128)(2,1)S(1)}, u32[]{:S(2)}, u32[]{:S(2)}) collective-permute-start(bf16[16,8,512]{2,1,0:T(8,128)(2,1)S(1)} %get-tuple-element.170), channel_id=1, source_target_pairs={{0,8},{8,0},{16,24},{24,16},{1,9},{9,1},{17,25},{25,17},{2,10},{10... | collective-permute-start | bytes 393224 | tf_op jit(solution)/shard_map/ppermute | solution.py:383
  8.6 2.6 %collective-permute-start.1 = (bf16[16,8,512]{2,1,0:T(8,128)(2,1)S(1)}, bf16[16,8,512]{2,1,0:T(8,128)(2,1)S(1)}, u32[]{:S(2)}, u32[]{:S(2)}) collective-permute-start(bf16[16,8,512]{2,1,0:T(8,128)(2,1)S(1)} %get-tuple-element.172), channel_id=1, source_target_pairs={{0,16},{8,24},{16,0},{24,8},{1,17},{9,25},{17,1},{25,9},{2,18},{10... | collective-permute-start | bytes 393224 | tf_op jit(solution)/shard_map/ppermute | solution.py:383
  11.4 2.2 %shard_map.67.turn_hbm.refs_5_ = bf16[7,512,512]{2,1,0:T(8,128)(2,1)} custom-call(), custom_call_target="tpu_custom_call" | custom-call | flops 1048576 | bytes 1024 | tf_op jit(solution)/shard_map/pallas_call | solution.py:371
  13.6 1.9 %all-to-all-done.x_ref = bf16[8,2,32,512]{3,2,1,0:T(8,128)(2,1)S(1)} async-done(((bf16[8,2,32,512]{3,2,1,0:T(8,128)(2,1)}), bf16[8,2,32,512]{3,2,1,0:T(8,128)(2,1)S(1)}, u32[]{:S(2)}, u32[]{:S(2)}) %all-to-all-start) | async-done | bytes 524320 | tf_op jit(solution)/shard_map/all_to_all | solution.py:451
  15.6 8.2 %shard_map.68 = (bf16[512,512]{1,0:T(8,128)(2,1)}, bf16[512,512]{1,0:T(8,128)(2,1)}, bf16[512,512]{1,0:T(8,128)(2,1)}, bf16[512,512]{1,0:T(8,128)(2,1)}, bf16[51...) custom-call(bf16[8,2,32,512]{3,2,1,0:T(8,128)(2,1)S(1)} %all-to-all-done.x_ref, ...), custom_call_target="tpu_custom_call" | custom-call | flops 1048576 | bytes 1024 | tf_op jit(solution)/shard_map/pallas_call | solution.py:371
  24.4 4.4 %all-to-all-start.1 = ((bf16[32,16,512]{2,1,0:T(8,128)(2,1)}), bf16[32,16,512]{2,1,0:T(8,128)(2,1)S(1)}, u32[]{:S(2)}, u32[]{:S(2)}) async-start(bf16[32,16,512]{2,1,0:T(8,128)(2,1)} %bitcast.71), calls=%async_computation.1 | async-start | bytes 1048576 | tf_op jit(solution)/shard_map/all_to_all | solution.py:449
  29.8 2.0 %shard_map.69 = (bf16[512,512]{1,0:T(8,128)(2,1)S(1)}, bf16[512,512]{1,0:T(8,128)(2,1)S(1)}, bf16[2,512,512]{2,1,0:T(8,128)(2,1)S(1)}) custom-call(bf16[128,512]{1,0:T(8,128)(2,1)S(1)} %get-tuple-element.88.refs_0_, bf16[128,512]{1,0:T(8,128)(2,1)S(1)} %bitcast.61, bf16[128,512]{1,0:T(8,128)(2,1)S(1)} %bitcast.62, bf16[128,512]{1,0:T(8,128)(2,1)S(1)} %bitcast.63, ...), custom_call_target="tpu_custom_call" | custom-call | flops 1048576 | bytes 1024 | tf_op jit(solution)/shard_map/pallas_call | solution.py:371
  31.8 12.6 %all-to-all-done.1 = bf16[32,16,512]{2,1,0:T(8,128)(2,1)S(1)} async-done(((bf16[32,16,512]{2,1,0:T(8,128)(2,1)}), bf16[32,16,512]{2,1,0:T(8,128)(2,1)S(1)}, u32[]{:S(2)}, u32[]{:S(2)}) %all-to-all-start.1) | async-done | bytes 524320 | tf_op jit(solution)/shard_map/all_to_all | solution.py:449
  44.4 14.9 %shard_map.70 = (bf16[512,512]{1,0:T(8,128)(2,1)}, bf16[512,512]{1,0:T(8,128)(2,1)}, bf16[512,512]{1,0:T(8,128)(2,1)}, bf16[512,512]{1,0:T(8,128)(2,1)}, bf16[512,1536]{1,0:T(8,128)(2,1)}) custom-call(bf16[512,512]{1,0:T(8,128)(2,1)S(1)} %bitcast.60, bf16[512,512]{1,0:T(8,128)(2,1)S(1)} %get-tuple-element.92.cot_ref.cot_hbm, ...), custom_call_target="tpu_custom_call" | custom-call | flops 1048576 | bytes 1024 | tf_op jit(solution)/shard_map/pallas_call | solution.py:371
  59.3 3.3 %all-to-all-start.2 = ((bf16[32,16,512]{2,1,0:T(8,128)(2,1)}), bf16[32,16,512]{2,1,0:T(8,128)(2,1)S(1)}, u32[]{:S(2)}, u32[]{:S(2)}) async-start(bf16[32,16,512]{2,1,0:T(8,128)(2,1)} %bitcast.70), calls=%async_computation.2 | async-start | bytes 1048576 | tf_op jit(solution)/shard_map/all_to_all | solution.py:449
  62.6 5.7 %shard_map.71 = (bf16[128,512]{1,0:T(8,128)(2,1)}, bf16[128,512]{1,0:T(8,128)(2,1)}, bf16[128,512]{1,0:T(8,128)(2,1)}, bf16[128,512]{1,0:T(8,128)(2,1)}, bf16[4,...) custom-call(bf16[512,512]{1,0:T(8,128)(2,1)} %copy-done, ...), custom_call_target="tpu_custom_call" | custom-call | flops 1048576 | bytes 1024 | tf_op jit(solution)/shard_map/pallas_call | solution.py:371
  72.6 1.7 %collective-permute-start.7 = (bf16[4,64,512]{2,1,0:T(8,128)(2,1)S(1)}, bf16[4,64,512]{2,1,0:T(8,128)(2,1)S(1)}, u32[]{:S(2)}, u32[]{:S(2)}) collective-permute-start(bf16[4,64,512]{2,1,0:T(8,128)(2,1)S(1)} %get-tuple-element.111), channel_id=1, source_target_pairs={{0,2},{1,3},{2,0},{3,1},{4,6},{5,7},{6,4},{7,5},{8,10},{9,11},{10,... | collective-permute-start | bytes 786440 | tf_op jit(solution)/shard_map/ppermute | solution.py:383
  76.2 1.6 %collective-permute-start.10 = (bf16[128,512]{1,0:T(8,128)(2,1)S(1)}, bf16[128,512]{1,0:T(8,128)(2,1)S(1)}, u32[]{:S(2)}, u32[]{:S(2)}) collective-permute-start(bf16[128,512]{1,0:T(8,128)(2,1)S(1)} %copy-done.8), channel_id=1, source_target_pairs={{0,8},{8,0},{16,24},{24,16},{1,9},{9,1},{17,25},{25,17},{2,10},{10... | collective-permute-start | bytes 393224 | tf_op jit(solution)/shard_map/ppermute | solution.py:383
  78.0 2.2 %collective-permute-start.11 = (bf16[128,512]{1,0:T(8,128)(2,1)S(1)}, bf16[128,512]{1,0:T(8,128)(2,1)S(1)}, u32[]{:S(2)}, u32[]{:S(2)}) collective-permute-start(bf16[128,512]{1,0:T(8,128)(2,1)S(1)} %copy-done.7), channel_id=1, source_target_pairs={{0,16},{8,24},{16,0},{24,8},{1,17},{9,25},{17,1},{25,9},{2,18},{10... | collective-permute-start | bytes 393224 | tf_op jit(solution)/shard_map/ppermute | solution.py:383
  80.2 10.6 %shard_map.73 = (bf16[512,512]{1,0:T(8,128)(2,1)S(1)}, bf16[512,1536]{1,0:T(8,128)(2,1)}, bf16[4,64,512]{2,1,0:T(8,128)(2,1)}, bf16[4,64,512]{2,1,0:T(8,128)(2,1...) custom-call(bf16[512,512]{1,0:T(8,128)(2,1)S(1)} %bitcast.59, ...), custom_call_target="tpu_custom_call" | custom-call | flops 1048576 | bytes 1024 | tf_op jit(solution)/shard_map/pallas_call | solution.py:371
  95.2 1.5 %collective-permute-start.16 = (bf16[4,64,512]{2,1,0:T(8,128)(2,1)S(1)}, bf16[4,64,512]{2,1,0:T(8,128)(2,1)S(1)}, u32[]{:S(2)}, u32[]{:S(2)}) collective-permute-start(bf16[4,64,512]{2,1,0:T(8,128)(2,1)S(1)} %get-tuple-element.149), channel_id=1, source_target_pairs={{0,2},{1,3},{2,0},{3,1},{4,6},{5,7},{6,4},{7,5},{8,10},{9,11},{10,... | collective-permute-start | bytes 786440 | tf_op jit(solution)/shard_map/ppermute | solution.py:383
  98.7 4.1 %shard_map.75 = bf16[8,2,32,512]{3,2,1,0:T(8,128)(2,1)} custom-call(bf16[8,2,32,512]{3,2,1,0:T(8,128)(2,1)S(1)} %all-to-all-done.x_ref, bf16[512,512]{1,0:T(8,128)(2,1)S(1)} %get-tuple-element.138.dm_ref, f32[2,512]{1,0:T(2,128)S(1)} %copy-done.3, bf16[512,1536]{1,0:T(8,128)(2,1)} %get-tuple-element.152.dqkv_hbm, bf16[2,4,512,512]{3,2,1,0:T(8,128)(2,1)} %w_hbm.9), custom_call_target="tpu_custom_call" | custom-call | flops 1048576 | bytes 1024 | tf_op jit(solution)/shard_map/pallas_call | solution.py:371
  105.0 2.5 %collective-permute-start.25 = (bf16[4,16,512]{2,1,0:T(8,128)(2,1)S(1)}, bf16[4,16,512]{2,1,0:T(8,128)(2,1)S(1)}, u32[]{:S(2)}, u32[]{:S(2)}) collective-permute-start(bf16[4,16,512]{2,1,0:T(8,128)(2,1)S(1)} %get-tuple-element.178), channel_id=1, source_target_pairs={{0,24},{8,16},{16,8},{24,0},{1,25},{9,17},{17,9},{25,1},{2,26},{10... | collective-permute-start | bytes 196616 | tf_op jit(solution)/shard_map/ppermute | solution.py:383
  107.4 2.9 %collective-permute-done.17 = bf16[4,64,512]{2,1,0:T(8,128)(2,1)S(1)} collective-permute-done((bf16[4,64,512]{2,1,0:T(8,128)(2,1)S(1)}, bf16[4,64,512]{2,1,0:T(8,128)(2,1)S(1)}, u32[]{:S(2)}, u32[]{:S(2)}) %collective-permute-start.17) | collective-permute-done | bytes 262176 | tf_op jit(solution)/shard_map/ppermute | solution.py:383
  111.7 3.3 %collective-permute-start.22 = (bf16[4,16,512]{2,1,0:T(8,128)(2,1)S(1)}, bf16[4,16,512]{2,1,0:T(8,128)(2,1)S(1)}, u32[]{:S(2)}, u32[]{:S(2)}) collective-permute-start(bf16[4,16,512]{2,1,0:T(8,128)(2,1)S(1)} %get-tuple-element.175), channel_id=1, source_target_pairs={{0,24},{8,16},{16,8},{24,0},{1,25},{9,17},{17,9},{25,1},{2,26},{10... | collective-permute-start | bytes 196616 | tf_op jit(solution)/shard_map/ppermute | solution.py:383
  115.6 3.5 %all-to-all-start.3 = ((bf16[8,2,32,512]{3,2,1,0:T(8,128)(2,1)}), bf16[8,2,32,512]{3,2,1,0:T(8,128)(2,1)S(1)}, u32[]{:S(2)}, u32[]{:S(2)}) async-start(bf16[8,2,32,512]{3,2,1,0:T(8,128)(2,1)} %shard_map.75), calls=%async_computation.3 | async-start | bytes 1048576 | tf_op jit(solution)/shard_map/all_to_all | solution.py:516
  119.1 2.9 %collective-permute-done.21 = bf16[4,16,512]{2,1,0:T(8,128)(2,1)S(1)} collective-permute-done((bf16[4,16,512]{2,1,0:T(8,128)(2,1)S(1)}, bf16[4,16,512]{2,1,0:T(8,128)(2,1)S(1)}, u32[]{:S(2)}, u32[]{:S(2)}) %collective-permute-start.21) | collective-permute-done | bytes 65568 | tf_op jit(solution)/shard_map/ppermute | solution.py:383
  122.8 6.0 %all-to-all-done.3 = bf16[8,2,32,512]{3,2,1,0:T(8,128)(2,1)S(1)} async-done(((bf16[8,2,32,512]{3,2,1,0:T(8,128)(2,1)}), bf16[8,2,32,512]{3,2,1,0:T(8,128)(2,1)S(1)}, u32[]{:S(2)}, u32[]{:S(2)}) %all-to-all-start.3) | async-done | bytes 524320 | tf_op jit(solution)/shard_map/all_to_all | solution.py:516
  (77 shorter events, 21.2 us)
Async XLA Ops:
  0.6 14.9 %all-to-all-start = ((bf16[8,2,32,512]{3,2,1,0:T(8,128)(2,1)}), bf16[8,2,32,512]{3,2,1,0:T(8,128)(2,1)S(1)}, u32[]{:S(2)}, u32[]{:S(2)}) async-start(bf16[8,2,32,512]{3,2,1,0:T(8,128)(2,1)} %bitcast.69), calls=%async_computation | async-start | bytes 1048576 | tf_op jit(solution)/shard_map/all_to_all | solution.py:451
  7.0 16.8 %collective-permute-start = (bf16[16,8,512]{2,1,0:T(8,128)(2,1)S(1)}, bf16[16,8,512]{2,1,0:T(8,128)(2,1)S(1)}, u32[]{:S(2)}, u32[]{:S(2)}) collective-permute-start(bf16[16,8,512]{2,1,0:T(8,128)(2,1)S(1)} %get-tuple-element.170), channel_id=1, source_target_pairs={{0,8},{8,0},{16,24},{24,16},{1,9},{9,1},{17,25},{25,17},{2,10},{10... | collective-permute-start | bytes 393224 | tf_op jit(solution)/shard_map/ppermute | solution.py:383
  8.6 15.1 %collective-permute-start.1 = (bf16[16,8,512]{2,1,0:T(8,128)(2,1)S(1)}, bf16[16,8,512]{2,1,0:T(8,128)(2,1)S(1)}, u32[]{:S(2)}, u32[]{:S(2)}) collective-permute-start(bf16[16,8,512]{2,1,0:T(8,128)(2,1)S(1)} %get-tuple-element.172), channel_id=1, source_target_pairs={{0,16},{8,24},{16,0},{24,8},{1,17},{9,25},{17,1},{25,9},{2,18},{10... | collective-permute-start | bytes 393224 | tf_op jit(solution)/shard_map/ppermute | solution.py:383
  11.2 12.6 %collective-permute-start.2 = (bf16[16,8,512]{2,1,0:T(8,128)(2,1)S(1)}, bf16[16,8,512]{2,1,0:T(8,128)(2,1)S(1)}, u32[]{:S(2)}, u32[]{:S(2)}) collective-permute-start(bf16[16,8,512]{2,1,0:T(8,128)(2,1)S(1)} %get-tuple-element.169), channel_id=1, source_target_pairs={{0,24},{8,16},{16,8},{24,0},{1,25},{9,17},{17,9},{25,1},{2,26},{10... | collective-permute-start | bytes 393224 | tf_op jit(solution)/shard_map/ppermute | solution.py:383
  24.4 20.0 %all-to-all-start.1 = ((bf16[32,16,512]{2,1,0:T(8,128)(2,1)}), bf16[32,16,512]{2,1,0:T(8,128)(2,1)S(1)}, u32[]{:S(2)}, u32[]{:S(2)}) async-start(bf16[32,16,512]{2,1,0:T(8,128)(2,1)} %bitcast.71), calls=%async_computation.1 | async-start | bytes 1048576 | tf_op jit(solution)/shard_map/all_to_all | solution.py:449
  59.3 18.7 %all-to-all-start.2 = ((bf16[32,16,512]{2,1,0:T(8,128)(2,1)}), bf16[32,16,512]{2,1,0:T(8,128)(2,1)S(1)}, u32[]{:S(2)}, u32[]{:S(2)}) async-start(bf16[32,16,512]{2,1,0:T(8,128)(2,1)} %bitcast.70), calls=%async_computation.2 | async-start | bytes 1048576 | tf_op jit(solution)/shard_map/all_to_all | solution.py:449
  69.0 2.3 %collective-permute-start.6 = (bf16[4,64,512]{2,1,0:T(8,128)(2,1)}, bf16[4,64,512]{2,1,0:T(8,128)(2,1)S(1)}, u32[]{:S(2)}, u32[]{:S(2)}) collective-permute-start(bf16[4,64,512]{2,1,0:T(8,128)(2,1)} %get-tuple-element.109), channel_id=1, source_target_pairs={{0,1},{1,0},{2,3},{3,2},{4,5},{5,4},{6,7},{7,6},{8,9},{9,8},{10,11... | collective-permute-start | bytes 786440 | tf_op jit(solution)/shard_map/ppermute | solution.py:383
  72.6 18.2 %collective-permute-start.7 = (bf16[4,64,512]{2,1,0:T(8,128)(2,1)S(1)}, bf16[4,64,512]{2,1,0:T(8,128)(2,1)S(1)}, u32[]{:S(2)}, u32[]{:S(2)}) collective-permute-start(bf16[4,64,512]{2,1,0:T(8,128)(2,1)S(1)} %get-tuple-element.111), channel_id=1, source_target_pairs={{0,2},{1,3},{2,0},{3,1},{4,6},{5,7},{6,4},{7,5},{8,10},{9,11},{10,... | collective-permute-start | bytes 786440 | tf_op jit(solution)/shard_map/ppermute | solution.py:383
  74.3 16.6 %collective-permute-start.8 = (bf16[4,64,512]{2,1,0:T(8,128)(2,1)S(1)}, bf16[4,64,512]{2,1,0:T(8,128)(2,1)S(1)}, u32[]{:S(2)}, u32[]{:S(2)}) collective-permute-start(bf16[4,64,512]{2,1,0:T(8,128)(2,1)S(1)} %get-tuple-element.112), channel_id=1, source_target_pairs={{0,4},{1,5},{2,6},{3,7},{4,0},{5,1},{6,2},{7,3},{8,12},{9,13},{10,... | collective-permute-start | bytes 786440 | tf_op jit(solution)/shard_map/ppermute | solution.py:383
  75.7 15.1 %collective-permute-start.9 = (bf16[4,64,512]{2,1,0:T(8,128)(2,1)S(1)}, bf16[4,64,512]{2,1,0:T(8,128)(2,1)S(1)}, u32[]{:S(2)}, u32[]{:S(2)}) collective-permute-start(bf16[4,64,512]{2,1,0:T(8,128)(2,1)S(1)} %get-tuple-element.113), channel_id=1, source_target_pairs={{0,6},{1,7},{2,4},{3,5},{4,2},{5,3},{6,0},{7,1},{8,14},{9,15},{10,... | collective-permute-start | bytes 786440 | tf_op jit(solution)/shard_map/ppermute | solution.py:383
  76.2 14.7 %collective-permute-start.10 = (bf16[128,512]{1,0:T(8,128)(2,1)S(1)}, bf16[128,512]{1,0:T(8,128)(2,1)S(1)}, u32[]{:S(2)}, u32[]{:S(2)}) collective-permute-start(bf16[128,512]{1,0:T(8,128)(2,1)S(1)} %copy-done.8), channel_id=1, source_target_pairs={{0,8},{8,0},{16,24},{24,16},{1,9},{9,1},{17,25},{25,17},{2,10},{10... | collective-permute-start | bytes 393224 | tf_op jit(solution)/shard_map/ppermute | solution.py:383
  78.0 12.9 %collective-permute-start.11 = (bf16[128,512]{1,0:T(8,128)(2,1)S(1)}, bf16[128,512]{1,0:T(8,128)(2,1)S(1)}, u32[]{:S(2)}, u32[]{:S(2)}) collective-permute-start(bf16[128,512]{1,0:T(8,128)(2,1)S(1)} %copy-done.7), channel_id=1, source_target_pairs={{0,16},{8,24},{16,0},{24,8},{1,17},{9,25},{17,1},{25,9},{2,18},{10... | collective-permute-start | bytes 393224 | tf_op jit(solution)/shard_map/ppermute | solution.py:383
  91.5 2.3 %collective-permute-start.15 = (bf16[4,64,512]{2,1,0:T(8,128)(2,1)}, bf16[4,64,512]{2,1,0:T(8,128)(2,1)S(1)}, u32[]{:S(2)}, u32[]{:S(2)}) collective-permute-start(bf16[4,64,512]{2,1,0:T(8,128)(2,1)} %get-tuple-element.147), channel_id=1, source_target_pairs={{0,1},{1,0},{2,3},{3,2},{4,5},{5,4},{6,7},{7,6},{8,9},{9,8},{10,11... | collective-permute-start | bytes 786440 | tf_op jit(solution)/shard_map/ppermute | solution.py:383
  95.2 9.8 %collective-permute-start.16 = (bf16[4,64,512]{2,1,0:T(8,128)(2,1)S(1)}, bf16[4,64,512]{2,1,0:T(8,128)(2,1)S(1)}, u32[]{:S(2)}, u32[]{:S(2)}) collective-permute-start(bf16[4,64,512]{2,1,0:T(8,128)(2,1)S(1)} %get-tuple-element.149), channel_id=1, source_target_pairs={{0,2},{1,3},{2,0},{3,1},{4,6},{5,7},{6,4},{7,5},{8,10},{9,11},{10,... | collective-permute-start | bytes 786440 | tf_op jit(solution)/shard_map/ppermute | solution.py:383
  96.7 13.7 %collective-permute-start.17 = (bf16[4,64,512]{2,1,0:T(8,128)(2,1)S(1)}, bf16[4,64,512]{2,1,0:T(8,128)(2,1)S(1)}, u32[]{:S(2)}, u32[]{:S(2)}) collective-permute-start(bf16[4,64,512]{2,1,0:T(8,128)(2,1)S(1)} %get-tuple-element.150), channel_id=1, source_target_pairs={{0,4},{1,5},{2,6},{3,7},{4,0},{5,1},{6,2},{7,3},{8,12},{9,13},{10,... | collective-permute-start | bytes 786440 | tf_op jit(solution)/shard_map/ppermute | solution.py:383
  98.2 12.2 %collective-permute-start.18 = (bf16[4,64,512]{2,1,0:T(8,128)(2,1)S(1)}, bf16[4,64,512]{2,1,0:T(8,128)(2,1)S(1)}, u32[]{:S(2)}, u32[]{:S(2)}) collective-permute-start(bf16[4,64,512]{2,1,0:T(8,128)(2,1)S(1)} %get-tuple-element.151), channel_id=1, source_target_pairs={{0,6},{1,7},{2,4},{3,5},{4,2},{5,3},{6,0},{7,1},{8,14},{9,15},{10,... | collective-permute-start | bytes 786440 | tf_op jit(solution)/shard_map/ppermute | solution.py:383
  103.0 8.7 %collective-permute-start.23 = (bf16[4,16,512]{2,1,0:T(8,128)(2,1)S(1)}, bf16[4,16,512]{2,1,0:T(8,128)(2,1)S(1)}, u32[]{:S(2)}, u32[]{:S(2)}) collective-permute-start(bf16[4,16,512]{2,1,0:T(8,128)(2,1)S(1)} %get-tuple-element.176), channel_id=1, source_target_pairs={{0,8},{8,0},{16,24},{24,16},{1,9},{9,1},{17,25},{25,17},{2,10},{10... | collective-permute-start | bytes 196616 | tf_op jit(solution)/shard_map/ppermute | solution.py:383
  103.5 11.5 %collective-permute-start.24 = (bf16[4,16,512]{2,1,0:T(8,128)(2,1)S(1)}, bf16[4,16,512]{2,1,0:T(8,128)(2,1)S(1)}, u32[]{:S(2)}, u32[]{:S(2)}) collective-permute-start(bf16[4,16,512]{2,1,0:T(8,128)(2,1)S(1)} %get-tuple-element.177), channel_id=1, source_target_pairs={{0,16},{8,24},{16,0},{24,8},{1,17},{9,25},{17,1},{25,9},{2,18},{10... | collective-permute-start | bytes 196616 | tf_op jit(solution)/shard_map/ppermute | solution.py:383
  105.0 10.0 %collective-permute-start.25 = (bf16[4,16,512]{2,1,0:T(8,128)(2,1)S(1)}, bf16[4,16,512]{2,1,0:T(8,128)(2,1)S(1)}, u32[]{:S(2)}, u32[]{:S(2)}) collective-permute-start(bf16[4,16,512]{2,1,0:T(8,128)(2,1)S(1)} %get-tuple-element.178), channel_id=1, source_target_pairs={{0,24},{8,16},{16,8},{24,0},{1,25},{9,17},{17,9},{25,1},{2,26},{10... | collective-permute-start | bytes 196616 | tf_op jit(solution)/shard_map/ppermute | solution.py:383
  110.5 8.6 %collective-permute-start.20 = (bf16[4,16,512]{2,1,0:T(8,128)(2,1)S(1)}, bf16[4,16,512]{2,1,0:T(8,128)(2,1)S(1)}, u32[]{:S(2)}, u32[]{:S(2)}) collective-permute-start(bf16[4,16,512]{2,1,0:T(8,128)(2,1)S(1)} %get-tuple-element.173), channel_id=1, source_target_pairs={{0,8},{8,0},{16,24},{24,16},{1,9},{9,1},{17,25},{25,17},{2,10},{10... | collective-permute-start | bytes 196616 | tf_op jit(solution)/shard_map/ppermute | solution.py:383
  111.1 10.9 %collective-permute-start.21 = (bf16[4,16,512]{2,1,0:T(8,128)(2,1)S(1)}, bf16[4,16,512]{2,1,0:T(8,128)(2,1)S(1)}, u32[]{:S(2)}, u32[]{:S(2)}) collective-permute-start(bf16[4,16,512]{2,1,0:T(8,128)(2,1)S(1)} %get-tuple-element.174), channel_id=1, source_target_pairs={{0,16},{8,24},{16,0},{24,8},{1,17},{9,25},{17,1},{25,9},{2,18},{10... | collective-permute-start | bytes 196616 | tf_op jit(solution)/shard_map/ppermute | solution.py:383
  111.7 10.3 %collective-permute-start.22 = (bf16[4,16,512]{2,1,0:T(8,128)(2,1)S(1)}, bf16[4,16,512]{2,1,0:T(8,128)(2,1)S(1)}, u32[]{:S(2)}, u32[]{:S(2)}) collective-permute-start(bf16[4,16,512]{2,1,0:T(8,128)(2,1)S(1)} %get-tuple-element.175), channel_id=1, source_target_pairs={{0,24},{8,16},{16,8},{24,0},{1,25},{9,17},{17,9},{25,1},{2,26},{10... | collective-permute-start | bytes 196616 | tf_op jit(solution)/shard_map/ppermute | solution.py:383
  115.1 7.7 %collective-permute-start.19 = (bf16[128,512]{1,0:T(8,128)(2,1)S(1)}, bf16[128,512]{1,0:T(8,128)(2,1)S(1)}, u32[]{:S(2)}, u32[]{:S(2)}) collective-permute-start(bf16[128,512]{1,0:T(8,128)(2,1)S(1)} %copy-done.6), channel_id=1, source_target_pairs={{0,24},{8,16},{16,8},{24,0},{1,25},{9,17},{17,9},{25,1},{2,26},{10... | collective-permute-start | bytes 393224 | tf_op jit(solution)/shard_map/ppermute | solution.py:383
  115.6 13.2 %all-to-all-start.3 = ((bf16[8,2,32,512]{3,2,1,0:T(8,128)(2,1)}), bf16[8,2,32,512]{3,2,1,0:T(8,128)(2,1)S(1)}, u32[]{:S(2)}, u32[]{:S(2)}) async-start(bf16[8,2,32,512]{3,2,1,0:T(8,128)(2,1)} %shard_map.75), calls=%async_computation.3 | async-start | bytes 1048576 | tf_op jit(solution)/shard_map/all_to_all | solution.py:516
  (15 other events, 97.9 us)

commit v13 on v12

--- a/solution.py
+++ b/solution.py
@@ -76,7 +76,7 @@
     return lax.broadcasted_iota(jnp.int32, (count, 2 * width), 1) < width
 
 
-def attention_forward(q_ref, k_ref, v_ref, att_ref, p_ref, groups, count, width, span, unroll=2):
+def attention_forward(q_ref, k_ref, v_ref, att_ref, p_ref, groups, count, width, span, unroll=4):
     first = head_lanes(count, width)
     pairs = HEADS // 2
     scale = width ** (-0.5)
@@ -107,7 +107,7 @@
     lax.fori_loop(0, groups * pairs, step, 0, unroll=unroll)
 
 
-def attention_back(q_ref, k_ref, v_ref, p_ref, da_ref, dqkv_ref, groups, count, width, unroll=2):
+def attention_back(q_ref, k_ref, v_ref, p_ref, da_ref, dqkv_ref, groups, count, width, unroll=4):
     first = head_lanes(count, width)
     pairs = HEADS // 2
     channels = HEADS * width
@@ -278,6 +278,10 @@
     start(fg_ref, fg_hbm, sems.at[2]).wait()
 
 
+def store(x_ref, x_hbm, sem):
+    start(x_ref, x_hbm, sem).wait()
+
+
 def column_first(parts, *refs):
     c_refs, (w_hbm, turn_hbm, cot_ref, da_ref, early_ref, w_ref, turn_ref, sems) = refs[:parts], refs[parts:]
     coming = [
@@ -315,9 +319,9 @@
     v_ref[...] = dot(normed, w_ref[1]).astype(BF16)
     count = together * height
     groups = cols // together
-    attention_forward(q_ref, k_ref, v_ref, att_ref, p_ref, groups, count, width, height, 4)
+    attention_forward(q_ref, k_ref, v_ref, att_ref, p_ref, groups, count, width, height)
     going.append(start(att_ref, att_hbm, sems.at[5]))
-    attention_back(q_ref, k_ref, v_ref, p_ref, da_ref, dqkv_ref, groups, count, width, 4)
+    attention_back(q_ref, k_ref, v_ref, p_ref, da_ref, dqkv_ref, groups, count, width)
     going.append(start(dqkv_ref, dqkv_hbm, sems.at[6]))
     d_normed = input_back(dqkv_ref, [early_ref.at[1], w_ref.at[0], w_ref.at[1]])
     middle = mid_ref[...].astype(F32)
@@ -361,7 +365,7 @@
 NEAR, FAR, ANY = pltpu.VMEM, pltpu.HBM, None
 
 
-def call(kernel, ins, outs, scratch):
+def call(kernel, ins, outs, scratch, flops=1 << 20):
     def spec(where):
         return pl.BlockSpec(memory_space=pltpu.HBM if where is FAR else pltpu.VMEM)
 
@@ -375,7 +379,7 @@
         out_shape=[jax.ShapeDtypeStruct(shape, BF16) if where is ANY else where(shape, BF16) for shape, where in outs],
         scratch_shapes=scratch,
         compiler_params=pltpu.CompilerParams(vmem_limit_bytes=48 * 1024 * 1024),
-        cost_estimate=pl.CostEstimate(flops=1 << 20, bytes_accessed=1 << 10, transcendentals=0),
+        cost_estimate=pl.CostEstimate(flops=flops, bytes_accessed=1 << 10, transcendentals=0),
     )(*[place(item, where) for item, where in ins])
 
 
@@ -417,7 +421,7 @@
     height = high * row_parts
     length = wide * col_parts
     width = channels // HEADS
-    together = min(cols, max(1, 128 // height))
+    together = min(cols, max(1, 256 // height))
     devices = row_parts * col_parts
     my_row = lax.axis_index("row")
 
@@ -492,7 +496,6 @@
     pieces_b = plane_pieces(sums_b, plane, core)
     pieces_out = [outs[0], swap(outs[1], "row", row_parts, 1)]
     d_mid, rest, _ = lax.optimization_barrier((d_mid, outs[2:], sums_b))
-    pieces_out += [swap(item, "row", row_parts, 2 + step) for step, item in enumerate(rest[:1])]
     results = call(
         functools.partial(row_back, (rows, length, width, plane)),
         at(ANY, d_mid) + at(FAR, weights, turn, normed, query, key, value, attended, prob),
@@ -501,20 +504,23 @@
         + [scratch(plane, *packed), scratch(plane, *packed), copies((11,)), copies((2 * plane,))],
     )
     (d_mid, dqkv, *grads), pieces_b, pieces_out, rest = lax.optimization_barrier(
-        (results, pieces_b, pieces_out, rest[1:])
-    )
+        (results, pieces_b, pieces_out, rest)
+    )
+    second = [swap(item, "row", row_parts, 2) for item in rest[:1]]
     sums_a = chip_sums(grads[:plane], grads[plane:], col_parts)
     pieces_a = plane_pieces(sums_a, plane, core)
-    dqkv, _ = lax.optimization_barrier((dqkv, sums_a))
+    dqkv, _, second = lax.optimization_barrier((dqkv, sums_a, second))
     field_grad, = call(
         field_back, at(ANY, x, d_mid, gains) + at(FAR, dqkv, weights), at(FAR, x.shape),
         [scratch(*triple), scratch(3, *flat), scratch(*x.shape), copies((3,))],
     )
     field_grad, pieces_b = lax.optimization_barrier((field_grad, pieces_b))
     grads_b = last_sums(pieces_b, row_parts)
-    field_grad, pieces_a, rest = lax.optimization_barrier((field_grad, pieces_a, rest))
-    field_grad = lax.all_to_all(field_grad, "col", 0, 0, tiled=True).reshape(high, wide, channels)
-    pieces_out += [swap(item, "row", row_parts, 3 + step) for step, item in enumerate(rest)]
+    field_grad, pieces_a, rest = lax.optimization_barrier((field_grad, pieces_a, rest[1:]))
+    field_grad = lax.all_to_all(field_grad, "col", 0, 0, tiled=True)
+    field_grad, = call(store, at(ANY, field_grad), at(FAR, field_grad.shape), [copies], 1 << 34)
+    field_grad = field_grad.reshape(high, wide, channels)
+    pieces_out += second + [swap(item, "row", row_parts, 3 + step) for step, item in enumerate(rest)]
     output = jnp.zeros((high, wide, channels), BF16)
     for step, piece in enumerate(pieces_out):
         piece = piece.reshape(high, cols, channels)

time: 130 us -> 128 us (0.985)
  Pallas kernels: 50.4 us -> 48.4 us
  waiting for transfers between devices: 30.1 us -> 28.6 us
  starting transfers between devices: 43.4 us -> 44.8 us
    ppermute x26, waiting for transfers between devices: 9.4 us -> 5.58 us  [swap(): return lax.ppermute(item, axis, [(at, at ^ step) for at in range(count)])]
    all_to_all x1, waiting for transfers between devices: 6.01 us -> 8.27 us  [body(): field_grad = lax.all_to_all(field_grad, 'col', 0, 0, tiled=True)]
    pallas_call x9 -> x10, Pallas kernels: 50.4 us -> 48.4 us  [call(): pl.pallas_call(kernel, in_specs=[spec(where) for _, where in ins], out_sp...]
    ppermute x26, starting transfers between devices: 27 us -> 28.6 us  [swap(): return lax.ppermute(item, axis, [(at, at ^ step) for at in range(count)])]
  transfers between devices with their start and end apart: 30 -> 30, of which waited for: 14 -> 13; matrix products, arithmetic and copies ran while one was open for 2% -> 2% of each run, Pallas kernels for 26% -> 27%
where the time goes in v13:
time: 128 us; the launch traced here: 127 us
  Pallas kernels  48.4 us (38%)
  starting transfers between devices  44.8 us (35%)
  waiting for transfers between devices  28.6 us (22%)
  local copies, waits for them, and re-layouts  2.85 us (2%)
    pallas_call x10, Pallas kernels, call(): pl.pallas_call(kernel, in_specs=[spec(where) for _, where in ins], out_sp...  48.4 us
    ppermute x26, starting transfers between devices, swap(): return lax.ppermute(item, axis, [(at, at ^ step) for at in range(count)])  28.6 us
    all_to_all x2, waiting for transfers between devices, all_to_all(): lax.all_to_all(item, ('row', 'col'), 0, 0, tiled=True)  12.8 us
    all_to_all x1, waiting for transfers between devices, body(): field_grad = lax.all_to_all(field_grad, 'col', 0, 0, tiled=True)  8.27 us
    all_to_all x2, starting transfers between devices, all_to_all(): lax.all_to_all(item, ('row', 'col'), 0, 0, tiled=True)  7.51 us
    ppermute x26, waiting for transfers between devices, swap(): return lax.ppermute(item, axis, [(at, at ^ step) for at in range(count)])  5.58 us
    all_to_all x1, starting transfers between devices, body(): lax.all_to_all(field.reshape(col_parts, rows, wide, channels), 'col', 0,...  5.18 us
    all_to_all x1, starting transfers between devices, body(): field_grad = lax.all_to_all(field_grad, 'col', 0, 0, tiled=True)  3.49 us
  transfers between devices with their start and end apart: 30, of which 13 were waited for; matrix products, arithmetic and copies ran while one was open for 2% of the time, Pallas kernels for 27%

profile of v13, /device:TPU:0, one launch (start us, length us, event | category | flops | bytes accessed | tf_op | source)
XLA Modules:
  0.0 126.9 jit_solution(2772397187161710876)
XLA Ops:
  0.6 5.2 %all-to-all-start = ((bf16[8,2,32,512]{3,2,1,0:T(8,128)(2,1)}), bf16[8,2,32,512]{3,2,1,0:T(8,128)(2,1)S(1)}, u32[]{:S(2)}, u32[]{:S(2)}) async-start(bf16[8,2,32,512]{3,2,1,0:T(8,128)(2,1)} %bitcast.68), calls=%async_computation | async-start | bytes 1048576 | tf_op jit(solution)/shard_map/all_to_all | solution.py:455
  7.0 1.6 %collective-permute-start = (bf16[16,8,512]{2,1,0:T(8,128)(2,1)S(1)}, bf16[16,8,512]{2,1,0:T(8,128)(2,1)S(1)}, u32[]{:S(2)}, u32[]{:S(2)}) collective-permute-start(bf16[16,8,512]{2,1,0:T(8,128)(2,1)S(1)} %get-tuple-element.172), channel_id=1, source_target_pairs={{0,8},{8,0},{16,24},{24,16},{1,9},{9,1},{17,25},{25,17},{2,10},{10... | collective-permute-start | bytes 393224 | tf_op jit(solution)/shard_map/ppermute | solution.py:387
  8.6 2.6 %collective-permute-start.1 = (bf16[16,8,512]{2,1,0:T(8,128)(2,1)S(1)}, bf16[16,8,512]{2,1,0:T(8,128)(2,1)S(1)}, u32[]{:S(2)}, u32[]{:S(2)}) collective-permute-start(bf16[16,8,512]{2,1,0:T(8,128)(2,1)S(1)} %get-tuple-element.174), channel_id=1, source_target_pairs={{0,16},{8,24},{16,0},{24,8},{1,17},{9,25},{17,1},{25,9},{2,18},{10... | collective-permute-start | bytes 393224 | tf_op jit(solution)/shard_map/ppermute | solution.py:387
  11.4 2.2 %shard_map.67.turn_hbm.refs_5_ = bf16[7,512,512]{2,1,0:T(8,128)(2,1)} custom-call(), custom_call_target="tpu_custom_call" | custom-call | flops 1048576 | bytes 1024 | tf_op jit(solution)/shard_map/pallas_call | solution.py:375
  13.6 1.9 %all-to-all-done.x_ref = bf16[8,2,32,512]{3,2,1,0:T(8,128)(2,1)S(1)} async-done(((bf16[8,2,32,512]{3,2,1,0:T(8,128)(2,1)}), bf16[8,2,32,512]{3,2,1,0:T(8,128)(2,1)S(1)}, u32[]{:S(2)}, u32[]{:S(2)}) %all-to-all-start) | async-done | bytes 524320 | tf_op jit(solution)/shard_map/all_to_all | solution.py:455
  15.6 7.8 %shard_map.68 = (bf16[512,512]{1,0:T(8,128)(2,1)}, bf16[512,512]{1,0:T(8,128)(2,1)}, bf16[512,512]{1,0:T(8,128)(2,1)}, bf16[512,512]{1,0:T(8,128)(2,1)}, bf16[51...) custom-call(bf16[8,2,32,512]{3,2,1,0:T(8,128)(2,1)S(1)} %all-to-all-done.x_ref, ...), custom_call_target="tpu_custom_call" | custom-call | flops 1048576 | bytes 1024 | tf_op jit(solution)/shard_map/pallas_call | solution.py:375
  24.1 4.4 %all-to-all-start.1 = ((bf16[32,16,512]{2,1,0:T(8,128)(2,1)}), bf16[32,16,512]{2,1,0:T(8,128)(2,1)S(1)}, u32[]{:S(2)}, u32[]{:S(2)}) async-start(bf16[32,16,512]{2,1,0:T(8,128)(2,1)} %bitcast.70), calls=%async_computation.1 | async-start | bytes 1048576 | tf_op jit(solution)/shard_map/all_to_all | solution.py:453
  29.4 2.0 %shard_map.69 = (bf16[512,512]{1,0:T(8,128)(2,1)S(1)}, bf16[512,512]{1,0:T(8,128)(2,1)S(1)}, bf16[2,512,512]{2,1,0:T(8,128)(2,1)S(1)}) custom-call(bf16[128,512]{1,0:T(8,128)(2,1)S(1)} %get-tuple-element.89.refs_0_, bf16[128,512]{1,0:T(8,128)(2,1)S(1)} %bitcast.61, bf16[128,512]{1,0:T(8,128)(2,1)S(1)} %bitcast.62, bf16[128,512]{1,0:T(8,128)(2,1)S(1)} %bitcast.63, ...), custom_call_target="tpu_custom_call" | custom-call | flops 1048576 | bytes 1024 | tf_op jit(solution)/shard_map/pallas_call | solution.py:375
  31.4 12.6 %all-to-all-done.1 = bf16[32,16,512]{2,1,0:T(8,128)(2,1)S(1)} async-done(((bf16[32,16,512]{2,1,0:T(8,128)(2,1)}), bf16[32,16,512]{2,1,0:T(8,128)(2,1)S(1)}, u32[]{:S(2)}, u32[]{:S(2)}) %all-to-all-start.1) | async-done | bytes 524320 | tf_op jit(solution)/shard_map/all_to_all | solution.py:453
  44.1 12.7 %shard_map.70 = (bf16[512,512]{1,0:T(8,128)(2,1)}, bf16[512,512]{1,0:T(8,128)(2,1)}, bf16[512,512]{1,0:T(8,128)(2,1)}, bf16[512,512]{1,0:T(8,128)(2,1)}, bf16[512,1536]{1,0:T(8,128)(2,1)}) custom-call(bf16[512,512]{1,0:T(8,128)(2,1)S(1)} %bitcast.60, bf16[512,512]{1,0:T(8,128)(2,1)S(1)} %get-tuple-element.93.cot_ref.cot_hbm, ...), custom_call_target="tpu_custom_call" | custom-call | flops 1048576 | bytes 1024 | tf_op jit(solution)/shard_map/pallas_call | solution.py:375
  56.8 3.1 %all-to-all-start.2 = ((bf16[32,16,512]{2,1,0:T(8,128)(2,1)}), bf16[32,16,512]{2,1,0:T(8,128)(2,1)S(1)}, u32[]{:S(2)}, u32[]{:S(2)}) async-start(bf16[32,16,512]{2,1,0:T(8,128)(2,1)} %bitcast.69), calls=%async_computation.2 | async-start | bytes 1048576 | tf_op jit(solution)/shard_map/all_to_all | solution.py:453
  59.9 5.7 %shard_map.71 = (bf16[128,512]{1,0:T(8,128)(2,1)}, bf16[128,512]{1,0:T(8,128)(2,1)}, bf16[128,512]{1,0:T(8,128)(2,1)}, bf16[128,512]{1,0:T(8,128)(2,1)}, bf16[4,...) custom-call(bf16[512,512]{1,0:T(8,128)(2,1)} %copy-done, ...), custom_call_target="tpu_custom_call" | custom-call | flops 1048576 | bytes 1024 | tf_op jit(solution)/shard_map/pallas_call | solution.py:375
  69.9 1.8 %collective-permute-start.7 = (bf16[4,64,512]{2,1,0:T(8,128)(2,1)S(1)}, bf16[4,64,512]{2,1,0:T(8,128)(2,1)S(1)}, u32[]{:S(2)}, u32[]{:S(2)}) collective-permute-start(bf16[4,64,512]{2,1,0:T(8,128)(2,1)S(1)} %get-tuple-element.112), channel_id=1, source_target_pairs={{0,2},{1,3},{2,0},{3,1},{4,6},{5,7},{6,4},{7,5},{8,10},{9,11},{10,... | collective-permute-start | bytes 786440 | tf_op jit(solution)/shard_map/ppermute | solution.py:387
  73.5 1.8 %collective-permute-start.10 = (bf16[128,512]{1,0:T(8,128)(2,1)S(1)}, bf16[128,512]{1,0:T(8,128)(2,1)S(1)}, u32[]{:S(2)}, u32[]{:S(2)}) collective-permute-start(bf16[128,512]{1,0:T(8,128)(2,1)S(1)} %copy-done.8), channel_id=1, source_target_pairs={{0,8},{8,0},{16,24},{24,16},{1,9},{9,1},{17,25},{25,17},{2,10},{10... | collective-permute-start | bytes 393224 | tf_op jit(solution)/shard_map/ppermute | solution.py:387
  75.5 10.3 %shard_map.73 = (bf16[512,512]{1,0:T(8,128)(2,1)S(1)}, bf16[512,1536]{1,0:T(8,128)(2,1)}, bf16[4,64,512]{2,1,0:T(8,128)(2,1)}, bf16[4,64,512]{2,1,0:T(8,128)(2,1...) custom-call(bf16[512,512]{1,0:T(8,128)(2,1)S(1)} %bitcast.59, ...), custom_call_target="tpu_custom_call" | custom-call | flops 1048576 | bytes 1024 | tf_op jit(solution)/shard_map/pallas_call | solution.py:375
  87.0 2.1 %collective-permute-start.15 = (bf16[128,512]{1,0:T(8,128)(2,1)S(1)}, bf16[128,512]{1,0:T(8,128)(2,1)S(1)}, u32[]{:S(2)}, u32[]{:S(2)}) collective-permute-start(bf16[128,512]{1,0:T(8,128)(2,1)S(1)} %copy-done.7), channel_id=1, source_target_pairs={{0,16},{8,24},{16,0},{24,8},{1,17},{9,25},{17,1},{25,9},{2,18},{10... | collective-permute-start | bytes 393224 | tf_op jit(solution)/shard_map/ppermute | solution.py:387
  90.6 1.5 %collective-permute-start.16 = (bf16[4,64,512]{2,1,0:T(8,128)(2,1)S(1)}, bf16[4,64,512]{2,1,0:T(8,128)(2,1)S(1)}, u32[]{:S(2)}, u32[]{:S(2)}) collective-permute-start(bf16[4,64,512]{2,1,0:T(8,128)(2,1)S(1)} %get-tuple-element.148), channel_id=1, source_target_pairs={{0,2},{1,3},{2,0},{3,1},{4,6},{5,7},{6,4},{7,5},{8,10},{9,11},{10,... | collective-permute-start | bytes 786440 | tf_op jit(solution)/shard_map/ppermute | solution.py:387
  94.2 1.9 %collective-permute-done.15 = bf16[128,512]{1,0:T(8,128)(2,1)S(1)} collective-permute-done((bf16[128,512]{1,0:T(8,128)(2,1)S(1)}, bf16[128,512]{1,0:T(8,128)(2,1)S(1)}, u32[]{:S(2)}, u32[]{:S(2)}) %collective-permute-start.15) | collective-permute-done | bytes 131104 | tf_op jit(solution)/shard_map/ppermute | solution.py:387
  96.1 4.1 %shard_map.75 = bf16[8,2,32,512]{3,2,1,0:T(8,128)(2,1)} custom-call(bf16[8,2,32,512]{3,2,1,0:T(8,128)(2,1)S(1)} %all-to-all-done.x_ref, bf16[512,512]{1,0:T(8,128)(2,1)S(1)} %get-tuple-element.153.dm_ref, f32[2,512]{1,0:T(2,128)S(1)} %copy-done.3, bf16[512,1536]{1,0:T(8,128)(2,1)} %get-tuple-element.154.dqkv_hbm, bf16[2,4,512,512]{3,2,1,0:T(8,128)(2,1)} %w_hbm.9), custom_call_target="tpu_custom_call" | custom-call | flops 1048576 | bytes 1024 | tf_op jit(solution)/shard_map/pallas_call | solution.py:375
  100.5 3.4 %collective-permute-start.24 = (bf16[4,16,512]{2,1,0:T(8,128)(2,1)S(1)}, bf16[4,16,512]{2,1,0:T(8,128)(2,1)S(1)}, u32[]{:S(2)}, u32[]{:S(2)}) collective-permute-start(bf16[4,16,512]{2,1,0:T(8,128)(2,1)S(1)} %get-tuple-element.179), channel_id=1, source_target_pairs={{0,16},{8,24},{16,0},{24,8},{1,17},{9,25},{17,1},{25,9},{2,18},{10... | collective-permute-start | bytes 196616 | tf_op jit(solution)/shard_map/ppermute | solution.py:387
  106.7 2.1 %collective-permute-start.21 = (bf16[4,16,512]{2,1,0:T(8,128)(2,1)S(1)}, bf16[4,16,512]{2,1,0:T(8,128)(2,1)S(1)}, u32[]{:S(2)}, u32[]{:S(2)}) collective-permute-start(bf16[4,16,512]{2,1,0:T(8,128)(2,1)S(1)} %get-tuple-element.176), channel_id=1, source_target_pairs={{0,16},{8,24},{16,0},{24,8},{1,17},{9,25},{17,1},{25,9},{2,18},{10... | collective-permute-start | bytes 196616 | tf_op jit(solution)/shard_map/ppermute | solution.py:387
  110.6 2.1 %collective-permute-start.19 = (bf16[128,512]{1,0:T(8,128)(2,1)S(1)}, bf16[128,512]{1,0:T(8,128)(2,1)S(1)}, u32[]{:S(2)}, u32[]{:S(2)}) collective-permute-start(bf16[128,512]{1,0:T(8,128)(2,1)S(1)} %copy-done.6), channel_id=1, source_target_pairs={{0,24},{8,16},{16,8},{24,0},{1,25},{9,17},{17,9},{25,1},{2,26},{10... | collective-permute-start | bytes 393224 | tf_op jit(solution)/shard_map/ppermute | solution.py:387
  112.7 3.5 %all-to-all-start.3 = ((bf16[8,2,32,512]{3,2,1,0:T(8,128)(2,1)}), bf16[8,2,32,512]{3,2,1,0:T(8,128)(2,1)S(1)}, u32[]{:S(2)}, u32[]{:S(2)}) async-start(bf16[8,2,32,512]{3,2,1,0:T(8,128)(2,1)} %shard_map.75), calls=%async_computation.3 | async-start | bytes 1048576 | tf_op jit(solution)/shard_map/all_to_all | solution.py:520
  117.6 8.3 %all-to-all-done.3.x_ref = bf16[8,2,32,512]{3,2,1,0:T(8,128)(2,1)S(1)} async-done(((bf16[8,2,32,512]{3,2,1,0:T(8,128)(2,1)}), bf16[8,2,32,512]{3,2,1,0:T(8,128)(2,1)S(1)}, u32[]{:S(2)}, u32[]{:S(2)}) %all-to-all-start.3) | async-done | bytes 524320 | tf_op jit(solution)/shard_map/all_to_all | solution.py:520
  (77 shorter events, 20.8 us)
Async XLA Ops:
  0.6 14.9 %all-to-all-start = ((bf16[8,2,32,512]{3,2,1,0:T(8,128)(2,1)}), bf16[8,2,32,512]{3,2,1,0:T(8,128)(2,1)S(1)}, u32[]{:S(2)}, u32[]{:S(2)}) async-start(bf16[8,2,32,512]{3,2,1,0:T(8,128)(2,1)} %bitcast.68), calls=%async_computation | async-start | bytes 1048576 | tf_op jit(solution)/shard_map/all_to_all | solution.py:455
  7.0 16.4 %collective-permute-start = (bf16[16,8,512]{2,1,0:T(8,128)(2,1)S(1)}, bf16[16,8,512]{2,1,0:T(8,128)(2,1)S(1)}, u32[]{:S(2)}, u32[]{:S(2)}) collective-permute-start(bf16[16,8,512]{2,1,0:T(8,128)(2,1)S(1)} %get-tuple-element.172), channel_id=1, source_target_pairs={{0,8},{8,0},{16,24},{24,16},{1,9},{9,1},{17,25},{25,17},{2,10},{10... | collective-permute-start | bytes 393224 | tf_op jit(solution)/shard_map/ppermute | solution.py:387
  8.6 14.8 %collective-permute-start.1 = (bf16[16,8,512]{2,1,0:T(8,128)(2,1)S(1)}, bf16[16,8,512]{2,1,0:T(8,128)(2,1)S(1)}, u32[]{:S(2)}, u32[]{:S(2)}) collective-permute-start(bf16[16,8,512]{2,1,0:T(8,128)(2,1)S(1)} %get-tuple-element.174), channel_id=1, source_target_pairs={{0,16},{8,24},{16,0},{24,8},{1,17},{9,25},{17,1},{25,9},{2,18},{10... | collective-permute-start | bytes 393224 | tf_op jit(solution)/shard_map/ppermute | solution.py:387
  11.2 12.2 %collective-permute-start.2 = (bf16[16,8,512]{2,1,0:T(8,128)(2,1)S(1)}, bf16[16,8,512]{2,1,0:T(8,128)(2,1)S(1)}, u32[]{:S(2)}, u32[]{:S(2)}) collective-permute-start(bf16[16,8,512]{2,1,0:T(8,128)(2,1)S(1)} %get-tuple-element.171), channel_id=1, source_target_pairs={{0,24},{8,16},{16,8},{24,0},{1,25},{9,17},{17,9},{25,1},{2,26},{10... | collective-permute-start | bytes 393224 | tf_op jit(solution)/shard_map/ppermute | solution.py:387
  24.1 20.0 %all-to-all-start.1 = ((bf16[32,16,512]{2,1,0:T(8,128)(2,1)}), bf16[32,16,512]{2,1,0:T(8,128)(2,1)S(1)}, u32[]{:S(2)}, u32[]{:S(2)}) async-start(bf16[32,16,512]{2,1,0:T(8,128)(2,1)} %bitcast.70), calls=%async_computation.1 | async-start | bytes 1048576 | tf_op jit(solution)/shard_map/all_to_all | solution.py:453
  56.8 18.7 %all-to-all-start.2 = ((bf16[32,16,512]{2,1,0:T(8,128)(2,1)}), bf16[32,16,512]{2,1,0:T(8,128)(2,1)S(1)}, u32[]{:S(2)}, u32[]{:S(2)}) async-start(bf16[32,16,512]{2,1,0:T(8,128)(2,1)} %bitcast.69), calls=%async_computation.2 | async-start | bytes 1048576 | tf_op jit(solution)/shard_map/all_to_all | solution.py:453
  69.9 15.9 %collective-permute-start.7 = (bf16[4,64,512]{2,1,0:T(8,128)(2,1)S(1)}, bf16[4,64,512]{2,1,0:T(8,128)(2,1)S(1)}, u32[]{:S(2)}, u32[]{:S(2)}) collective-permute-start(bf16[4,64,512]{2,1,0:T(8,128)(2,1)S(1)} %get-tuple-element.112), channel_id=1, source_target_pairs={{0,2},{1,3},{2,0},{3,1},{4,6},{5,7},{6,4},{7,5},{8,10},{9,11},{10,... | collective-permute-start | bytes 786440 | tf_op jit(solution)/shard_map/ppermute | solution.py:387
  71.8 14.1 %collective-permute-start.8 = (bf16[4,64,512]{2,1,0:T(8,128)(2,1)S(1)}, bf16[4,64,512]{2,1,0:T(8,128)(2,1)S(1)}, u32[]{:S(2)}, u32[]{:S(2)}) collective-permute-start(bf16[4,64,512]{2,1,0:T(8,128)(2,1)S(1)} %get-tuple-element.113), channel_id=1, source_target_pairs={{0,4},{1,5},{2,6},{3,7},{4,0},{5,1},{6,2},{7,3},{8,12},{9,13},{10,... | collective-permute-start | bytes 786440 | tf_op jit(solution)/shard_map/ppermute | solution.py:387
  73.2 12.8 %collective-permute-start.9 = (bf16[4,64,512]{2,1,0:T(8,128)(2,1)S(1)}, bf16[4,64,512]{2,1,0:T(8,128)(2,1)S(1)}, u32[]{:S(2)}, u32[]{:S(2)}) collective-permute-start(bf16[4,64,512]{2,1,0:T(8,128)(2,1)S(1)} %get-tuple-element.114), channel_id=1, source_target_pairs={{0,6},{1,7},{2,4},{3,5},{4,2},{5,3},{6,0},{7,1},{8,14},{9,15},{10,... | collective-permute-start | bytes 786440 | tf_op jit(solution)/shard_map/ppermute | solution.py:387
  73.5 12.3 %collective-permute-start.10 = (bf16[128,512]{1,0:T(8,128)(2,1)S(1)}, bf16[128,512]{1,0:T(8,128)(2,1)S(1)}, u32[]{:S(2)}, u32[]{:S(2)}) collective-permute-start(bf16[128,512]{1,0:T(8,128)(2,1)S(1)} %copy-done.8), channel_id=1, source_target_pairs={{0,8},{8,0},{16,24},{24,16},{1,9},{9,1},{17,25},{25,17},{2,10},{10... | collective-permute-start | bytes 393224 | tf_op jit(solution)/shard_map/ppermute | solution.py:387
  86.0 3.3 %collective-permute-start.11 = (bf16[4,64,512]{2,1,0:T(8,128)(2,1)}, bf16[4,64,512]{2,1,0:T(8,128)(2,1)S(1)}, u32[]{:S(2)}, u32[]{:S(2)}) collective-permute-start(bf16[4,64,512]{2,1,0:T(8,128)(2,1)} %get-tuple-element.143), channel_id=1, source_target_pairs={{0,1},{1,0},{2,3},{3,2},{4,5},{5,4},{6,7},{7,6},{8,9},{9,8},{10,11... | collective-permute-start | bytes 786440 | tf_op jit(solution)/shard_map/ppermute | solution.py:387
  86.0 3.3 %collective-permute-start.12 = (bf16[4,64,512]{2,1,0:T(8,128)(2,1)}, bf16[4,64,512]{2,1,0:T(8,128)(2,1)S(1)}, u32[]{:S(2)}, u32[]{:S(2)}) collective-permute-start(bf16[4,64,512]{2,1,0:T(8,128)(2,1)} %get-tuple-element.144), channel_id=1, source_target_pairs={{0,1},{1,0},{2,3},{3,2},{4,5},{5,4},{6,7},{7,6},{8,9},{9,8},{10,11... | collective-permute-start | bytes 786440 | tf_op jit(solution)/shard_map/ppermute | solution.py:387
  87.0 9.1 %collective-permute-start.15 = (bf16[128,512]{1,0:T(8,128)(2,1)S(1)}, bf16[128,512]{1,0:T(8,128)(2,1)S(1)}, u32[]{:S(2)}, u32[]{:S(2)}) collective-permute-start(bf16[128,512]{1,0:T(8,128)(2,1)S(1)} %copy-done.7), channel_id=1, source_target_pairs={{0,16},{8,24},{16,0},{24,8},{1,17},{9,25},{17,1},{25,9},{2,18},{10... | collective-permute-start | bytes 393224 | tf_op jit(solution)/shard_map/ppermute | solution.py:387
  90.6 13.2 %collective-permute-start.16 = (bf16[4,64,512]{2,1,0:T(8,128)(2,1)S(1)}, bf16[4,64,512]{2,1,0:T(8,128)(2,1)S(1)}, u32[]{:S(2)}, u32[]{:S(2)}) collective-permute-start(bf16[4,64,512]{2,1,0:T(8,128)(2,1)S(1)} %get-tuple-element.148), channel_id=1, source_target_pairs={{0,2},{1,3},{2,0},{3,1},{4,6},{5,7},{6,4},{7,5},{8,10},{9,11},{10,... | collective-permute-start | bytes 786440 | tf_op jit(solution)/shard_map/ppermute | solution.py:387
  92.2 13.3 %collective-permute-start.17 = (bf16[4,64,512]{2,1,0:T(8,128)(2,1)S(1)}, bf16[4,64,512]{2,1,0:T(8,128)(2,1)S(1)}, u32[]{:S(2)}, u32[]{:S(2)}) collective-permute-start(bf16[4,64,512]{2,1,0:T(8,128)(2,1)S(1)} %get-tuple-element.149), channel_id=1, source_target_pairs={{0,4},{1,5},{2,6},{3,7},{4,0},{5,1},{6,2},{7,3},{8,12},{9,13},{10,... | collective-permute-start | bytes 786440 | tf_op jit(solution)/shard_map/ppermute | solution.py:387
  93.7 11.9 %collective-permute-start.18 = (bf16[4,64,512]{2,1,0:T(8,128)(2,1)S(1)}, bf16[4,64,512]{2,1,0:T(8,128)(2,1)S(1)}, u32[]{:S(2)}, u32[]{:S(2)}) collective-permute-start(bf16[4,64,512]{2,1,0:T(8,128)(2,1)S(1)} %get-tuple-element.150), channel_id=1, source_target_pairs={{0,6},{1,7},{2,4},{3,5},{4,2},{5,3},{6,0},{7,1},{8,14},{9,15},{10,... | collective-permute-start | bytes 786440 | tf_op jit(solution)/shard_map/ppermute | solution.py:387
  100.4 8.4 %collective-permute-start.23 = (bf16[4,16,512]{2,1,0:T(8,128)(2,1)S(1)}, bf16[4,16,512]{2,1,0:T(8,128)(2,1)S(1)}, u32[]{:S(2)}, u32[]{:S(2)}) collective-permute-start(bf16[4,16,512]{2,1,0:T(8,128)(2,1)S(1)} %get-tuple-element.178), channel_id=1, source_target_pairs={{0,8},{8,0},{16,24},{24,16},{1,9},{9,1},{17,25},{25,17},{2,10},{10... | collective-permute-start | bytes 196616 | tf_op jit(solution)/shard_map/ppermute | solution.py:387
  100.5 9.7 %collective-permute-start.24 = (bf16[4,16,512]{2,1,0:T(8,128)(2,1)S(1)}, bf16[4,16,512]{2,1,0:T(8,128)(2,1)S(1)}, u32[]{:S(2)}, u32[]{:S(2)}) collective-permute-start(bf16[4,16,512]{2,1,0:T(8,128)(2,1)S(1)} %get-tuple-element.179), channel_id=1, source_target_pairs={{0,16},{8,24},{16,0},{24,8},{1,17},{9,25},{17,1},{25,9},{2,18},{10... | collective-permute-start | bytes 196616 | tf_op jit(solution)/shard_map/ppermute | solution.py:387
  103.9 6.7 %collective-permute-start.25 = (bf16[4,16,512]{2,1,0:T(8,128)(2,1)S(1)}, bf16[4,16,512]{2,1,0:T(8,128)(2,1)S(1)}, u32[]{:S(2)}, u32[]{:S(2)}) collective-permute-start(bf16[4,16,512]{2,1,0:T(8,128)(2,1)S(1)} %get-tuple-element.180), channel_id=1, source_target_pairs={{0,24},{8,16},{16,8},{24,0},{1,25},{9,17},{17,9},{25,1},{2,26},{10... | collective-permute-start | bytes 196616 | tf_op jit(solution)/shard_map/ppermute | solution.py:387
  105.7 10.5 %collective-permute-start.20 = (bf16[4,16,512]{2,1,0:T(8,128)(2,1)S(1)}, bf16[4,16,512]{2,1,0:T(8,128)(2,1)S(1)}, u32[]{:S(2)}, u32[]{:S(2)}) collective-permute-start(bf16[4,16,512]{2,1,0:T(8,128)(2,1)S(1)} %get-tuple-element.175), channel_id=1, source_target_pairs={{0,8},{8,0},{16,24},{24,16},{1,9},{9,1},{17,25},{25,17},{2,10},{10... | collective-permute-start | bytes 196616 | tf_op jit(solution)/shard_map/ppermute | solution.py:387
  106.7 9.6 %collective-permute-start.21 = (bf16[4,16,512]{2,1,0:T(8,128)(2,1)S(1)}, bf16[4,16,512]{2,1,0:T(8,128)(2,1)S(1)}, u32[]{:S(2)}, u32[]{:S(2)}) collective-permute-start(bf16[4,16,512]{2,1,0:T(8,128)(2,1)S(1)} %get-tuple-element.176), channel_id=1, source_target_pairs={{0,16},{8,24},{16,0},{24,8},{1,17},{9,25},{17,1},{25,9},{2,18},{10... | collective-permute-start | bytes 196616 | tf_op jit(solution)/shard_map/ppermute | solution.py:387
  108.8 7.5 %collective-permute-start.22 = (bf16[4,16,512]{2,1,0:T(8,128)(2,1)S(1)}, bf16[4,16,512]{2,1,0:T(8,128)(2,1)S(1)}, u32[]{:S(2)}, u32[]{:S(2)}) collective-permute-start(bf16[4,16,512]{2,1,0:T(8,128)(2,1)S(1)} %get-tuple-element.177), channel_id=1, source_target_pairs={{0,24},{8,16},{16,8},{24,0},{1,25},{9,17},{17,9},{25,1},{2,26},{10... | collective-permute-start | bytes 196616 | tf_op jit(solution)/shard_map/ppermute | solution.py:387
  110.6 6.9 %collective-permute-start.19 = (bf16[128,512]{1,0:T(8,128)(2,1)S(1)}, bf16[128,512]{1,0:T(8,128)(2,1)S(1)}, u32[]{:S(2)}, u32[]{:S(2)}) collective-permute-start(bf16[128,512]{1,0:T(8,128)(2,1)S(1)} %copy-done.6), channel_id=1, source_target_pairs={{0,24},{8,16},{16,8},{24,0},{1,25},{9,17},{17,9},{25,1},{2,26},{10... | collective-permute-start | bytes 393224 | tf_op jit(solution)/shard_map/ppermute | solution.py:387
  112.7 13.2 %all-to-all-start.3 = ((bf16[8,2,32,512]{3,2,1,0:T(8,128)(2,1)}), bf16[8,2,32,512]{3,2,1,0:T(8,128)(2,1)S(1)}, u32[]{:S(2)}, u32[]{:S(2)}) async-start(bf16[8,2,32,512]{3,2,1,0:T(8,128)(2,1)} %shard_map.75), calls=%async_computation.3 | async-start | bytes 1048576 | tf_op jit(solution)/shard_map/all_to_all | solution.py:520
  (15 other events, 101.5 us)

commit v14 on v13

--- a/solution.py
+++ b/solution.py
@@ -233,49 +233,43 @@
     finish(going + send_turned(turn_ref, middle, mid_ref, quarters(mid_hbm), sems))
 
 
-def row_back(sizes, d_ref, w_hbm, turn_hbm, n_hbm, q_hbm, k_hbm, v_hbm, att_hbm, p_hbm, *refs):
+def row_back(sizes, d_ref, x_ref, g_ref, w_hbm, turn_hbm, n_hbm, q_hbm, k_hbm, v_hbm, att_hbm, p_hbm, *refs):
     rows, length, width, plane = sizes
-    dm_ref, dqkv_hbm, keep_hbms, send_hbms = refs[0], refs[1], refs[2 : 2 + plane], refs[2 + plane : 2 + 2 * plane]
-    w_ref, turn_ref, n_ref, q_ref, k_ref, v_ref, att_ref, p_ref, da_ref, dqkv_ref = refs[2 + 2 * plane : -4]
-    keep_ref, send_ref, sems, out_sems = refs[-4:]
+    fg_hbm, keep_hbms, send_hbms = refs[0], refs[1 : 1 + plane], refs[1 + plane : 1 + 2 * plane]
+    w_ref, turn_ref, dm_ref, n_ref, q_ref, k_ref, v_ref, att_ref, p_ref, da_ref, dqkv_ref = refs[1 + 2 * plane : -5]
+    fg_ref, keep_ref, send_ref, sems, out_sems = refs[-5:]
     half = p_ref.shape[0] // 2
     coming = [
-        start(turn_hbm.at[1], turn_ref.at[0], sems.at[0]), start(w_hbm.at[0, 3], w_ref, sems.at[1]),
+        start(turn_hbm.at[1], turn_ref.at[0], sems.at[0]), start(w_hbm.at[0, 3], w_ref.at[3], sems.at[1]),
         start(v_hbm, v_ref, sems.at[2]), start(k_hbm, k_ref, sems.at[3]), start(q_hbm, q_ref, sems.at[4]),
         start(p_hbm.at[pl.ds(0, half)], p_ref.at[pl.ds(0, half)], sems.at[5]),
         start(p_hbm.at[pl.ds(half, half)], p_ref.at[pl.ds(half, half)], sems.at[6]),
-        start(turn_hbm.at[6], turn_ref.at[1], sems.at[7]), start(att_hbm, att_ref, sems.at[8]),
-        start(n_hbm, n_ref, sems.at[9]),
+        start(w_hbm.at[0, 0:3], w_ref.at[0:3], sems.at[7]),
+        start(turn_hbm.at[6], turn_ref.at[1], sems.at[8]), start(att_hbm, att_ref, sems.at[9]),
+        start(n_hbm, n_ref, sems.at[10]),
     ]
     coming[0].wait()
     d_middle = dot(turn_ref[0], d_ref[...]).astype(BF16)
     dm_ref[...] = d_middle
     coming[1].wait()
-    da_ref[...] = dot_nt(d_middle, w_ref[...]).astype(BF16)
+    da_ref[...] = dot_nt(d_middle, w_ref[3]).astype(BF16)
     finish(coming[2:7])
     attention_back(q_ref, k_ref, v_ref, p_ref, da_ref, dqkv_ref, rows, length, width)
-    going = [start(dqkv_ref, dqkv_hbm, sems.at[10])]
-    finish(coming[7:])
+    coming[7].wait()
+    d_normed = input_back(dqkv_ref, [w_ref.at[part] for part in range(3)])
+    result = dm_ref[...].astype(F32) + norm_back(rows_of(x_ref), g_ref[0:1], d_normed)
+    result = result.astype(BF16)
+    for i in range(rows):
+        piece = result[i * length : (i + 1) * length]
+        fg_ref[:, i] = piece.reshape(fg_ref.shape[0], fg_ref.shape[2], fg_ref.shape[3])
+    going = [start(fg_ref, fg_hbm, sems.at[11])]
+    finish(coming[8:])
     normed = dot(n_ref[...], turn_ref[1]).astype(BF16)
     for part in range(3):
         weight_grad(part, normed, third(dqkv_ref, part), keep_ref, send_ref)
     attended = dot(att_ref[...], turn_ref[1]).astype(BF16)
     weight_grad(3, attended, dm_ref[...], keep_ref, send_ref)
     finish(going + send_grads(keep_ref, send_ref, keep_hbms, send_hbms, out_sems))
-
-
-def field_back(x_ref, dm_ref, g_ref, dqkv_hbm, w_hbm, fg_hbm, dqkv_ref, w_ref, fg_ref, sems):
-    coming = [start(dqkv_hbm, dqkv_ref, sems.at[0]), start(w_hbm.at[0, 0:3], w_ref, sems.at[1])]
-    _, rows, _, channels = x_ref.shape
-    length = x_ref.shape[0] * x_ref.shape[2]
-    finish(coming)
-    d_normed = input_back(dqkv_ref, [w_ref.at[part] for part in range(3)])
-    result = dm_ref[...].astype(F32) + norm_back(rows_of(x_ref), g_ref[0:1], d_normed)
-    result = result.astype(BF16)
-    for i in range(rows):
-        piece = result[i * length : (i + 1) * length]
-        fg_ref[:, i] = piece.reshape(fg_ref.shape[0], fg_ref.shape[2], channels)
-    start(fg_ref, fg_hbm, sems.at[2]).wait()
 
 
 def store(x_ref, x_hbm, sem):
@@ -365,7 +359,7 @@
 NEAR, FAR, ANY = pltpu.VMEM, pltpu.HBM, None
 
 
-def call(kernel, ins, outs, scratch, flops=1 << 20):
+def call(kernel, ins, outs, scratch):
     def spec(where):
         return pl.BlockSpec(memory_space=pltpu.HBM if where is FAR else pltpu.VMEM)
 
@@ -379,7 +373,7 @@
         out_shape=[jax.ShapeDtypeStruct(shape, BF16) if where is ANY else where(shape, BF16) for shape, where in outs],
         scratch_shapes=scratch,
         compiler_params=pltpu.CompilerParams(vmem_limit_bytes=48 * 1024 * 1024),
-        cost_estimate=pl.CostEstimate(flops=flops, bytes_accessed=1 << 10, transcendentals=0),
+        cost_estimate=pl.CostEstimate(flops=1 << 20, bytes_accessed=1 << 10, transcendentals=0),
     )(*[place(item, where) for item, where in ins])
 
 
@@ -498,29 +492,20 @@
     d_mid, rest, _ = lax.optimization_barrier((d_mid, outs[2:], sums_b))
     results = call(
         functools.partial(row_back, (rows, length, width, plane)),
-        at(ANY, d_mid) + at(FAR, weights, turn, normed, query, key, value, attended, prob),
-        at(ANY, flat) + at(FAR, triple, *[packed] * (2 * plane)),
-        [square, scratch(2, *flat)] + [square] * 5 + [scratch(*probs), square, scratch(*triple)]
-        + [scratch(plane, *packed), scratch(plane, *packed), copies((11,)), copies((2 * plane,))],
-    )
-    (d_mid, dqkv, *grads), pieces_b, pieces_out, rest = lax.optimization_barrier(
-        (results, pieces_b, pieces_out, rest)
-    )
-    second = [swap(item, "row", row_parts, 2) for item in rest[:1]]
-    sums_a = chip_sums(grads[:plane], grads[plane:], col_parts)
-    pieces_a = plane_pieces(sums_a, plane, core)
-    dqkv, _, second = lax.optimization_barrier((dqkv, sums_a, second))
-    field_grad, = call(
-        field_back, at(ANY, x, d_mid, gains) + at(FAR, dqkv, weights), at(FAR, x.shape),
-        [scratch(*triple), scratch(3, *flat), scratch(*x.shape), copies((3,))],
-    )
-    field_grad, pieces_b = lax.optimization_barrier((field_grad, pieces_b))
+        at(ANY, d_mid, x, gains) + at(FAR, weights, turn, normed, query, key, value, attended, prob),
+        at(FAR, x.shape, *[packed] * (2 * plane)),
+        [scratch(4, *flat), scratch(2, *flat)] + [square] * 6 + [scratch(*probs), square, scratch(*triple)]
+        + [scratch(*x.shape), scratch(plane, *packed), scratch(plane, *packed), copies((12,)), copies((2 * plane,))],
+    )
+    (field_grad, *grads), pieces_b, pieces_out, rest = lax.optimization_barrier((results, pieces_b, pieces_out, rest))
+    field_grad = lax.all_to_all(field_grad, "col", 0, 0, tiled=True)
+    pieces_out += [swap(item, "row", row_parts, 2) for item in rest[:1]]
+    pieces_a = plane_pieces(chip_sums(grads[:plane], grads[plane:], col_parts), plane, core)
+    field_grad, pieces_b, rest = lax.optimization_barrier((field_grad, pieces_b, rest[1:]))
     grads_b = last_sums(pieces_b, row_parts)
-    field_grad, pieces_a, rest = lax.optimization_barrier((field_grad, pieces_a, rest[1:]))
-    field_grad = lax.all_to_all(field_grad, "col", 0, 0, tiled=True)
-    field_grad, = call(store, at(ANY, field_grad), at(FAR, field_grad.shape), [copies], 1 << 34)
+    pieces_out += [swap(item, "row", row_parts, 3 + step) for step, item in enumerate(rest)]
+    field_grad, = call(store, at(ANY, field_grad), at(FAR, field_grad.shape), [copies])
     field_grad = field_grad.reshape(high, wide, channels)
-    pieces_out += second + [swap(item, "row", row_parts, 3 + step) for step, item in enumerate(rest)]
     output = jnp.zeros((high, wide, channels), BF16)
     for step, piece in enumerate(pieces_out):
         piece = piece.reshape(high, cols, channels)

time: 128 us -> 131 us (1.023)
  Pallas kernels: 48.4 us -> 45.5 us
  local copies, waits for them, and re-layouts: 2.85 us -> 5.34 us
  waiting for transfers between devices: 28.6 us -> 30.5 us
    ppermute x26, waiting for transfers between devices: 5.58 us -> 15.6 us  [swap(): return lax.ppermute(item, axis, [(at, at ^ step) for at in range(count)])]
    all_to_all x1, waiting for transfers between devices: 8.27 us -> 0.01 us  [body(): field_grad = lax.all_to_all(field_grad, 'col', 0, 0, tiled=True)]
    pallas_call x10 -> x9, Pallas kernels: 48.4 us -> 45.5 us  [call(): pl.pallas_call(kernel, in_specs=[spec(where) for _, where in ins], out_sp...]
    unnamed x18 -> x20, local copies, waits for them, and re-layouts: 1.58 us -> 3.17 us
  transfers between devices with their start and end apart: 30 -> 30, of which waited for: 13 -> 12; matrix products, arithmetic and copies ran while one was open for 2% -> 3% of each run, Pallas kernels for 27% -> 25%
where the time goes in v14:
time: 131 us
  starting transfers between devices  46.1 us (35%)
  Pallas kernels  45.5 us (35%)
  waiting for transfers between devices  30.5 us (23%)
  local copies, waits for them, and re-layouts  5.34 us (4%)
  other arithmetic  2.17 us (2%)
    pallas_call x9, Pallas kernels, call(): pl.pallas_call(kernel, in_specs=[spec(where) for _, where in ins], out_sp...  45.5 us
    ppermute x26, starting transfers between devices, swap(): return lax.ppermute(item, axis, [(at, at ^ step) for at in range(count)])  29.9 us
    ppermute x26, waiting for transfers between devices, swap(): return lax.ppermute(item, axis, [(at, at ^ step) for at in range(count)])  15.6 us
    all_to_all x2, waiting for transfers between devices, all_to_all(): lax.all_to_all(item, ('row', 'col'), 0, 0, tiled=True)  12.9 us
    all_to_all x2, starting transfers between devices, all_to_all(): lax.all_to_all(item, ('row', 'col'), 0, 0, tiled=True)  7.51 us
    all_to_all x1, starting transfers between devices, body(): lax.all_to_all(field.reshape(col_parts, rows, wide, channels), 'col', 0,...  5.18 us
    all_to_all x1, starting transfers between devices, body(): field_grad = lax.all_to_all(field_grad, 'col', 0, 0, tiled=True)  3.49 us
    unnamed x20, local copies, waits for them, and re-layouts  3.17 us
  transfers between devices with their start and end apart: 30, of which 12 were waited for; matrix products, arithmetic and copies ran while one was open for 3% of the time, Pallas kernels for 25%

profile of v14, /device:TPU:0, one launch (start us, length us, event | category | flops | bytes accessed | tf_op | source)
XLA Modules:
  0.0 130.5 jit_solution(10014894197274669004)
XLA Ops:
  0.6 5.2 %all-to-all-start = ((bf16[8,2,32,512]{3,2,1,0:T(8,128)(2,1)}), bf16[8,2,32,512]{3,2,1,0:T(8,128)(2,1)S(1)}, u32[]{:S(2)}, u32[]{:S(2)}) async-start(bf16[8,2,32,512]{3,2,1,0:T(8,128)(2,1)} %bitcast.68), calls=%async_computation | async-start | bytes 1048576 | tf_op jit(solution)/shard_map/all_to_all | solution.py:449
  8.6 2.6 %collective-permute-start.1 = (bf16[16,8,512]{2,1,0:T(8,128)(2,1)S(1)}, bf16[16,8,512]{2,1,0:T(8,128)(2,1)S(1)}, u32[]{:S(2)}, u32[]{:S(2)}) collective-permute-start(bf16[16,8,512]{2,1,0:T(8,128)(2,1)S(1)} %get-tuple-element.156), channel_id=1, source_target_pairs={{0,16},{8,24},{16,0},{24,8},{1,17},{9,25},{17,1},{25,9},{2,18},{10... | collective-permute-start | bytes 393224 | tf_op jit(solution)/shard_map/ppermute | solution.py:381
  11.4 2.2 %shard_map.67.turn_hbm.refs_5_ = bf16[7,512,512]{2,1,0:T(8,128)(2,1)} custom-call(), custom_call_target="tpu_custom_call" | custom-call | flops 1048576 | bytes 1024 | tf_op jit(solution)/shard_map/pallas_call | solution.py:369
  13.6 1.9 %all-to-all-done.x_ref = bf16[8,2,32,512]{3,2,1,0:T(8,128)(2,1)S(1)} async-done(((bf16[8,2,32,512]{3,2,1,0:T(8,128)(2,1)}), bf16[8,2,32,512]{3,2,1,0:T(8,128)(2,1)S(1)}, u32[]{:S(2)}, u32[]{:S(2)}) %all-to-all-start) | async-done | bytes 524320 | tf_op jit(solution)/shard_map/all_to_all | solution.py:449
  15.6 7.8 %shard_map.68 = (bf16[512,512]{1,0:T(8,128)(2,1)}, bf16[512,512]{1,0:T(8,128)(2,1)}, bf16[512,512]{1,0:T(8,128)(2,1)}, bf16[512,512]{1,0:T(8,128)(2,1)}, bf16[51...) custom-call(bf16[8,2,32,512]{3,2,1,0:T(8,128)(2,1)S(1)} %all-to-all-done.x_ref, ...), custom_call_target="tpu_custom_call" | custom-call | flops 1048576 | bytes 1024 | tf_op jit(solution)/shard_map/pallas_call | solution.py:369
  24.1 4.4 %all-to-all-start.1 = ((bf16[32,16,512]{2,1,0:T(8,128)(2,1)}), bf16[32,16,512]{2,1,0:T(8,128)(2,1)S(1)}, u32[]{:S(2)}, u32[]{:S(2)}) async-start(bf16[32,16,512]{2,1,0:T(8,128)(2,1)} %bitcast.71), calls=%async_computation.1 | async-start | bytes 1048576 | tf_op jit(solution)/shard_map/all_to_all | solution.py:447
  29.4 2.0 %shard_map.69 = (bf16[512,512]{1,0:T(8,128)(2,1)S(1)}, bf16[512,512]{1,0:T(8,128)(2,1)S(1)}, bf16[2,512,512]{2,1,0:T(8,128)(2,1)S(1)}) custom-call(bf16[128,512]{1,0:T(8,128)(2,1)S(1)} %get-tuple-element.80.refs_0_, bf16[128,512]{1,0:T(8,128)(2,1)S(1)} %bitcast.61, bf16[128,512]{1,0:T(8,128)(2,1)S(1)} %bitcast.62, bf16[128,512]{1,0:T(8,128)(2,1)S(1)} %bitcast.63, ...), custom_call_target="tpu_custom_call" | custom-call | flops 1048576 | bytes 1024 | tf_op jit(solution)/shard_map/pallas_call | solution.py:369
  31.4 12.6 %all-to-all-done.1 = bf16[32,16,512]{2,1,0:T(8,128)(2,1)S(1)} async-done(((bf16[32,16,512]{2,1,0:T(8,128)(2,1)}), bf16[32,16,512]{2,1,0:T(8,128)(2,1)S(1)}, u32[]{:S(2)}, u32[]{:S(2)}) %all-to-all-start.1) | async-done | bytes 524320 | tf_op jit(solution)/shard_map/all_to_all | solution.py:447
  44.1 12.7 %shard_map.70 = (bf16[512,512]{1,0:T(8,128)(2,1)}, bf16[512,512]{1,0:T(8,128)(2,1)}, bf16[512,512]{1,0:T(8,128)(2,1)}, bf16[512,512]{1,0:T(8,128)(2,1)}, bf16[512,1536]{1,0:T(8,128)(2,1)}) custom-call(bf16[512,512]{1,0:T(8,128)(2,1)S(1)} %bitcast.60, bf16[512,512]{1,0:T(8,128)(2,1)S(1)} %get-tuple-element.84.cot_ref.cot_hbm, ...), custom_call_target="tpu_custom_call" | custom-call | flops 1048576 | bytes 1024 | tf_op jit(solution)/shard_map/pallas_call | solution.py:369
  56.7 3.1 %all-to-all-start.2 = ((bf16[32,16,512]{2,1,0:T(8,128)(2,1)}), bf16[32,16,512]{2,1,0:T(8,128)(2,1)S(1)}, u32[]{:S(2)}, u32[]{:S(2)}) async-start(bf16[32,16,512]{2,1,0:T(8,128)(2,1)} %bitcast.70), calls=%async_computation.2 | async-start | bytes 1048576 | tf_op jit(solution)/shard_map/all_to_all | solution.py:447
  59.8 5.7 %shard_map.71 = (bf16[128,512]{1,0:T(8,128)(2,1)}, bf16[128,512]{1,0:T(8,128)(2,1)}, bf16[128,512]{1,0:T(8,128)(2,1)}, bf16[128,512]{1,0:T(8,128)(2,1)}, bf16[4,...) custom-call(bf16[512,512]{1,0:T(8,128)(2,1)} %copy-done, ...), custom_call_target="tpu_custom_call" | custom-call | flops 1048576 | bytes 1024 | tf_op jit(solution)/shard_map/pallas_call | solution.py:369
  69.8 1.8 %collective-permute-start.7 = (bf16[4,64,512]{2,1,0:T(8,128)(2,1)S(1)}, bf16[4,64,512]{2,1,0:T(8,128)(2,1)S(1)}, u32[]{:S(2)}, u32[]{:S(2)}) collective-permute-start(bf16[4,64,512]{2,1,0:T(8,128)(2,1)S(1)} %get-tuple-element.103), channel_id=1, source_target_pairs={{0,2},{1,3},{2,0},{3,1},{4,6},{5,7},{6,4},{7,5},{8,10},{9,11},{10,... | collective-permute-start | bytes 786440 | tf_op jit(solution)/shard_map/ppermute | solution.py:381
  73.4 1.8 %collective-permute-start.10 = (bf16[128,512]{1,0:T(8,128)(2,1)}, bf16[128,512]{1,0:T(8,128)(2,1)S(1)}, u32[]{:S(2)}, u32[]{:S(2)}) collective-permute-start(bf16[128,512]{1,0:T(8,128)(2,1)} %get-tuple-element.123), channel_id=1, source_target_pairs={{0,8},{8,0},{16,24},{24,16},{1,9},{9,1},{17,25},{25,17},{2,10},{10... | collective-permute-start | bytes 393224 | tf_op jit(solution)/shard_map/ppermute | solution.py:381
  75.4 11.7 %shard_map.73 = (bf16[8,2,32,512]{3,2,1,0:T(8,128)(2,1)}, bf16[4,64,512]{2,1,0:T(8,128)(2,1)}, bf16[4,64,512]{2,1,0:T(8,128)(2,1)}, bf16[4,64,512]{2,1,0:T(8,128...) custom-call(bf16[512,512]{1,0:T(8,128)(2,1)S(1)} %bitcast.59, ...), custom_call_target="tpu_custom_call" | custom-call | flops 1048576 | bytes 1024 | tf_op jit(solution)/shard_map/pallas_call | solution.py:369
  89.0 3.5 %all-to-all-start.3 = ((bf16[8,2,32,512]{3,2,1,0:T(8,128)(2,1)}), bf16[8,2,32,512]{3,2,1,0:T(8,128)(2,1)S(1)}, u32[]{:S(2)}, u32[]{:S(2)}) async-start(bf16[8,2,32,512]{3,2,1,0:T(8,128)(2,1)} %get-tuple-element.129), calls=%async_computation.3 | async-start | bytes 1048576 | tf_op jit(solution)/shard_map/all_to_all | solution.py:501
  92.5 2.3 %collective-permute-start.11 = (bf16[128,512]{1,0:T(8,128)(2,1)}, bf16[128,512]{1,0:T(8,128)(2,1)S(1)}, u32[]{:S(2)}, u32[]{:S(2)}) collective-permute-start(bf16[128,512]{1,0:T(8,128)(2,1)} %get-tuple-element.128), channel_id=1, source_target_pairs={{0,16},{8,24},{16,0},{24,8},{1,17},{9,25},{17,1},{25,9},{2,18},{10... | collective-permute-start | bytes 393224 | tf_op jit(solution)/shard_map/ppermute | solution.py:381
  95.9 6.4 %collective-permute-done.11 = bf16[128,512]{1,0:T(8,128)(2,1)S(1)} collective-permute-done((bf16[128,512]{1,0:T(8,128)(2,1)}, bf16[128,512]{1,0:T(8,128)(2,1)S(1)}, u32[]{:S(2)}, u32[]{:S(2)}) %collective-permute-start.11) | collective-permute-done | bytes 131104 | tf_op jit(solution)/shard_map/ppermute | solution.py:381
  108.5 2.9 %collective-permute-start.24 = (bf16[4,16,512]{2,1,0:T(8,128)(2,1)S(1)}, bf16[4,16,512]{2,1,0:T(8,128)(2,1)S(1)}, u32[]{:S(2)}, u32[]{:S(2)}) collective-permute-start(bf16[4,16,512]{2,1,0:T(8,128)(2,1)S(1)} %get-tuple-element.161), channel_id=1, source_target_pairs={{0,16},{8,24},{16,0},{24,8},{1,17},{9,25},{17,1},{25,9},{2,18},{10... | collective-permute-start | bytes 196616 | tf_op jit(solution)/shard_map/ppermute | solution.py:381
  112.9 2.3 %collective-permute-start.25 = (bf16[4,16,512]{2,1,0:T(8,128)(2,1)S(1)}, bf16[4,16,512]{2,1,0:T(8,128)(2,1)S(1)}, u32[]{:S(2)}, u32[]{:S(2)}) collective-permute-start(bf16[4,16,512]{2,1,0:T(8,128)(2,1)S(1)} %get-tuple-element.162), channel_id=1, source_target_pairs={{0,24},{8,16},{16,8},{24,0},{1,25},{9,17},{17,9},{25,1},{2,26},{10... | collective-permute-start | bytes 196616 | tf_op jit(solution)/shard_map/ppermute | solution.py:381
  115.3 3.0 %collective-permute-done.18 = bf16[4,64,512]{2,1,0:T(8,128)(2,1)S(1)} collective-permute-done((bf16[4,64,512]{2,1,0:T(8,128)(2,1)S(1)}, bf16[4,64,512]{2,1,0:T(8,128)(2,1)S(1)}, u32[]{:S(2)}, u32[]{:S(2)}) %collective-permute-start.18) | collective-permute-done | bytes 262176 | tf_op jit(solution)/shard_map/ppermute | solution.py:381
  118.3 2.3 %collective-permute-start.12 = (bf16[128,512]{1,0:T(8,128)(2,1)}, bf16[128,512]{1,0:T(8,128)(2,1)S(1)}, u32[]{:S(2)}, u32[]{:S(2)}) collective-permute-start(bf16[128,512]{1,0:T(8,128)(2,1)} %get-tuple-element.135), channel_id=1, source_target_pairs={{0,24},{8,16},{16,8},{24,0},{1,25},{9,17},{17,9},{25,1},{2,26},{10... | collective-permute-start | bytes 393224 | tf_op jit(solution)/shard_map/ppermute | solution.py:381
  120.8 2.0 %collective-permute-start.21 = (bf16[4,16,512]{2,1,0:T(8,128)(2,1)S(1)}, bf16[4,16,512]{2,1,0:T(8,128)(2,1)S(1)}, u32[]{:S(2)}, u32[]{:S(2)}) collective-permute-start(bf16[4,16,512]{2,1,0:T(8,128)(2,1)S(1)} %get-tuple-element.158), channel_id=1, source_target_pairs={{0,16},{8,24},{16,0},{24,8},{1,17},{9,25},{17,1},{25,9},{2,18},{10... | collective-permute-start | bytes 196616 | tf_op jit(solution)/shard_map/ppermute | solution.py:381
  122.9 2.3 %collective-permute-start.22 = (bf16[4,16,512]{2,1,0:T(8,128)(2,1)S(1)}, bf16[4,16,512]{2,1,0:T(8,128)(2,1)S(1)}, u32[]{:S(2)}, u32[]{:S(2)}) collective-permute-start(bf16[4,16,512]{2,1,0:T(8,128)(2,1)S(1)} %get-tuple-element.159), channel_id=1, source_target_pairs={{0,24},{8,16},{16,8},{24,0},{1,25},{9,17},{17,9},{25,1},{2,26},{10... | collective-permute-start | bytes 196616 | tf_op jit(solution)/shard_map/ppermute | solution.py:381
  127.0 2.0 %collective-permute-done.22 = bf16[4,16,512]{2,1,0:T(8,128)(2,1)S(1)} collective-permute-done((bf16[4,16,512]{2,1,0:T(8,128)(2,1)S(1)}, bf16[4,16,512]{2,1,0:T(8,128)(2,1)S(1)}, u32[]{:S(2)}, u32[]{:S(2)}) %collective-permute-start.22) | collective-permute-done | bytes 65568 | tf_op jit(solution)/shard_map/ppermute | solution.py:381
  (78 shorter events, 24.8 us)
Async XLA Ops:
  0.6 14.9 %all-to-all-start = ((bf16[8,2,32,512]{3,2,1,0:T(8,128)(2,1)}), bf16[8,2,32,512]{3,2,1,0:T(8,128)(2,1)S(1)}, u32[]{:S(2)}, u32[]{:S(2)}) async-start(bf16[8,2,32,512]{3,2,1,0:T(8,128)(2,1)} %bitcast.68), calls=%async_computation | async-start | bytes 1048576 | tf_op jit(solution)/shard_map/all_to_all | solution.py:449
  7.0 16.4 %collective-permute-start = (bf16[16,8,512]{2,1,0:T(8,128)(2,1)S(1)}, bf16[16,8,512]{2,1,0:T(8,128)(2,1)S(1)}, u32[]{:S(2)}, u32[]{:S(2)}) collective-permute-start(bf16[16,8,512]{2,1,0:T(8,128)(2,1)S(1)} %get-tuple-element.154), channel_id=1, source_target_pairs={{0,8},{8,0},{16,24},{24,16},{1,9},{9,1},{17,25},{25,17},{2,10},{10... | collective-permute-start | bytes 393224 | tf_op jit(solution)/shard_map/ppermute | solution.py:381
  8.6 14.8 %collective-permute-start.1 = (bf16[16,8,512]{2,1,0:T(8,128)(2,1)S(1)}, bf16[16,8,512]{2,1,0:T(8,128)(2,1)S(1)}, u32[]{:S(2)}, u32[]{:S(2)}) collective-permute-start(bf16[16,8,512]{2,1,0:T(8,128)(2,1)S(1)} %get-tuple-element.156), channel_id=1, source_target_pairs={{0,16},{8,24},{16,0},{24,8},{1,17},{9,25},{17,1},{25,9},{2,18},{10... | collective-permute-start | bytes 393224 | tf_op jit(solution)/shard_map/ppermute | solution.py:381
  11.2 12.2 %collective-permute-start.2 = (bf16[16,8,512]{2,1,0:T(8,128)(2,1)S(1)}, bf16[16,8,512]{2,1,0:T(8,128)(2,1)S(1)}, u32[]{:S(2)}, u32[]{:S(2)}) collective-permute-start(bf16[16,8,512]{2,1,0:T(8,128)(2,1)S(1)} %get-tuple-element.153), channel_id=1, source_target_pairs={{0,24},{8,16},{16,8},{24,0},{1,25},{9,17},{17,9},{25,1},{2,26},{10... | collective-permute-start | bytes 393224 | tf_op jit(solution)/shard_map/ppermute | solution.py:381
  24.1 20.0 %all-to-all-start.1 = ((bf16[32,16,512]{2,1,0:T(8,128)(2,1)}), bf16[32,16,512]{2,1,0:T(8,128)(2,1)S(1)}, u32[]{:S(2)}, u32[]{:S(2)}) async-start(bf16[32,16,512]{2,1,0:T(8,128)(2,1)} %bitcast.71), calls=%async_computation.1 | async-start | bytes 1048576 | tf_op jit(solution)/shard_map/all_to_all | solution.py:447
  56.7 18.7 %all-to-all-start.2 = ((bf16[32,16,512]{2,1,0:T(8,128)(2,1)}), bf16[32,16,512]{2,1,0:T(8,128)(2,1)S(1)}, u32[]{:S(2)}, u32[]{:S(2)}) async-start(bf16[32,16,512]{2,1,0:T(8,128)(2,1)} %bitcast.70), calls=%async_computation.2 | async-start | bytes 1048576 | tf_op jit(solution)/shard_map/all_to_all | solution.py:447
  69.8 17.3 %collective-permute-start.7 = (bf16[4,64,512]{2,1,0:T(8,128)(2,1)S(1)}, bf16[4,64,512]{2,1,0:T(8,128)(2,1)S(1)}, u32[]{:S(2)}, u32[]{:S(2)}) collective-permute-start(bf16[4,64,512]{2,1,0:T(8,128)(2,1)S(1)} %get-tuple-element.103), channel_id=1, source_target_pairs={{0,2},{1,3},{2,0},{3,1},{4,6},{5,7},{6,4},{7,5},{8,10},{9,11},{10,... | collective-permute-start | bytes 786440 | tf_op jit(solution)/shard_map/ppermute | solution.py:381
  71.6 15.5 %collective-permute-start.8 = (bf16[4,64,512]{2,1,0:T(8,128)(2,1)S(1)}, bf16[4,64,512]{2,1,0:T(8,128)(2,1)S(1)}, u32[]{:S(2)}, u32[]{:S(2)}) collective-permute-start(bf16[4,64,512]{2,1,0:T(8,128)(2,1)S(1)} %get-tuple-element.104), channel_id=1, source_target_pairs={{0,4},{1,5},{2,6},{3,7},{4,0},{5,1},{6,2},{7,3},{8,12},{9,13},{10,... | collective-permute-start | bytes 786440 | tf_op jit(solution)/shard_map/ppermute | solution.py:381
  73.1 14.1 %collective-permute-start.9 = (bf16[4,64,512]{2,1,0:T(8,128)(2,1)S(1)}, bf16[4,64,512]{2,1,0:T(8,128)(2,1)S(1)}, u32[]{:S(2)}, u32[]{:S(2)}) collective-permute-start(bf16[4,64,512]{2,1,0:T(8,128)(2,1)S(1)} %get-tuple-element.105), channel_id=1, source_target_pairs={{0,6},{1,7},{2,4},{3,5},{4,2},{5,3},{6,0},{7,1},{8,14},{9,15},{10,... | collective-permute-start | bytes 786440 | tf_op jit(solution)/shard_map/ppermute | solution.py:381
  73.4 13.7 %collective-permute-start.10 = (bf16[128,512]{1,0:T(8,128)(2,1)}, bf16[128,512]{1,0:T(8,128)(2,1)S(1)}, u32[]{:S(2)}, u32[]{:S(2)}) collective-permute-start(bf16[128,512]{1,0:T(8,128)(2,1)} %get-tuple-element.123), channel_id=1, source_target_pairs={{0,8},{8,0},{16,24},{24,16},{1,9},{9,1},{17,25},{25,17},{2,10},{10... | collective-permute-start | bytes 393224 | tf_op jit(solution)/shard_map/ppermute | solution.py:381
  88.0 14.3 %collective-permute-start.13 = (bf16[4,64,512]{2,1,0:T(8,128)(2,1)}, bf16[4,64,512]{2,1,0:T(8,128)(2,1)S(1)}, u32[]{:S(2)}, u32[]{:S(2)}) collective-permute-start(bf16[4,64,512]{2,1,0:T(8,128)(2,1)} %get-tuple-element.141), channel_id=1, source_target_pairs={{0,1},{1,0},{2,3},{3,2},{4,5},{5,4},{6,7},{7,6},{8,9},{9,8},{10,11... | collective-permute-start | bytes 786440 | tf_op jit(solution)/shard_map/ppermute | solution.py:381
  88.0 14.3 %collective-permute-start.14 = (bf16[4,64,512]{2,1,0:T(8,128)(2,1)}, bf16[4,64,512]{2,1,0:T(8,128)(2,1)S(1)}, u32[]{:S(2)}, u32[]{:S(2)}) collective-permute-start(bf16[4,64,512]{2,1,0:T(8,128)(2,1)} %get-tuple-element.142), channel_id=1, source_target_pairs={{0,1},{1,0},{2,3},{3,2},{4,5},{5,4},{6,7},{7,6},{8,9},{9,8},{10,11... | collective-permute-start | bytes 786440 | tf_op jit(solution)/shard_map/ppermute | solution.py:381
  88.5 13.8 %collective-permute-start.15 = (bf16[4,64,512]{2,1,0:T(8,128)(2,1)}, bf16[4,64,512]{2,1,0:T(8,128)(2,1)S(1)}, u32[]{:S(2)}, u32[]{:S(2)}) collective-permute-start(bf16[4,64,512]{2,1,0:T(8,128)(2,1)} %get-tuple-element.143), channel_id=1, source_target_pairs={{0,1},{1,0},{2,3},{3,2},{4,5},{5,4},{6,7},{7,6},{8,9},{9,8},{10,11... | collective-permute-start | bytes 786440 | tf_op jit(solution)/shard_map/ppermute | solution.py:381
  88.5 13.8 %collective-permute-start.16 = (bf16[4,64,512]{2,1,0:T(8,128)(2,1)}, bf16[4,64,512]{2,1,0:T(8,128)(2,1)S(1)}, u32[]{:S(2)}, u32[]{:S(2)}) collective-permute-start(bf16[4,64,512]{2,1,0:T(8,128)(2,1)} %get-tuple-element.144), channel_id=1, source_target_pairs={{0,1},{1,0},{2,3},{3,2},{4,5},{5,4},{6,7},{7,6},{8,9},{9,8},{10,11... | collective-permute-start | bytes 786440 | tf_op jit(solution)/shard_map/ppermute | solution.py:381
  89.0 18.2 %all-to-all-start.3 = ((bf16[8,2,32,512]{3,2,1,0:T(8,128)(2,1)}), bf16[8,2,32,512]{3,2,1,0:T(8,128)(2,1)S(1)}, u32[]{:S(2)}, u32[]{:S(2)}) async-start(bf16[8,2,32,512]{3,2,1,0:T(8,128)(2,1)} %get-tuple-element.129), calls=%async_computation.3 | async-start | bytes 1048576 | tf_op jit(solution)/shard_map/all_to_all | solution.py:501
  92.5 9.7 %collective-permute-start.11 = (bf16[128,512]{1,0:T(8,128)(2,1)}, bf16[128,512]{1,0:T(8,128)(2,1)S(1)}, u32[]{:S(2)}, u32[]{:S(2)}) collective-permute-start(bf16[128,512]{1,0:T(8,128)(2,1)} %get-tuple-element.128), channel_id=1, source_target_pairs={{0,16},{8,24},{16,0},{24,8},{1,17},{9,25},{17,1},{25,9},{2,18},{10... | collective-permute-start | bytes 393224 | tf_op jit(solution)/shard_map/ppermute | solution.py:381
  103.6 9.3 %collective-permute-start.17 = (bf16[4,64,512]{2,1,0:T(8,128)(2,1)S(1)}, bf16[4,64,512]{2,1,0:T(8,128)(2,1)S(1)}, u32[]{:S(2)}, u32[]{:S(2)}) collective-permute-start(bf16[4,64,512]{2,1,0:T(8,128)(2,1)S(1)} %get-tuple-element.146), channel_id=1, source_target_pairs={{0,2},{1,3},{2,0},{3,1},{4,6},{5,7},{6,4},{7,5},{8,10},{9,11},{10,... | collective-permute-start | bytes 786440 | tf_op jit(solution)/shard_map/ppermute | solution.py:381
  105.4 12.9 %collective-permute-start.18 = (bf16[4,64,512]{2,1,0:T(8,128)(2,1)S(1)}, bf16[4,64,512]{2,1,0:T(8,128)(2,1)S(1)}, u32[]{:S(2)}, u32[]{:S(2)}) collective-permute-start(bf16[4,64,512]{2,1,0:T(8,128)(2,1)S(1)} %get-tuple-element.147), channel_id=1, source_target_pairs={{0,4},{1,5},{2,6},{3,7},{4,0},{5,1},{6,2},{7,3},{8,12},{9,13},{10,... | collective-permute-start | bytes 786440 | tf_op jit(solution)/shard_map/ppermute | solution.py:381
  106.8 13.7 %collective-permute-start.19 = (bf16[4,64,512]{2,1,0:T(8,128)(2,1)S(1)}, bf16[4,64,512]{2,1,0:T(8,128)(2,1)S(1)}, u32[]{:S(2)}, u32[]{:S(2)}) collective-permute-start(bf16[4,64,512]{2,1,0:T(8,128)(2,1)S(1)} %get-tuple-element.148), channel_id=1, source_target_pairs={{0,6},{1,7},{2,4},{3,5},{4,2},{5,3},{6,0},{7,1},{8,14},{9,15},{10,... | collective-permute-start | bytes 786440 | tf_op jit(solution)/shard_map/ppermute | solution.py:381
  108.4 12.4 %collective-permute-start.23 = (bf16[4,16,512]{2,1,0:T(8,128)(2,1)S(1)}, bf16[4,16,512]{2,1,0:T(8,128)(2,1)S(1)}, u32[]{:S(2)}, u32[]{:S(2)}) collective-permute-start(bf16[4,16,512]{2,1,0:T(8,128)(2,1)S(1)} %get-tuple-element.160), channel_id=1, source_target_pairs={{0,8},{8,0},{16,24},{24,16},{1,9},{9,1},{17,25},{25,17},{2,10},{10... | collective-permute-start | bytes 196616 | tf_op jit(solution)/shard_map/ppermute | solution.py:381
  108.5 14.4 %collective-permute-start.24 = (bf16[4,16,512]{2,1,0:T(8,128)(2,1)S(1)}, bf16[4,16,512]{2,1,0:T(8,128)(2,1)S(1)}, u32[]{:S(2)}, u32[]{:S(2)}) collective-permute-start(bf16[4,16,512]{2,1,0:T(8,128)(2,1)S(1)} %get-tuple-element.161), channel_id=1, source_target_pairs={{0,16},{8,24},{16,0},{24,8},{1,17},{9,25},{17,1},{25,9},{2,18},{10... | collective-permute-start | bytes 196616 | tf_op jit(solution)/shard_map/ppermute | solution.py:381
  112.9 12.3 %collective-permute-start.25 = (bf16[4,16,512]{2,1,0:T(8,128)(2,1)S(1)}, bf16[4,16,512]{2,1,0:T(8,128)(2,1)S(1)}, u32[]{:S(2)}, u32[]{:S(2)}) collective-permute-start(bf16[4,16,512]{2,1,0:T(8,128)(2,1)S(1)} %get-tuple-element.162), channel_id=1, source_target_pairs={{0,24},{8,16},{16,8},{24,0},{1,25},{9,17},{17,9},{25,1},{2,26},{10... | collective-permute-start | bytes 196616 | tf_op jit(solution)/shard_map/ppermute | solution.py:381
  118.3 11.5 %collective-permute-start.12 = (bf16[128,512]{1,0:T(8,128)(2,1)}, bf16[128,512]{1,0:T(8,128)(2,1)S(1)}, u32[]{:S(2)}, u32[]{:S(2)}) collective-permute-start(bf16[128,512]{1,0:T(8,128)(2,1)} %get-tuple-element.135), channel_id=1, source_target_pairs={{0,24},{8,16},{16,8},{24,0},{1,25},{9,17},{17,9},{25,1},{2,26},{10... | collective-permute-start | bytes 393224 | tf_op jit(solution)/shard_map/ppermute | solution.py:381
  120.8 6.2 %collective-permute-start.20 = (bf16[4,16,512]{2,1,0:T(8,128)(2,1)S(1)}, bf16[4,16,512]{2,1,0:T(8,128)(2,1)S(1)}, u32[]{:S(2)}, u32[]{:S(2)}) collective-permute-start(bf16[4,16,512]{2,1,0:T(8,128)(2,1)S(1)} %get-tuple-element.157), channel_id=1, source_target_pairs={{0,8},{8,0},{16,24},{24,16},{1,9},{9,1},{17,25},{25,17},{2,10},{10... | collective-permute-start | bytes 196616 | tf_op jit(solution)/shard_map/ppermute | solution.py:381
  (16 other events, 99.7 us)

commit v15 on v14

--- a/solution.py
+++ b/solution.py
@@ -499,11 +499,14 @@
     )
     (field_grad, *grads), pieces_b, pieces_out, rest = lax.optimization_barrier((results, pieces_b, pieces_out, rest))
     field_grad = lax.all_to_all(field_grad, "col", 0, 0, tiled=True)
-    pieces_out += [swap(item, "row", row_parts, 2) for item in rest[:1]]
-    pieces_a = plane_pieces(chip_sums(grads[:plane], grads[plane:], col_parts), plane, core)
+    sums_a = chip_sums(grads[:plane], grads[plane:], col_parts)
+    pieces_a = plane_pieces(sums_a, plane, core)
+    second, _ = lax.optimization_barrier((rest[:1], sums_a))
+    second = [swap(item, "row", row_parts, 2) for item in second]
     field_grad, pieces_b, rest = lax.optimization_barrier((field_grad, pieces_b, rest[1:]))
     grads_b = last_sums(pieces_b, row_parts)
-    pieces_out += [swap(item, "row", row_parts, 3 + step) for step, item in enumerate(rest)]
+    pieces_a, second, pieces_out = lax.optimization_barrier((pieces_a, second, pieces_out))
+    pieces_out += second + [swap(item, "row", row_parts, 3 + step) for step, item in enumerate(rest)]
     field_grad, = call(store, at(ANY, field_grad), at(FAR, field_grad.shape), [copies])
     field_grad = field_grad.reshape(high, wide, channels)
     output = jnp.zeros((high, wide, channels), BF16)

time: 131 us -> 128 us (0.977)
  starting transfers between devices: 46.1 us -> 43.2 us
  waiting for transfers between devices: 30.5 us -> 31.9 us
    ppermute x26, starting transfers between devices: 29.9 us -> 27 us  [swap(): return lax.ppermute(item, axis, [(at, at ^ step) for at in range(count)])]
    ppermute x26, waiting for transfers between devices: 15.6 us -> 17.1 us  [swap(): return lax.ppermute(item, axis, [(at, at ^ step) for at in range(count)])]
    unnamed x20 -> x16, local copies, waits for them, and re-layouts: 3.17 us -> 2.36 us
  transfers between devices with their start and end apart: 30 -> 30, of which waited for: 12 -> 14; matrix products, arithmetic and copies ran while one was open for 3% -> 3% of each run, Pallas kernels for 25% -> 26%
where the time goes in v15:
time: 128 us; the launch traced here: 127 us
  Pallas kernels  45.5 us (36%)
  starting transfers between devices  43.2 us (34%)
  waiting for transfers between devices  31.9 us (25%)
  local copies, waits for them, and re-layouts  4.53 us (4%)
    pallas_call x9, Pallas kernels, call(): pl.pallas_call(kernel, in_specs=[spec(where) for _, where in ins], out_sp...  45.5 us
    ppermute x26, starting transfers between devices, swap(): return lax.ppermute(item, axis, [(at, at ^ step) for at in range(count)])  27 us
    ppermute x26, waiting for transfers between devices, swap(): return lax.ppermute(item, axis, [(at, at ^ step) for at in range(count)])  17.1 us
    all_to_all x2, waiting for transfers between devices, all_to_all(): lax.all_to_all(item, ('row', 'col'), 0, 0, tiled=True)  12.9 us
    all_to_all x2, starting transfers between devices, all_to_all(): lax.all_to_all(item, ('row', 'col'), 0, 0, tiled=True)  7.52 us
    all_to_all x1, starting transfers between devices, body(): lax.all_to_all(field.reshape(col_parts, rows, wide, channels), 'col', 0,...  5.18 us
    all_to_all x1, starting transfers between devices, body(): field_grad = lax.all_to_all(field_grad, 'col', 0, 0, tiled=True)  3.51 us
  transfers between devices with their start and end apart: 30, of which 14 were waited for; matrix products, arithmetic and copies ran while one was open for 3% of the time, Pallas kernels for 26%

profile of v15, /device:TPU:0, one launch (start us, length us, event | category | flops | bytes accessed | tf_op | source)
XLA Modules:
  0.0 127.2 jit_solution(6470074684983517437)
XLA Ops:
  0.6 5.2 %all-to-all-start = ((bf16[8,2,32,512]{3,2,1,0:T(8,128)(2,1)}), bf16[8,2,32,512]{3,2,1,0:T(8,128)(2,1)S(1)}, u32[]{:S(2)}, u32[]{:S(2)}) async-start(bf16[8,2,32,512]{3,2,1,0:T(8,128)(2,1)} %bitcast.68), calls=%async_computation | async-start | bytes 1048576 | tf_op jit(solution)/shard_map/all_to_all | solution.py:449
  7.0 1.6 %collective-permute-start = (bf16[16,8,512]{2,1,0:T(8,128)(2,1)S(1)}, bf16[16,8,512]{2,1,0:T(8,128)(2,1)S(1)}, u32[]{:S(2)}, u32[]{:S(2)}) collective-permute-start(bf16[16,8,512]{2,1,0:T(8,128)(2,1)S(1)} %get-tuple-element.170), channel_id=1, source_target_pairs={{0,8},{8,0},{16,24},{24,16},{1,9},{9,1},{17,25},{25,17},{2,10},{10... | collective-permute-start | bytes 393224 | tf_op jit(solution)/shard_map/ppermute | solution.py:381
  8.6 2.6 %collective-permute-start.1 = (bf16[16,8,512]{2,1,0:T(8,128)(2,1)S(1)}, bf16[16,8,512]{2,1,0:T(8,128)(2,1)S(1)}, u32[]{:S(2)}, u32[]{:S(2)}) collective-permute-start(bf16[16,8,512]{2,1,0:T(8,128)(2,1)S(1)} %get-tuple-element.172), channel_id=1, source_target_pairs={{0,16},{8,24},{16,0},{24,8},{1,17},{9,25},{17,1},{25,9},{2,18},{10... | collective-permute-start | bytes 393224 | tf_op jit(solution)/shard_map/ppermute | solution.py:381
  11.4 2.2 %shard_map.67.turn_hbm.refs_5_ = bf16[7,512,512]{2,1,0:T(8,128)(2,1)} custom-call(), custom_call_target="tpu_custom_call" | custom-call | flops 1048576 | bytes 1024 | tf_op jit(solution)/shard_map/pallas_call | solution.py:369
  13.7 1.9 %all-to-all-done.x_ref = bf16[8,2,32,512]{3,2,1,0:T(8,128)(2,1)S(1)} async-done(((bf16[8,2,32,512]{3,2,1,0:T(8,128)(2,1)}), bf16[8,2,32,512]{3,2,1,0:T(8,128)(2,1)S(1)}, u32[]{:S(2)}, u32[]{:S(2)}) %all-to-all-start) | async-done | bytes 524320 | tf_op jit(solution)/shard_map/all_to_all | solution.py:449
  15.6 7.8 %shard_map.68 = (bf16[512,512]{1,0:T(8,128)(2,1)}, bf16[512,512]{1,0:T(8,128)(2,1)}, bf16[512,512]{1,0:T(8,128)(2,1)}, bf16[512,512]{1,0:T(8,128)(2,1)}, bf16[51...) custom-call(bf16[8,2,32,512]{3,2,1,0:T(8,128)(2,1)S(1)} %all-to-all-done.x_ref, ...), custom_call_target="tpu_custom_call" | custom-call | flops 1048576 | bytes 1024 | tf_op jit(solution)/shard_map/pallas_call | solution.py:369
  24.1 4.4 %all-to-all-start.1 = ((bf16[32,16,512]{2,1,0:T(8,128)(2,1)}), bf16[32,16,512]{2,1,0:T(8,128)(2,1)S(1)}, u32[]{:S(2)}, u32[]{:S(2)}) async-start(bf16[32,16,512]{2,1,0:T(8,128)(2,1)} %bitcast.71), calls=%async_computation.1 | async-start | bytes 1048576 | tf_op jit(solution)/shard_map/all_to_all | solution.py:447
  29.4 2.0 %shard_map.69 = (bf16[512,512]{1,0:T(8,128)(2,1)S(1)}, bf16[512,512]{1,0:T(8,128)(2,1)S(1)}, bf16[2,512,512]{2,1,0:T(8,128)(2,1)S(1)}) custom-call(bf16[128,512]{1,0:T(8,128)(2,1)S(1)} %get-tuple-element.88.refs_0_, bf16[128,512]{1,0:T(8,128)(2,1)S(1)} %bitcast.61, bf16[128,512]{1,0:T(8,128)(2,1)S(1)} %bitcast.62, bf16[128,512]{1,0:T(8,128)(2,1)S(1)} %bitcast.63, ...), custom_call_target="tpu_custom_call" | custom-call | flops 1048576 | bytes 1024 | tf_op jit(solution)/shard_map/pallas_call | solution.py:369
  31.4 12.6 %all-to-all-done.1 = bf16[32,16,512]{2,1,0:T(8,128)(2,1)S(1)} async-done(((bf16[32,16,512]{2,1,0:T(8,128)(2,1)}), bf16[32,16,512]{2,1,0:T(8,128)(2,1)S(1)}, u32[]{:S(2)}, u32[]{:S(2)}) %all-to-all-start.1) | async-done | bytes 524320 | tf_op jit(solution)/shard_map/all_to_all | solution.py:447
  44.1 12.7 %shard_map.70 = (bf16[512,512]{1,0:T(8,128)(2,1)}, bf16[512,512]{1,0:T(8,128)(2,1)}, bf16[512,512]{1,0:T(8,128)(2,1)}, bf16[512,512]{1,0:T(8,128)(2,1)}, bf16[512,1536]{1,0:T(8,128)(2,1)}) custom-call(bf16[512,512]{1,0:T(8,128)(2,1)S(1)} %bitcast.60, bf16[512,512]{1,0:T(8,128)(2,1)S(1)} %get-tuple-element.92.cot_ref.cot_hbm, ...), custom_call_target="tpu_custom_call" | custom-call | flops 1048576 | bytes 1024 | tf_op jit(solution)/shard_map/pallas_call | solution.py:369
  56.8 3.1 %all-to-all-start.2 = ((bf16[32,16,512]{2,1,0:T(8,128)(2,1)}), bf16[32,16,512]{2,1,0:T(8,128)(2,1)S(1)}, u32[]{:S(2)}, u32[]{:S(2)}) async-start(bf16[32,16,512]{2,1,0:T(8,128)(2,1)} %bitcast.70), calls=%async_computation.2 | async-start | bytes 1048576 | tf_op jit(solution)/shard_map/all_to_all | solution.py:447
  59.8 5.7 %shard_map.71 = (bf16[128,512]{1,0:T(8,128)(2,1)}, bf16[128,512]{1,0:T(8,128)(2,1)}, bf16[128,512]{1,0:T(8,128)(2,1)}, bf16[128,512]{1,0:T(8,128)(2,1)}, bf16[4,...) custom-call(bf16[512,512]{1,0:T(8,128)(2,1)} %copy-done, ...), custom_call_target="tpu_custom_call" | custom-call | flops 1048576 | bytes 1024 | tf_op jit(solution)/shard_map/pallas_call | solution.py:369
  69.8 1.8 %collective-permute-start.7 = (bf16[4,64,512]{2,1,0:T(8,128)(2,1)S(1)}, bf16[4,64,512]{2,1,0:T(8,128)(2,1)S(1)}, u32[]{:S(2)}, u32[]{:S(2)}) collective-permute-start(bf16[4,64,512]{2,1,0:T(8,128)(2,1)S(1)} %get-tuple-element.111), channel_id=1, source_target_pairs={{0,2},{1,3},{2,0},{3,1},{4,6},{5,7},{6,4},{7,5},{8,10},{9,11},{10,... | collective-permute-start | bytes 786440 | tf_op jit(solution)/shard_map/ppermute | solution.py:381
  73.4 1.8 %collective-permute-start.10 = (bf16[128,512]{1,0:T(8,128)(2,1)}, bf16[128,512]{1,0:T(8,128)(2,1)S(1)}, u32[]{:S(2)}, u32[]{:S(2)}) collective-permute-start(bf16[128,512]{1,0:T(8,128)(2,1)} %get-tuple-element.131), channel_id=1, source_target_pairs={{0,8},{8,0},{16,24},{24,16},{1,9},{9,1},{17,25},{25,17},{2,10},{10... | collective-permute-start | bytes 393224 | tf_op jit(solution)/shard_map/ppermute | solution.py:381
  75.4 11.7 %shard_map.73 = (bf16[8,2,32,512]{3,2,1,0:T(8,128)(2,1)}, bf16[4,64,512]{2,1,0:T(8,128)(2,1)}, bf16[4,64,512]{2,1,0:T(8,128)(2,1)}, bf16[4,64,512]{2,1,0:T(8,128...) custom-call(bf16[512,512]{1,0:T(8,128)(2,1)S(1)} %bitcast.59, ...), custom_call_target="tpu_custom_call" | custom-call | flops 1048576 | bytes 1024 | tf_op jit(solution)/shard_map/pallas_call | solution.py:369
  87.2 3.5 %all-to-all-start.3 = ((bf16[8,2,32,512]{3,2,1,0:T(8,128)(2,1)}), bf16[8,2,32,512]{3,2,1,0:T(8,128)(2,1)S(1)}, u32[]{:S(2)}, u32[]{:S(2)}) async-start(bf16[8,2,32,512]{3,2,1,0:T(8,128)(2,1)} %get-tuple-element.153), calls=%async_computation.3 | async-start | bytes 1048576 | tf_op jit(solution)/shard_map/all_to_all | solution.py:501
  94.9 1.9 %collective-permute-start.15 = (bf16[4,64,512]{2,1,0:T(8,128)(2,1)S(1)}, bf16[4,64,512]{2,1,0:T(8,128)(2,1)S(1)}, u32[]{:S(2)}, u32[]{:S(2)}) collective-permute-start(bf16[4,64,512]{2,1,0:T(8,128)(2,1)S(1)} %get-tuple-element.143), channel_id=1, source_target_pairs={{0,2},{1,3},{2,0},{3,1},{4,6},{5,7},{6,4},{7,5},{8,10},{9,11},{10,... | collective-permute-start | bytes 786440 | tf_op jit(solution)/shard_map/ppermute | solution.py:381
  98.5 2.4 %collective-permute-start.18 = (bf16[128,512]{1,0:T(8,128)(2,1)}, bf16[128,512]{1,0:T(8,128)(2,1)}, u32[]{:S(2)}, u32[]{:S(2)}) collective-permute-start(bf16[128,512]{1,0:T(8,128)(2,1)} %get-tuple-element.147), channel_id=1, source_target_pairs={{0,16},{8,24},{16,0},{24,8},{1,17},{9,25},{17,1},{25,9},{2,18},{10... | collective-permute-start | bytes 393224 | tf_op jit(solution)/shard_map/ppermute | solution.py:381
  103.1 4.3 %collective-permute-done.18 = bf16[128,512]{1,0:T(8,128)(2,1)} collective-permute-done((bf16[128,512]{1,0:T(8,128)(2,1)}, bf16[128,512]{1,0:T(8,128)(2,1)}, u32[]{:S(2)}, u32[]{:S(2)}) %collective-permute-start.18) | collective-permute-done | bytes 131104 | tf_op jit(solution)/shard_map/ppermute | solution.py:381
  107.8 2.0 %collective-permute-start.25 = (bf16[4,16,512]{2,1,0:T(8,128)(2,1)S(1)}, bf16[4,16,512]{2,1,0:T(8,128)(2,1)S(1)}, u32[]{:S(2)}, u32[]{:S(2)}) collective-permute-start(bf16[4,16,512]{2,1,0:T(8,128)(2,1)S(1)} %get-tuple-element.178), channel_id=1, source_target_pairs={{0,24},{8,16},{16,8},{24,0},{1,25},{9,17},{17,9},{25,1},{2,26},{10... | collective-permute-start | bytes 196616 | tf_op jit(solution)/shard_map/ppermute | solution.py:381
  109.8 1.8 %collective-permute-start.19 = (bf16[128,512]{1,0:T(8,128)(2,1)}, bf16[128,512]{1,0:T(8,128)(2,1)S(1)}, u32[]{:S(2)}, u32[]{:S(2)}) collective-permute-start(bf16[128,512]{1,0:T(8,128)(2,1)} %get-tuple-element.159), channel_id=1, source_target_pairs={{0,24},{8,16},{16,8},{24,0},{1,25},{9,17},{17,9},{25,1},{2,26},{10... | collective-permute-start | bytes 393224 | tf_op jit(solution)/shard_map/ppermute | solution.py:381
  114.1 1.7 %collective-permute-start.21 = (bf16[4,16,512]{2,1,0:T(8,128)(2,1)S(1)}, bf16[4,16,512]{2,1,0:T(8,128)(2,1)S(1)}, u32[]{:S(2)}, u32[]{:S(2)}) collective-permute-start(bf16[4,16,512]{2,1,0:T(8,128)(2,1)S(1)} %get-tuple-element.174), channel_id=1, source_target_pairs={{0,16},{8,24},{16,0},{24,8},{1,17},{9,25},{17,1},{25,9},{2,18},{10... | collective-permute-start | bytes 196616 | tf_op jit(solution)/shard_map/ppermute | solution.py:381
  115.8 2.0 %collective-permute-done.24 = bf16[4,16,512]{2,1,0:T(8,128)(2,1)S(1)} collective-permute-done((bf16[4,16,512]{2,1,0:T(8,128)(2,1)S(1)}, bf16[4,16,512]{2,1,0:T(8,128)(2,1)S(1)}, u32[]{:S(2)}, u32[]{:S(2)}) %collective-permute-start.24) | collective-permute-done | bytes 65568 | tf_op jit(solution)/shard_map/ppermute | solution.py:381
  118.5 7.1 %collective-permute-done.21 = bf16[4,16,512]{2,1,0:T(8,128)(2,1)S(1)} collective-permute-done((bf16[4,16,512]{2,1,0:T(8,128)(2,1)S(1)}, bf16[4,16,512]{2,1,0:T(8,128)(2,1)S(1)}, u32[]{:S(2)}, u32[]{:S(2)}) %collective-permute-start.21) | collective-permute-done | bytes 65568 | tf_op jit(solution)/shard_map/ppermute | solution.py:381
  (74 shorter events, 22.3 us)
Async XLA Ops:
  0.6 14.9 %all-to-all-start = ((bf16[8,2,32,512]{3,2,1,0:T(8,128)(2,1)}), bf16[8,2,32,512]{3,2,1,0:T(8,128)(2,1)S(1)}, u32[]{:S(2)}, u32[]{:S(2)}) async-start(bf16[8,2,32,512]{3,2,1,0:T(8,128)(2,1)} %bitcast.68), calls=%async_computation | async-start | bytes 1048576 | tf_op jit(solution)/shard_map/all_to_all | solution.py:449
  7.0 16.4 %collective-permute-start = (bf16[16,8,512]{2,1,0:T(8,128)(2,1)S(1)}, bf16[16,8,512]{2,1,0:T(8,128)(2,1)S(1)}, u32[]{:S(2)}, u32[]{:S(2)}) collective-permute-start(bf16[16,8,512]{2,1,0:T(8,128)(2,1)S(1)} %get-tuple-element.170), channel_id=1, source_target_pairs={{0,8},{8,0},{16,24},{24,16},{1,9},{9,1},{17,25},{25,17},{2,10},{10... | collective-permute-start | bytes 393224 | tf_op jit(solution)/shard_map/ppermute | solution.py:381
  8.6 14.8 %collective-permute-start.1 = (bf16[16,8,512]{2,1,0:T(8,128)(2,1)S(1)}, bf16[16,8,512]{2,1,0:T(8,128)(2,1)S(1)}, u32[]{:S(2)}, u32[]{:S(2)}) collective-permute-start(bf16[16,8,512]{2,1,0:T(8,128)(2,1)S(1)} %get-tuple-element.172), channel_id=1, source_target_pairs={{0,16},{8,24},{16,0},{24,8},{1,17},{9,25},{17,1},{25,9},{2,18},{10... | collective-permute-start | bytes 393224 | tf_op jit(solution)/shard_map/ppermute | solution.py:381
  11.2 12.2 %collective-permute-start.2 = (bf16[16,8,512]{2,1,0:T(8,128)(2,1)S(1)}, bf16[16,8,512]{2,1,0:T(8,128)(2,1)S(1)}, u32[]{:S(2)}, u32[]{:S(2)}) collective-permute-start(bf16[16,8,512]{2,1,0:T(8,128)(2,1)S(1)} %get-tuple-element.169), channel_id=1, source_target_pairs={{0,24},{8,16},{16,8},{24,0},{1,25},{9,17},{17,9},{25,1},{2,26},{10... | collective-permute-start | bytes 393224 | tf_op jit(solution)/shard_map/ppermute | solution.py:381
  24.1 20.0 %all-to-all-start.1 = ((bf16[32,16,512]{2,1,0:T(8,128)(2,1)}), bf16[32,16,512]{2,1,0:T(8,128)(2,1)S(1)}, u32[]{:S(2)}, u32[]{:S(2)}) async-start(bf16[32,16,512]{2,1,0:T(8,128)(2,1)} %bitcast.71), calls=%async_computation.1 | async-start | bytes 1048576 | tf_op jit(solution)/shard_map/all_to_all | solution.py:447
  56.8 18.7 %all-to-all-start.2 = ((bf16[32,16,512]{2,1,0:T(8,128)(2,1)}), bf16[32,16,512]{2,1,0:T(8,128)(2,1)S(1)}, u32[]{:S(2)}, u32[]{:S(2)}) async-start(bf16[32,16,512]{2,1,0:T(8,128)(2,1)} %bitcast.70), calls=%async_computation.2 | async-start | bytes 1048576 | tf_op jit(solution)/shard_map/all_to_all | solution.py:447
  66.4 2.1 %collective-permute-start.6 = (bf16[4,64,512]{2,1,0:T(8,128)(2,1)}, bf16[4,64,512]{2,1,0:T(8,128)(2,1)S(1)}, u32[]{:S(2)}, u32[]{:S(2)}) collective-permute-start(bf16[4,64,512]{2,1,0:T(8,128)(2,1)} %get-tuple-element.109), channel_id=1, source_target_pairs={{0,1},{1,0},{2,3},{3,2},{4,5},{5,4},{6,7},{7,6},{8,9},{9,8},{10,11... | collective-permute-start | bytes 786440 | tf_op jit(solution)/shard_map/ppermute | solution.py:381
  69.8 17.3 %collective-permute-start.7 = (bf16[4,64,512]{2,1,0:T(8,128)(2,1)S(1)}, bf16[4,64,512]{2,1,0:T(8,128)(2,1)S(1)}, u32[]{:S(2)}, u32[]{:S(2)}) collective-permute-start(bf16[4,64,512]{2,1,0:T(8,128)(2,1)S(1)} %get-tuple-element.111), channel_id=1, source_target_pairs={{0,2},{1,3},{2,0},{3,1},{4,6},{5,7},{6,4},{7,5},{8,10},{9,11},{10,... | collective-permute-start | bytes 786440 | tf_op jit(solution)/shard_map/ppermute | solution.py:381
  71.6 15.5 %collective-permute-start.8 = (bf16[4,64,512]{2,1,0:T(8,128)(2,1)S(1)}, bf16[4,64,512]{2,1,0:T(8,128)(2,1)S(1)}, u32[]{:S(2)}, u32[]{:S(2)}) collective-permute-start(bf16[4,64,512]{2,1,0:T(8,128)(2,1)S(1)} %get-tuple-element.112), channel_id=1, source_target_pairs={{0,4},{1,5},{2,6},{3,7},{4,0},{5,1},{6,2},{7,3},{8,12},{9,13},{10,... | collective-permute-start | bytes 786440 | tf_op jit(solution)/shard_map/ppermute | solution.py:381
  73.1 14.0 %collective-permute-start.9 = (bf16[4,64,512]{2,1,0:T(8,128)(2,1)S(1)}, bf16[4,64,512]{2,1,0:T(8,128)(2,1)S(1)}, u32[]{:S(2)}, u32[]{:S(2)}) collective-permute-start(bf16[4,64,512]{2,1,0:T(8,128)(2,1)S(1)} %get-tuple-element.113), channel_id=1, source_target_pairs={{0,6},{1,7},{2,4},{3,5},{4,2},{5,3},{6,0},{7,1},{8,14},{9,15},{10,... | collective-permute-start | bytes 786440 | tf_op jit(solution)/shard_map/ppermute | solution.py:381
  73.4 13.7 %collective-permute-start.10 = (bf16[128,512]{1,0:T(8,128)(2,1)}, bf16[128,512]{1,0:T(8,128)(2,1)S(1)}, u32[]{:S(2)}, u32[]{:S(2)}) collective-permute-start(bf16[128,512]{1,0:T(8,128)(2,1)} %get-tuple-element.131), channel_id=1, source_target_pairs={{0,8},{8,0},{16,24},{24,16},{1,9},{9,1},{17,25},{25,17},{2,10},{10... | collective-permute-start | bytes 393224 | tf_op jit(solution)/shard_map/ppermute | solution.py:381
  87.2 13.7 %all-to-all-start.3 = ((bf16[8,2,32,512]{3,2,1,0:T(8,128)(2,1)}), bf16[8,2,32,512]{3,2,1,0:T(8,128)(2,1)S(1)}, u32[]{:S(2)}, u32[]{:S(2)}) async-start(bf16[8,2,32,512]{3,2,1,0:T(8,128)(2,1)} %get-tuple-element.153), calls=%async_computation.3 | async-start | bytes 1048576 | tf_op jit(solution)/shard_map/all_to_all | solution.py:501
  91.6 2.0 %collective-permute-start.14 = (bf16[4,64,512]{2,1,0:T(8,128)(2,1)}, bf16[4,64,512]{2,1,0:T(8,128)(2,1)S(1)}, u32[]{:S(2)}, u32[]{:S(2)}) collective-permute-start(bf16[4,64,512]{2,1,0:T(8,128)(2,1)} %get-tuple-element.141), channel_id=1, source_target_pairs={{0,1},{1,0},{2,3},{3,2},{4,5},{5,4},{6,7},{7,6},{8,9},{9,8},{10,11... | collective-permute-start | bytes 786440 | tf_op jit(solution)/shard_map/ppermute | solution.py:381
  94.9 12.8 %collective-permute-start.15 = (bf16[4,64,512]{2,1,0:T(8,128)(2,1)S(1)}, bf16[4,64,512]{2,1,0:T(8,128)(2,1)S(1)}, u32[]{:S(2)}, u32[]{:S(2)}) collective-permute-start(bf16[4,64,512]{2,1,0:T(8,128)(2,1)S(1)} %get-tuple-element.143), channel_id=1, source_target_pairs={{0,2},{1,3},{2,0},{3,1},{4,6},{5,7},{6,4},{7,5},{8,10},{9,11},{10,... | collective-permute-start | bytes 786440 | tf_op jit(solution)/shard_map/ppermute | solution.py:381
  96.8 12.9 %collective-permute-start.16 = (bf16[4,64,512]{2,1,0:T(8,128)(2,1)S(1)}, bf16[4,64,512]{2,1,0:T(8,128)(2,1)S(1)}, u32[]{:S(2)}, u32[]{:S(2)}) collective-permute-start(bf16[4,64,512]{2,1,0:T(8,128)(2,1)S(1)} %get-tuple-element.144), channel_id=1, source_target_pairs={{0,4},{1,5},{2,6},{3,7},{4,0},{5,1},{6,2},{7,3},{8,12},{9,13},{10,... | collective-permute-start | bytes 786440 | tf_op jit(solution)/shard_map/ppermute | solution.py:381
  98.3 13.3 %collective-permute-start.17 = (bf16[4,64,512]{2,1,0:T(8,128)(2,1)S(1)}, bf16[4,64,512]{2,1,0:T(8,128)(2,1)S(1)}, u32[]{:S(2)}, u32[]{:S(2)}) collective-permute-start(bf16[4,64,512]{2,1,0:T(8,128)(2,1)S(1)} %get-tuple-element.145), channel_id=1, source_target_pairs={{0,6},{1,7},{2,4},{3,5},{4,2},{5,3},{6,0},{7,1},{8,14},{9,15},{10,... | collective-permute-start | bytes 786440 | tf_op jit(solution)/shard_map/ppermute | solution.py:381
  98.5 8.9 %collective-permute-start.18 = (bf16[128,512]{1,0:T(8,128)(2,1)}, bf16[128,512]{1,0:T(8,128)(2,1)}, u32[]{:S(2)}, u32[]{:S(2)}) collective-permute-start(bf16[128,512]{1,0:T(8,128)(2,1)} %get-tuple-element.147), channel_id=1, source_target_pairs={{0,16},{8,24},{16,0},{24,8},{1,17},{9,25},{17,1},{25,9},{2,18},{10... | collective-permute-start | bytes 393224 | tf_op jit(solution)/shard_map/ppermute | solution.py:381
  101.0 13.1 %collective-permute-start.23 = (bf16[4,16,512]{2,1,0:T(8,128)(2,1)S(1)}, bf16[4,16,512]{2,1,0:T(8,128)(2,1)S(1)}, u32[]{:S(2)}, u32[]{:S(2)}) collective-permute-start(bf16[4,16,512]{2,1,0:T(8,128)(2,1)S(1)} %get-tuple-element.176), channel_id=1, source_target_pairs={{0,8},{8,0},{16,24},{24,16},{1,9},{9,1},{17,25},{25,17},{2,10},{10... | collective-permute-start | bytes 196616 | tf_op jit(solution)/shard_map/ppermute | solution.py:381
  107.4 10.4 %collective-permute-start.24 = (bf16[4,16,512]{2,1,0:T(8,128)(2,1)S(1)}, bf16[4,16,512]{2,1,0:T(8,128)(2,1)S(1)}, u32[]{:S(2)}, u32[]{:S(2)}) collective-permute-start(bf16[4,16,512]{2,1,0:T(8,128)(2,1)S(1)} %get-tuple-element.177), channel_id=1, source_target_pairs={{0,16},{8,24},{16,0},{24,8},{1,17},{9,25},{17,1},{25,9},{2,18},{10... | collective-permute-start | bytes 196616 | tf_op jit(solution)/shard_map/ppermute | solution.py:381
  107.8 10.7 %collective-permute-start.25 = (bf16[4,16,512]{2,1,0:T(8,128)(2,1)S(1)}, bf16[4,16,512]{2,1,0:T(8,128)(2,1)S(1)}, u32[]{:S(2)}, u32[]{:S(2)}) collective-permute-start(bf16[4,16,512]{2,1,0:T(8,128)(2,1)S(1)} %get-tuple-element.178), channel_id=1, source_target_pairs={{0,24},{8,16},{16,8},{24,0},{1,25},{9,17},{17,9},{25,1},{2,26},{10... | collective-permute-start | bytes 196616 | tf_op jit(solution)/shard_map/ppermute | solution.py:381
  109.8 16.6 %collective-permute-start.19 = (bf16[128,512]{1,0:T(8,128)(2,1)}, bf16[128,512]{1,0:T(8,128)(2,1)S(1)}, u32[]{:S(2)}, u32[]{:S(2)}) collective-permute-start(bf16[128,512]{1,0:T(8,128)(2,1)} %get-tuple-element.159), channel_id=1, source_target_pairs={{0,24},{8,16},{16,8},{24,0},{1,25},{9,17},{17,9},{25,1},{2,26},{10... | collective-permute-start | bytes 393224 | tf_op jit(solution)/shard_map/ppermute | solution.py:381
  111.7 6.7 %collective-permute-start.20 = (bf16[4,16,512]{2,1,0:T(8,128)(2,1)S(1)}, bf16[4,16,512]{2,1,0:T(8,128)(2,1)S(1)}, u32[]{:S(2)}, u32[]{:S(2)}) collective-permute-start(bf16[4,16,512]{2,1,0:T(8,128)(2,1)S(1)} %get-tuple-element.173), channel_id=1, source_target_pairs={{0,8},{8,0},{16,24},{24,16},{1,9},{9,1},{17,25},{25,17},{2,10},{10... | collective-permute-start | bytes 196616 | tf_op jit(solution)/shard_map/ppermute | solution.py:381
  114.1 11.5 %collective-permute-start.21 = (bf16[4,16,512]{2,1,0:T(8,128)(2,1)S(1)}, bf16[4,16,512]{2,1,0:T(8,128)(2,1)S(1)}, u32[]{:S(2)}, u32[]{:S(2)}) collective-permute-start(bf16[4,16,512]{2,1,0:T(8,128)(2,1)S(1)} %get-tuple-element.174), channel_id=1, source_target_pairs={{0,16},{8,24},{16,0},{24,8},{1,17},{9,25},{17,1},{25,9},{2,18},{10... | collective-permute-start | bytes 196616 | tf_op jit(solution)/shard_map/ppermute | solution.py:381
  117.8 7.8 %collective-permute-start.22 = (bf16[4,16,512]{2,1,0:T(8,128)(2,1)S(1)}, bf16[4,16,512]{2,1,0:T(8,128)(2,1)S(1)}, u32[]{:S(2)}, u32[]{:S(2)}) collective-permute-start(bf16[4,16,512]{2,1,0:T(8,128)(2,1)S(1)} %get-tuple-element.175), channel_id=1, source_target_pairs={{0,24},{8,16},{16,8},{24,0},{1,25},{9,17},{17,9},{25,1},{2,26},{10... | collective-permute-start | bytes 196616 | tf_op jit(solution)/shard_map/ppermute | solution.py:381
  (14 other events, 98.3 us)

commit v16 on v15

--- a/solution.py
+++ b/solution.py
@@ -503,10 +503,10 @@
     pieces_a = plane_pieces(sums_a, plane, core)
     second, _ = lax.optimization_barrier((rest[:1], sums_a))
     second = [swap(item, "row", row_parts, 2) for item in second]
-    field_grad, pieces_b, rest = lax.optimization_barrier((field_grad, pieces_b, rest[1:]))
+    field_grad, pieces_b, rest, second = lax.optimization_barrier((field_grad, pieces_b, rest[1:], second))
+    pieces_out += second
     grads_b = last_sums(pieces_b, row_parts)
-    pieces_a, second, pieces_out = lax.optimization_barrier((pieces_a, second, pieces_out))
-    pieces_out += second + [swap(item, "row", row_parts, 3 + step) for step, item in enumerate(rest)]
+    pieces_out += [swap(item, "row", row_parts, 3 + step) for step, item in enumerate(rest)]
     field_grad, = call(store, at(ANY, field_grad), at(FAR, field_grad.shape), [copies])
     field_grad = field_grad.reshape(high, wide, channels)
     output = jnp.zeros((high, wide, channels), BF16)

time: 128 us -> 127 us (level)
  waiting for transfers between devices: 31.9 us -> 28.7 us
    ppermute x26, waiting for transfers between devices: 17.1 us -> 13.8 us  [swap(): return lax.ppermute(item, axis, [(at, at ^ step) for at in range(count)])]
    unnamed x16 -> x20, local copies, waits for them, and re-layouts: 2.36 us -> 3.18 us
  transfers between devices with their start and end apart: 30 -> 30, of which waited for: 14 -> 12; matrix products, arithmetic and copies ran while one was open for 3% -> 3% of each run, Pallas kernels for 26% -> 26%
where the time goes in v16:
time: 127 us
  Pallas kernels  45.5 us (36%)
  starting transfers between devices  43.9 us (35%)
  waiting for transfers between devices  28.7 us (23%)
  local copies, waits for them, and re-layouts  5.35 us (4%)
  other arithmetic  2.17 us (2%)
    pallas_call x9, Pallas kernels, call(): pl.pallas_call(kernel, in_specs=[spec(where) for _, where in ins], out_sp...  45.5 us
    ppermute x26, starting transfers between devices, swap(): return lax.ppermute(item, axis, [(at, at ^ step) for at in range(count)])  27.7 us
    ppermute x26, waiting for transfers between devices, swap(): return lax.ppermute(item, axis, [(at, at ^ step) for at in range(count)])  13.8 us
    all_to_all x2, waiting for transfers between devices, all_to_all(): lax.all_to_all(item, ('row', 'col'), 0, 0, tiled=True)  12.9 us
    all_to_all x2, starting transfers between devices, all_to_all(): lax.all_to_all(item, ('row', 'col'), 0, 0, tiled=True)  7.51 us
    all_to_all x1, starting transfers between devices, body(): lax.all_to_all(field.reshape(col_parts, rows, wide, channels), 'col', 0,...  5.18 us
    all_to_all x1, starting transfers between devices, body(): field_grad = lax.all_to_all(field_grad, 'col', 0, 0, tiled=True)  3.49 us
    unnamed x20, local copies, waits for them, and re-layouts  3.18 us
  transfers between devices with their start and end apart: 30, of which 12 were waited for; matrix products, arithmetic and copies ran while one was open for 3% of the time, Pallas kernels for 26%

profile of v16, /device:TPU:0, one launch (start us, length us, event | category | flops | bytes accessed | tf_op | source)
XLA Modules:
  0.0 126.6 jit_solution(8157060259226329391)
XLA Ops:
  0.6 5.2 %all-to-all-start = ((bf16[8,2,32,512]{3,2,1,0:T(8,128)(2,1)}), bf16[8,2,32,512]{3,2,1,0:T(8,128)(2,1)S(1)}, u32[]{:S(2)}, u32[]{:S(2)}) async-start(bf16[8,2,32,512]{3,2,1,0:T(8,128)(2,1)} %bitcast.68), calls=%async_computation | async-start | bytes 1048576 | tf_op jit(solution)/shard_map/all_to_all | solution.py:449
  7.0 1.6 %collective-permute-start = (bf16[16,8,512]{2,1,0:T(8,128)(2,1)S(1)}, bf16[16,8,512]{2,1,0:T(8,128)(2,1)S(1)}, u32[]{:S(2)}, u32[]{:S(2)}) collective-permute-start(bf16[16,8,512]{2,1,0:T(8,128)(2,1)S(1)} %get-tuple-element.158), channel_id=1, source_target_pairs={{0,8},{8,0},{16,24},{24,16},{1,9},{9,1},{17,25},{25,17},{2,10},{10... | collective-permute-start | bytes 393224 | tf_op jit(solution)/shard_map/ppermute | solution.py:381
  8.6 2.6 %collective-permute-start.1 = (bf16[16,8,512]{2,1,0:T(8,128)(2,1)S(1)}, bf16[16,8,512]{2,1,0:T(8,128)(2,1)S(1)}, u32[]{:S(2)}, u32[]{:S(2)}) collective-permute-start(bf16[16,8,512]{2,1,0:T(8,128)(2,1)S(1)} %get-tuple-element.160), channel_id=1, source_target_pairs={{0,16},{8,24},{16,0},{24,8},{1,17},{9,25},{17,1},{25,9},{2,18},{10... | collective-permute-start | bytes 393224 | tf_op jit(solution)/shard_map/ppermute | solution.py:381
  11.4 2.2 %shard_map.67.turn_hbm.refs_5_ = bf16[7,512,512]{2,1,0:T(8,128)(2,1)} custom-call(), custom_call_target="tpu_custom_call" | custom-call | flops 1048576 | bytes 1024 | tf_op jit(solution)/shard_map/pallas_call | solution.py:369
  13.6 1.9 %all-to-all-done.x_ref = bf16[8,2,32,512]{3,2,1,0:T(8,128)(2,1)S(1)} async-done(((bf16[8,2,32,512]{3,2,1,0:T(8,128)(2,1)}), bf16[8,2,32,512]{3,2,1,0:T(8,128)(2,1)S(1)}, u32[]{:S(2)}, u32[]{:S(2)}) %all-to-all-start) | async-done | bytes 524320 | tf_op jit(solution)/shard_map/all_to_all | solution.py:449
  15.6 7.8 %shard_map.68 = (bf16[512,512]{1,0:T(8,128)(2,1)}, bf16[512,512]{1,0:T(8,128)(2,1)}, bf16[512,512]{1,0:T(8,128)(2,1)}, bf16[512,512]{1,0:T(8,128)(2,1)}, bf16[51...) custom-call(bf16[8,2,32,512]{3,2,1,0:T(8,128)(2,1)S(1)} %all-to-all-done.x_ref, ...), custom_call_target="tpu_custom_call" | custom-call | flops 1048576 | bytes 1024 | tf_op jit(solution)/shard_map/pallas_call | solution.py:369
  24.1 4.4 %all-to-all-start.1 = ((bf16[32,16,512]{2,1,0:T(8,128)(2,1)}), bf16[32,16,512]{2,1,0:T(8,128)(2,1)S(1)}, u32[]{:S(2)}, u32[]{:S(2)}) async-start(bf16[32,16,512]{2,1,0:T(8,128)(2,1)} %bitcast.71), calls=%async_computation.1 | async-start | bytes 1048576 | tf_op jit(solution)/shard_map/all_to_all | solution.py:447
  29.4 2.0 %shard_map.69 = (bf16[512,512]{1,0:T(8,128)(2,1)S(1)}, bf16[512,512]{1,0:T(8,128)(2,1)S(1)}, bf16[2,512,512]{2,1,0:T(8,128)(2,1)S(1)}) custom-call(bf16[128,512]{1,0:T(8,128)(2,1)S(1)} %get-tuple-element.82.refs_0_, bf16[128,512]{1,0:T(8,128)(2,1)S(1)} %bitcast.61, bf16[128,512]{1,0:T(8,128)(2,1)S(1)} %bitcast.62, bf16[128,512]{1,0:T(8,128)(2,1)S(1)} %bitcast.63, ...), custom_call_target="tpu_custom_call" | custom-call | flops 1048576 | bytes 1024 | tf_op jit(solution)/shard_map/pallas_call | solution.py:369
  31.4 12.6 %all-to-all-done.1 = bf16[32,16,512]{2,1,0:T(8,128)(2,1)S(1)} async-done(((bf16[32,16,512]{2,1,0:T(8,128)(2,1)}), bf16[32,16,512]{2,1,0:T(8,128)(2,1)S(1)}, u32[]{:S(2)}, u32[]{:S(2)}) %all-to-all-start.1) | async-done | bytes 524320 | tf_op jit(solution)/shard_map/all_to_all | solution.py:447
  44.1 12.7 %shard_map.70 = (bf16[512,512]{1,0:T(8,128)(2,1)}, bf16[512,512]{1,0:T(8,128)(2,1)}, bf16[512,512]{1,0:T(8,128)(2,1)}, bf16[512,512]{1,0:T(8,128)(2,1)}, bf16[512,1536]{1,0:T(8,128)(2,1)}) custom-call(bf16[512,512]{1,0:T(8,128)(2,1)S(1)} %bitcast.60, bf16[512,512]{1,0:T(8,128)(2,1)S(1)} %get-tuple-element.86.cot_ref.cot_hbm, ...), custom_call_target="tpu_custom_call" | custom-call | flops 1048576 | bytes 1024 | tf_op jit(solution)/shard_map/pallas_call | solution.py:369
  56.7 3.1 %all-to-all-start.2 = ((bf16[32,16,512]{2,1,0:T(8,128)(2,1)}), bf16[32,16,512]{2,1,0:T(8,128)(2,1)S(1)}, u32[]{:S(2)}, u32[]{:S(2)}) async-start(bf16[32,16,512]{2,1,0:T(8,128)(2,1)} %bitcast.70), calls=%async_computation.2 | async-start | bytes 1048576 | tf_op jit(solution)/shard_map/all_to_all | solution.py:447
  59.8 5.7 %shard_map.71 = (bf16[128,512]{1,0:T(8,128)(2,1)}, bf16[128,512]{1,0:T(8,128)(2,1)}, bf16[128,512]{1,0:T(8,128)(2,1)}, bf16[128,512]{1,0:T(8,128)(2,1)}, bf16[4,...) custom-call(bf16[512,512]{1,0:T(8,128)(2,1)} %copy-done, ...), custom_call_target="tpu_custom_call" | custom-call | flops 1048576 | bytes 1024 | tf_op jit(solution)/shard_map/pallas_call | solution.py:369
  69.8 1.8 %collective-permute-start.7 = (bf16[4,64,512]{2,1,0:T(8,128)(2,1)S(1)}, bf16[4,64,512]{2,1,0:T(8,128)(2,1)S(1)}, u32[]{:S(2)}, u32[]{:S(2)}) collective-permute-start(bf16[4,64,512]{2,1,0:T(8,128)(2,1)S(1)} %get-tuple-element.105), channel_id=1, source_target_pairs={{0,2},{1,3},{2,0},{3,1},{4,6},{5,7},{6,4},{7,5},{8,10},{9,11},{10,... | collective-permute-start | bytes 786440 | tf_op jit(solution)/shard_map/ppermute | solution.py:381
  73.4 1.8 %collective-permute-start.10 = (bf16[128,512]{1,0:T(8,128)(2,1)}, bf16[128,512]{1,0:T(8,128)(2,1)S(1)}, u32[]{:S(2)}, u32[]{:S(2)}) collective-permute-start(bf16[128,512]{1,0:T(8,128)(2,1)} %get-tuple-element.125), channel_id=1, source_target_pairs={{0,8},{8,0},{16,24},{24,16},{1,9},{9,1},{17,25},{25,17},{2,10},{10... | collective-permute-start | bytes 393224 | tf_op jit(solution)/shard_map/ppermute | solution.py:381
  75.4 11.7 %shard_map.73 = (bf16[8,2,32,512]{3,2,1,0:T(8,128)(2,1)}, bf16[4,64,512]{2,1,0:T(8,128)(2,1)}, bf16[4,64,512]{2,1,0:T(8,128)(2,1)}, bf16[4,64,512]{2,1,0:T(8,128...) custom-call(bf16[512,512]{1,0:T(8,128)(2,1)S(1)} %bitcast.59, ...), custom_call_target="tpu_custom_call" | custom-call | flops 1048576 | bytes 1024 | tf_op jit(solution)/shard_map/pallas_call | solution.py:369
  89.0 3.5 %all-to-all-start.3 = ((bf16[8,2,32,512]{3,2,1,0:T(8,128)(2,1)}), bf16[8,2,32,512]{3,2,1,0:T(8,128)(2,1)S(1)}, u32[]{:S(2)}, u32[]{:S(2)}) async-start(bf16[8,2,32,512]{3,2,1,0:T(8,128)(2,1)} %get-tuple-element.130), calls=%async_computation.3 | async-start | bytes 1048576 | tf_op jit(solution)/shard_map/all_to_all | solution.py:501
  94.0 2.4 %collective-permute-start.15 = (bf16[128,512]{1,0:T(8,128)(2,1)}, bf16[128,512]{1,0:T(8,128)(2,1)S(1)}, u32[]{:S(2)}, u32[]{:S(2)}) collective-permute-start(bf16[128,512]{1,0:T(8,128)(2,1)} %get-tuple-element.149), channel_id=1, source_target_pairs={{0,16},{8,24},{16,0},{24,8},{1,17},{9,25},{17,1},{25,9},{2,18},{10... | collective-permute-start | bytes 393224 | tf_op jit(solution)/shard_map/ppermute | solution.py:381
  97.3 2.1 %collective-permute-start.17 = (bf16[4,64,512]{2,1,0:T(8,128)(2,1)S(1)}, bf16[4,64,512]{2,1,0:T(8,128)(2,1)S(1)}, u32[]{:S(2)}, u32[]{:S(2)}) collective-permute-start(bf16[4,64,512]{2,1,0:T(8,128)(2,1)S(1)} %get-tuple-element.146), channel_id=1, source_target_pairs={{0,2},{1,3},{2,0},{3,1},{4,6},{5,7},{6,4},{7,5},{8,10},{9,11},{10,... | collective-permute-start | bytes 786440 | tf_op jit(solution)/shard_map/ppermute | solution.py:381
  100.9 2.9 %collective-permute-done.15 = bf16[128,512]{1,0:T(8,128)(2,1)S(1)} collective-permute-done((bf16[128,512]{1,0:T(8,128)(2,1)}, bf16[128,512]{1,0:T(8,128)(2,1)S(1)}, u32[]{:S(2)}, u32[]{:S(2)}) %collective-permute-start.15) | collective-permute-done | bytes 131104 | tf_op jit(solution)/shard_map/ppermute | solution.py:381
  105.3 2.8 %collective-permute-start.24 = (bf16[4,16,512]{2,1,0:T(8,128)(2,1)S(1)}, bf16[4,16,512]{2,1,0:T(8,128)(2,1)S(1)}, u32[]{:S(2)}, u32[]{:S(2)}) collective-permute-start(bf16[4,16,512]{2,1,0:T(8,128)(2,1)S(1)} %get-tuple-element.165), channel_id=1, source_target_pairs={{0,16},{8,24},{16,0},{24,8},{1,17},{9,25},{17,1},{25,9},{2,18},{10... | collective-permute-start | bytes 196616 | tf_op jit(solution)/shard_map/ppermute | solution.py:381
  108.9 1.5 %collective-permute-start.25 = (bf16[4,16,512]{2,1,0:T(8,128)(2,1)S(1)}, bf16[4,16,512]{2,1,0:T(8,128)(2,1)S(1)}, u32[]{:S(2)}, u32[]{:S(2)}) collective-permute-start(bf16[4,16,512]{2,1,0:T(8,128)(2,1)S(1)} %get-tuple-element.166), channel_id=1, source_target_pairs={{0,24},{8,16},{16,8},{24,0},{1,25},{9,17},{17,9},{25,1},{2,26},{10... | collective-permute-start | bytes 196616 | tf_op jit(solution)/shard_map/ppermute | solution.py:381
  114.9 1.6 %collective-permute-start.21 = (bf16[4,16,512]{2,1,0:T(8,128)(2,1)S(1)}, bf16[4,16,512]{2,1,0:T(8,128)(2,1)S(1)}, u32[]{:S(2)}, u32[]{:S(2)}) collective-permute-start(bf16[4,16,512]{2,1,0:T(8,128)(2,1)S(1)} %get-tuple-element.162), channel_id=1, source_target_pairs={{0,16},{8,24},{16,0},{24,8},{1,17},{9,25},{17,1},{25,9},{2,18},{10... | collective-permute-start | bytes 196616 | tf_op jit(solution)/shard_map/ppermute | solution.py:381
  116.6 1.5 %collective-permute-start.22 = (bf16[4,16,512]{2,1,0:T(8,128)(2,1)S(1)}, bf16[4,16,512]{2,1,0:T(8,128)(2,1)S(1)}, u32[]{:S(2)}, u32[]{:S(2)}) collective-permute-start(bf16[4,16,512]{2,1,0:T(8,128)(2,1)S(1)} %get-tuple-element.163), channel_id=1, source_target_pairs={{0,24},{8,16},{16,8},{24,0},{1,25},{9,17},{17,9},{25,1},{2,26},{10... | collective-permute-start | bytes 196616 | tf_op jit(solution)/shard_map/ppermute | solution.py:381
  118.6 6.4 %collective-permute-done.21 = bf16[4,16,512]{2,1,0:T(8,128)(2,1)S(1)} collective-permute-done((bf16[4,16,512]{2,1,0:T(8,128)(2,1)S(1)}, bf16[4,16,512]{2,1,0:T(8,128)(2,1)S(1)}, u32[]{:S(2)}, u32[]{:S(2)}) %collective-permute-start.21) | collective-permute-done | bytes 65568 | tf_op jit(solution)/shard_map/ppermute | solution.py:381
  (78 shorter events, 23.7 us)
Async XLA Ops:
  0.6 14.9 %all-to-all-start = ((bf16[8,2,32,512]{3,2,1,0:T(8,128)(2,1)}), bf16[8,2,32,512]{3,2,1,0:T(8,128)(2,1)S(1)}, u32[]{:S(2)}, u32[]{:S(2)}) async-start(bf16[8,2,32,512]{3,2,1,0:T(8,128)(2,1)} %bitcast.68), calls=%async_computation | async-start | bytes 1048576 | tf_op jit(solution)/shard_map/all_to_all | solution.py:449
  7.0 16.4 %collective-permute-start = (bf16[16,8,512]{2,1,0:T(8,128)(2,1)S(1)}, bf16[16,8,512]{2,1,0:T(8,128)(2,1)S(1)}, u32[]{:S(2)}, u32[]{:S(2)}) collective-permute-start(bf16[16,8,512]{2,1,0:T(8,128)(2,1)S(1)} %get-tuple-element.158), channel_id=1, source_target_pairs={{0,8},{8,0},{16,24},{24,16},{1,9},{9,1},{17,25},{25,17},{2,10},{10... | collective-permute-start | bytes 393224 | tf_op jit(solution)/shard_map/ppermute | solution.py:381
  8.6 14.8 %collective-permute-start.1 = (bf16[16,8,512]{2,1,0:T(8,128)(2,1)S(1)}, bf16[16,8,512]{2,1,0:T(8,128)(2,1)S(1)}, u32[]{:S(2)}, u32[]{:S(2)}) collective-permute-start(bf16[16,8,512]{2,1,0:T(8,128)(2,1)S(1)} %get-tuple-element.160), channel_id=1, source_target_pairs={{0,16},{8,24},{16,0},{24,8},{1,17},{9,25},{17,1},{25,9},{2,18},{10... | collective-permute-start | bytes 393224 | tf_op jit(solution)/shard_map/ppermute | solution.py:381
  11.2 12.2 %collective-permute-start.2 = (bf16[16,8,512]{2,1,0:T(8,128)(2,1)S(1)}, bf16[16,8,512]{2,1,0:T(8,128)(2,1)S(1)}, u32[]{:S(2)}, u32[]{:S(2)}) collective-permute-start(bf16[16,8,512]{2,1,0:T(8,128)(2,1)S(1)} %get-tuple-element.157), channel_id=1, source_target_pairs={{0,24},{8,16},{16,8},{24,0},{1,25},{9,17},{17,9},{25,1},{2,26},{10... | collective-permute-start | bytes 393224 | tf_op jit(solution)/shard_map/ppermute | solution.py:381
  24.1 20.0 %all-to-all-start.1 = ((bf16[32,16,512]{2,1,0:T(8,128)(2,1)}), bf16[32,16,512]{2,1,0:T(8,128)(2,1)S(1)}, u32[]{:S(2)}, u32[]{:S(2)}) async-start(bf16[32,16,512]{2,1,0:T(8,128)(2,1)} %bitcast.71), calls=%async_computation.1 | async-start | bytes 1048576 | tf_op jit(solution)/shard_map/all_to_all | solution.py:447
  56.7 18.7 %all-to-all-start.2 = ((bf16[32,16,512]{2,1,0:T(8,128)(2,1)}), bf16[32,16,512]{2,1,0:T(8,128)(2,1)S(1)}, u32[]{:S(2)}, u32[]{:S(2)}) async-start(bf16[32,16,512]{2,1,0:T(8,128)(2,1)} %bitcast.70), calls=%async_computation.2 | async-start | bytes 1048576 | tf_op jit(solution)/shard_map/all_to_all | solution.py:447
  69.8 17.3 %collective-permute-start.7 = (bf16[4,64,512]{2,1,0:T(8,128)(2,1)S(1)}, bf16[4,64,512]{2,1,0:T(8,128)(2,1)S(1)}, u32[]{:S(2)}, u32[]{:S(2)}) collective-permute-start(bf16[4,64,512]{2,1,0:T(8,128)(2,1)S(1)} %get-tuple-element.105), channel_id=1, source_target_pairs={{0,2},{1,3},{2,0},{3,1},{4,6},{5,7},{6,4},{7,5},{8,10},{9,11},{10,... | collective-permute-start | bytes 786440 | tf_op jit(solution)/shard_map/ppermute | solution.py:381
  71.6 15.5 %collective-permute-start.8 = (bf16[4,64,512]{2,1,0:T(8,128)(2,1)S(1)}, bf16[4,64,512]{2,1,0:T(8,128)(2,1)S(1)}, u32[]{:S(2)}, u32[]{:S(2)}) collective-permute-start(bf16[4,64,512]{2,1,0:T(8,128)(2,1)S(1)} %get-tuple-element.106), channel_id=1, source_target_pairs={{0,4},{1,5},{2,6},{3,7},{4,0},{5,1},{6,2},{7,3},{8,12},{9,13},{10,... | collective-permute-start | bytes 786440 | tf_op jit(solution)/shard_map/ppermute | solution.py:381
  73.1 14.1 %collective-permute-start.9 = (bf16[4,64,512]{2,1,0:T(8,128)(2,1)S(1)}, bf16[4,64,512]{2,1,0:T(8,128)(2,1)S(1)}, u32[]{:S(2)}, u32[]{:S(2)}) collective-permute-start(bf16[4,64,512]{2,1,0:T(8,128)(2,1)S(1)} %get-tuple-element.107), channel_id=1, source_target_pairs={{0,6},{1,7},{2,4},{3,5},{4,2},{5,3},{6,0},{7,1},{8,14},{9,15},{10,... | collective-permute-start | bytes 786440 | tf_op jit(solution)/shard_map/ppermute | solution.py:381
  73.4 13.7 %collective-permute-start.10 = (bf16[128,512]{1,0:T(8,128)(2,1)}, bf16[128,512]{1,0:T(8,128)(2,1)S(1)}, u32[]{:S(2)}, u32[]{:S(2)}) collective-permute-start(bf16[128,512]{1,0:T(8,128)(2,1)} %get-tuple-element.125), channel_id=1, source_target_pairs={{0,8},{8,0},{16,24},{24,16},{1,9},{9,1},{17,25},{25,17},{2,10},{10... | collective-permute-start | bytes 393224 | tf_op jit(solution)/shard_map/ppermute | solution.py:381
  88.0 4.6 %collective-permute-start.11 = (bf16[4,64,512]{2,1,0:T(8,128)(2,1)}, bf16[4,64,512]{2,1,0:T(8,128)(2,1)S(1)}, u32[]{:S(2)}, u32[]{:S(2)}) collective-permute-start(bf16[4,64,512]{2,1,0:T(8,128)(2,1)} %get-tuple-element.141), channel_id=1, source_target_pairs={{0,1},{1,0},{2,3},{3,2},{4,5},{5,4},{6,7},{7,6},{8,9},{9,8},{10,11... | collective-permute-start | bytes 786440 | tf_op jit(solution)/shard_map/ppermute | solution.py:381
  88.0 4.6 %collective-permute-start.12 = (bf16[4,64,512]{2,1,0:T(8,128)(2,1)}, bf16[4,64,512]{2,1,0:T(8,128)(2,1)S(1)}, u32[]{:S(2)}, u32[]{:S(2)}) collective-permute-start(bf16[4,64,512]{2,1,0:T(8,128)(2,1)} %get-tuple-element.142), channel_id=1, source_target_pairs={{0,1},{1,0},{2,3},{3,2},{4,5},{5,4},{6,7},{7,6},{8,9},{9,8},{10,11... | collective-permute-start | bytes 786440 | tf_op jit(solution)/shard_map/ppermute | solution.py:381
  89.0 14.8 %all-to-all-start.3 = ((bf16[8,2,32,512]{3,2,1,0:T(8,128)(2,1)}), bf16[8,2,32,512]{3,2,1,0:T(8,128)(2,1)S(1)}, u32[]{:S(2)}, u32[]{:S(2)}) async-start(bf16[8,2,32,512]{3,2,1,0:T(8,128)(2,1)} %get-tuple-element.130), calls=%async_computation.3 | async-start | bytes 1048576 | tf_op jit(solution)/shard_map/all_to_all | solution.py:501
  94.0 9.8 %collective-permute-start.15 = (bf16[128,512]{1,0:T(8,128)(2,1)}, bf16[128,512]{1,0:T(8,128)(2,1)S(1)}, u32[]{:S(2)}, u32[]{:S(2)}) collective-permute-start(bf16[128,512]{1,0:T(8,128)(2,1)} %get-tuple-element.149), channel_id=1, source_target_pairs={{0,16},{8,24},{16,0},{24,8},{1,17},{9,25},{17,1},{25,9},{2,18},{10... | collective-permute-start | bytes 393224 | tf_op jit(solution)/shard_map/ppermute | solution.py:381
  97.3 11.6 %collective-permute-start.17 = (bf16[4,64,512]{2,1,0:T(8,128)(2,1)S(1)}, bf16[4,64,512]{2,1,0:T(8,128)(2,1)S(1)}, u32[]{:S(2)}, u32[]{:S(2)}) collective-permute-start(bf16[4,64,512]{2,1,0:T(8,128)(2,1)S(1)} %get-tuple-element.146), channel_id=1, source_target_pairs={{0,2},{1,3},{2,0},{3,1},{4,6},{5,7},{6,4},{7,5},{8,10},{9,11},{10,... | collective-permute-start | bytes 786440 | tf_op jit(solution)/shard_map/ppermute | solution.py:381
  99.4 12.5 %collective-permute-start.18 = (bf16[4,64,512]{2,1,0:T(8,128)(2,1)S(1)}, bf16[4,64,512]{2,1,0:T(8,128)(2,1)S(1)}, u32[]{:S(2)}, u32[]{:S(2)}) collective-permute-start(bf16[4,64,512]{2,1,0:T(8,128)(2,1)S(1)} %get-tuple-element.147), channel_id=1, source_target_pairs={{0,4},{1,5},{2,6},{3,7},{4,0},{5,1},{6,2},{7,3},{8,12},{9,13},{10,... | collective-permute-start | bytes 786440 | tf_op jit(solution)/shard_map/ppermute | solution.py:381
  100.8 12.6 %collective-permute-start.19 = (bf16[4,64,512]{2,1,0:T(8,128)(2,1)S(1)}, bf16[4,64,512]{2,1,0:T(8,128)(2,1)S(1)}, u32[]{:S(2)}, u32[]{:S(2)}) collective-permute-start(bf16[4,64,512]{2,1,0:T(8,128)(2,1)S(1)} %get-tuple-element.148), channel_id=1, source_target_pairs={{0,6},{1,7},{2,4},{3,5},{4,2},{5,3},{6,0},{7,1},{8,14},{9,15},{10,... | collective-permute-start | bytes 786440 | tf_op jit(solution)/shard_map/ppermute | solution.py:381
  105.1 9.9 %collective-permute-start.23 = (bf16[4,16,512]{2,1,0:T(8,128)(2,1)S(1)}, bf16[4,16,512]{2,1,0:T(8,128)(2,1)S(1)}, u32[]{:S(2)}, u32[]{:S(2)}) collective-permute-start(bf16[4,16,512]{2,1,0:T(8,128)(2,1)S(1)} %get-tuple-element.164), channel_id=1, source_target_pairs={{0,8},{8,0},{16,24},{24,16},{1,9},{9,1},{17,25},{25,17},{2,10},{10... | collective-permute-start | bytes 196616 | tf_op jit(solution)/shard_map/ppermute | solution.py:381
  105.3 11.3 %collective-permute-start.24 = (bf16[4,16,512]{2,1,0:T(8,128)(2,1)S(1)}, bf16[4,16,512]{2,1,0:T(8,128)(2,1)S(1)}, u32[]{:S(2)}, u32[]{:S(2)}) collective-permute-start(bf16[4,16,512]{2,1,0:T(8,128)(2,1)S(1)} %get-tuple-element.165), channel_id=1, source_target_pairs={{0,16},{8,24},{16,0},{24,8},{1,17},{9,25},{17,1},{25,9},{2,18},{10... | collective-permute-start | bytes 196616 | tf_op jit(solution)/shard_map/ppermute | solution.py:381
  108.9 9.2 %collective-permute-start.25 = (bf16[4,16,512]{2,1,0:T(8,128)(2,1)S(1)}, bf16[4,16,512]{2,1,0:T(8,128)(2,1)S(1)}, u32[]{:S(2)}, u32[]{:S(2)}) collective-permute-start(bf16[4,16,512]{2,1,0:T(8,128)(2,1)S(1)} %get-tuple-element.166), channel_id=1, source_target_pairs={{0,24},{8,16},{16,8},{24,0},{1,25},{9,17},{17,9},{25,1},{2,26},{10... | collective-permute-start | bytes 196616 | tf_op jit(solution)/shard_map/ppermute | solution.py:381
  111.9 13.9 %collective-permute-start.16 = (bf16[128,512]{1,0:T(8,128)(2,1)}, bf16[128,512]{1,0:T(8,128)(2,1)S(1)}, u32[]{:S(2)}, u32[]{:S(2)}) collective-permute-start(bf16[128,512]{1,0:T(8,128)(2,1)} %get-tuple-element.151), channel_id=1, source_target_pairs={{0,24},{8,16},{16,8},{24,0},{1,25},{9,17},{17,9},{25,1},{2,26},{10... | collective-permute-start | bytes 393224 | tf_op jit(solution)/shard_map/ppermute | solution.py:381
  113.6 5.0 %collective-permute-start.20 = (bf16[4,16,512]{2,1,0:T(8,128)(2,1)S(1)}, bf16[4,16,512]{2,1,0:T(8,128)(2,1)S(1)}, u32[]{:S(2)}, u32[]{:S(2)}) collective-permute-start(bf16[4,16,512]{2,1,0:T(8,128)(2,1)S(1)} %get-tuple-element.161), channel_id=1, source_target_pairs={{0,8},{8,0},{16,24},{24,16},{1,9},{9,1},{17,25},{25,17},{2,10},{10... | collective-permute-start | bytes 196616 | tf_op jit(solution)/shard_map/ppermute | solution.py:381
  114.9 10.1 %collective-permute-start.21 = (bf16[4,16,512]{2,1,0:T(8,128)(2,1)S(1)}, bf16[4,16,512]{2,1,0:T(8,128)(2,1)S(1)}, u32[]{:S(2)}, u32[]{:S(2)}) collective-permute-start(bf16[4,16,512]{2,1,0:T(8,128)(2,1)S(1)} %get-tuple-element.162), channel_id=1, source_target_pairs={{0,16},{8,24},{16,0},{24,8},{1,17},{9,25},{17,1},{25,9},{2,18},{10... | collective-permute-start | bytes 196616 | tf_op jit(solution)/shard_map/ppermute | solution.py:381
  116.6 8.5 %collective-permute-start.22 = (bf16[4,16,512]{2,1,0:T(8,128)(2,1)S(1)}, bf16[4,16,512]{2,1,0:T(8,128)(2,1)S(1)}, u32[]{:S(2)}, u32[]{:S(2)}) collective-permute-start(bf16[4,16,512]{2,1,0:T(8,128)(2,1)S(1)} %get-tuple-element.163), channel_id=1, source_target_pairs={{0,24},{8,16},{16,8},{24,0},{1,25},{9,17},{17,9},{25,1},{2,26},{10... | collective-permute-start | bytes 196616 | tf_op jit(solution)/shard_map/ppermute | solution.py:381
  (16 other events, 83.9 us)
